TPU v7x, 32 devices: a whole 2x2x4 slice. The times are simulated.
32 devices in a mesh: wide: 8 (over z, x), narrow: 4 (over y, core).
Axes of the slice: x: 2, y: 2, z: 4, core: 2. Of those that a mesh axis runs over, the one named last changes fastest.
Arguments:
- records: bfloat16 [8, 512, 12288], P(None, 'narrow', 'wide'), may hold values from -6 to 6
- taps: float32 [201], replicated, may hold values from -0.4375 to 0.4375
- pair_sources: int32 [8, 4], replicated, may hold values from 0 to 7, as said below
- pair_counts: int32 [8], P('wide'), may hold values from 1 to 4, as said below
Outputs:
- correlations: bfloat16 [8, 4, 512, 32, 256], P('wide', None, 'narrow')
Inputs may be any that keep to these rules, and one draw needn't show every extreme that they name: `pair_sources`: each row lists 4 different blocks; only the first pair_counts[r] of row r are paired with r. `pair_counts`: some block has 4 pairs in every draw.
All inputs are finite; a program needn't handle non-finite values.
Results may differ from a plain program's by a relative error of at most 0.0096.
Values may be sent and summed in bfloat16 or wider, within the bound.
No kernel may reach another device: no remote copies, remote signals or barrier semaphores. Data moves between devices by JAX's collectives and lax.ppermute only.
A program may use at most 128 MiB of HBM per device.

v0:
```python
import math

import jax
import jax.numpy as jnp
from jax import lax
from jax.sharding import PartitionSpec as P

BLOCK_CHANNELS = 512
VIRTUAL_SOURCES = 32
TAPS = 201
WLEN = 512
FREQUENCY_BINS = 128
F_LO = 4
LAG_COUNT = 256
MAX_PAIRED_SRC = 4


def shifted(shard, axis, by):
    count = lax.axis_size(axis)
    pairs = [(i, i + by) for i in range(count) if 0 <= i + by < count]
    return lax.ppermute(shard, axis, pairs)


def taps_matrix(taps):
    kernel = taps.astype(jnp.bfloat16)
    span = WLEN + TAPS - 1
    padded = jnp.concatenate([kernel[::-1], jnp.zeros((WLEN,), kernel.dtype)])
    tiled = jnp.tile(padded, WLEN)[: WLEN * span].reshape(WLEN, span)
    return tiled.T


def dft_table():
    times = jnp.arange(WLEN, dtype=jnp.int32)[:, None]
    bins = (F_LO + jnp.arange(FREQUENCY_BINS, dtype=jnp.int32))[None, :]
    phase = jnp.mod(times * bins, WLEN)
    angle = phase.astype(jnp.float32) * (2.0 * math.pi / WLEN)
    scale = 1.0 / math.sqrt(WLEN)
    return jnp.concatenate([jnp.cos(angle) * scale, -jnp.sin(angle) * scale], 1).astype(
        jnp.bfloat16
    )


def lag_table():
    bins = (F_LO + jnp.arange(FREQUENCY_BINS, dtype=jnp.int32))[:, None]
    lags = (jnp.arange(LAG_COUNT, dtype=jnp.int32) - LAG_COUNT // 2)[None, :]
    phase = jnp.mod(bins * lags, WLEN)
    angle = phase.astype(jnp.float32) * (2.0 * math.pi / WLEN)
    scale = 1.0 / math.sqrt(FREQUENCY_BINS)
    return jnp.concatenate([jnp.cos(angle) * scale, -jnp.sin(angle) * scale], 0).astype(
        jnp.bfloat16
    )


def cross_spectra(recv, source_indices, count):
    rec_re = recv[:, :, 0]
    rec_im = recv[:, :, 1]
    src_re = source_indices[:, :, :, 0]
    src_im = source_indices[:, :, :, 1]
    form = "iwf,kjwf->kijf"
    real = jnp.einsum(form, rec_re, src_re, preferred_element_type=jnp.float32) + jnp.einsum(
        form, rec_im, src_im, preferred_element_type=jnp.float32
    )
    imag = jnp.einsum(form, rec_im, src_re, preferred_element_type=jnp.float32) - jnp.einsum(
        form, rec_re, src_im, preferred_element_type=jnp.float32
    )
    scale = 1.0 / math.sqrt(recv.shape[1])
    live = (jnp.arange(MAX_PAIRED_SRC, dtype=jnp.int32) < count).astype(jnp.float32)[
        :, None, None, None
    ]
    return jnp.stack([real * scale * live, imag * scale * live], 3).astype(jnp.bfloat16)


def on_device(records, taps, pair_sources, pair_counts):
    channel_blocks, subset_channels, time_dev = records.shape
    windows_per_shard = time_dev // WLEN
    main = records.reshape(channel_blocks * subset_channels, windows_per_shard, WLEN)
    tails = main[:, :, WLEN - (TAPS - 1) :]
    history = shifted(tails[:, windows_per_shard - 1], "wide", 1)
    previous = jnp.concatenate([history[:, None], tails[:, : windows_per_shard - 1]], 1)
    windows = jnp.concatenate([previous, main], 2)
    whitened = jnp.dot(windows, taps_matrix(taps), preferred_element_type=jnp.float32).astype(
        jnp.bfloat16
    )
    block_spectrum = jnp.dot(whitened, dft_table(), preferred_element_type=jnp.float32).astype(
        jnp.bfloat16
    )
    block_spectrum = block_spectrum.reshape(
        channel_blocks, subset_channels, windows_per_shard, 2, FREQUENCY_BINS
    )
    virtual_channels = block_spectrum[:, :: BLOCK_CHANNELS // VIRTUAL_SOURCES]
    source_slots = pair_sources.reshape(-1)
    count = pair_counts[0]
    finished_pairs = lax.all_gather(virtual_channels, "narrow", axis=1, tiled=True)
    picked_sources = jnp.take(finished_pairs, source_slots, axis=0).reshape(
        channel_blocks, MAX_PAIRED_SRC * VIRTUAL_SOURCES, windows_per_shard, 2, FREQUENCY_BINS
    )
    recv = lax.all_to_all(block_spectrum, "wide", split_axis=0, concat_axis=2, tiled=True)
    source_indices = lax.all_to_all(picked_sources, "wide", split_axis=0, concat_axis=2, tiled=True)
    source_blocks = source_indices[0].reshape(
        MAX_PAIRED_SRC, VIRTUAL_SOURCES, source_indices.shape[2], 2, source_indices.shape[4]
    )
    cross = cross_spectra(recv[0], source_blocks, count)
    lag_domain = jnp.dot(
        cross.reshape(-1, 2 * FREQUENCY_BINS), lag_table(), preferred_element_type=jnp.float32
    )
    return lag_domain.astype(jnp.bfloat16).reshape(
        1, MAX_PAIRED_SRC, subset_channels, VIRTUAL_SOURCES, LAG_COUNT
    )


def solution(mesh):
    return jax.shard_map(
        on_device,
        mesh=mesh,
        in_specs=(P(None, "narrow", "wide"), P(), P(), P("wide")),
        out_specs=P("wide", None, "narrow", None, None),
        check_vma=False,
    )
```

profile of v0, /device:TPU:0, one launch (start us, length us, event | category | flops | bytes accessed | tf_op | source)
XLA Modules:
  0.0 207.3 jit_solution(11192349580006985657)
XLA Ops:
  0.0 3.8 %copy.33 = bf16[8,128,1536]{1,0,2:T(8,128)(2,1)S(1)} copy(bf16[8,128,1536]{2,1,0:T(8,128)(2,1)} %param.4) | data formatting | bytes 6291456 | tf_op args[0]
  3.8 3.3 %reshape.77 = bf16[1024,3,512]{0,2,1:T(8,128)(2,1)} reshape(bf16[8,128,1536]{1,0,2:T(8,128)(2,1)S(1)} %copy.33) | data formatting | bytes 6291456 | tf_op jit(solution)/shard_map/reshape | solution.py:76
  8.3 5.6 %collective-permute-start = (bf16[1024,200]{0,1:T(8,128)(2,1)S(1)}, bf16[1024,200]{0,1:T(8,128)(2,1)}, u32[]{:S(2)}, u32[]{:S(2)}) collective-permute-start(bf16[1024,200]{0,1:T(8,128)(2,1)S(1)} %slice_bitcast_fusion), channel_id=1, source_target_pairs={{0,4},{4,8},{8,12},{12,16},{16,20},{20,24},{24,28},{1,5},{5,9},{9,... | collective-permute-start | bytes 1228808 | tf_op jit(solution)/shard_map/ppermute | solution.py:21
  13.9 2.1 %slice.38 = bf16[1024,2,200]{0,2,1:T(8,128)(2,1)} slice(bf16[1024,3,512]{0,2,1:T(8,128)(2,1)} %reshape.77), slice={[0:1024], [0:2], [312:512]} | slice | bytes 1638400 | tf_op jit(solution)/shard_map/slice | solution.py:79
  16.1 1.3 copy.36
  22.9 3.2 %tile.10 = bf16[365056]{0:T(1024)(128)(2,1)} reshape(bf16[512,713]{1,0:T(8,128)(2,1)} %tile.4) | data formatting | bytes 1460224 | tf_op jit(solution)/shard_map/tile | solution.py:28
  26.1 2.0 slice.39
  28.1 3.7 %reshape.78 = bf16[512,712]{1,0:T(8,128)(2,1)} reshape(bf16[364544]{0:T(1024)(128)(2,1)} %slice.39) | data formatting | bytes 1458176 | tf_op jit(solution)/shard_map/reshape | solution.py:28
  31.8 1.3 reshape.80
  34.2 1.3 copy.32
  35.6 1.3 broadcast_in_dim.23
  36.9 1.3 broadcast_in_dim.24
  39.5 1.8 multiply_convert_fusion.3
  41.2 6.4 %fusion.22 = bf16[1024,3,256]{2,0,1:T(8,128)(2,1)} fusion(bf16[1024,3,512]{0,2,1:T(8,128)(2,1)S(1)} %copy-done.3, bf16[1024,2,200]{0,2,1:T(8,128)(2,1)} %slice.38, bf16[1024,1,200]{0,2,1:T(8,128)(2,1)} %bitcast.1, bf16[512,712]{1,0:T(8,128)(2,1)} %reshape.78, bf16[512,128]{1,0:T(8,128)(2,1)} %get-tuple-element.12, bf16[512,128]{1,0:T(8,128)(2,1)} %get-tuple-element.11), kind=kOutput, calls=%fused_computation.23 | convolution fusion | flops 3061071872 | bytes 6938624 | tf_op jit(solution)/shard_map/dot_general | solution.py:84
  47.6 2.4 %reshape.79 = bf16[8,128,3,2,128]{4,3,1,0,2:T(2,128)(2,1)S(1)} reshape(bf16[1024,3,256]{2,0,1:T(8,128)(2,1)} %fusion.22) | data formatting | bytes 3145728 | tf_op jit(solution)/shard_map/reshape | solution.py:87
  50.0 1.6 copy.35
  51.5 10.4 %slice.30 = bf16[8,8,3,2,128]{4,1,3,2,0:T(8,128)(2,1)S(1)} slice(bf16[8,128,3,2,128]{4,1,3,2,0:T(8,128)(2,1)} %copy.35), slice={[0:8:1], [0:128:16], [0:3:1], [0:2:1], [0:128:1]} | slice | bytes 196608 | tf_op jit(solution)/shard_map/slice | solution.py:90
  62.0 6.5 %all_gather.3 = bf16[8,32,3,2,128]{4,1,3,2,0:T(8,128)(2,1)S(1)} all-gather(bf16[8,8,3,2,128]{4,1,3,2,0:T(8,128)(2,1)S(1)} %slice.30), channel_id=1, replica_groups=mesh['wide'=8,'narrow'=4] {'narrow'}, dimensions={1}, use_global_device_ids=true | all-gather | bytes 491520 | tf_op jit(solution)/shard_map/all_gather | solution.py:93
  70.2 41.4 %all_to_all.30 = bf16[8,128,3,2,128]{4,1,3,2,0:T(8,128)(2,1)S(1)} all-to-all(bf16[8,128,3,2,128]{4,1,3,2,0:T(8,128)(2,1)S(1)} %copy.38), channel_id=1, replica_groups=mesh['wide'=8,'narrow'=4] {'wide'}, dimensions={0} | all-to-all | bytes 3145728 | tf_op jit(solution)/shard_map/all_to_all | solution.py:98
  111.6 3.8 %all-to-all-start.1 = ((bf16[8,128,3,2,128]{4,1,3,2,0:T(8,128)(2,1)}), bf16[8,128,3,2,128]{4,1,3,2,0:T(8,128)(2,1)S(1)}, u32[]{:S(2)}, u32[]{:S(2)}) async-start(bf16[8,128,3,2,128]{4,1,3,2,0:T(8,128)(2,1)} %copy.35), calls=%async_computation.1 | async-start | bytes 3145728 | tf_op jit(solution)/shard_map/all_to_all | solution.py:97
  116.6 1.4 fusion.52
  118.1 5.9 %copy.49 = bf16[4,32,24,1,128]{1,2,0,4,3:T(8,128)(2,1)} copy(bf16[4,32,24,1,128]{4,1,0,3,2:T(8,128)(2,1)} %get-tuple-element.8) | data formatting | bytes 1572864
  123.9 28.4 %all-to-all-done.1 = bf16[8,128,3,2,128]{4,1,3,2,0:T(8,128)(2,1)S(1)} async-done(((bf16[8,128,3,2,128]{4,1,3,2,0:T(8,128)(2,1)}), bf16[8,128,3,2,128]{4,1,3,2,0:T(8,128)(2,1)S(1)}, u32[]{:S(2)}, u32[]{:S(2)}) %all-to-all-start.1) | async-done | bytes 1572896 | tf_op jit(solution)/shard_map/all_to_all | solution.py:97
  154.6 5.5 %copy.51 = bf16[4,32,24,1,128]{1,2,0,4,3:T(8,128)(2,1)S(1)} copy(bf16[4,32,24,1,128]{4,1,0,3,2:T(8,128)(2,1)} %get-tuple-element.7) | data formatting | bytes 1572864
  160.1 2.4 %copy.52 = bf16[128,24,1,128]{0,1,3,2:T(8,128)(2,1)} copy(bf16[128,24,1,128]{3,0,2,1:T(8,128)(2,1)} %get-tuple-element.6) | data formatting | bytes 1572864
  162.6 3.6 %fusion.14 = f32[128,4,32,128]{3,2,1,0:T(8,128)S(1)} fusion(bf16[4,32,24,1,128]{1,2,0,4,3:T(8,128)(2,1)} %copy.49, bf16[128,24,1,128]{0,1,3,2:T(8,128)(2,1)} %copy.50), kind=kOutput, calls=%fused_computation.19 | convolution fusion | flops 100663296 | bytes 9961472 | tf_op jit(solution)/shard_map/iwf,kjwf->kijf/dot_general | solution.py:60
  166.2 1.4 fusion.12
  167.6 3.5 %fusion.8 = bf16[4,128,32,1,128]{1,2,0,4,3:T(8,128)(2,1)} fusion(f32[128,4,32,128]{3,2,1,0:T(8,128)S(1)} %fusion.14, f32[4]{0:T(128)S(1)} %compare_select_fusion.2, bf16[4,32,24,1,128]{1,2,0,4,3:T(8,128)(2,1)S(1)} %copy.51, bf16[128,24,1,128]{0,1,3,2:T(8,128)(2,1)S(1)} %copy-done.2), kind=kOutput, calls=%fused_computation.13 | convolution fusion | flops 106954752 | bytes 14155792 | tf_op jit(solution)/shard_map/iwf,kjwf->kijf/dot_general | solution.py:60
  171.1 3.5 %fusion.9 = bf16[4,128,32,1,128]{1,2,0,4,3:T(8,128)(2,1)} fusion(f32[128,4,32,128]{3,2,1,0:T(8,128)S(1)} %fusion.12, f32[4]{0:T(128)S(1)} %compare_select_fusion.2, bf16[4,32,24,1,128]{1,2,0,4,3:T(8,128)(2,1)S(1)} %copy.51, bf16[128,24,1,128]{0,1,3,2:T(8,128)(2,1)S(1)} %copy-done.1), kind=kOutput, calls=%fused_computation.14 | convolution fusion | flops 106954752 | bytes 14155792 | tf_op jit(solution)/shard_map/iwf,kjwf->kijf/dot_general | solution.py:63
  174.6 7.6 %pad_maximum_fusion = bf16[4,128,32,2,128]{1,2,0,4,3:T(8,128)(2,1)} fusion(bf16[4,128,32,1,128]{1,2,0,4,3:T(8,128)(2,1)} %fusion.9, bf16[4,128,32,1,128]{1,2,0,4,3:T(8,128)(2,1)} %fusion.8), kind=kLoop, calls=%fused_computation.4 | loop fusion | flops 4194304 | bytes 16777216 | tf_op jit(solution)/shard_map/stack | solution.py:70
  182.2 15.9 %copy.44 = bf16[4,128,32,2,128]{4,3,2,1,0:T(2,128)(2,1)} copy(bf16[4,128,32,2,128]{1,2,0,4,3:T(8,128)(2,1)} %pad_maximum_fusion) | data formatting | bytes 16777216 | tf_op jit(solution)/shard_map/stack | solution.py:70
  198.1 9.1 %convolution_convert_fusion = bf16[16384,256]{1,0:T(8,128)(2,1)} fusion(bf16[2048,8,2,128]{3,2,1,0:T(2,128)(2,1)} %bitcast.72, bf16[128,256]{1,0:T(8,128)(2,1)S(1)} %get-tuple-element.10, bf16[128,256]{1,0:T(8,128)(2,1)S(1)} %get-tuple-element.9), kind=kOutput, calls=%fused_computation.1 | convolution fusion | flops 2151940096 | bytes 16908288 | tf_op jit(solution)/shard_map/dot_general | solution.py:103
  (34 shorter events, 13.5 us)
Async XLA Ops:
  7.1 34.1 %copy-start.3 = (bf16[1024,3,512]{0,2,1:T(8,128)(2,1)S(1)}, bf16[1024,3,512]{0,2,1:T(8,128)(2,1)}, u32[]{:S(2)}) copy-start(bf16[1024,3,512]{0,2,1:T(8,128)(2,1)} %reshape.77) | copy-start | bytes 9437188
  8.3 32.9 %collective-permute-start = (bf16[1024,200]{0,1:T(8,128)(2,1)S(1)}, bf16[1024,200]{0,1:T(8,128)(2,1)}, u32[]{:S(2)}, u32[]{:S(2)}) collective-permute-start(bf16[1024,200]{0,1:T(8,128)(2,1)S(1)} %slice_bitcast_fusion), channel_id=1, source_target_pairs={{0,4},{4,8},{8,12},{12,16},{16,20},{20,24},{24,28},{1,5},{5,9},{9,... | collective-permute-start | bytes 1228808 | tf_op jit(solution)/shard_map/ppermute | solution.py:21
  38.3 3.0 %copy-start.5 = (s32[128]{0:T(128)}, s32[128]{0:T(128)S(1)}, u32[]{:S(2)}) copy-start(s32[128]{0:T(128)S(1)} %iota_add_fusion.1) | copy-start | bytes 1540
  51.5 18.3 %copy-start.4 = (pred[8,128]{1,0:T(8,128)(4,1)S(1)}, pred[8,128]{1,0:T(8,128)(4,1)}, u32[]{:S(2)}) copy-start(pred[8,128]{1,0:T(8,128)(4,1)} %broadcast_in_dim.24) | copy-start | bytes 3076
  70.0 46.0 %copy-start.6 = (s32[128]{0:T(128)S(1)}, s32[128]{0:T(128)}, u32[]{:S(2)}) copy-start(s32[128]{0:T(128)} %copy-done.5) | copy-start | bytes 1540
  111.6 40.7 %all-to-all-start.1 = ((bf16[8,128,3,2,128]{4,1,3,2,0:T(8,128)(2,1)}), bf16[8,128,3,2,128]{4,1,3,2,0:T(8,128)(2,1)S(1)}, u32[]{:S(2)}, u32[]{:S(2)}) async-start(bf16[8,128,3,2,128]{4,1,3,2,0:T(8,128)(2,1)} %copy.35), calls=%async_computation.1 | async-start | bytes 3145728 | tf_op jit(solution)/shard_map/all_to_all | solution.py:97
  162.6 3.6 %copy-start = (bf16[4,32,24,1,128]{1,2,0,4,3:T(8,128)(2,1)S(1)}, bf16[4,32,24,1,128]{1,2,0,4,3:T(8,128)(2,1)}, u32[]{:S(2)}) copy-start(bf16[4,32,24,1,128]{1,2,0,4,3:T(8,128)(2,1)} %copy.49) | copy-start | bytes 2359300
  162.6 3.6 %copy-start.2 = (bf16[128,24,1,128]{0,1,3,2:T(8,128)(2,1)S(1)}, bf16[128,24,1,128]{0,1,3,2:T(8,128)(2,1)}, u32[]{:S(2)}) copy-start(bf16[128,24,1,128]{0,1,3,2:T(8,128)(2,1)} %copy.52) | copy-start | bytes 2359300
  167.6 3.5 %copy-start.1 = (bf16[128,24,1,128]{0,1,3,2:T(8,128)(2,1)S(1)}, bf16[128,24,1,128]{0,1,3,2:T(8,128)(2,1)}, u32[]{:S(2)}) copy-start(bf16[128,24,1,128]{0,1,3,2:T(8,128)(2,1)} %copy.50) | copy-start | bytes 2359300
where the time goes:
time: 209 us; the launch traced here: 207 us
  local copies, waits for them, and re-layouts  78.2 us (37%)
  blocking collectives  47.9 us (23%)
  waiting for transfers between devices  28.4 us (14%)
  matrix products  27.5 us (13%)
  other arithmetic  15.1 us (7%)
  starting transfers between devices  9.37 us (4%)
    all_to_all x1, blocking collectives, on_device(): lax.all_to_all(picked_sources, 'wide', split_axis=0, concat_axis=2, tiled...  41.4 us
    all_to_all x1, waiting for transfers between devices, on_device(): lax.all_to_all(block_spectrum, 'wide', split_axis=0, concat_axis=2, tiled...  28.4 us
    unnamed x22, local copies, waits for them, and re-layouts  22.2 us
    another operation x1, local copies, waits for them, and re-layouts, cross_spectra(): jnp.stack([real * scale * live, imag * scale * live], 3)  15.9 us
    slice x1, local copies, waits for them, and re-layouts, on_device(): virtual_channels = block_spectrum[:, ::BLOCK_CHANNELS // VIRTUAL_SOURCES]  10.4 us
    dot_general x1, matrix products, on_device(): jnp.dot(cross.reshape(-1, 2 * FREQUENCY_BINS), lag_table(), preferred_ele...  9.13 us
    another operation x1, other arithmetic, cross_spectra(): jnp.stack([real * scale * live, imag * scale * live], 3)  7.63 us
    all_gather x1, blocking collectives, on_device(): lax.all_gather(virtual_channels, 'narrow', axis=1, tiled=True)  6.52 us
  transfers between devices with their start and end apart: 2, of which 1 were waited for; matrix products, arithmetic and copies ran while one was open for 17% of the time, Pallas kernels for 0%

commit v1 on v0

v1 whole, which is shorter than its diff:
```python
import math

import jax
import jax.numpy as jnp
import numpy as np
from jax import lax
from jax.experimental import pallas as pl
from jax.experimental.pallas import tpu as pltpu
from jax.sharding import PartitionSpec as P

BLOCK_CHANNELS = 512
VIRTUAL_SOURCES = 32
VSTEP = BLOCK_CHANNELS // VIRTUAL_SOURCES
TAPS = 201
WLEN = 512
HALF = 256
BINS = 128
F_LO = 4
LAG_COUNT = 256
SLOTS = 4
BF = jnp.bfloat16
F32 = jnp.float32
MIB = 1 << 20


def dft_table():
    times = np.arange(WLEN, dtype=np.int32)[:, None]
    bins = (F_LO + np.arange(BINS, dtype=np.int32))[None, :]
    angle = np.mod(times * bins, WLEN).astype(np.float32) * np.float32(2.0 * math.pi / WLEN)
    scale = np.float32(1.0 / math.sqrt(WLEN))
    return np.concatenate([np.cos(angle) * scale, -np.sin(angle) * scale], 1).astype(BF).astype(np.float32)


def lag_table():
    bins = (F_LO + np.arange(BINS, dtype=np.int32))[:, None]
    lags = (np.arange(LAG_COUNT, dtype=np.int32) - LAG_COUNT // 2)[None, :]
    angle = np.mod(bins * lags, WLEN).astype(np.float32) * np.float32(2.0 * math.pi / WLEN)
    scale = np.float32(1.0 / math.sqrt(BINS))
    return np.concatenate([np.cos(angle) * scale, -np.sin(angle) * scale], 0).astype(BF).astype(np.float32)


def dot(a, b):
    return lax.dot_general(a, b, (((1,), (0,)), ((), ())), preferred_element_type=F32)


def build_toeplitz(taps_ref, row, toeplitz):
    row[...] = jnp.zeros_like(row)
    row[:, 128 : 128 + TAPS] = jnp.broadcast_to(taps_ref[...].astype(BF).astype(F32), (8, TAPS))
    bands = jnp.broadcast_to(row[0:1, :], (128, 512))
    bands = pltpu.roll(bands, 0, 1, stride=1, stride_axis=0).astype(BF)
    zero = jnp.zeros((128, 128), BF)
    far, mid, near = [bands[:, at : at + 128] for at in (128, 256, 384)]
    toeplitz[:, :128] = jnp.concatenate([near, mid, far, zero], 0)
    toeplitz[:, 128:] = jnp.concatenate([zero, near, mid, far], 0)


def transform(blocks, wins, chans, toeplitz, table):
    rows = []
    for halo, rec in blocks:
        rows.append(jnp.concatenate([halo, rec[:, :HALF]], 1))
        rows += [rec[:, HALF * (m - 1) : HALF * (m + 1)] for m in range(1, 2 * wins)]
    white = dot(jnp.concatenate(rows, 0), toeplitz).astype(BF)
    pieces = [
        jnp.concatenate([white[2 * w * chans : (2 * w + 1) * chans], white[(2 * w + 1) * chans : (2 * w + 2) * chans]], 1)
        for w in range(len(blocks) * wins)
    ]
    return dot(jnp.concatenate(pieces, 0), table)


def select_kernel(nv, sizes, rec_ref, *refs):
    tails, virt_ref, near_ref = refs[: len(sizes)], refs[-2], refs[-1]
    time = rec_ref.shape[2]
    at = 0
    for tail, size in zip(tails, sizes):
        tail[...] = rec_ref[:, at : at + size, time - HALF :]
        at += size
    for b in range(rec_ref.shape[0]):
        rows = [rec_ref[b, r * VSTEP : (r + 1) * VSTEP, :].astype(F32)[0:1] for r in range(nv)]
        rows = jnp.concatenate(rows, 0)
        virt_ref[b * nv : (b + 1) * nv, :] = rows
        near_ref[b * nv : (b + 1) * nv, :] = rows[:, time - HALF :]


def select(records, sizes):
    nblk, chans, time = records.shape
    nv = chans // VSTEP
    per = 2 if nv % 8 == 0 else 4
    return pl.pallas_call(
        lambda *refs: select_kernel(nv, sizes, *refs),
        grid=(nblk // per,),
        in_specs=[pl.BlockSpec((per, chans, time), lambda b: (b, 0, 0))],
        out_specs=[pl.BlockSpec((per, size, HALF), lambda b: (b, 0, 0)) for size in sizes]
        + [pl.BlockSpec((per * nv, time), lambda b: (b, 0)), pl.BlockSpec((per * nv, HALF), lambda b: (b, 0))],
        out_shape=[jax.ShapeDtypeStruct((nblk, size, HALF), BF) for size in sizes]
        + [jax.ShapeDtypeStruct((nblk * nv, time), F32), jax.ShapeDtypeStruct((nblk * nv, HALF), F32)],
        compiler_params=pltpu.CompilerParams(vmem_limit_bytes=60 * MIB),
        cost_estimate=pl.CostEstimate(flops=0, bytes_accessed=records.size * 2, transcendentals=0),
        name="select",
    )(records)


def virtual_kernel(nblk, nv, wins, pairs_ref, virt_ref, halo_ref, taps_ref, table_ref, out_ref, toeplitz, row, held):
    build_toeplitz(taps_ref, row, toeplitz)
    count = nblk * nv
    block = (halo_ref[...].astype(BF), virt_ref[...].astype(BF))
    result = transform([block], wins, count, toeplitz[...], table_ref[...].astype(BF))
    for b in range(nblk):
        rows = [
            result[w * count + b * nv : w * count + (b + 1) * nv, p * BINS : (p + 1) * BINS]
            for w in range(wins)
            for p in range(2)
        ]
        held[b] = jnp.concatenate(rows, 0).astype(BF)
    for r in range(nblk):
        for k in range(SLOTS):
            out_ref[r, k] = held[pairs_ref[r, k]]


def virtual(virt, halo, taps, pairs, nblk):
    nv = virt.shape[0] // nblk
    wins = virt.shape[1] // WLEN
    rows = wins * 2 * nv
    shape = (nblk, SLOTS, rows, BINS)
    return pl.pallas_call(
        lambda *refs: virtual_kernel(nblk, nv, wins, *refs),
        grid_spec=pltpu.PrefetchScalarGridSpec(
            num_scalar_prefetch=1,
            grid=(1,),
            in_specs=[
                pl.BlockSpec(virt.shape, lambda t, s: (0, 0)),
                pl.BlockSpec(halo.shape, lambda t, s: (0, 0)),
                pl.BlockSpec((1, TAPS), lambda t, s: (0, 0)),
                pl.BlockSpec((WLEN, 2 * BINS), lambda t, s: (0, 0)),
            ],
            out_specs=pl.BlockSpec(shape, lambda t, s: (0, 0, 0, 0)),
            scratch_shapes=[
                pltpu.VMEM((WLEN, HALF), BF),
                pltpu.VMEM((8, 512), F32),
                pltpu.VMEM((nblk, rows, BINS), BF),
            ],
        ),
        out_shape=jax.ShapeDtypeStruct(shape, BF),
        compiler_params=pltpu.CompilerParams(vmem_limit_bytes=60 * MIB),
        cost_estimate=pl.CostEstimate(flops=10**8, bytes_accessed=virt.size * 8, transcendentals=0),
        name="virtual",
    )(pairs, virt, halo, taps, jnp.asarray(dft_table()))


def spectra_kernel(per, size, wins, rec_ref, halo_ref, taps_ref, table_ref, out_ref, toeplitz, table, row):
    @pl.when(pl.program_id(0) == 0)
    def _():
        table[...] = table_ref[...].astype(BF)
        build_toeplitz(taps_ref, row, toeplitz)

    blocks = [(halo_ref[b], rec_ref[b]) for b in range(per)]
    result = transform(blocks, wins, size, toeplitz[...], table[...]).astype(BF)
    for b in range(per):
        for w in range(wins):
            at = (b * wins + w) * size
            for p in range(2):
                out_ref[b, w, p] = result[at : at + size, p * BINS : (p + 1) * BINS]


def spectra(records, halo, taps, index):
    nblk, _, time = records.shape
    size = halo.shape[1]
    wins = time // WLEN
    per = 4
    return pl.pallas_call(
        lambda *refs: spectra_kernel(per, size, wins, *refs),
        grid=(nblk // per,),
        in_specs=[
            pl.BlockSpec((per, size, time), lambda b: (b, index, 0)),
            pl.BlockSpec((per, size, HALF), lambda b: (b, 0, 0)),
            pl.BlockSpec((1, TAPS), lambda b: (0, 0)),
            pl.BlockSpec((WLEN, 2 * BINS), lambda b: (0, 0)),
        ],
        out_specs=pl.BlockSpec((per, wins, 2, size, BINS), lambda b: (b, 0, 0, 0, 0)),
        out_shape=jax.ShapeDtypeStruct((nblk, wins, 2, size, BINS), BF),
        scratch_shapes=[pltpu.VMEM((WLEN, HALF), BF), pltpu.VMEM((WLEN, 2 * BINS), BF), pltpu.VMEM((8, 512), F32)],
        compiler_params=pltpu.CompilerParams(vmem_limit_bytes=60 * MIB),
        cost_estimate=pl.CostEstimate(
            flops=nblk * size * wins * 3 * 2 * 512 * 256, bytes_accessed=nblk * size * time * 3, transcendentals=0
        ),
        name="spectra",
    )(records, halo, taps, jnp.asarray(dft_table()))


def sources_kernel(nsrc, nnar, wins, nv, me_ref, *refs):
    virts, out_ref, held, turned = refs[:nnar], refs[-3], refs[-2], refs[-1]
    nw = nsrc * wins
    pitch = BINS + 8
    for n in range(nnar):
        held[me_ref[0] ^ n] = virts[n][...]

    def turn(src, carry):
        tiles = [[held[n, src, k].astype(F32) for n in range(nnar)] for k in range(SLOTS)]
        for w in range(wins):
            for p in range(2):
                at = (w * 2 + p) * nv
                tile = jnp.concatenate([tiles[k][n][at : at + nv] for k in range(SLOTS) for n in range(nnar)], 0)
                row = pl.multiple_of((p * nw + src * wins + w) * pitch, 8)
                turned[pl.ds(row, BINS), :] = tile.T
        return carry

    lax.fori_loop(0, nsrc, turn, 0, unroll=4)

    def one(j, carry):
        re = turned[pl.ds(j, nw, stride=pitch), :]
        im = turned[pl.ds(nw * pitch + j, nw, stride=pitch), :]
        top = jnp.concatenate([re, -im], 1)
        low = jnp.concatenate([im, re], 1)
        out_ref[j] = jnp.concatenate([top, low], 0).astype(BF)
        return carry

    lax.fori_loop(0, BINS, one, 0, unroll=8)


def sources(virts, me, wins, nv):
    nnar, nsrc = len(virts), virts[0].shape[0]
    nw = nsrc * wins
    width = SLOTS * nnar * nv
    return pl.pallas_call(
        lambda *refs: sources_kernel(nsrc, nnar, wins, nv, *refs),
        grid_spec=pltpu.PrefetchScalarGridSpec(
            num_scalar_prefetch=1,
            grid=(1,),
            in_specs=[pl.BlockSpec(v.shape, lambda t, e: (0,) * 4) for v in virts],
            out_specs=pl.BlockSpec((BINS, 2 * nw, 2 * width), lambda t, e: (0, 0, 0)),
            scratch_shapes=[
                pltpu.VMEM((nnar,) + virts[0].shape, BF),
                pltpu.VMEM((2 * nw * (BINS + 8), width), F32),
            ],
        ),
        out_shape=jax.ShapeDtypeStruct((BINS, 2 * nw, 2 * width), BF),
        compiler_params=pltpu.CompilerParams(vmem_limit_bytes=48 * MIB),
        cost_estimate=pl.CostEstimate(flops=10**8, bytes_accessed=8 * nnar * virts[0].size, transcendentals=0),
        name="sources",
    )(me, *virts)


def stack_kernel(nw, size, group, count_ref, *refs):
    recv, src_ref, lag_ref = refs[:3]
    out_ref, lag, wide, turned, cross = refs[-5:]
    step = pl.program_id(0)
    width = SLOTS * VIRTUAL_SOURCES
    depth = 2 * nw
    wins = recv.shape[1]
    pack = src_ref.shape[1] // depth
    full = pack * depth
    pitch, bpitch = size + 8, BINS + 8

    @pl.when(step == 0)
    def _():
        lag[...] = lag_ref[...].astype(BF)
        for src in range(recv.shape[0]):
            for w in range(wins):
                for p in range(2):
                    row = (p * nw + src * wins + w) * pitch
                    wide[row : row + size, :] = recv[src, w, p].astype(F32)

        def turn(i, carry):
            flat = wide[pl.ds(i, depth, stride=pitch), :]
            flat = jnp.concatenate([flat] * pack, 0).T
            if pack > 1:
                flat = jnp.where(own, flat, 0.0)
            for c in range(0, full, 128):
                part = flat[:, c : min(c + 128, full)]
                turned[c // 128, pl.ds(pl.multiple_of(i * bpitch, 8), BINS), 0 : part.shape[1]] = part
            return carry

        shape = (BINS, full)
        own = lax.broadcasted_iota(jnp.int32, shape, 0) % pack == lax.broadcasted_iota(jnp.int32, shape, 1) // depth
        lax.fori_loop(0, size, turn, 0, unroll=8)
        slot = lax.broadcasted_iota(jnp.int32, (1, 2 * width), 1) % width // VIRTUAL_SOURCES
        scale = jnp.where(slot < count_ref[0], 1.0 / math.sqrt(nw), 0.0).astype(F32)

        def one(j, carry):
            rows = []
            for u in range(pack):
                at = pl.ds(j * pack + u, size, stride=bpitch)
                rows.append(jnp.concatenate([turned[c, at, :] for c in range(turned.shape[0])], 1))
            left = jnp.concatenate(rows, 0)[:, :full].astype(BF)
            value = dot(left, src_ref[j]) * scale
            for u in range(pack):
                at = pl.ds(pl.multiple_of((j * pack + u) * pitch, 8), size)
                for p in range(2):
                    cross[p, at, :] = value[u * size : (u + 1) * size, p * width : (p + 1) * width]
            return carry

        lax.fori_loop(0, BINS // pack, one, 0, unroll=8 // pack)

    for q in range(0, group, 4):
        lefts = []
        for u in range(4):
            at = step * group + q + u
            tiles = [cross[p, pl.ds(at, BINS, stride=pitch), :].astype(BF).T for p in range(2)]
            lefts.append(jnp.concatenate(tiles, 1))
        value = dot(jnp.concatenate(lefts, 0), lag[...]).astype(BF)
        for u in range(4):
            for k in range(SLOTS):
                at = u * width + k * VIRTUAL_SOURCES
                out_ref[0, k, q + u] = value[at : at + VIRTUAL_SOURCES]


def stack(recv, table, count, lag, before, start, chans):
    nsrc, wins, _, size, _ = recv.shape
    nw = nsrc * wins
    group = 16
    pack = 2 if 4 * nw <= 128 else 1
    table = table.reshape(BINS // pack, pack * 2 * nw, table.shape[2])
    shape = (1, SLOTS, chans, VIRTUAL_SOURCES, LAG_COUNT)
    first = start // group
    operands = [count, recv, table, lag]
    in_specs = [
        pl.BlockSpec(recv.shape, lambda t, c: (0,) * 5),
        pl.BlockSpec(table.shape, lambda t, c: (0,) * 3),
        pl.BlockSpec(lag.shape, lambda t, c: (0, 0)),
    ]
    aliases = {}
    if before is not None:
        operands.append(before)
        in_specs.append(pl.BlockSpec(memory_space=pl.ANY))
        aliases = {4: 0}
    return pl.pallas_call(
        lambda *refs: stack_kernel(nw, size, group, *refs),
        grid_spec=pltpu.PrefetchScalarGridSpec(
            num_scalar_prefetch=1,
            grid=(size // group,),
            in_specs=in_specs,
            out_specs=pl.BlockSpec(
                (1, SLOTS, group, VIRTUAL_SOURCES, LAG_COUNT), lambda t, c: (0, 0, first + t, 0, 0)
            ),
            scratch_shapes=[
                pltpu.VMEM(lag.shape, BF),
                pltpu.VMEM((2 * nw * (size + 8), BINS), F32),
                pltpu.VMEM((-(-2 * nw * pack // 128), size * (BINS + 8), 128), F32),
                pltpu.VMEM((2, BINS * (size + 8), SLOTS * VIRTUAL_SOURCES), F32),
            ],
        ),
        out_shape=jax.ShapeDtypeStruct(shape, BF),
        input_output_aliases=aliases,
        compiler_params=pltpu.CompilerParams(vmem_limit_bytes=36 * MIB),
        cost_estimate=pl.CostEstimate(
            flops=size * 128 * 256 * 256 * 4, bytes_accessed=2 * (table.size + size * 32768), transcendentals=0
        ),
        name="stack",
    )(*operands)


def on_device(records, taps, pair_sources, pair_counts):
    nblk, chans, time = records.shape
    wins = time // WLEN
    nv = chans // VSTEP
    nwide, nnar = lax.axis_size("wide"), lax.axis_size("narrow")
    ahead = [(i, i + 1) for i in range(nwide - 1)]
    taps = taps[None]
    sizes = (chans // 2,) * 2
    *tails, rows, near = select(records, sizes)
    near = lax.ppermute(near, "wide", ahead)
    tails, near = lax.optimization_barrier((tails, near))
    halos = [lax.ppermute(tail, "wide", ahead) for tail in tails]
    picked = virtual(rows, near, taps, pair_sources, nblk)
    picked = lax.all_to_all(picked, "wide", split_axis=0, concat_axis=0, tiled=True)
    chunks = [spectra(records, halo, taps, i) for i, halo in enumerate(halos)]
    before, recvs = picked, []
    for chunk in chunks:
        chunk, _ = lax.optimization_barrier((chunk, before))
        before = lax.all_to_all(chunk, "wide", split_axis=0, concat_axis=0, tiled=True)
        recvs.append(before)
    virts = {0: picked}
    bit = nnar // 2
    while bit:
        for slot in sorted(virts):
            virts[slot ^ bit] = lax.ppermute(virts[slot], "narrow", [(i, i ^ bit) for i in range(nnar)])
        bit //= 2
    me = lax.axis_index("narrow").astype(jnp.int32)[None]
    table = sources([virts[slot] for slot in range(nnar)], me, wins, nv)
    lag = jnp.asarray(lag_table())
    out, start = None, 0
    for recv, size in zip(recvs, sizes):
        out = stack(recv, table, pair_counts, lag, out, start, chans)
        start += size
    return out


def solution(mesh):
    return jax.shard_map(
        on_device,
        mesh=mesh,
        in_specs=(P(None, "narrow", "wide"), P(), P(), P("wide")),
        out_specs=P("wide", None, "narrow", None, None),
        check_vma=False,
    )
```

time: 209 us -> 119 us (0.57)
  local copies, waits for them, and re-layouts: 78.2 us -> 11.7 us
  blocking collectives: 47.9 us -> 0 us
  Pallas kernels: 0 us -> 36 us
  starting transfers between devices: 9.37 us -> 42.9 us
  matrix products: 27.5 us -> 0 us
  other arithmetic: 15.1 us -> 0 us
    all_to_all x1 -> x0, blocking collectives: 41.4 us -> none  [on_device(): lax.all_to_all(picked_sources, 'wide', split_axis=0, concat_axis=2, tiled...]
    pallas_call x0 -> x7, Pallas kernels: none -> 36 us  [the longest x2 18.7 us: stack(): pl.pallas_call(lambda *refs: stack_kernel(nw, size, group, *refs), grid_s...]
    dot_general x6 -> x0, matrix products: 27.5 us -> none  [the longest x1 9.13 us: on_device(): jnp.dot(cross.reshape(-1, 2 * FREQUENCY_BINS), lag_table(), preferred_ele...]
    all_to_all x1 -> x3, waiting for transfers between devices: 28.4 us -> 1.81 us  [the longest x2 1.8 us: on_device(): lax.all_to_all(chunk, 'wide', split_axis=0, concat_axis=0, tiled=True)]
    ppermute x1 -> x6, waiting for transfers between devices: 0.01 us -> 25.3 us  [the longest x2 15.1 us: on_device(): halos = [lax.ppermute(tail, 'wide', ahead) for tail in tails]]
    all_to_all x1 -> x3, starting transfers between devices: 3.76 us -> 28.5 us  [the longest x2 21.9 us: on_device(): lax.all_to_all(chunk, 'wide', split_axis=0, concat_axis=0, tiled=True)]
    another operation x3 -> x0, local copies, waits for them, and re-layouts: 20.1 us -> none  [the longest x1 15.9 us: cross_spectra(): jnp.stack([real * scale * live, imag * scale * live], 3)]
    slice x5 -> x0, local copies, waits for them, and re-layouts: 17 us -> none  [the longest x1 10.4 us: on_device(): virtual_channels = block_spectrum[:, ::BLOCK_CHANNELS // VIRTUAL_SOURCES]]
  transfers between devices with their start and end apart: 2 -> 9, of which waited for: 1 -> 5; matrix products, arithmetic and copies ran while one was open for 17% -> 1% of each run, Pallas kernels for 0% -> 16%
where the time goes in v1:
time: 119 us; the launch traced here: 118 us
  starting transfers between devices  42.9 us (36%)
  Pallas kernels  36 us (30%)
  waiting for transfers between devices  27.1 us (23%)
  local copies, waits for them, and re-layouts  11.7 us (10%)
    all_to_all x2, starting transfers between devices, on_device(): lax.all_to_all(chunk, 'wide', split_axis=0, concat_axis=0, tiled=True)  21.9 us
    pallas_call x2, Pallas kernels, stack(): pl.pallas_call(lambda *refs: stack_kernel(nw, size, group, *refs), grid_s...  18.7 us
    ppermute x2, waiting for transfers between devices, on_device(): halos = [lax.ppermute(tail, 'wide', ahead) for tail in tails]  15.1 us
    unnamed x29, local copies, waits for them, and re-layouts  11.7 us
    ppermute x3, waiting for transfers between devices, on_device(): lax.ppermute(virts[slot], 'narrow', [(i, i ^ bit) for i in range(nnar)])  9.25 us
    pallas_call x2, Pallas kernels, spectra(): pl.pallas_call(lambda *refs: spectra_kernel(per, size, wins, *refs), grid...  8.94 us
    ppermute x2, starting transfers between devices, on_device(): halos = [lax.ppermute(tail, 'wide', ahead) for tail in tails]  7.86 us
    all_to_all x1, starting transfers between devices, on_device(): lax.all_to_all(picked, 'wide', split_axis=0, concat_axis=0, tiled=True)  6.57 us
  transfers between devices with their start and end apart: 9, of which 5 were waited for; matrix products, arithmetic and copies ran while one was open for 1% of the time, Pallas kernels for 16%

profile of v1, /device:TPU:0, one launch (start us, length us, event | category | flops | bytes accessed | tf_op | source)
XLA Modules:
  0.0 118.4 jit_solution(17390667658569329482)
XLA Ops:
  0.0 3.8 %select.1 = (bf16[8,64,256]{2,1,0:T(8,128)(2,1)}, bf16[8,64,256]{2,1,0:T(8,128)(2,1)}, f32[64,1536]{1,0:T(8,128)}, f32[64,256]{1,0:T(8,128)}) custom-call(bf16[8,128,1536]{2,1,0:T(8,128)(2,1)} %refs_0_.8), custom_call_target="tpu_custom_call" | custom-call | bytes 3145728 | tf_op jit(solution)/shard_map/select/pallas_call | solution.py:88
  3.8 5.0 %collective-permute-start = (f32[64,256]{1,0:T(8,128)}, f32[64,256]{1,0:T(8,128)S(1)}, u32[]{:S(2)}, u32[]{:S(2)}) collective-permute-start(f32[64,256]{1,0:T(8,128)} %get-tuple-element.16), channel_id=1, source_target_pairs={{0,4},{4,8},{8,12},{12,16},{16,20},{20,24},{24,28},{1,5},{5,9},{9,... | collective-permute-start | bytes 196616 | tf_op jit(solution)/shard_map/ppermute | solution.py:360
  8.7 1.3 %copy.10.refs_0_ = s32[8,4]{1,0:T(8,128)} copy(s32[8,4]{0,1:T(4,128)} %param.10) | data formatting | bytes 256 | tf_op args[2]
  10.1 0.9 collective-permute-done.refs_2_
  10.9 0.6 copy-done.12
  11.6 3.3 %virtual.1 = bf16[8,4,48,128]{3,2,1,0:T(8,128)(2,1)} custom-call(s32[8,4]{1,0:T(8,128)} %copy.10.refs_0_, f32[64,1536]{1,0:T(8,128)} %get-tuple-element.19.refs_1_, f32[64,256]{1,0:T(8,128)} %copy-done.12, f32[1,201]{1,0:T(1,128)} %bitcast.5, f32[512,256]{1,0:T(8,128)} %constant.8.clone.refs_3_.refs_4_), custom_call_target="tpu_custom_call" | custom-call | flops 100000000 | bytes 786432 | tf_op jit(solution)/shard_map/virtual/pallas_call | solution.py:124
  14.9 6.6 %all-to-all-start = ((bf16[8,4,48,128]{3,2,1,0:T(8,128)(2,1)}), bf16[8,4,48,128]{3,2,1,0:T(8,128)(2,1)S(1)}, u32[]{:S(2)}, u32[]{:S(2)}) async-start(bf16[8,4,48,128]{3,2,1,0:T(8,128)(2,1)} %virtual.1), calls=%async_computation | async-start | bytes 786432 | tf_op jit(solution)/shard_map/all_to_all | solution.py:364
  21.4 3.9 %collective-permute-start.2 = (bf16[8,64,256]{2,1,0:T(8,128)(2,1)}, bf16[8,64,256]{2,1,0:T(8,128)(2,1)S(1)}, u32[]{:S(2)}, u32[]{:S(2)}) collective-permute-start(bf16[8,64,256]{2,1,0:T(8,128)(2,1)} %get-tuple-element.18), channel_id=1, source_target_pairs={{0,4},{4,8},{8,12},{12,16},{16,20},{20,24},{24,28},{1,5},{5,9},{9,... | collective-permute-start | bytes 786440 | tf_op jit(solution)/shard_map/ppermute | solution.py:362
  25.4 6.6 %collective-permute-done.2.refs_1_ = bf16[8,64,256]{2,1,0:T(8,128)(2,1)S(1)} collective-permute-done((bf16[8,64,256]{2,1,0:T(8,128)(2,1)}, bf16[8,64,256]{2,1,0:T(8,128)(2,1)S(1)}, u32[]{:S(2)}, u32[]{:S(2)}) %collective-permute-start.2) | collective-permute-done | bytes 262176 | tf_op jit(solution)/shard_map/ppermute | solution.py:362
  31.9 0.7 copy-done.11
  32.6 4.5 %spectra.3 = bf16[8,3,2,64,128]{4,3,2,1,0:T(8,128)(2,1)} custom-call(bf16[8,128,1536]{2,1,0:T(8,128)(2,1)} %refs_0_.8, bf16[8,64,256]{2,1,0:T(8,128)(2,1)} %copy-done.11, f32[1,201]{1,0:T(1,128)} %bitcast.6, f32[512,256]{1,0:T(8,128)} %constant.8.clone.refs_3_.refs_4_), custom_call_target="tpu_custom_call" | custom-call | flops 1207959552 | bytes 2359296 | tf_op jit(solution)/shard_map/spectra/pallas_call | solution.py:169
  37.1 8.4 %all-to-all-start.1 = ((bf16[8,3,2,64,128]{4,3,2,1,0:T(8,128)(2,1)}), bf16[8,3,2,64,128]{4,3,2,1,0:T(8,128)(2,1)S(1)}, u32[]{:S(2)}, u32[]{:S(2)}) async-start(bf16[8,3,2,64,128]{4,3,2,1,0:T(8,128)(2,1)} %spectra.3), calls=%async_computation.1 | async-start | bytes 1572864 | tf_op jit(solution)/shard_map/all_to_all | solution.py:369
  45.6 3.9 %collective-permute-start.1 = (bf16[8,64,256]{2,1,0:T(8,128)(2,1)S(1)}, bf16[8,64,256]{2,1,0:T(8,128)(2,1)S(1)}, u32[]{:S(2)}, u32[]{:S(2)}) collective-permute-start(bf16[8,64,256]{2,1,0:T(8,128)(2,1)S(1)} %copy-done.13), channel_id=1, source_target_pairs={{0,4},{4,8},{8,12},{12,16},{16,20},{20,24},{24,28},{1,5},{5,9},{9,... | collective-permute-start | bytes 786440 | tf_op jit(solution)/shard_map/ppermute | solution.py:362
  49.5 8.6 %collective-permute-done.1.refs_1_ = bf16[8,64,256]{2,1,0:T(8,128)(2,1)S(1)} collective-permute-done((bf16[8,64,256]{2,1,0:T(8,128)(2,1)S(1)}, bf16[8,64,256]{2,1,0:T(8,128)(2,1)S(1)}, u32[]{:S(2)}, u32[]{:S(2)}) %collective-permute-start.1) | collective-permute-done | bytes 262176 | tf_op jit(solution)/shard_map/ppermute | solution.py:362
  58.1 0.7 copy-done.10
  58.8 4.5 %spectra.2 = bf16[8,3,2,64,128]{4,3,2,1,0:T(8,128)(2,1)} custom-call(bf16[8,128,1536]{2,1,0:T(8,128)(2,1)} %refs_0_.8, bf16[8,64,256]{2,1,0:T(8,128)(2,1)} %copy-done.10, f32[1,201]{1,0:T(1,128)} %bitcast.7, f32[512,256]{1,0:T(8,128)} %constant.8.clone.refs_3_.refs_4_), custom_call_target="tpu_custom_call" | custom-call | flops 1207959552 | bytes 2359296 | tf_op jit(solution)/shard_map/spectra/pallas_call | solution.py:169
  63.3 1.8 %all-to-all-done.1.refs_1_ = bf16[8,3,2,64,128]{4,3,2,1,0:T(8,128)(2,1)S(1)} async-done(((bf16[8,3,2,64,128]{4,3,2,1,0:T(8,128)(2,1)}), bf16[8,3,2,64,128]{4,3,2,1,0:T(8,128)(2,1)S(1)}, u32[]{:S(2)}, u32[]{:S(2)}) %all-to-all-start.1) | async-done | bytes 786464 | tf_op jit(solution)/shard_map/all_to_all | solution.py:369
  65.1 13.5 %all-to-all-start.2 = ((bf16[8,3,2,64,128]{4,3,2,1,0:T(8,128)(2,1)}), bf16[8,3,2,64,128]{4,3,2,1,0:T(8,128)(2,1)}, u32[]{:S(2)}, u32[]{:S(2)}) async-start(bf16[8,3,2,64,128]{4,3,2,1,0:T(8,128)(2,1)} %spectra.2), calls=%async_computation.2 | async-start | bytes 1572864 | tf_op jit(solution)/shard_map/all_to_all | solution.py:369
  78.6 1.5 %collective-permute-start.4 = (bf16[8,4,48,128]{3,2,1,0:T(8,128)(2,1)S(1)}, bf16[8,4,48,128]{3,2,1,0:T(8,128)(2,1)S(1)}, u32[]{:S(2)}, u32[]{:S(2)}) collective-permute-start(bf16[8,4,48,128]{3,2,1,0:T(8,128)(2,1)S(1)} %all-to-all-done.refs_1_), channel_id=1, source_target_pairs={{0,2},{1,3},{2,0},{3,1},{4,6},{5,7},{6,4},{7,5},{8,10},{9,11},{10,... | collective-permute-start | bytes 1179656 | tf_op jit(solution)/shard_map/ppermute | solution.py:375
  80.1 9.2 %collective-permute-done.4.refs_3_ = bf16[8,4,48,128]{3,2,1,0:T(8,128)(2,1)S(1)} collective-permute-done((bf16[8,4,48,128]{3,2,1,0:T(8,128)(2,1)S(1)}, bf16[8,4,48,128]{3,2,1,0:T(8,128)(2,1)S(1)}, u32[]{:S(2)}, u32[]{:S(2)}) %collective-permute-start.4) | collective-permute-done | bytes 393248 | tf_op jit(solution)/shard_map/ppermute | solution.py:375
  89.3 0.8 copy-done.4
  90.8 0.7 copy-done.6
  91.5 0.8 copy-done.8
  92.3 1.0 copy-done.5
  93.3 1.0 copy-done.7
  94.3 1.0 copy-done.9
  95.3 1.3 %sources.1 = bf16[128,48,256]{2,1,0:T(8,128)(2,1)S(1)} custom-call(s32[1]{0:T(128)} %bitcast.1.refs_0_, bf16[8,4,48,128]{3,2,1,0:T(8,128)(2,1)S(1)} %all-to-all-done.refs_1_, bf16[8,4,48,128]{3,2,1,0:T(8,128)(2,1)S(1)} %copy-done.7, bf16[8,4,48,128]{3,2,1,0:T(8,128)(2,1)S(1)} %copy-done.5, bf16[8,4,48,128]{3,2,1,0:T(8,128)(2,1)S(1)} %copy-done.9), custom_call_target="tpu_custom_call" | custom-call | flops 100000000 | bytes 6291456 | tf_op jit(solution)/shard_map/sources/pallas_call | solution.py:223
  96.6 1.1 copy-done.1
  97.7 0.9 copy-done.2
  98.7 8.8 %stack.2.refs_4_ = bf16[1,4,128,32,256]{4,3,2,1,0:T(8,128)(2,1)} custom-call(s32[1]{0:T(128)S(6)} %copy.12.refs_0_, bf16[8,3,2,64,128]{4,3,2,1,0:T(8,128)(2,1)S(1)} %copy-done.1, bf16[64,96,256]{2,1,0:T(8,128)(2,1)S(1)} %bitcast.3, f32[256,256]{1,0:T(8,128)S(1)} %copy-done.2), custom_call_target="tpu_custom_call" | custom-call | flops 2147483648 | bytes 7340032 | tf_op jit(solution)/shard_map/stack/pallas_call | solution.py:325
  107.5 0.9 copy-done.3
  108.4 9.9 %stack.3 = bf16[1,4,128,32,256]{4,3,2,1,0:T(8,128)(2,1)} custom-call(s32[1]{0:T(128)S(6)} %copy.12.refs_0_, bf16[8,3,2,64,128]{4,3,2,1,0:T(8,128)(2,1)} %all-to-all-done.2.refs_1_, bf16[64,96,256]{2,1,0:T(8,128)(2,1)S(1)} %bitcast.4, f32[256,256]{1,0:T(8,128)S(1)} %copy-done.3, ...), custom_call_target="tpu_custom_call", output_to_operand_aliasing={{}: (4, {})} | custom-call | flops 2147483648 | bytes 7340032 | tf_op jit(solution)/shard_map/stack/pallas_call | solution.py:325
  (22 shorter events, 0.0 us)
Async XLA Ops:
  3.8 41.8 %copy-start.13 = (bf16[8,64,256]{2,1,0:T(8,128)(2,1)S(1)}, bf16[8,64,256]{2,1,0:T(8,128)(2,1)}, u32[]{:S(2)}) copy-start(bf16[8,64,256]{2,1,0:T(8,128)(2,1)} %get-tuple-element.17) | copy-start | bytes 786436
  3.8 7.2 %collective-permute-start = (f32[64,256]{1,0:T(8,128)}, f32[64,256]{1,0:T(8,128)S(1)}, u32[]{:S(2)}, u32[]{:S(2)}) collective-permute-start(f32[64,256]{1,0:T(8,128)} %get-tuple-element.16), channel_id=1, source_target_pairs={{0,4},{4,8},{8,12},{12,16},{16,20},{20,24},{24,28},{1,5},{5,9},{9,... | collective-permute-start | bytes 196616 | tf_op jit(solution)/shard_map/ppermute | solution.py:360
  10.9 0.6 copy-start.12
  14.9 22.2 %all-to-all-start = ((bf16[8,4,48,128]{3,2,1,0:T(8,128)(2,1)}), bf16[8,4,48,128]{3,2,1,0:T(8,128)(2,1)S(1)}, u32[]{:S(2)}, u32[]{:S(2)}) async-start(bf16[8,4,48,128]{3,2,1,0:T(8,128)(2,1)} %virtual.1), calls=%async_computation | async-start | bytes 786432 | tf_op jit(solution)/shard_map/all_to_all | solution.py:364
  21.4 10.5 %collective-permute-start.2 = (bf16[8,64,256]{2,1,0:T(8,128)(2,1)}, bf16[8,64,256]{2,1,0:T(8,128)(2,1)S(1)}, u32[]{:S(2)}, u32[]{:S(2)}) collective-permute-start(bf16[8,64,256]{2,1,0:T(8,128)(2,1)} %get-tuple-element.18), channel_id=1, source_target_pairs={{0,4},{4,8},{8,12},{12,16},{16,20},{20,24},{24,28},{1,5},{5,9},{9,... | collective-permute-start | bytes 786440 | tf_op jit(solution)/shard_map/ppermute | solution.py:362
  31.9 0.7 copy-start.11
  37.1 28.0 %all-to-all-start.1 = ((bf16[8,3,2,64,128]{4,3,2,1,0:T(8,128)(2,1)}), bf16[8,3,2,64,128]{4,3,2,1,0:T(8,128)(2,1)S(1)}, u32[]{:S(2)}, u32[]{:S(2)}) async-start(bf16[8,3,2,64,128]{4,3,2,1,0:T(8,128)(2,1)} %spectra.3), calls=%async_computation.1 | async-start | bytes 1572864 | tf_op jit(solution)/shard_map/all_to_all | solution.py:369
  45.6 12.5 %collective-permute-start.1 = (bf16[8,64,256]{2,1,0:T(8,128)(2,1)S(1)}, bf16[8,64,256]{2,1,0:T(8,128)(2,1)S(1)}, u32[]{:S(2)}, u32[]{:S(2)}) collective-permute-start(bf16[8,64,256]{2,1,0:T(8,128)(2,1)S(1)} %copy-done.13), channel_id=1, source_target_pairs={{0,4},{4,8},{8,12},{12,16},{16,20},{20,24},{24,28},{1,5},{5,9},{9,... | collective-permute-start | bytes 786440 | tf_op jit(solution)/shard_map/ppermute | solution.py:362
  58.1 0.7 copy-start.10
  65.1 26.5 %copy-start = (bf16[8,3,2,64,128]{4,3,2,1,0:T(8,128)(2,1)}, bf16[8,3,2,64,128]{4,3,2,1,0:T(8,128)(2,1)S(1)}, u32[]{:S(2)}) copy-start(bf16[8,3,2,64,128]{4,3,2,1,0:T(8,128)(2,1)S(1)} %all-to-all-done.1.refs_1_) | copy-start | bytes 2359300
  65.1 42.4 %all-to-all-start.2 = ((bf16[8,3,2,64,128]{4,3,2,1,0:T(8,128)(2,1)}), bf16[8,3,2,64,128]{4,3,2,1,0:T(8,128)(2,1)}, u32[]{:S(2)}, u32[]{:S(2)}) async-start(bf16[8,3,2,64,128]{4,3,2,1,0:T(8,128)(2,1)} %spectra.2), calls=%async_computation.2 | async-start | bytes 1572864 | tf_op jit(solution)/shard_map/all_to_all | solution.py:369
  78.6 10.8 %collective-permute-start.4 = (bf16[8,4,48,128]{3,2,1,0:T(8,128)(2,1)S(1)}, bf16[8,4,48,128]{3,2,1,0:T(8,128)(2,1)S(1)}, u32[]{:S(2)}, u32[]{:S(2)}) collective-permute-start(bf16[8,4,48,128]{3,2,1,0:T(8,128)(2,1)S(1)} %all-to-all-done.refs_1_), channel_id=1, source_target_pairs={{0,2},{1,3},{2,0},{3,1},{4,6},{5,7},{6,4},{7,5},{8,10},{9,11},{10,... | collective-permute-start | bytes 1179656 | tf_op jit(solution)/shard_map/ppermute | solution.py:375
  80.1 10.7 %collective-permute-start.3 = (bf16[8,4,48,128]{3,2,1,0:T(8,128)(2,1)S(1)}, bf16[8,4,48,128]{3,2,1,0:T(8,128)(2,1)S(1)}, u32[]{:S(2)}, u32[]{:S(2)}) collective-permute-start(bf16[8,4,48,128]{3,2,1,0:T(8,128)(2,1)S(1)} %all-to-all-done.refs_1_), channel_id=1, source_target_pairs={{0,1},{1,0},{2,3},{3,2},{4,5},{5,4},{6,7},{7,6},{8,9},{9,8},{10,11... | collective-permute-start | bytes 1179656 | tf_op jit(solution)/shard_map/ppermute | solution.py:375
  89.3 2.2 %collective-permute-start.5 = (bf16[8,4,48,128]{3,2,1,0:T(8,128)(2,1)S(1)}, bf16[8,4,48,128]{3,2,1,0:T(8,128)(2,1)S(1)}, u32[]{:S(2)}, u32[]{:S(2)}) collective-permute-start(bf16[8,4,48,128]{3,2,1,0:T(8,128)(2,1)S(1)} %collective-permute-done.4.refs_3_), channel_id=1, source_target_pairs={{0,1},{1,0},{2,3},{3,2},{4,5},{5,4},{6,7},{7,6},{8,9},{9,8},{10,11... | collective-permute-start | bytes 1179656 | tf_op jit(solution)/shard_map/ppermute | solution.py:375
  89.3 0.8 copy-start.4
  90.8 0.7 copy-start.6
  91.5 0.8 copy-start.8
  92.3 1.0 copy-start.5
  93.3 1.0 copy-start.7
  94.3 1.0 copy-start.9
  96.6 1.1 copy-start.1
  97.7 0.9 copy-start.2
  107.5 1.0 copy-start.3

commit v2 on v1

v2 whole, which is shorter than its diff:
```python
import math

import jax
import jax.numpy as jnp
import numpy as np
from jax import lax
from jax.experimental import pallas as pl
from jax.experimental.pallas import tpu as pltpu
from jax.sharding import PartitionSpec as P

BLOCK_CHANNELS = 512
VIRTUAL_SOURCES = 32
VSTEP = BLOCK_CHANNELS // VIRTUAL_SOURCES
TAPS = 201
WLEN = 512
HALF = 256
BINS = 128
F_LO = 4
LAG_COUNT = 256
SLOTS = 4
BF = jnp.bfloat16
F32 = jnp.float32
MIB = 1 << 20


def dft_table():
    times = np.arange(WLEN, dtype=np.int32)[:, None]
    bins = (F_LO + np.arange(BINS, dtype=np.int32))[None, :]
    angle = np.mod(times * bins, WLEN).astype(np.float32) * np.float32(2.0 * math.pi / WLEN)
    scale = np.float32(1.0 / math.sqrt(WLEN))
    return np.concatenate([np.cos(angle) * scale, -np.sin(angle) * scale], 1).astype(BF).astype(np.float32)


def lag_table():
    bins = (F_LO + np.arange(BINS, dtype=np.int32))[:, None]
    lags = (np.arange(LAG_COUNT, dtype=np.int32) - LAG_COUNT // 2)[None, :]
    angle = np.mod(bins * lags, WLEN).astype(np.float32) * np.float32(2.0 * math.pi / WLEN)
    scale = np.float32(1.0 / math.sqrt(BINS))
    return np.concatenate([np.cos(angle) * scale, -np.sin(angle) * scale], 0).astype(BF).astype(np.float32)


def dot(a, b):
    return lax.dot_general(a, b, (((1,), (0,)), ((), ())), preferred_element_type=F32)


def build_toeplitz(taps_ref, row, toeplitz):
    row[...] = jnp.zeros_like(row)
    row[:, 128 : 128 + TAPS] = jnp.broadcast_to(taps_ref[...].astype(BF).astype(F32), (8, TAPS))
    bands = jnp.broadcast_to(row[0:1, :], (128, 512))
    bands = pltpu.roll(bands, 0, 1, stride=1, stride_axis=0).astype(BF)
    zero = jnp.zeros((128, 128), BF)
    far, mid, near = [bands[:, at : at + 128] for at in (128, 256, 384)]
    toeplitz[:, :128] = jnp.concatenate([near, mid, far, zero], 0)
    toeplitz[:, 128:] = jnp.concatenate([zero, near, mid, far], 0)


def transform(blocks, wins, chans, toeplitz, table):
    rows = []
    for halo, rec in blocks:
        rows.append(jnp.concatenate([halo, rec[:, :HALF]], 1))
        rows += [rec[:, HALF * (m - 1) : HALF * (m + 1)] for m in range(1, 2 * wins)]
    white = dot(jnp.concatenate(rows, 0), toeplitz).astype(BF)
    pieces = [
        jnp.concatenate([white[2 * w * chans : (2 * w + 1) * chans], white[(2 * w + 1) * chans : (2 * w + 2) * chans]], 1)
        for w in range(len(blocks) * wins)
    ]
    return dot(jnp.concatenate(pieces, 0), table)


def virtual_rows(ref, nv):
    rows = [ref[b, r * VSTEP : (r + 1) * VSTEP, :].astype(F32)[0:1] for b in range(ref.shape[0]) for r in range(nv)]
    return jnp.concatenate(rows, 0).astype(BF)


def block_rows(result, b, nv, wins, count):
    parts = [
        result[w * count + b * nv : w * count + (b + 1) * nv, p * BINS : (p + 1) * BINS]
        for w in range(wins)
        for p in range(2)
    ]
    return jnp.concatenate(parts, 0).astype(BF)


def early_kernel(rec_ref, taps_ref, table_ref, virt_ref, rows_ref, toeplitz_ref, forward_ref, row):
    nblk, chans, time = rec_ref.shape
    wins = time // WLEN - 1
    nv = chans // VSTEP
    count = nblk * nv
    build_toeplitz(taps_ref, row, toeplitz_ref)
    forward_ref[...] = table_ref[...].astype(BF)
    rows = virtual_rows(rec_ref, nv)
    rows_ref[...] = rows[:, :WLEN]
    block = (rows[:, HALF:WLEN], rows[:, WLEN:])
    result = transform([block], wins, count, toeplitz_ref[...], forward_ref[...])
    for b in range(nblk):
        virt_ref[b] = block_rows(result, b, nv, wins, count)


def early(records, taps):
    nblk, chans, time = records.shape
    nv = chans // VSTEP
    vmem = pl.BlockSpec(memory_space=pltpu.VMEM)
    return pl.pallas_call(
        early_kernel,
        in_specs=[vmem] * 3,
        out_specs=[vmem] * 4,
        out_shape=[
            jax.ShapeDtypeStruct((nblk, (time // WLEN - 1) * 2 * nv, BINS), BF),
            jax.ShapeDtypeStruct((nblk * nv, WLEN), BF),
            jax.ShapeDtypeStruct((WLEN, HALF), BF),
            jax.ShapeDtypeStruct((WLEN, 2 * BINS), BF),
        ],
        scratch_shapes=[pltpu.VMEM((8, 512), F32)],
        compiler_params=pltpu.CompilerParams(vmem_limit_bytes=40 * MIB),
        cost_estimate=pl.CostEstimate(flops=4 * 10**8, bytes_accessed=records.size * 2, transcendentals=0),
        name="early",
    )(records, taps, jnp.asarray(dft_table()))


def spectra_kernel(start, size, pairs_ref, me_ref, rec_ref, halo_ref, toeplitz_ref, forward_ref, *refs):
    held, sems = refs[-2:]
    nblk, chans, time = rec_ref.shape
    wins = time // WLEN
    nv = chans // VSTEP
    me = me_ref[0]
    copies = []
    for m in range(nblk):
        source = rec_ref.at[me ^ m, pl.ds(start, size)]
        copies.append(pltpu.make_async_copy(source, held.at[m], sems.at[m]))
        copies[-1].start()
    if len(refs) > nblk + 2:
        rows_ref, virt_ref, outs, virt = refs[0], refs[1], refs[2 : nblk + 2], refs[nblk + 2]
        block = (virtual_rows(halo_ref, nv), rows_ref[...])
        result = transform([block], 1, nblk * nv, toeplitz_ref[...], forward_ref[...])
        for b in range(nblk):
            virt[b] = block_rows(result, b, nv, 1, nblk * nv)
        for m in range(nblk):
            for k in range(SLOTS):
                block = pairs_ref[me ^ m, k]
                lo = wins * 2 * size + k * wins * 2 * nv
                outs[m][lo : lo + 2 * nv] = virt[block]
                outs[m][lo + 2 * nv : lo + wins * 2 * nv] = virt_ref[block]
    else:
        outs = refs[:nblk]
    per = 2
    for m in range(0, nblk, per):
        blocks = []
        for u in range(per):
            copies[m + u].wait()
            blocks.append((halo_ref[me ^ (m + u), start : start + size], held[m + u]))
        result = transform(blocks, wins, size, toeplitz_ref[...], forward_ref[...]).astype(BF)
        for u in range(per):
            for w in range(wins):
                for p in range(2):
                    lo = (u * wins + w) * size
                    row = (w * 2 + p) * size
                    outs[m + u][row : row + size] = result[lo : lo + size, p * BINS : (p + 1) * BINS]


def spectra(records, halo, toeplitz, forward, pairs, me, start, size, virtual=()):
    nblk, chans, time = records.shape
    wins = time // WLEN
    nv = chans // VSTEP
    shape = (wins * 2 * size + (SLOTS * wins * 2 * nv if virtual else 0), BINS)
    smem, vmem = pl.BlockSpec(memory_space=pltpu.SMEM), pl.BlockSpec(memory_space=pltpu.VMEM)
    operands = [pairs, me, records, halo, toeplitz, forward, *virtual]
    scratch = [pltpu.VMEM((nblk, 2 * nv, BINS), BF)] if virtual else []
    outs = pl.pallas_call(
        lambda *refs: spectra_kernel(start, size, *refs),
        in_specs=[smem, smem, pl.BlockSpec(memory_space=pl.ANY)] + [vmem] * (len(operands) - 3),
        out_specs=[vmem] * nblk,
        out_shape=[jax.ShapeDtypeStruct(shape, BF)] * nblk,
        scratch_shapes=scratch + [pltpu.VMEM((nblk, size, time), BF), pltpu.SemaphoreType.DMA((nblk,))],
        compiler_params=pltpu.CompilerParams(vmem_limit_bytes=40 * MIB),
        cost_estimate=pl.CostEstimate(
            flops=nblk * size * wins * 3 * 2 * 512 * 256, bytes_accessed=nblk * size * time * 3, transcendentals=0
        ),
        name="spectra",
    )(*operands)
    return list(outs)


def collect_kernel(rows, *refs):
    out_ref = refs[-1]
    for m, ref in enumerate(refs[:-1]):
        at = ref.shape[0] - SLOTS * rows
        for k in range(SLOTS):
            out_ref[m, k] = ref[at + k * rows : at + (k + 1) * rows]


def collect(chunks, rows):
    vmem = pl.BlockSpec(memory_space=pltpu.VMEM)
    return pl.pallas_call(
        lambda *refs: collect_kernel(rows, *refs),
        in_specs=[vmem] * len(chunks),
        out_specs=vmem,
        out_shape=jax.ShapeDtypeStruct((len(chunks), SLOTS, rows, BINS), BF),
        compiler_params=pltpu.CompilerParams(vmem_limit_bytes=32 * MIB),
        cost_estimate=pl.CostEstimate(flops=0, bytes_accessed=len(chunks) * rows * 2048, transcendentals=0),
        name="collect",
    )(*chunks)


def sources_kernel(nsrc, nnar, wins, nv, me_ref, place_ref, *refs):
    virts, out_ref, held, turned = refs[:nnar], refs[nnar], refs[nnar + 1], refs[nnar + 2]
    nw = nsrc * wins
    pitch = BINS + 8
    for n in range(nnar):
        held[place_ref[0] ^ n] = virts[n][...]

    def turn(m, carry):
        tiles = [[held[n, m, k].astype(F32) for n in range(nnar)] for k in range(SLOTS)]
        for w in range(wins):
            for p in range(2):
                at = (w * 2 + p) * nv
                tile = jnp.concatenate([tiles[k][n][at : at + nv] for k in range(SLOTS) for n in range(nnar)], 0)
                row = pl.multiple_of((p * nw + (me_ref[0] ^ m) * wins + w) * pitch, 8)
                turned[pl.ds(row, BINS), :] = tile.T
        return carry

    lax.fori_loop(0, nsrc, turn, 0, unroll=4)

    def one(j, carry):
        re = turned[pl.ds(j, nw, stride=pitch), :]
        im = turned[pl.ds(nw * pitch + j, nw, stride=pitch), :]
        top = jnp.concatenate([re, -im], 1)
        low = jnp.concatenate([im, re], 1)
        out_ref[j] = jnp.concatenate([top, low], 0).astype(BF)
        return carry

    lax.fori_loop(0, BINS, one, 0, unroll=8)


def sources(virts, me, place, wins, nv):
    nnar, nsrc = len(virts), virts[0].shape[0]
    nw = nsrc * wins
    width = SLOTS * nnar * nv
    smem, vmem = pl.BlockSpec(memory_space=pltpu.SMEM), pl.BlockSpec(memory_space=pltpu.VMEM)
    return pl.pallas_call(
        lambda *refs: sources_kernel(nsrc, nnar, wins, nv, *refs),
        in_specs=[smem, smem] + [vmem] * nnar,
        out_specs=vmem,
        out_shape=jax.ShapeDtypeStruct((BINS, 2 * nw, 2 * width), BF),
        scratch_shapes=[
            pltpu.VMEM((nnar,) + virts[0].shape, BF),
            pltpu.VMEM((2 * nw * (BINS + 8), width), F32),
        ],
        compiler_params=pltpu.CompilerParams(vmem_limit_bytes=40 * MIB),
        cost_estimate=pl.CostEstimate(flops=10**8, bytes_accessed=8 * nnar * virts[0].size, transcendentals=0),
        name="sources",
    )(me, place, *virts)


def stack_kernel(nw, wins, size, group, count_ref, me_ref, *refs):
    nsrc = nw // wins
    recvs, src_ref, lag_ref = refs[:nsrc], refs[nsrc], refs[nsrc + 1]
    out_ref, lag, wide, turned, cross = refs[-5:]
    step = pl.program_id(0)
    width = SLOTS * VIRTUAL_SOURCES
    depth = 2 * nw
    pack = src_ref.shape[1] // depth
    full = pack * depth
    pitch, bpitch = size + 8, BINS + 8

    @pl.when(step == 0)
    def _():
        lag[...] = lag_ref[...].astype(BF)
        for m in range(nsrc):
            src = me_ref[0] ^ m
            for w in range(wins):
                for p in range(2):
                    row = pl.multiple_of((p * nw + src * wins + w) * pitch, 8)
                    at = (w * 2 + p) * size
                    wide[pl.ds(row, size), :] = recvs[m][at : at + size].astype(F32)

        def turn(i, carry):
            flat = wide[pl.ds(i, depth, stride=pitch), :]
            flat = jnp.concatenate([flat] * pack, 0).T
            if pack > 1:
                flat = jnp.where(own, flat, 0.0)
            for c in range(0, full, 128):
                part = flat[:, c : min(c + 128, full)]
                turned[c // 128, pl.ds(pl.multiple_of(i * bpitch, 8), BINS), 0 : part.shape[1]] = part
            return carry

        shape = (BINS, full)
        own = lax.broadcasted_iota(jnp.int32, shape, 0) % pack == lax.broadcasted_iota(jnp.int32, shape, 1) // depth
        lax.fori_loop(0, size, turn, 0, unroll=8)
        slot = lax.broadcasted_iota(jnp.int32, (1, 2 * width), 1) % width // VIRTUAL_SOURCES
        scale = jnp.where(slot < count_ref[0], 1.0 / math.sqrt(nw), 0.0).astype(F32)

        def one(j, carry):
            rows = []
            for u in range(pack):
                at = pl.ds(j * pack + u, size, stride=bpitch)
                rows.append(jnp.concatenate([turned[c, at, :] for c in range(turned.shape[0])], 1))
            left = jnp.concatenate(rows, 0)[:, :full].astype(BF)
            value = dot(left, src_ref[j]) * scale
            for u in range(pack):
                at = pl.ds(pl.multiple_of((j * pack + u) * pitch, 8), size)
                for p in range(2):
                    cross[p, at, :] = value[u * size : (u + 1) * size, p * width : (p + 1) * width]
            return carry

        lax.fori_loop(0, BINS // pack, one, 0, unroll=8 // pack)

    for q in range(0, group, 4):
        lefts = []
        for u in range(4):
            at = step * group + q + u
            tiles = [cross[p, pl.ds(at, BINS, stride=pitch), :].astype(BF).T for p in range(2)]
            lefts.append(jnp.concatenate(tiles, 1))
        value = dot(jnp.concatenate(lefts, 0), lag[...]).astype(BF)
        for u in range(4):
            for k in range(SLOTS):
                at = u * width + k * VIRTUAL_SOURCES
                out_ref[0, k, q + u] = value[at : at + VIRTUAL_SOURCES]


def stack(recvs, table, count, me, lag, before, start, size, wins, chans):
    nw = wins * len(recvs)
    group = 16
    pack = 2 if 4 * nw <= 128 else 1
    table = table.reshape(BINS // pack, pack * 2 * nw, table.shape[2])
    shape = (1, SLOTS, chans, VIRTUAL_SOURCES, LAG_COUNT)
    first = start // group
    operands = [count, me, *recvs, table, lag]
    in_specs = [pl.BlockSpec(recv.shape, lambda t, c, e: (0, 0)) for recv in recvs] + [
        pl.BlockSpec(table.shape, lambda t, c, e: (0,) * 3),
        pl.BlockSpec(lag.shape, lambda t, c, e: (0, 0)),
    ]
    aliases = {}
    if before is not None:
        operands.append(before)
        in_specs.append(pl.BlockSpec(memory_space=pl.ANY))
        aliases = {len(operands) - 1: 0}
    return pl.pallas_call(
        lambda *refs: stack_kernel(nw, wins, size, group, *refs),
        grid_spec=pltpu.PrefetchScalarGridSpec(
            num_scalar_prefetch=2,
            grid=(size // group,),
            in_specs=in_specs,
            out_specs=pl.BlockSpec(
                (1, SLOTS, group, VIRTUAL_SOURCES, LAG_COUNT), lambda t, c, e: (0, 0, first + t, 0, 0)
            ),
            scratch_shapes=[
                pltpu.VMEM(lag.shape, BF),
                pltpu.VMEM((2 * nw * (size + 8), BINS), F32),
                pltpu.VMEM((-(-2 * nw * pack // 128), size * (BINS + 8), 128), F32),
                pltpu.VMEM((2, BINS * (size + 8), SLOTS * VIRTUAL_SOURCES), F32),
            ],
        ),
        out_shape=jax.ShapeDtypeStruct(shape, BF),
        input_output_aliases=aliases,
        compiler_params=pltpu.CompilerParams(vmem_limit_bytes=36 * MIB),
        cost_estimate=pl.CostEstimate(
            flops=size * 128 * 256 * 256 * 4, bytes_accessed=2 * (table.size + size * 32768), transcendentals=0
        ),
        name="stack",
    )(*operands)


def swap(value, axis, mask):
    return lax.ppermute(value, axis, [(i, i ^ mask) for i in range(lax.axis_size(axis))])


def after(value, others):
    return lax.optimization_barrier((value, others))[0] if others else value


def on_device(records, taps, pair_sources, pair_counts):
    nblk, chans, time = records.shape
    wins = time // WLEN
    nv = chans // VSTEP
    nwide, nnar = lax.axis_size("wide"), lax.axis_size("narrow")
    half = chans // 2
    me = lax.axis_index("wide").astype(jnp.int32)[None]
    place = lax.axis_index("narrow").astype(jnp.int32)[None]
    halo = lax.ppermute(records[:, :, time - HALF :], "wide", [(i, i + 1) for i in range(nwide - 1)])
    virt, rows, toeplitz, forward = early(records, taps[None])
    near = spectra(records, halo, toeplitz, forward, pair_sources, me, 0, half, (rows, virt))
    order = list(range(nwide - 1, 0, -1))
    for m in order[:-2]:
        near[m] = swap(near[m], "wide", m)
    held = after(halo, [near[n] for n in order[:2]])
    far = spectra(records, held, toeplitz, forward, pair_sources, me, half, half)
    for m in order[-2:]:
        near[m] = swap(after(near[m], [far[0]]), "wide", m)

    top = nnar // 2
    picked = collect(near, wins * 2 * nv)
    slots = {0: picked, **{n: swap(picked, "narrow", n) for n in (top, 1) if n}}
    for i, m in enumerate(order):
        if i == 3:
            waits = [far[n] for n in order[:2]]
            bit = top
            while bit:
                for n in sorted(slots):
                    if n ^ bit not in slots:
                        slots[n ^ bit] = swap(after(slots[n], waits), "narrow", bit)
                bit //= 2
        far[m] = swap(after(far[m], [near[order[min(i + 2, nwide - 2)]]]), "wide", m)
    table = sources([slots[n] for n in range(nnar)], me, place, wins, nv)
    lag = jnp.asarray(lag_table())
    out = stack(near, table, pair_counts, me, lag, None, 0, half, wins, chans)
    return stack(far, table, pair_counts, me, lag, out, half, half, wins, chans)


def solution(mesh):
    return jax.shard_map(
        on_device,
        mesh=mesh,
        in_specs=(P(None, "narrow", "wide"), P(), P(), P("wide")),
        out_specs=P("wide", None, "narrow", None, None),
        check_vma=False,
    )
```

time: 119 us -> 105 us (0.88)
  waiting for transfers between devices: 27.1 us -> 19.3 us
  local copies, waits for them, and re-layouts: 11.7 us -> 5.46 us
  starting transfers between devices: 42.9 us -> 47.2 us
  Pallas kernels: 36 us -> 31.7 us
    ppermute x6 -> x18, starting transfers between devices: 14.3 us -> 47.2 us  [the longest x17 42.3 us: swap(): lax.ppermute(value, axis, [(i, i ^ mask) for i in range(lax.axis_size(axi...]
    all_to_all x3 -> x0, starting transfers between devices: 28.5 us -> none  [the longest x2 21.9 us: on_device(): lax.all_to_all(chunk, 'wide', split_axis=0, concat_axis=0, tiled=True)]
    unnamed x29 -> x15, local copies, waits for them, and re-layouts: 11.7 us -> 4.38 us
    ppermute x6 -> x18, waiting for transfers between devices: 25.3 us -> 19.3 us  [the longest x17 13.2 us: swap(): lax.ppermute(value, axis, [(i, i ^ mask) for i in range(lax.axis_size(axi...]
    pallas_call x6, Pallas kernels: 34.7 us -> 30.4 us  [the longest x2 17.7 us: stack(): pl.pallas_call(lambda *refs: stack_kernel(nw, wins, size, group, *refs),...]
    all_to_all x3 -> x0, waiting for transfers between devices: 1.81 us -> none  [the longest x2 1.8 us: on_device(): lax.all_to_all(chunk, 'wide', split_axis=0, concat_axis=0, tiled=True)]
  transfers between devices with their start and end apart: 9 -> 18, of which waited for: 5 -> 6; matrix products, arithmetic and copies ran while one was open for 1% -> 1% of each run, Pallas kernels for 16% -> 16%
where the time goes in v2:
time: 105 us
  starting transfers between devices  47.2 us (45%)
  Pallas kernels  31.7 us (30%)
  waiting for transfers between devices  19.3 us (18%)
  local copies, waits for them, and re-layouts  5.46 us (5%)
    ppermute x17, starting transfers between devices, swap(): lax.ppermute(value, axis, [(i, i ^ mask) for i in range(lax.axis_size(axi...  42.3 us
    pallas_call x2, Pallas kernels, stack(): pl.pallas_call(lambda *refs: stack_kernel(nw, wins, size, group, *refs),...  17.7 us
    ppermute x17, waiting for transfers between devices, swap(): lax.ppermute(value, axis, [(i, i ^ mask) for i in range(lax.axis_size(axi...  13.2 us
    pallas_call x2, Pallas kernels, spectra(): pl.pallas_call(lambda *refs: spectra_kernel(start, size, *refs), in_specs...  12 us
    ppermute x1, waiting for transfers between devices, on_device(): lax.ppermute(records[:, :, time - HALF:], 'wide', [(i, i + 1) for i in ra...  6.09 us
    ppermute x1, starting transfers between devices, on_device(): lax.ppermute(records[:, :, time - HALF:], 'wide', [(i, i + 1) for i in ra...  4.88 us
    unnamed x15, local copies, waits for them, and re-layouts  4.38 us
  transfers between devices with their start and end apart: 18, of which 6 were waited for; matrix products, arithmetic and copies ran while one was open for 1% of the time, Pallas kernels for 16%

profile of v2, /device:TPU:0, one launch (start us, length us, event | category | flops | bytes accessed | tf_op | source)
XLA Modules:
  0.0 104.5 jit_solution(10717479125023007017)
XLA Ops:
  0.0 1.1 %slice.3 = bf16[8,128,256]{2,1,0:T(8,128)(2,1)S(1)} slice(bf16[8,128,1536]{2,1,0:T(8,128)(2,1)} %refs_2_.3), slice={[0:8], [0:128], [1280:1536]} | slice | bytes 1048576 | tf_op jit(solution)/shard_map/slice | solution.py:379
  1.1 4.9 %collective-permute-start = (bf16[8,128,256]{2,1,0:T(8,128)(2,1)S(1)}, bf16[8,128,256]{2,1,0:T(8,128)(2,1)S(1)}, u32[]{:S(2)}, u32[]{:S(2)}) collective-permute-start(bf16[8,128,256]{2,1,0:T(8,128)(2,1)S(1)} %slice.3), channel_id=1, source_target_pairs={{0,4},{4,8},{8,12},{12,16},{16,20},{20,24},{24,28},{1,5},{5,9},{9,... | collective-permute-start | bytes 1572872 | tf_op jit(solution)/shard_map/ppermute | solution.py:379
  6.0 0.8 copy.9.refs_0_
  6.7 1.9 %copy-done = bf16[8,128,1536]{2,1,0:T(8,128)(2,1)S(1)} copy-done((bf16[8,128,1536]{2,1,0:T(8,128)(2,1)S(1)}, bf16[8,128,1536]{2,1,0:T(8,128)(2,1)}, u32[]{:S(2)}) %copy-start) | copy-done | bytes 3145752
  8.6 1.0 copy-done.2
  9.7 0.7 copy-done.3
  10.3 0.7 early.1
  11.0 6.1 %collective-permute-done.refs_3_ = bf16[8,128,256]{2,1,0:T(8,128)(2,1)S(1)} collective-permute-done((bf16[8,128,256]{2,1,0:T(8,128)(2,1)S(1)}, bf16[8,128,256]{2,1,0:T(8,128)(2,1)S(1)}, u32[]{:S(2)}, u32[]{:S(2)}) %collective-permute-start) | collective-permute-done | bytes 524320 | tf_op jit(solution)/shard_map/ppermute | solution.py:379
  17.1 6.2 %spectra.2 = (bf16[576,128]{1,0:T(8,128)(2,1)S(1)}, bf16[576,128]{1,0:T(8,128)(2,1)S(1)}, bf16[576,128]{1,0:T(8,128)(2,1)S(1)}, bf16[576,128]{1,0:T(8,128)(2,1)S...) custom-call(s32[8,4]{1,0:T(8,128)S(1)} %copy.9.refs_0_, ...), custom_call_target="tpu_custom_call" | custom-call | flops 1207959552 | bytes 2359296 | tf_op jit(solution)/shard_map/spectra/pallas_call | solution.py:168
  23.3 5.6 %collective-permute-start.1 = (bf16[576,128]{1,0:T(8,128)(2,1)S(1)}, bf16[576,128]{1,0:T(8,128)(2,1)S(1)}, u32[]{:S(2)}, u32[]{:S(2)}) collective-permute-start(bf16[576,128]{1,0:T(8,128)(2,1)S(1)} %get-tuple-element.40), channel_id=1, source_target_pairs={{0,28},{4,24},{8,20},{12,16},{16,12},{20,8},{24,4},{28,0},{1,29},{... | collective-permute-start | bytes 442376 | tf_op jit(solution)/shard_map/ppermute | solution.py:364
  28.9 0.2 collective-permute-start.2
  29.1 0.6 collective-permute-start.9
  29.8 4.4 %collective-permute-start.11 = (bf16[576,128]{1,0:T(8,128)(2,1)S(1)}, bf16[576,128]{1,0:T(8,128)(2,1)S(1)}, u32[]{:S(2)}, u32[]{:S(2)}) collective-permute-start(bf16[576,128]{1,0:T(8,128)(2,1)S(1)} %get-tuple-element.60), channel_id=1, source_target_pairs={{0,16},{4,20},{8,24},{12,28},{16,0},{20,4},{24,8},{28,12},{1,17},{... | collective-permute-start | bytes 442376 | tf_op jit(solution)/shard_map/ppermute | solution.py:364
  34.2 3.4 %collective-permute-done.2.refs_6_.refs_8_ = bf16[576,128]{1,0:T(8,128)(2,1)S(1)} collective-permute-done((bf16[576,128]{1,0:T(8,128)(2,1)S(1)}, bf16[576,128]{1,0:T(8,128)(2,1)S(1)}, u32[]{:S(2)}, u32[]{:S(2)}) %collective-permute-start.2) | collective-permute-done | bytes 147488 | tf_op jit(solution)/shard_map/ppermute | solution.py:364
  37.6 5.8 %spectra.3 = (bf16[384,128]{1,0:T(8,128)(2,1)S(1)}, bf16[384,128]{1,0:T(8,128)(2,1)S(1)}, bf16[384,128]{1,0:T(8,128)(2,1)S(1)}, bf16[384,128]{1,0:T(8,128)(2,1)S...) custom-call(s32[8,4]{1,0:T(8,128)S(1)} %copy.9.refs_0_, ...), custom_call_target="tpu_custom_call" | custom-call | flops 1207959552 | bytes 2359296 | tf_op jit(solution)/shard_map/spectra/pallas_call | solution.py:168
  43.5 1.5 %collective-permute-start.3 = (bf16[576,128]{1,0:T(8,128)(2,1)S(1)}, bf16[576,128]{1,0:T(8,128)(2,1)S(1)}, u32[]{:S(2)}, u32[]{:S(2)}) collective-permute-start(bf16[576,128]{1,0:T(8,128)(2,1)S(1)} %get-tuple-element.46), channel_id=1, source_target_pairs={{0,4},{4,0},{8,12},{12,8},{16,20},{20,16},{24,28},{28,24},{1,5},{5... | collective-permute-start | bytes 442376 | tf_op jit(solution)/shard_map/ppermute | solution.py:364
  45.0 11.0 %collective-permute-start.7 = (bf16[576,128]{1,0:T(8,128)(2,1)S(1)}, bf16[576,128]{1,0:T(8,128)(2,1)S(1)}, u32[]{:S(2)}, u32[]{:S(2)}) collective-permute-start(bf16[576,128]{1,0:T(8,128)(2,1)S(1)} %get-tuple-element.54), channel_id=1, source_target_pairs={{0,8},{4,12},{8,0},{12,4},{16,24},{20,28},{24,16},{28,20},{1,9},{5... | collective-permute-start | bytes 442376 | tf_op jit(solution)/shard_map/ppermute | solution.py:364
  55.9 3.1 %collective-permute-done.7.refs_2_.refs_4_ = bf16[576,128]{1,0:T(8,128)(2,1)S(1)} collective-permute-done((bf16[576,128]{1,0:T(8,128)(2,1)S(1)}, bf16[576,128]{1,0:T(8,128)(2,1)S(1)}, u32[]{:S(2)}, u32[]{:S(2)}) %collective-permute-start.7) | collective-permute-done | bytes 147488 | tf_op jit(solution)/shard_map/ppermute | solution.py:364
  59.1 3.4 %collective-permute-start.12 = (bf16[384,128]{1,0:T(8,128)(2,1)S(1)}, bf16[384,128]{1,0:T(8,128)(2,1)S(1)}, u32[]{:S(2)}, u32[]{:S(2)}) collective-permute-start(bf16[384,128]{1,0:T(8,128)(2,1)S(1)} %get-tuple-element.61), channel_id=1, source_target_pairs={{0,24},{4,28},{8,16},{12,20},{16,8},{20,12},{24,0},{28,4},{1,25},{... | collective-permute-start | bytes 294920 | tf_op jit(solution)/shard_map/ppermute | solution.py:364
  62.6 0.5 collective-permute-start.14
  63.1 1.5 %collective-permute-start.16 = (bf16[8,4,48,128]{3,2,1,0:T(8,128)(2,1)S(1)}, bf16[8,4,48,128]{3,2,1,0:T(8,128)(2,1)S(1)}, u32[]{:S(2)}, u32[]{:S(2)}) collective-permute-start(bf16[8,4,48,128]{3,2,1,0:T(8,128)(2,1)S(1)} %collect.1.refs_2_), channel_id=1, source_target_pairs={{0,2},{1,3},{2,0},{3,1},{4,6},{5,7},{6,4},{7,5},{8,10},{9,11},{10,... | collective-permute-start | bytes 1179656 | tf_op jit(solution)/shard_map/ppermute | solution.py:364
  64.6 1.7 %collective-permute-done.12.refs_8_ = bf16[384,128]{1,0:T(8,128)(2,1)S(1)} collective-permute-done((bf16[384,128]{1,0:T(8,128)(2,1)S(1)}, bf16[384,128]{1,0:T(8,128)(2,1)S(1)}, u32[]{:S(2)}, u32[]{:S(2)}) %collective-permute-start.12) | collective-permute-done | bytes 98336 | tf_op jit(solution)/shard_map/ppermute | solution.py:364
  66.3 4.0 %collective-permute-done.14.refs_9_ = bf16[384,128]{1,0:T(8,128)(2,1)S(1)} collective-permute-done((bf16[384,128]{1,0:T(8,128)(2,1)S(1)}, bf16[384,128]{1,0:T(8,128)(2,1)S(1)}, u32[]{:S(2)}, u32[]{:S(2)}) %collective-permute-start.14) | collective-permute-done | bytes 98336 | tf_op jit(solution)/shard_map/ppermute | solution.py:364
  70.3 1.6 %collective-permute-start.17 = (bf16[8,4,48,128]{3,2,1,0:T(8,128)(2,1)S(1)}, bf16[8,4,48,128]{3,2,1,0:T(8,128)(2,1)S(1)}, u32[]{:S(2)}, u32[]{:S(2)}) collective-permute-start(bf16[8,4,48,128]{3,2,1,0:T(8,128)(2,1)S(1)} %collective-permute-done.15.refs_3_), channel_id=1, source_target_pairs={{0,2},{1,3},{2,0},{3,1},{4,6},{5,7},{6,4},{7,5},{8,10},{9,11},{10,... | collective-permute-start | bytes 1179656 | tf_op jit(solution)/shard_map/ppermute | solution.py:364
  72.5 5.3 %collective-permute-start.10 = (bf16[384,128]{1,0:T(8,128)(2,1)}, bf16[384,128]{1,0:T(8,128)(2,1)S(1)}, u32[]{:S(2)}, u32[]{:S(2)}) collective-permute-start(bf16[384,128]{1,0:T(8,128)(2,1)} %copy-done.6), channel_id=1, source_target_pairs={{0,20},{4,16},{8,28},{12,24},{16,4},{20,0},{24,12},{28,8},{1,21},{... | collective-permute-start | bytes 294920 | tf_op jit(solution)/shard_map/ppermute | solution.py:364
  77.8 0.6 collective-permute-start.4
  78.4 2.9 %collective-permute-start.6 = (bf16[384,128]{1,0:T(8,128)(2,1)S(1)}, bf16[384,128]{1,0:T(8,128)(2,1)S(1)}, u32[]{:S(2)}, u32[]{:S(2)}) collective-permute-start(bf16[384,128]{1,0:T(8,128)(2,1)S(1)} %get-tuple-element.51), channel_id=1, source_target_pairs={{0,12},{4,8},{8,4},{12,0},{16,28},{20,24},{24,20},{28,16},{1,13},{... | collective-permute-start | bytes 294920 | tf_op jit(solution)/shard_map/ppermute | solution.py:364
  81.3 1.1 %collective-permute-done.17.refs_5_ = bf16[8,4,48,128]{3,2,1,0:T(8,128)(2,1)S(1)} collective-permute-done((bf16[8,4,48,128]{3,2,1,0:T(8,128)(2,1)S(1)}, bf16[8,4,48,128]{3,2,1,0:T(8,128)(2,1)S(1)}, u32[]{:S(2)}, u32[]{:S(2)}) %collective-permute-start.17) | collective-permute-done | bytes 393248 | tf_op jit(solution)/shard_map/ppermute | solution.py:364
  82.4 3.1 %collective-permute-start.8 = (bf16[384,128]{1,0:T(8,128)(2,1)S(1)}, bf16[384,128]{1,0:T(8,128)(2,1)S(1)}, u32[]{:S(2)}, u32[]{:S(2)}) collective-permute-start(bf16[384,128]{1,0:T(8,128)(2,1)S(1)} %get-tuple-element.55), channel_id=1, source_target_pairs={{0,16},{4,20},{8,24},{12,28},{16,0},{20,4},{24,8},{28,12},{1,17},{... | collective-permute-start | bytes 294920 | tf_op jit(solution)/shard_map/ppermute | solution.py:364
  85.5 1.3 %sources.1 = bf16[128,48,256]{2,1,0:T(8,128)(2,1)S(1)} custom-call(s32[1]{0:T(128)} %bitcast.refs_1_.refs_0_, s32[1]{0:T(128)} %bitcast.2.refs_1_, bf16[8,4,48,128]{3,2,1,0:T(8,128)(2,1)S(1)} %collect.1.refs_2_, bf16[8,4,48,128]{3,2,1,0:T(8,128)(2,1)S(1)} %collective-permute-done.15.refs_3_, bf16[8,4,48,128]{3,2,1,0:T(8,128)(2,1)S(1)} %collective-permute-done.16.refs_4_, ...), custom_call_target="tpu_custom_call" | custom-call | flops 100000000 | bytes 6291456 | tf_op jit(solution)/shard_map/sources/pallas_call | solution.py:239
  86.8 8.8 %stack.2.refs_12_ = bf16[1,4,128,32,256]{4,3,2,1,0:T(8,128)(2,1)} custom-call(s32[1]{0:T(128)S(6)} %copy.11.refs_0_, s32[1]{0:T(128)} %bitcast.refs_1_.refs_0_, bf16[576,128]{1,0:T(8,128)(2,1)S(1)} %get-tuple-element.65.refs_0_.refs_2_, bf16[576,128]{1,0:T(8,128)(2,1)S(1)} %collective-permute-done.3.refs_1_.refs_3_, ...), custom_call_target="tpu_custom_call" | custom-call | flops 2147483648 | bytes 7340032 | tf_op jit(solution)/shard_map/stack/pallas_call | solution.py:337
  95.7 8.8 %stack.3 = bf16[1,4,128,32,256]{4,3,2,1,0:T(8,128)(2,1)} custom-call(s32[1]{0:T(128)S(6)} %copy.11.refs_0_, s32[1]{0:T(128)} %bitcast.refs_1_.refs_0_, bf16[384,128]{1,0:T(8,128)(2,1)S(1)} %get-tuple-element.43.refs_2_, bf16[384,128]{1,0:T(8,128)(2,1)S(1)} %collective-permute-done.4.refs_3_, ...), custom_call_target="tpu_custom_call", output_to_operand_aliasing={{}: (12, {})} | custom-call | flops 2147483648 | bytes 7340032 | tf_op jit(solution)/shard_map/stack/pallas_call | solution.py:337
  (27 shorter events, 0.2 us)
Async XLA Ops:
  1.1 16.0 %collective-permute-start = (bf16[8,128,256]{2,1,0:T(8,128)(2,1)S(1)}, bf16[8,128,256]{2,1,0:T(8,128)(2,1)S(1)}, u32[]{:S(2)}, u32[]{:S(2)}) collective-permute-start(bf16[8,128,256]{2,1,0:T(8,128)(2,1)S(1)} %slice.3), channel_id=1, source_target_pairs={{0,4},{4,8},{8,12},{12,16},{16,20},{20,24},{24,28},{1,5},{5,9},{9,... | collective-permute-start | bytes 1572872 | tf_op jit(solution)/shard_map/ppermute | solution.py:379
  6.7 1.9 %copy-start = (bf16[8,128,1536]{2,1,0:T(8,128)(2,1)S(1)}, bf16[8,128,1536]{2,1,0:T(8,128)(2,1)}, u32[]{:S(2)}) copy-start(bf16[8,128,1536]{2,1,0:T(8,128)(2,1)} %refs_2_.3) | copy-start | bytes 9437188
  8.6 1.0 copy-start.2
  9.7 0.7 copy-start.3
  11.0 75.8 %copy-start.1 = (f32[256,256]{1,0:T(8,128)S(1)}, f32[256,256]{1,0:T(8,128)}, u32[]{:S(2)}) copy-start(f32[256,256]{1,0:T(8,128)} %constant.14.clone.refs_11_) | copy-start | bytes 786436
  23.3 10.9 %collective-permute-start.1 = (bf16[576,128]{1,0:T(8,128)(2,1)S(1)}, bf16[576,128]{1,0:T(8,128)(2,1)S(1)}, u32[]{:S(2)}, u32[]{:S(2)}) collective-permute-start(bf16[576,128]{1,0:T(8,128)(2,1)S(1)} %get-tuple-element.40), channel_id=1, source_target_pairs={{0,28},{4,24},{8,20},{12,16},{16,12},{20,8},{24,4},{28,0},{1,29},{... | collective-permute-start | bytes 442376 | tf_op jit(solution)/shard_map/ppermute | solution.py:364
  28.9 8.7 %collective-permute-start.2 = (bf16[576,128]{1,0:T(8,128)(2,1)S(1)}, bf16[576,128]{1,0:T(8,128)(2,1)S(1)}, u32[]{:S(2)}, u32[]{:S(2)}) collective-permute-start(bf16[576,128]{1,0:T(8,128)(2,1)S(1)} %get-tuple-element.41), channel_id=1, source_target_pairs={{0,24},{4,28},{8,16},{12,20},{16,8},{20,12},{24,0},{28,4},{1,25},{... | collective-permute-start | bytes 442376 | tf_op jit(solution)/shard_map/ppermute | solution.py:364
  29.1 26.8 %collective-permute-start.9 = (bf16[576,128]{1,0:T(8,128)(2,1)S(1)}, bf16[576,128]{1,0:T(8,128)(2,1)S(1)}, u32[]{:S(2)}, u32[]{:S(2)}) collective-permute-start(bf16[576,128]{1,0:T(8,128)(2,1)S(1)} %get-tuple-element.57), channel_id=1, source_target_pairs={{0,12},{4,8},{8,4},{12,0},{16,28},{20,24},{24,20},{28,16},{1,13},{... | collective-permute-start | bytes 442376 | tf_op jit(solution)/shard_map/ppermute | solution.py:364
  29.8 26.1 %collective-permute-start.11 = (bf16[576,128]{1,0:T(8,128)(2,1)S(1)}, bf16[576,128]{1,0:T(8,128)(2,1)S(1)}, u32[]{:S(2)}, u32[]{:S(2)}) collective-permute-start(bf16[576,128]{1,0:T(8,128)(2,1)S(1)} %get-tuple-element.60), channel_id=1, source_target_pairs={{0,16},{4,20},{8,24},{12,28},{16,0},{20,4},{24,8},{28,12},{1,17},{... | collective-permute-start | bytes 442376 | tf_op jit(solution)/shard_map/ppermute | solution.py:364
  34.2 21.8 %collective-permute-start.13 = (bf16[576,128]{1,0:T(8,128)(2,1)S(1)}, bf16[576,128]{1,0:T(8,128)(2,1)S(1)}, u32[]{:S(2)}, u32[]{:S(2)}) collective-permute-start(bf16[576,128]{1,0:T(8,128)(2,1)S(1)} %get-tuple-element.63), channel_id=1, source_target_pairs={{0,20},{4,16},{8,28},{12,24},{16,4},{20,0},{24,12},{28,8},{1,21},{... | collective-permute-start | bytes 442376 | tf_op jit(solution)/shard_map/ppermute | solution.py:364
  43.4 26.8 %copy-start.4 = (bf16[384,128]{1,0:T(8,128)(2,1)}, bf16[384,128]{1,0:T(8,128)(2,1)S(1)}, u32[]{:S(2)}) copy-start(bf16[384,128]{1,0:T(8,128)(2,1)S(1)} %get-tuple-element.49) | copy-start | bytes 294916
  43.4 26.8 %copy-start.5 = (bf16[384,128]{1,0:T(8,128)(2,1)}, bf16[384,128]{1,0:T(8,128)(2,1)S(1)}, u32[]{:S(2)}) copy-start(bf16[384,128]{1,0:T(8,128)(2,1)S(1)} %get-tuple-element.47) | copy-start | bytes 294916
  43.4 26.8 %copy-start.6 = (bf16[384,128]{1,0:T(8,128)(2,1)}, bf16[384,128]{1,0:T(8,128)(2,1)S(1)}, u32[]{:S(2)}) copy-start(bf16[384,128]{1,0:T(8,128)(2,1)S(1)} %get-tuple-element.58) | copy-start | bytes 294916
  43.5 12.5 %collective-permute-start.3 = (bf16[576,128]{1,0:T(8,128)(2,1)S(1)}, bf16[576,128]{1,0:T(8,128)(2,1)S(1)}, u32[]{:S(2)}, u32[]{:S(2)}) collective-permute-start(bf16[576,128]{1,0:T(8,128)(2,1)S(1)} %get-tuple-element.46), channel_id=1, source_target_pairs={{0,4},{4,0},{8,12},{12,8},{16,20},{20,16},{24,28},{28,24},{1,5},{5... | collective-permute-start | bytes 442376 | tf_op jit(solution)/shard_map/ppermute | solution.py:364
  45.0 14.1 %collective-permute-start.7 = (bf16[576,128]{1,0:T(8,128)(2,1)S(1)}, bf16[576,128]{1,0:T(8,128)(2,1)S(1)}, u32[]{:S(2)}, u32[]{:S(2)}) collective-permute-start(bf16[576,128]{1,0:T(8,128)(2,1)S(1)} %get-tuple-element.54), channel_id=1, source_target_pairs={{0,8},{4,12},{8,0},{12,4},{16,24},{20,28},{24,16},{28,20},{1,9},{5... | collective-permute-start | bytes 442376 | tf_op jit(solution)/shard_map/ppermute | solution.py:364
  59.1 11.2 %collective-permute-start.15 = (bf16[8,4,48,128]{3,2,1,0:T(8,128)(2,1)S(1)}, bf16[8,4,48,128]{3,2,1,0:T(8,128)(2,1)S(1)}, u32[]{:S(2)}, u32[]{:S(2)}) collective-permute-start(bf16[8,4,48,128]{3,2,1,0:T(8,128)(2,1)S(1)} %collect.1.refs_2_), channel_id=1, source_target_pairs={{0,1},{1,0},{2,3},{3,2},{4,5},{5,4},{6,7},{7,6},{8,9},{9,8},{10,11... | collective-permute-start | bytes 1179656 | tf_op jit(solution)/shard_map/ppermute | solution.py:364
  59.1 7.1 %collective-permute-start.12 = (bf16[384,128]{1,0:T(8,128)(2,1)S(1)}, bf16[384,128]{1,0:T(8,128)(2,1)S(1)}, u32[]{:S(2)}, u32[]{:S(2)}) collective-permute-start(bf16[384,128]{1,0:T(8,128)(2,1)S(1)} %get-tuple-element.61), channel_id=1, source_target_pairs={{0,24},{4,28},{8,16},{12,20},{16,8},{20,12},{24,0},{28,4},{1,25},{... | collective-permute-start | bytes 294920 | tf_op jit(solution)/shard_map/ppermute | solution.py:364
  62.6 7.7 %collective-permute-start.14 = (bf16[384,128]{1,0:T(8,128)(2,1)S(1)}, bf16[384,128]{1,0:T(8,128)(2,1)S(1)}, u32[]{:S(2)}, u32[]{:S(2)}) collective-permute-start(bf16[384,128]{1,0:T(8,128)(2,1)S(1)} %get-tuple-element.64), channel_id=1, source_target_pairs={{0,28},{4,24},{8,20},{12,16},{16,12},{20,8},{24,4},{28,0},{1,29},{... | collective-permute-start | bytes 294920 | tf_op jit(solution)/shard_map/ppermute | solution.py:364
  63.1 15.4 %collective-permute-start.16 = (bf16[8,4,48,128]{3,2,1,0:T(8,128)(2,1)S(1)}, bf16[8,4,48,128]{3,2,1,0:T(8,128)(2,1)S(1)}, u32[]{:S(2)}, u32[]{:S(2)}) collective-permute-start(bf16[8,4,48,128]{3,2,1,0:T(8,128)(2,1)S(1)} %collect.1.refs_2_), channel_id=1, source_target_pairs={{0,2},{1,3},{2,0},{3,1},{4,6},{5,7},{6,4},{7,5},{8,10},{9,11},{10,... | collective-permute-start | bytes 1179656 | tf_op jit(solution)/shard_map/ppermute | solution.py:364
  70.3 12.1 %collective-permute-start.17 = (bf16[8,4,48,128]{3,2,1,0:T(8,128)(2,1)S(1)}, bf16[8,4,48,128]{3,2,1,0:T(8,128)(2,1)S(1)}, u32[]{:S(2)}, u32[]{:S(2)}) collective-permute-start(bf16[8,4,48,128]{3,2,1,0:T(8,128)(2,1)S(1)} %collective-permute-done.15.refs_3_), channel_id=1, source_target_pairs={{0,2},{1,3},{2,0},{3,1},{4,6},{5,7},{6,4},{7,5},{8,10},{9,11},{10,... | collective-permute-start | bytes 1179656 | tf_op jit(solution)/shard_map/ppermute | solution.py:364
  72.5 23.1 %collective-permute-start.10 = (bf16[384,128]{1,0:T(8,128)(2,1)}, bf16[384,128]{1,0:T(8,128)(2,1)S(1)}, u32[]{:S(2)}, u32[]{:S(2)}) collective-permute-start(bf16[384,128]{1,0:T(8,128)(2,1)} %copy-done.6), channel_id=1, source_target_pairs={{0,20},{4,16},{8,28},{12,24},{16,4},{20,0},{24,12},{28,8},{1,21},{... | collective-permute-start | bytes 294920 | tf_op jit(solution)/shard_map/ppermute | solution.py:364
  77.8 17.8 %collective-permute-start.4 = (bf16[384,128]{1,0:T(8,128)(2,1)}, bf16[384,128]{1,0:T(8,128)(2,1)S(1)}, u32[]{:S(2)}, u32[]{:S(2)}) collective-permute-start(bf16[384,128]{1,0:T(8,128)(2,1)} %copy-done.5), channel_id=1, source_target_pairs={{0,4},{4,0},{8,12},{12,8},{16,20},{20,16},{24,28},{28,24},{1,5},{5... | collective-permute-start | bytes 294920 | tf_op jit(solution)/shard_map/ppermute | solution.py:364
  78.4 17.2 %collective-permute-start.5 = (bf16[384,128]{1,0:T(8,128)(2,1)}, bf16[384,128]{1,0:T(8,128)(2,1)S(1)}, u32[]{:S(2)}, u32[]{:S(2)}) collective-permute-start(bf16[384,128]{1,0:T(8,128)(2,1)} %copy-done.4), channel_id=1, source_target_pairs={{0,8},{4,12},{8,0},{12,4},{16,24},{20,28},{24,16},{28,20},{1,9},{5... | collective-permute-start | bytes 294920 | tf_op jit(solution)/shard_map/ppermute | solution.py:364
  78.4 17.2 %collective-permute-start.6 = (bf16[384,128]{1,0:T(8,128)(2,1)S(1)}, bf16[384,128]{1,0:T(8,128)(2,1)S(1)}, u32[]{:S(2)}, u32[]{:S(2)}) collective-permute-start(bf16[384,128]{1,0:T(8,128)(2,1)S(1)} %get-tuple-element.51), channel_id=1, source_target_pairs={{0,12},{4,8},{8,4},{12,0},{16,28},{20,24},{24,20},{28,16},{1,13},{... | collective-permute-start | bytes 294920 | tf_op jit(solution)/shard_map/ppermute | solution.py:364
  82.4 13.3 %collective-permute-start.8 = (bf16[384,128]{1,0:T(8,128)(2,1)S(1)}, bf16[384,128]{1,0:T(8,128)(2,1)S(1)}, u32[]{:S(2)}, u32[]{:S(2)}) collective-permute-start(bf16[384,128]{1,0:T(8,128)(2,1)S(1)} %get-tuple-element.55), channel_id=1, source_target_pairs={{0,16},{4,20},{8,24},{12,28},{16,0},{20,4},{24,8},{28,12},{1,17},{... | collective-permute-start | bytes 294920 | tf_op jit(solution)/shard_map/ppermute | solution.py:364

commit v3 on v2

--- a/solution.py
+++ b/solution.py
@@ -81,124 +81,104 @@
     return jnp.concatenate(parts, 0).astype(BF)
 
 
-def early_kernel(rec_ref, taps_ref, table_ref, virt_ref, rows_ref, toeplitz_ref, forward_ref, row):
-    nblk, chans, time = rec_ref.shape
-    wins = time // WLEN - 1
-    nv = chans // VSTEP
-    count = nblk * nv
+def rows_kernel(rec_ref, rows_ref, near_ref, same_ref):
+    time = rec_ref.shape[2]
+    rows = virtual_rows(rec_ref, rec_ref.shape[1] // VSTEP)
+    rows_ref[...] = rows
+    near_ref[...] = rows[:, time - HALF :]
+
+
+def extract(records):
+    nblk, chans, time = records.shape
+    count = nblk * (chans // VSTEP)
+    vmem = pl.BlockSpec(memory_space=pltpu.VMEM)
+    return pl.pallas_call(
+        rows_kernel,
+        in_specs=[vmem],
+        out_specs=[vmem] * 3,
+        out_shape=[
+            jax.ShapeDtypeStruct((count, time), BF),
+            jax.ShapeDtypeStruct((count, HALF), BF),
+            jax.ShapeDtypeStruct(records.shape, BF),
+        ],
+        input_output_aliases={0: 2},
+        compiler_params=pltpu.CompilerParams(vmem_limit_bytes=40 * MIB),
+        cost_estimate=pl.CostEstimate(flops=0, bytes_accessed=records.size, transcendentals=0),
+        name="extract",
+    )(records)
+
+
+def virtual_kernel(nblk, pairs_ref, me_ref, rows_ref, halo_ref, taps_ref, table_ref, *refs):
+    picks, (toeplitz_ref, forward_ref, row, virt) = refs[:nblk], refs[nblk:]
+    count, time = rows_ref.shape
+    nv, wins = count // nblk, time // WLEN
     build_toeplitz(taps_ref, row, toeplitz_ref)
     forward_ref[...] = table_ref[...].astype(BF)
-    rows = virtual_rows(rec_ref, nv)
-    rows_ref[...] = rows[:, :WLEN]
-    block = (rows[:, HALF:WLEN], rows[:, WLEN:])
+    block = (halo_ref[...], rows_ref[...])
     result = transform([block], wins, count, toeplitz_ref[...], forward_ref[...])
     for b in range(nblk):
-        virt_ref[b] = block_rows(result, b, nv, wins, count)
-
-
-def early(records, taps):
-    nblk, chans, time = records.shape
-    nv = chans // VSTEP
-    vmem = pl.BlockSpec(memory_space=pltpu.VMEM)
-    return pl.pallas_call(
-        early_kernel,
-        in_specs=[vmem] * 3,
-        out_specs=[vmem] * 4,
-        out_shape=[
-            jax.ShapeDtypeStruct((nblk, (time // WLEN - 1) * 2 * nv, BINS), BF),
-            jax.ShapeDtypeStruct((nblk * nv, WLEN), BF),
-            jax.ShapeDtypeStruct((WLEN, HALF), BF),
-            jax.ShapeDtypeStruct((WLEN, 2 * BINS), BF),
-        ],
-        scratch_shapes=[pltpu.VMEM((8, 512), F32)],
+        virt[b] = block_rows(result, b, nv, wins, count)
+    for m in range(nblk):
+        for k in range(SLOTS):
+            picks[m][k] = virt[pairs_ref[me_ref[0] ^ m, k]]
+
+
+def virtual(rows, halo, taps, pairs, me, nblk):
+    count, time = rows.shape
+    size = (time // WLEN) * 2 * (count // nblk)
+    smem, vmem = pl.BlockSpec(memory_space=pltpu.SMEM), pl.BlockSpec(memory_space=pltpu.VMEM)
+    outs = pl.pallas_call(
+        lambda *refs: virtual_kernel(nblk, *refs),
+        in_specs=[smem, smem] + [vmem] * 4,
+        out_specs=[vmem] * (nblk + 2),
+        out_shape=[jax.ShapeDtypeStruct((SLOTS, size, BINS), BF)] * nblk
+        + [jax.ShapeDtypeStruct((WLEN, HALF), BF), jax.ShapeDtypeStruct((WLEN, 2 * BINS), BF)],
+        scratch_shapes=[pltpu.VMEM((8, 512), F32), pltpu.VMEM((nblk, size, BINS), BF)],
         compiler_params=pltpu.CompilerParams(vmem_limit_bytes=40 * MIB),
-        cost_estimate=pl.CostEstimate(flops=4 * 10**8, bytes_accessed=records.size * 2, transcendentals=0),
-        name="early",
-    )(records, taps, jnp.asarray(dft_table()))
-
-
-def spectra_kernel(start, size, pairs_ref, me_ref, rec_ref, halo_ref, toeplitz_ref, forward_ref, *refs):
-    held, sems = refs[-2:]
+        cost_estimate=pl.CostEstimate(flops=10**8, bytes_accessed=rows.size * 8, transcendentals=0),
+        name="virtual",
+    )(pairs, me, rows, halo, taps, jnp.asarray(dft_table()))
+    return list(outs[:nblk]), outs[nblk], outs[nblk + 1]
+
+
+def spectra_kernel(sizes, me_ref, rec_ref, halo_ref, toeplitz_ref, forward_ref, *refs):
     nblk, chans, time = rec_ref.shape
     wins = time // WLEN
-    nv = chans // VSTEP
+    outs = [refs[nblk * q : nblk * (q + 1)] for q in range(len(sizes))]
     me = me_ref[0]
-    copies = []
-    for m in range(nblk):
-        source = rec_ref.at[me ^ m, pl.ds(start, size)]
-        copies.append(pltpu.make_async_copy(source, held.at[m], sems.at[m]))
-        copies[-1].start()
-    if len(refs) > nblk + 2:
-        rows_ref, virt_ref, outs, virt = refs[0], refs[1], refs[2 : nblk + 2], refs[nblk + 2]
-        block = (virtual_rows(halo_ref, nv), rows_ref[...])
-        result = transform([block], 1, nblk * nv, toeplitz_ref[...], forward_ref[...])
-        for b in range(nblk):
-            virt[b] = block_rows(result, b, nv, 1, nblk * nv)
-        for m in range(nblk):
-            for k in range(SLOTS):
-                block = pairs_ref[me ^ m, k]
-                lo = wins * 2 * size + k * wins * 2 * nv
-                outs[m][lo : lo + 2 * nv] = virt[block]
-                outs[m][lo + 2 * nv : lo + wins * 2 * nv] = virt_ref[block]
-    else:
-        outs = refs[:nblk]
     per = 2
     for m in range(0, nblk, per):
-        blocks = []
-        for u in range(per):
-            copies[m + u].wait()
-            blocks.append((halo_ref[me ^ (m + u), start : start + size], held[m + u]))
-        result = transform(blocks, wins, size, toeplitz_ref[...], forward_ref[...]).astype(BF)
+        blocks = [(halo_ref[me ^ (m + u)], rec_ref[me ^ (m + u)]) for u in range(per)]
+        result = transform(blocks, wins, chans, toeplitz_ref[...], forward_ref[...]).astype(BF)
         for u in range(per):
             for w in range(wins):
                 for p in range(2):
-                    lo = (u * wins + w) * size
-                    row = (w * 2 + p) * size
-                    outs[m + u][row : row + size] = result[lo : lo + size, p * BINS : (p + 1) * BINS]
-
-
-def spectra(records, halo, toeplitz, forward, pairs, me, start, size, virtual=()):
+                    lo = (u * wins + w) * chans
+                    for out, size in zip(outs, sizes):
+                        row = (w * 2 + p) * size
+                        out[m + u][row : row + size] = result[lo : lo + size, p * BINS : (p + 1) * BINS]
+                        lo += size
+
+
+def spectra(records, halo, toeplitz, forward, me, sizes):
     nblk, chans, time = records.shape
     wins = time // WLEN
-    nv = chans // VSTEP
-    shape = (wins * 2 * size + (SLOTS * wins * 2 * nv if virtual else 0), BINS)
+    shapes = []
+    for size in sizes:
+        shapes += [(wins * 2 * size, BINS)] * nblk
     smem, vmem = pl.BlockSpec(memory_space=pltpu.SMEM), pl.BlockSpec(memory_space=pltpu.VMEM)
-    operands = [pairs, me, records, halo, toeplitz, forward, *virtual]
-    scratch = [pltpu.VMEM((nblk, 2 * nv, BINS), BF)] if virtual else []
     outs = pl.pallas_call(
-        lambda *refs: spectra_kernel(start, size, *refs),
-        in_specs=[smem, smem, pl.BlockSpec(memory_space=pl.ANY)] + [vmem] * (len(operands) - 3),
-        out_specs=[vmem] * nblk,
-        out_shape=[jax.ShapeDtypeStruct(shape, BF)] * nblk,
-        scratch_shapes=scratch + [pltpu.VMEM((nblk, size, time), BF), pltpu.SemaphoreType.DMA((nblk,))],
+        lambda *refs: spectra_kernel(sizes, *refs),
+        in_specs=[smem] + [vmem] * 4,
+        out_specs=[vmem] * len(shapes),
+        out_shape=[jax.ShapeDtypeStruct(shape, BF) for shape in shapes],
         compiler_params=pltpu.CompilerParams(vmem_limit_bytes=40 * MIB),
         cost_estimate=pl.CostEstimate(
-            flops=nblk * size * wins * 3 * 2 * 512 * 256, bytes_accessed=nblk * size * time * 3, transcendentals=0
+            flops=nblk * chans * wins * 3 * 2 * 512 * 256, bytes_accessed=nblk * chans * time * 3, transcendentals=0
         ),
         name="spectra",
-    )(*operands)
-    return list(outs)
-
-
-def collect_kernel(rows, *refs):
-    out_ref = refs[-1]
-    for m, ref in enumerate(refs[:-1]):
-        at = ref.shape[0] - SLOTS * rows
-        for k in range(SLOTS):
-            out_ref[m, k] = ref[at + k * rows : at + (k + 1) * rows]
-
-
-def collect(chunks, rows):
-    vmem = pl.BlockSpec(memory_space=pltpu.VMEM)
-    return pl.pallas_call(
-        lambda *refs: collect_kernel(rows, *refs),
-        in_specs=[vmem] * len(chunks),
-        out_specs=vmem,
-        out_shape=jax.ShapeDtypeStruct((len(chunks), SLOTS, rows, BINS), BF),
-        compiler_params=pltpu.CompilerParams(vmem_limit_bytes=32 * MIB),
-        cost_estimate=pl.CostEstimate(flops=0, bytes_accessed=len(chunks) * rows * 2048, transcendentals=0),
-        name="collect",
-    )(*chunks)
+    )(me, records, halo, toeplitz, forward)
+    return [list(outs[i : i + nblk]) for i in range(0, len(outs), nblk)]
 
 
 def sources_kernel(nsrc, nnar, wins, nv, me_ref, place_ref, *refs):
@@ -376,29 +356,30 @@
     half = chans // 2
     me = lax.axis_index("wide").astype(jnp.int32)[None]
     place = lax.axis_index("narrow").astype(jnp.int32)[None]
-    halo = lax.ppermute(records[:, :, time - HALF :], "wide", [(i, i + 1) for i in range(nwide - 1)])
-    virt, rows, toeplitz, forward = early(records, taps[None])
-    near = spectra(records, halo, toeplitz, forward, pair_sources, me, 0, half, (rows, virt))
+    ahead = [(i, i + 1) for i in range(nwide - 1)]
     order = list(range(nwide - 1, 0, -1))
-    for m in order[:-2]:
-        near[m] = swap(near[m], "wide", m)
-    held = after(halo, [near[n] for n in order[:2]])
-    far = spectra(records, held, toeplitz, forward, pair_sources, me, half, half)
-    for m in order[-2:]:
-        near[m] = swap(after(near[m], [far[0]]), "wide", m)
+    rows, tip, records = extract(records)
+    tip = lax.ppermute(tip, "wide", ahead)
+    halo = lax.ppermute(after(records[:, :, time - HALF :], [tip]), "wide", ahead)
+    picked, toeplitz, forward = virtual(rows, tip, taps[None], pair_sources, me, nblk)
+    for m in order:
+        picked[m] = swap(picked[m], "wide", m)
 
     top = nnar // 2
-    picked = collect(near, wins * 2 * nv)
+    picked = jnp.stack(picked)
     slots = {0: picked, **{n: swap(picked, "narrow", n) for n in (top, 1) if n}}
+    near, far = spectra(records, halo, toeplitz, forward, me, (half, half))
     for i, m in enumerate(order):
-        if i == 3:
-            waits = [far[n] for n in order[:2]]
+        if i == len(order) - 1:
             bit = top
             while bit:
                 for n in sorted(slots):
                     if n ^ bit not in slots:
-                        slots[n ^ bit] = swap(after(slots[n], waits), "narrow", bit)
+                        slots[n ^ bit] = swap(after(slots[n], [near[order[1]]]), "narrow", bit)
                 bit //= 2
+        waits = [slots[n] for n in sorted(slots) if n] if i >= len(order) - 2 else []
+        near[m] = swap(after(near[m], waits), "wide", m)
+    for i, m in enumerate(order):
         far[m] = swap(after(far[m], [near[order[min(i + 2, nwide - 2)]]]), "wide", m)
     table = sources([slots[n] for n in range(nnar)], me, place, wins, nv)
     lag = jnp.asarray(lag_table())

time: 105 us -> 109 us (1.038)
  Pallas kernels: 31.7 us -> 25.7 us
  waiting for transfers between devices: 19.3 us -> 24.6 us
  local copies, waits for them, and re-layouts: 5.46 us -> 9.31 us
    ppermute x17 -> x24, waiting for transfers between devices: 13.2 us -> 23.2 us  [swap(): lax.ppermute(value, axis, [(i, i ^ mask) for i in range(lax.axis_size(axi...]
    pallas_call x4 -> x3, Pallas kernels: 12.7 us -> 6.75 us  [the longest x1 5.25 us: spectra(): pl.pallas_call(lambda *refs: spectra_kernel(sizes, *refs), in_specs=[smem...]
    unnamed x15 -> x47, local copies, waits for them, and re-layouts: 4.38 us -> 9.26 us
    ppermute x1 -> x2, waiting for transfers between devices: 6.09 us -> 1.44 us  [the longest x1 1.44 us: on_device(): tip = lax.ppermute(tip, 'wide', ahead)]
    ppermute x1 -> x2, starting transfers between devices: 4.88 us -> 9.09 us  [the longest x1 4.84 us: on_device(): tip = lax.ppermute(tip, 'wide', ahead)]
    ppermute x17 -> x24, starting transfers between devices: 42.3 us -> 38.6 us  [swap(): lax.ppermute(value, axis, [(i, i ^ mask) for i in range(lax.axis_size(axi...]
  transfers between devices with their start and end apart: 18 -> 26, of which waited for: 6 -> 8; matrix products, arithmetic and copies ran while one was open for 1% -> 0% of each run, Pallas kernels for 16% -> 15%
where the time goes in v3:
time: 109 us; the launch traced here: 108 us
  starting transfers between devices  47.7 us (44%)
  Pallas kernels  25.7 us (24%)
  waiting for transfers between devices  24.6 us (23%)
  local copies, waits for them, and re-layouts  9.31 us (9%)
    ppermute x24, starting transfers between devices, swap(): lax.ppermute(value, axis, [(i, i ^ mask) for i in range(lax.axis_size(axi...  38.6 us
    ppermute x24, waiting for transfers between devices, swap(): lax.ppermute(value, axis, [(i, i ^ mask) for i in range(lax.axis_size(axi...  23.2 us
    pallas_call x2, Pallas kernels, stack(): pl.pallas_call(lambda *refs: stack_kernel(nw, wins, size, group, *refs),...  17.6 us
    unnamed x47, local copies, waits for them, and re-layouts  9.26 us
    pallas_call x1, Pallas kernels, spectra(): pl.pallas_call(lambda *refs: spectra_kernel(sizes, *refs), in_specs=[smem...  5.25 us
    ppermute x1, starting transfers between devices, on_device(): tip = lax.ppermute(tip, 'wide', ahead)  4.84 us
    ppermute x1, starting transfers between devices, on_device(): lax.ppermute(after(records[:, :, time - HALF:], [tip]), 'wide', ahead)  4.24 us
  transfers between devices with their start and end apart: 26, of which 8 were waited for; matrix products, arithmetic and copies ran while one was open for 0% of the time, Pallas kernels for 15%

profile of v3, /device:TPU:0, one launch (start us, length us, event | category | flops | bytes accessed | tf_op | source)
XLA Modules:
  0.0 108.3 jit_solution(3188820240073924253)
XLA Ops:
  0.0 1.9 %copy.21.rec_ref = bf16[8,128,1536]{2,1,0:T(8,128)(2,1)S(1)} copy(bf16[8,128,1536]{2,1,0:T(8,128)(2,1)} %param.6) | data formatting | bytes 6291456
  2.2 4.8 %collective-permute-start = (bf16[64,256]{1,0:T(8,128)(2,1)S(1)}, bf16[64,256]{1,0:T(8,128)(2,1)S(1)}, u32[]{:S(2)}, u32[]{:S(2)}) collective-permute-start(bf16[64,256]{1,0:T(8,128)(2,1)S(1)} %get-tuple-element.46), channel_id=1, source_target_pairs={{0,4},{4,8},{8,12},{12,16},{16,20},{20,24},{24,28},{1,5},{5,9},{9,... | collective-permute-start | bytes 98312 | tf_op jit(solution)/shard_map/ppermute | solution.py:362
  7.2 1.4 %collective-permute-done.refs_3_ = bf16[64,256]{1,0:T(8,128)(2,1)S(1)} collective-permute-done((bf16[64,256]{1,0:T(8,128)(2,1)S(1)}, bf16[64,256]{1,0:T(8,128)(2,1)S(1)}, u32[]{:S(2)}, u32[]{:S(2)}) %collective-permute-start) | collective-permute-done | bytes 32800 | tf_op jit(solution)/shard_map/ppermute | solution.py:362
  8.6 4.2 %collective-permute-start.1 = (bf16[8,128,256]{2,1,0:T(8,128)(2,1)S(1)}, bf16[8,128,256]{2,1,0:T(8,128)(2,1)S(1)}, u32[]{:S(2)}, u32[]{:S(2)}) collective-permute-start(bf16[8,128,256]{2,1,0:T(8,128)(2,1)S(1)} %slice.3), channel_id=1, source_target_pairs={{0,4},{4,8},{8,12},{12,16},{16,20},{20,24},{24,28},{1,5},{5,9},{9,... | collective-permute-start | bytes 1572872 | tf_op jit(solution)/shard_map/ppermute | solution.py:363
  12.9 1.0 copy-done.1
  13.9 1.2 %virtual.1 = (bf16[4,48,128]{2,1,0:T(8,128)(2,1)S(1)}, bf16[4,48,128]{2,1,0:T(8,128)(2,1)S(1)}, bf16[4,48,128]{2,1,0:T(8,128)(2,1)S(1)}, bf16[4,48,128]{2,1,0:T(...) custom-call(s32[8,4]{1,0:T(8,128)S(1)} %copy.9.refs_0_, ...), custom_call_target="tpu_custom_call" | custom-call | flops 100000000 | bytes 786432 | tf_op jit(solution)/shard_map/virtual/pallas_call | solution.py:130
  15.1 2.5 %collective-permute-start.2 = (bf16[4,48,128]{2,1,0:T(8,128)(2,1)S(1)}, bf16[4,48,128]{2,1,0:T(8,128)(2,1)S(1)}, u32[]{:S(2)}, u32[]{:S(2)}) collective-permute-start(bf16[4,48,128]{2,1,0:T(8,128)(2,1)S(1)} %get-tuple-element.55), channel_id=1, source_target_pairs={{0,4},{4,0},{8,12},{12,8},{16,20},{20,16},{24,28},{28,24},{1,5},{5... | collective-permute-start | bytes 147464 | tf_op jit(solution)/shard_map/ppermute | solution.py:344
  17.6 1.6 %collective-permute-start.3 = (bf16[4,48,128]{2,1,0:T(8,128)(2,1)S(1)}, bf16[4,48,128]{2,1,0:T(8,128)(2,1)S(1)}, u32[]{:S(2)}, u32[]{:S(2)}) collective-permute-start(bf16[4,48,128]{2,1,0:T(8,128)(2,1)S(1)} %get-tuple-element.56), channel_id=1, source_target_pairs={{0,8},{4,12},{8,0},{12,4},{16,24},{20,28},{24,16},{28,20},{1,9},{5... | collective-permute-start | bytes 147464 | tf_op jit(solution)/shard_map/ppermute | solution.py:344
  19.2 2.6 %collective-permute-start.5 = (bf16[4,48,128]{2,1,0:T(8,128)(2,1)S(1)}, bf16[4,48,128]{2,1,0:T(8,128)(2,1)S(1)}, u32[]{:S(2)}, u32[]{:S(2)}) collective-permute-start(bf16[4,48,128]{2,1,0:T(8,128)(2,1)S(1)} %get-tuple-element.58), channel_id=1, source_target_pairs={{0,16},{4,20},{8,24},{12,28},{16,0},{20,4},{24,8},{28,12},{1,17},{... | collective-permute-start | bytes 147464 | tf_op jit(solution)/shard_map/ppermute | solution.py:344
  21.8 3.2 %collective-permute-done.2 = bf16[4,48,128]{2,1,0:T(8,128)(2,1)S(1)} collective-permute-done((bf16[4,48,128]{2,1,0:T(8,128)(2,1)S(1)}, bf16[4,48,128]{2,1,0:T(8,128)(2,1)S(1)}, u32[]{:S(2)}, u32[]{:S(2)}) %collective-permute-start.2) | collective-permute-done | bytes 49184 | tf_op jit(solution)/shard_map/ppermute | solution.py:344
  25.0 4.5 %collective-permute-start.6 = (bf16[4,48,128]{2,1,0:T(8,128)(2,1)S(1)}, bf16[4,48,128]{2,1,0:T(8,128)(2,1)S(1)}, u32[]{:S(2)}, u32[]{:S(2)}) collective-permute-start(bf16[4,48,128]{2,1,0:T(8,128)(2,1)S(1)} %get-tuple-element.59), channel_id=1, source_target_pairs={{0,20},{4,16},{8,28},{12,24},{16,4},{20,0},{24,12},{28,8},{1,21},{... | collective-permute-start | bytes 147464 | tf_op jit(solution)/shard_map/ppermute | solution.py:344
  29.5 1.4 %collective-permute-start.7 = (bf16[4,48,128]{2,1,0:T(8,128)(2,1)S(1)}, bf16[4,48,128]{2,1,0:T(8,128)(2,1)S(1)}, u32[]{:S(2)}, u32[]{:S(2)}) collective-permute-start(bf16[4,48,128]{2,1,0:T(8,128)(2,1)S(1)} %get-tuple-element.60), channel_id=1, source_target_pairs={{0,24},{4,28},{8,16},{12,20},{16,8},{20,12},{24,0},{28,4},{1,25},{... | collective-permute-start | bytes 147464 | tf_op jit(solution)/shard_map/ppermute | solution.py:344
  30.9 2.9 %collective-permute-start.8 = (bf16[4,48,128]{2,1,0:T(8,128)(2,1)S(1)}, bf16[4,48,128]{2,1,0:T(8,128)(2,1)S(1)}, u32[]{:S(2)}, u32[]{:S(2)}) collective-permute-start(bf16[4,48,128]{2,1,0:T(8,128)(2,1)S(1)} %get-tuple-element.61), channel_id=1, source_target_pairs={{0,28},{4,24},{8,20},{12,16},{16,12},{20,8},{24,4},{28,0},{1,29},{... | collective-permute-start | bytes 147464 | tf_op jit(solution)/shard_map/ppermute | solution.py:344
  33.8 2.0 %collective-permute-done.7 = bf16[4,48,128]{2,1,0:T(8,128)(2,1)S(1)} collective-permute-done((bf16[4,48,128]{2,1,0:T(8,128)(2,1)S(1)}, bf16[4,48,128]{2,1,0:T(8,128)(2,1)S(1)}, u32[]{:S(2)}, u32[]{:S(2)}) %collective-permute-start.7) | collective-permute-done | bytes 49184 | tf_op jit(solution)/shard_map/ppermute | solution.py:344
  35.8 1.9 %collective-permute-done.8 = bf16[4,48,128]{2,1,0:T(8,128)(2,1)S(1)} collective-permute-done((bf16[4,48,128]{2,1,0:T(8,128)(2,1)S(1)}, bf16[4,48,128]{2,1,0:T(8,128)(2,1)S(1)}, u32[]{:S(2)}, u32[]{:S(2)}) %collective-permute-start.8) | collective-permute-done | bytes 49184 | tf_op jit(solution)/shard_map/ppermute | solution.py:344
  37.9 5.3 %spectra.1 = (bf16[384,128]{1,0:T(8,128)(2,1)S(1)}, bf16[384,128]{1,0:T(8,128)(2,1)}, bf16[384,128]{1,0:T(8,128)(2,1)}, bf16[384,128]{1,0:T(8,128)(2,1)S(1)}, bf...) custom-call(s32[1]{0:T(128)} %bitcast.refs_1_.refs_0_, ...), custom_call_target="tpu_custom_call" | custom-call | flops 2415919104 | bytes 4718592 | tf_op jit(solution)/shard_map/spectra/pallas_call | solution.py:170
  47.5 2.5 %collective-permute-start.11 = (bf16[384,128]{1,0:T(8,128)(2,1)S(1)}, bf16[384,128]{1,0:T(8,128)(2,1)S(1)}, u32[]{:S(2)}, u32[]{:S(2)}) collective-permute-start(bf16[384,128]{1,0:T(8,128)(2,1)S(1)} %get-tuple-element.62), channel_id=1, source_target_pairs={{0,24},{4,28},{8,16},{12,20},{16,8},{20,12},{24,0},{28,4},{1,25},{... | collective-permute-start | bytes 294920 | tf_op jit(solution)/shard_map/ppermute | solution.py:344
  50.0 1.5 %collective-permute-start.10 = (bf16[8,4,48,128]{3,2,1,0:T(8,128)(2,1)S(1)}, bf16[8,4,48,128]{3,2,1,0:T(8,128)(2,1)S(1)}, u32[]{:S(2)}, u32[]{:S(2)}) collective-permute-start(bf16[8,4,48,128]{3,2,1,0:T(8,128)(2,1)S(1)} %bitcast_dynamic-update-slice_fusion.refs_2_), channel_id=1, source_target_pairs={{0,2},{1,3},{2,0},{3,1},{4,6},{5,7},{6,4},{7,5},{8,10},{9,11},{10,... | collective-permute-start | bytes 1179656 | tf_op jit(solution)/shard_map/ppermute | solution.py:344
  51.5 3.0 %collective-permute-done.11.refs_8_ = bf16[384,128]{1,0:T(8,128)(2,1)S(1)} collective-permute-done((bf16[384,128]{1,0:T(8,128)(2,1)S(1)}, bf16[384,128]{1,0:T(8,128)(2,1)S(1)}, u32[]{:S(2)}, u32[]{:S(2)}) %collective-permute-start.11) | collective-permute-done | bytes 98336 | tf_op jit(solution)/shard_map/ppermute | solution.py:344
  54.5 1.5 %collective-permute-start.12 = (bf16[8,4,48,128]{3,2,1,0:T(8,128)(2,1)S(1)}, bf16[8,4,48,128]{3,2,1,0:T(8,128)(2,1)S(1)}, u32[]{:S(2)}, u32[]{:S(2)}) collective-permute-start(bf16[8,4,48,128]{3,2,1,0:T(8,128)(2,1)S(1)} %collective-permute-done.9.refs_3_), channel_id=1, source_target_pairs={{0,2},{1,3},{2,0},{3,1},{4,6},{5,7},{6,4},{7,5},{8,10},{9,11},{10,... | collective-permute-start | bytes 1179656 | tf_op jit(solution)/shard_map/ppermute | solution.py:344
  56.8 3.4 %collective-permute-start.21 = (bf16[384,128]{1,0:T(8,128)(2,1)S(1)}, bf16[384,128]{1,0:T(8,128)(2,1)S(1)}, u32[]{:S(2)}, u32[]{:S(2)}) collective-permute-start(bf16[384,128]{1,0:T(8,128)(2,1)S(1)} %get-tuple-element.78), channel_id=1, source_target_pairs={{0,16},{4,20},{8,24},{12,28},{16,0},{20,4},{24,8},{28,12},{1,17},{... | collective-permute-start | bytes 294920 | tf_op jit(solution)/shard_map/ppermute | solution.py:344
  60.7 1.2 %collective-permute-done.10.refs_4_ = bf16[8,4,48,128]{3,2,1,0:T(8,128)(2,1)S(1)} collective-permute-done((bf16[8,4,48,128]{3,2,1,0:T(8,128)(2,1)S(1)}, bf16[8,4,48,128]{3,2,1,0:T(8,128)(2,1)S(1)}, u32[]{:S(2)}, u32[]{:S(2)}) %collective-permute-start.10) | collective-permute-done | bytes 393248 | tf_op jit(solution)/shard_map/ppermute | solution.py:344
  62.6 7.0 %collective-permute-done.12.refs_5_ = bf16[8,4,48,128]{3,2,1,0:T(8,128)(2,1)S(1)} collective-permute-done((bf16[8,4,48,128]{3,2,1,0:T(8,128)(2,1)S(1)}, bf16[8,4,48,128]{3,2,1,0:T(8,128)(2,1)S(1)}, u32[]{:S(2)}, u32[]{:S(2)}) %collective-permute-start.12) | collective-permute-done | bytes 393248 | tf_op jit(solution)/shard_map/ppermute | solution.py:344
  70.6 1.9 %collective-permute-start.25 = (bf16[384,128]{1,0:T(8,128)(2,1)}, bf16[384,128]{1,0:T(8,128)(2,1)S(1)}, u32[]{:S(2)}, u32[]{:S(2)}) collective-permute-start(bf16[384,128]{1,0:T(8,128)(2,1)} %get-tuple-element.84), channel_id=1, source_target_pairs={{0,28},{4,24},{8,20},{12,16},{16,12},{20,8},{24,4},{28,0},{1,29},{... | collective-permute-start | bytes 294920 | tf_op jit(solution)/shard_map/ppermute | solution.py:344
  72.5 2.5 %collective-permute-start.22 = (bf16[384,128]{1,0:T(8,128)(2,1)}, bf16[384,128]{1,0:T(8,128)(2,1)S(1)}, u32[]{:S(2)}, u32[]{:S(2)}) collective-permute-start(bf16[384,128]{1,0:T(8,128)(2,1)} %get-tuple-element.79), channel_id=1, source_target_pairs={{0,24},{4,28},{8,16},{12,20},{16,8},{20,12},{24,0},{28,4},{1,25},{... | collective-permute-start | bytes 294920 | tf_op jit(solution)/shard_map/ppermute | solution.py:344
  75.7 2.4 %collective-permute-start.24 = (bf16[384,128]{1,0:T(8,128)(2,1)}, bf16[384,128]{1,0:T(8,128)(2,1)S(1)}, u32[]{:S(2)}, u32[]{:S(2)}) collective-permute-start(bf16[384,128]{1,0:T(8,128)(2,1)} %copy-done.17), channel_id=1, source_target_pairs={{0,28},{4,24},{8,20},{12,16},{16,12},{20,8},{24,4},{28,0},{1,29},{... | collective-permute-start | bytes 294920 | tf_op jit(solution)/shard_map/ppermute | solution.py:344
  79.1 1.3 %sources.1 = bf16[128,48,256]{2,1,0:T(8,128)(2,1)S(1)} custom-call(s32[1]{0:T(128)} %bitcast.refs_1_.refs_0_, s32[1]{0:T(128)} %bitcast.10.refs_1_, bf16[8,4,48,128]{3,2,1,0:T(8,128)(2,1)S(1)} %bitcast_dynamic-update-slice_fusion.refs_2_, bf16[8,4,48,128]{3,2,1,0:T(8,128)(2,1)S(1)} %copy-done.3, bf16[8,4,48,128]{3,2,1,0:T(8,128)(2,1)S(1)} %collective-permute-done.10.refs_4_, ...), custom_call_target="tpu_custom_call" | custom-call | flops 100000000 | bytes 6291456 | tf_op jit(solution)/shard_map/sources/pallas_call | solution.py:219
  81.5 1.6 %collective-permute-start.14 = (bf16[384,128]{1,0:T(8,128)(2,1)S(1)}, bf16[384,128]{1,0:T(8,128)(2,1)S(1)}, u32[]{:S(2)}, u32[]{:S(2)}) collective-permute-start(bf16[384,128]{1,0:T(8,128)(2,1)S(1)} %copy-done.14), channel_id=1, source_target_pairs={{0,4},{4,0},{8,12},{12,8},{16,20},{20,16},{24,28},{28,24},{1,5},{5... | collective-permute-start | bytes 294920 | tf_op jit(solution)/shard_map/ppermute | solution.py:344
  83.1 4.8 %collective-permute-done.20.refs_7_ = bf16[384,128]{1,0:T(8,128)(2,1)S(1)} collective-permute-done((bf16[384,128]{1,0:T(8,128)(2,1)}, bf16[384,128]{1,0:T(8,128)(2,1)S(1)}, u32[]{:S(2)}, u32[]{:S(2)}) %collective-permute-start.20) | collective-permute-done | bytes 98336 | tf_op jit(solution)/shard_map/ppermute | solution.py:344
  87.9 2.7 %collective-permute-start.16 = (bf16[384,128]{1,0:T(8,128)(2,1)S(1)}, bf16[384,128]{1,0:T(8,128)(2,1)S(1)}, u32[]{:S(2)}, u32[]{:S(2)}) collective-permute-start(bf16[384,128]{1,0:T(8,128)(2,1)S(1)} %copy-done.10), channel_id=1, source_target_pairs={{0,12},{4,8},{8,4},{12,0},{16,28},{20,24},{24,20},{28,16},{1,13},{... | collective-permute-start | bytes 294920 | tf_op jit(solution)/shard_map/ppermute | solution.py:344
  90.6 8.8 %stack.38.refs_12_ = bf16[1,4,128,32,256]{4,3,2,1,0:T(8,128)(2,1)} custom-call(s32[1]{0:T(128)S(6)} %copy.20.refs_0_, s32[1]{0:T(128)} %bitcast.refs_1_.refs_0_, bf16[384,128]{1,0:T(8,128)(2,1)S(1)} %copy-done.7, bf16[384,128]{1,0:T(8,128)(2,1)S(1)} %collective-permute-done.13.refs_3_, bf16[384,128]{1,0:T(8,128)(2,1)S(1)} %collective-permute-done.17.refs_4_, ...), custom_call_target="tpu_custom_call" | custom-call | flops 2147483648 | bytes 7340032 | tf_op jit(solution)/shard_map/stack/pallas_call | solution.py:317
  99.4 8.8 %stack.39 = bf16[1,4,128,32,256]{4,3,2,1,0:T(8,128)(2,1)} custom-call(s32[1]{0:T(128)S(6)} %copy.20.refs_0_, s32[1]{0:T(128)} %bitcast.refs_1_.refs_0_, bf16[384,128]{1,0:T(8,128)(2,1)S(1)} %copy-done.5, bf16[384,128]{1,0:T(8,128)(2,1)S(1)} %collective-permute-done.14.refs_3_, ...), custom_call_target="tpu_custom_call", output_to_operand_aliasing={{}: (12, {})} | custom-call | flops 2147483648 | bytes 7340032 | tf_op jit(solution)/shard_map/stack/pallas_call | solution.py:317
  (75 shorter events, 9.9 us)
Async XLA Ops:
  1.9 11.0 %copy-start.8 = (f32[201]{0:T(256)S(1)}, f32[201]{0:T(256)}, u32[]{:S(2)}) copy-start(f32[201]{0:T(256)} %param.7) | copy-start | bytes 2416
  2.2 6.4 %collective-permute-start = (bf16[64,256]{1,0:T(8,128)(2,1)S(1)}, bf16[64,256]{1,0:T(8,128)(2,1)S(1)}, u32[]{:S(2)}, u32[]{:S(2)}) collective-permute-start(bf16[64,256]{1,0:T(8,128)(2,1)S(1)} %get-tuple-element.46), channel_id=1, source_target_pairs={{0,4},{4,8},{8,12},{12,16},{16,20},{20,24},{24,28},{1,5},{5,9},{9,... | collective-permute-start | bytes 98312 | tf_op jit(solution)/shard_map/ppermute | solution.py:362
  8.6 29.2 %collective-permute-start.1 = (bf16[8,128,256]{2,1,0:T(8,128)(2,1)S(1)}, bf16[8,128,256]{2,1,0:T(8,128)(2,1)S(1)}, u32[]{:S(2)}, u32[]{:S(2)}) collective-permute-start(bf16[8,128,256]{2,1,0:T(8,128)(2,1)S(1)} %slice.3), channel_id=1, source_target_pairs={{0,4},{4,8},{8,12},{12,16},{16,20},{20,24},{24,28},{1,5},{5,9},{9,... | collective-permute-start | bytes 1572872 | tf_op jit(solution)/shard_map/ppermute | solution.py:363
  15.1 9.8 %collective-permute-start.2 = (bf16[4,48,128]{2,1,0:T(8,128)(2,1)S(1)}, bf16[4,48,128]{2,1,0:T(8,128)(2,1)S(1)}, u32[]{:S(2)}, u32[]{:S(2)}) collective-permute-start(bf16[4,48,128]{2,1,0:T(8,128)(2,1)S(1)} %get-tuple-element.55), channel_id=1, source_target_pairs={{0,4},{4,0},{8,12},{12,8},{16,20},{20,16},{24,28},{28,24},{1,5},{5... | collective-permute-start | bytes 147464 | tf_op jit(solution)/shard_map/ppermute | solution.py:344
  17.6 11.9 %collective-permute-start.3 = (bf16[4,48,128]{2,1,0:T(8,128)(2,1)S(1)}, bf16[4,48,128]{2,1,0:T(8,128)(2,1)S(1)}, u32[]{:S(2)}, u32[]{:S(2)}) collective-permute-start(bf16[4,48,128]{2,1,0:T(8,128)(2,1)S(1)} %get-tuple-element.56), channel_id=1, source_target_pairs={{0,8},{4,12},{8,0},{12,4},{16,24},{20,28},{24,16},{28,20},{1,9},{5... | collective-permute-start | bytes 147464 | tf_op jit(solution)/shard_map/ppermute | solution.py:344
  19.2 11.7 %collective-permute-start.4 = (bf16[4,48,128]{2,1,0:T(8,128)(2,1)S(1)}, bf16[4,48,128]{2,1,0:T(8,128)(2,1)S(1)}, u32[]{:S(2)}, u32[]{:S(2)}) collective-permute-start(bf16[4,48,128]{2,1,0:T(8,128)(2,1)S(1)} %get-tuple-element.57), channel_id=1, source_target_pairs={{0,12},{4,8},{8,4},{12,0},{16,28},{20,24},{24,20},{28,16},{1,13},{... | collective-permute-start | bytes 147464 | tf_op jit(solution)/shard_map/ppermute | solution.py:344
  19.2 14.6 %collective-permute-start.5 = (bf16[4,48,128]{2,1,0:T(8,128)(2,1)S(1)}, bf16[4,48,128]{2,1,0:T(8,128)(2,1)S(1)}, u32[]{:S(2)}, u32[]{:S(2)}) collective-permute-start(bf16[4,48,128]{2,1,0:T(8,128)(2,1)S(1)} %get-tuple-element.58), channel_id=1, source_target_pairs={{0,16},{4,20},{8,24},{12,28},{16,0},{20,4},{24,8},{28,12},{1,17},{... | collective-permute-start | bytes 147464 | tf_op jit(solution)/shard_map/ppermute | solution.py:344
  25.0 8.9 %collective-permute-start.6 = (bf16[4,48,128]{2,1,0:T(8,128)(2,1)S(1)}, bf16[4,48,128]{2,1,0:T(8,128)(2,1)S(1)}, u32[]{:S(2)}, u32[]{:S(2)}) collective-permute-start(bf16[4,48,128]{2,1,0:T(8,128)(2,1)S(1)} %get-tuple-element.59), channel_id=1, source_target_pairs={{0,20},{4,16},{8,28},{12,24},{16,4},{20,0},{24,12},{28,8},{1,21},{... | collective-permute-start | bytes 147464 | tf_op jit(solution)/shard_map/ppermute | solution.py:344
  29.5 6.3 %collective-permute-start.7 = (bf16[4,48,128]{2,1,0:T(8,128)(2,1)S(1)}, bf16[4,48,128]{2,1,0:T(8,128)(2,1)S(1)}, u32[]{:S(2)}, u32[]{:S(2)}) collective-permute-start(bf16[4,48,128]{2,1,0:T(8,128)(2,1)S(1)} %get-tuple-element.60), channel_id=1, source_target_pairs={{0,24},{4,28},{8,16},{12,20},{16,8},{20,12},{24,0},{28,4},{1,25},{... | collective-permute-start | bytes 147464 | tf_op jit(solution)/shard_map/ppermute | solution.py:344
  30.9 6.9 %collective-permute-start.8 = (bf16[4,48,128]{2,1,0:T(8,128)(2,1)S(1)}, bf16[4,48,128]{2,1,0:T(8,128)(2,1)S(1)}, u32[]{:S(2)}, u32[]{:S(2)}) collective-permute-start(bf16[4,48,128]{2,1,0:T(8,128)(2,1)S(1)} %get-tuple-element.61), channel_id=1, source_target_pairs={{0,28},{4,24},{8,20},{12,16},{16,12},{20,8},{24,4},{28,0},{1,29},{... | collective-permute-start | bytes 147464 | tf_op jit(solution)/shard_map/ppermute | solution.py:344
  37.8 13.8 %collective-permute-start.9 = (bf16[8,4,48,128]{3,2,1,0:T(8,128)(2,1)S(1)}, bf16[8,4,48,128]{3,2,1,0:T(8,128)(2,1)S(1)}, u32[]{:S(2)}, u32[]{:S(2)}) collective-permute-start(bf16[8,4,48,128]{3,2,1,0:T(8,128)(2,1)S(1)} %bitcast_dynamic-update-slice_fusion.refs_2_), channel_id=1, source_target_pairs={{0,1},{1,0},{2,3},{3,2},{4,5},{5,4},{6,7},{7,6},{8,9},{9,8},{10,11... | collective-permute-start | bytes 1179656 | tf_op jit(solution)/shard_map/ppermute | solution.py:344
  47.5 43.0 %copy-start = (f32[256,256]{1,0:T(8,128)S(1)}, f32[256,256]{1,0:T(8,128)}, u32[]{:S(2)}) copy-start(f32[256,256]{1,0:T(8,128)} %constant.14.clone.refs_11_) | copy-start | bytes 786436
  47.5 7.0 %collective-permute-start.11 = (bf16[384,128]{1,0:T(8,128)(2,1)S(1)}, bf16[384,128]{1,0:T(8,128)(2,1)S(1)}, u32[]{:S(2)}, u32[]{:S(2)}) collective-permute-start(bf16[384,128]{1,0:T(8,128)(2,1)S(1)} %get-tuple-element.62), channel_id=1, source_target_pairs={{0,24},{4,28},{8,16},{12,20},{16,8},{20,12},{24,0},{28,4},{1,25},{... | collective-permute-start | bytes 294920 | tf_op jit(solution)/shard_map/ppermute | solution.py:344
  50.0 12.0 %collective-permute-start.10 = (bf16[8,4,48,128]{3,2,1,0:T(8,128)(2,1)S(1)}, bf16[8,4,48,128]{3,2,1,0:T(8,128)(2,1)S(1)}, u32[]{:S(2)}, u32[]{:S(2)}) collective-permute-start(bf16[8,4,48,128]{3,2,1,0:T(8,128)(2,1)S(1)} %bitcast_dynamic-update-slice_fusion.refs_2_), channel_id=1, source_target_pairs={{0,2},{1,3},{2,0},{3,1},{4,6},{5,7},{6,4},{7,5},{8,10},{9,11},{10,... | collective-permute-start | bytes 1179656 | tf_op jit(solution)/shard_map/ppermute | solution.py:344
  54.5 15.1 %collective-permute-start.12 = (bf16[8,4,48,128]{3,2,1,0:T(8,128)(2,1)S(1)}, bf16[8,4,48,128]{3,2,1,0:T(8,128)(2,1)S(1)}, u32[]{:S(2)}, u32[]{:S(2)}) collective-permute-start(bf16[8,4,48,128]{3,2,1,0:T(8,128)(2,1)S(1)} %collective-permute-done.9.refs_3_), channel_id=1, source_target_pairs={{0,2},{1,3},{2,0},{3,1},{4,6},{5,7},{6,4},{7,5},{8,10},{9,11},{10,... | collective-permute-start | bytes 1179656 | tf_op jit(solution)/shard_map/ppermute | solution.py:344
  56.8 13.8 %collective-permute-start.19 = (bf16[384,128]{1,0:T(8,128)(2,1)S(1)}, bf16[384,128]{1,0:T(8,128)(2,1)S(1)}, u32[]{:S(2)}, u32[]{:S(2)}) collective-permute-start(bf16[384,128]{1,0:T(8,128)(2,1)S(1)} %get-tuple-element.75), channel_id=1, source_target_pairs={{0,12},{4,8},{8,4},{12,0},{16,28},{20,24},{24,20},{28,16},{1,13},{... | collective-permute-start | bytes 294920 | tf_op jit(solution)/shard_map/ppermute | solution.py:344
  56.8 15.7 %collective-permute-start.21 = (bf16[384,128]{1,0:T(8,128)(2,1)S(1)}, bf16[384,128]{1,0:T(8,128)(2,1)S(1)}, u32[]{:S(2)}, u32[]{:S(2)}) collective-permute-start(bf16[384,128]{1,0:T(8,128)(2,1)S(1)} %get-tuple-element.78), channel_id=1, source_target_pairs={{0,16},{4,20},{8,24},{12,28},{16,0},{20,4},{24,8},{28,12},{1,17},{... | collective-permute-start | bytes 294920 | tf_op jit(solution)/shard_map/ppermute | solution.py:344
  60.1 12.3 %collective-permute-start.23 = (bf16[384,128]{1,0:T(8,128)(2,1)S(1)}, bf16[384,128]{1,0:T(8,128)(2,1)S(1)}, u32[]{:S(2)}, u32[]{:S(2)}) collective-permute-start(bf16[384,128]{1,0:T(8,128)(2,1)S(1)} %get-tuple-element.81), channel_id=1, source_target_pairs={{0,20},{4,16},{8,28},{12,24},{16,4},{20,0},{24,12},{28,8},{1,21},{... | collective-permute-start | bytes 294920 | tf_op jit(solution)/shard_map/ppermute | solution.py:344
  62.0 13.7 %collective-permute-start.17 = (bf16[384,128]{1,0:T(8,128)(2,1)}, bf16[384,128]{1,0:T(8,128)(2,1)S(1)}, u32[]{:S(2)}, u32[]{:S(2)}) collective-permute-start(bf16[384,128]{1,0:T(8,128)(2,1)} %get-tuple-element.72), channel_id=1, source_target_pairs={{0,8},{4,12},{8,0},{12,4},{16,24},{20,28},{24,16},{28,20},{1,9},{5... | collective-permute-start | bytes 294920 | tf_op jit(solution)/shard_map/ppermute | solution.py:344
  69.7 10.8 %collective-permute-start.13 = (bf16[384,128]{1,0:T(8,128)(2,1)}, bf16[384,128]{1,0:T(8,128)(2,1)S(1)}, u32[]{:S(2)}, u32[]{:S(2)}) collective-permute-start(bf16[384,128]{1,0:T(8,128)(2,1)} %get-tuple-element.64), channel_id=1, source_target_pairs={{0,4},{4,0},{8,12},{12,8},{16,20},{20,16},{24,28},{28,24},{1,5},{5... | collective-permute-start | bytes 294920 | tf_op jit(solution)/shard_map/ppermute | solution.py:344
  70.6 11.0 %collective-permute-start.25 = (bf16[384,128]{1,0:T(8,128)(2,1)}, bf16[384,128]{1,0:T(8,128)(2,1)S(1)}, u32[]{:S(2)}, u32[]{:S(2)}) collective-permute-start(bf16[384,128]{1,0:T(8,128)(2,1)} %get-tuple-element.84), channel_id=1, source_target_pairs={{0,28},{4,24},{8,20},{12,16},{16,12},{20,8},{24,4},{28,0},{1,29},{... | collective-permute-start | bytes 294920 | tf_op jit(solution)/shard_map/ppermute | solution.py:344
  72.5 15.4 %collective-permute-start.20 = (bf16[384,128]{1,0:T(8,128)(2,1)}, bf16[384,128]{1,0:T(8,128)(2,1)S(1)}, u32[]{:S(2)}, u32[]{:S(2)}) collective-permute-start(bf16[384,128]{1,0:T(8,128)(2,1)} %get-tuple-element.76), channel_id=1, source_target_pairs={{0,20},{4,16},{8,28},{12,24},{16,4},{20,0},{24,12},{28,8},{1,21},{... | collective-permute-start | bytes 294920 | tf_op jit(solution)/shard_map/ppermute | solution.py:344
  72.5 15.4 %collective-permute-start.22 = (bf16[384,128]{1,0:T(8,128)(2,1)}, bf16[384,128]{1,0:T(8,128)(2,1)S(1)}, u32[]{:S(2)}, u32[]{:S(2)}) collective-permute-start(bf16[384,128]{1,0:T(8,128)(2,1)} %get-tuple-element.79), channel_id=1, source_target_pairs={{0,24},{4,28},{8,16},{12,20},{16,8},{20,12},{24,0},{28,4},{1,25},{... | collective-permute-start | bytes 294920 | tf_op jit(solution)/shard_map/ppermute | solution.py:344
  75.7 23.7 %collective-permute-start.24 = (bf16[384,128]{1,0:T(8,128)(2,1)}, bf16[384,128]{1,0:T(8,128)(2,1)S(1)}, u32[]{:S(2)}, u32[]{:S(2)}) collective-permute-start(bf16[384,128]{1,0:T(8,128)(2,1)} %copy-done.17), channel_id=1, source_target_pairs={{0,28},{4,24},{8,20},{12,16},{16,12},{20,8},{24,4},{28,0},{1,29},{... | collective-permute-start | bytes 294920 | tf_op jit(solution)/shard_map/ppermute | solution.py:344
  79.1 8.8 %copy-start.12 = (bf16[384,128]{1,0:T(8,128)(2,1)S(1)}, bf16[384,128]{1,0:T(8,128)(2,1)}, u32[]{:S(2)}) copy-start(bf16[384,128]{1,0:T(8,128)(2,1)} %copy-done.11) | copy-start | bytes 294916
  79.1 8.8 %copy-start.10 = (bf16[384,128]{1,0:T(8,128)(2,1)S(1)}, bf16[384,128]{1,0:T(8,128)(2,1)}, u32[]{:S(2)}) copy-start(bf16[384,128]{1,0:T(8,128)(2,1)} %copy-done.9) | copy-start | bytes 294916
  79.1 11.4 %copy-start.7 = (bf16[384,128]{1,0:T(8,128)(2,1)S(1)}, bf16[384,128]{1,0:T(8,128)(2,1)}, u32[]{:S(2)}) copy-start(bf16[384,128]{1,0:T(8,128)(2,1)} %copy-done.6) | copy-start | bytes 294916
  80.5 18.9 %collective-permute-start.18 = (bf16[384,128]{1,0:T(8,128)(2,1)S(1)}, bf16[384,128]{1,0:T(8,128)(2,1)S(1)}, u32[]{:S(2)}, u32[]{:S(2)}) collective-permute-start(bf16[384,128]{1,0:T(8,128)(2,1)S(1)} %copy-done.16), channel_id=1, source_target_pairs={{0,16},{4,20},{8,24},{12,28},{16,0},{20,4},{24,8},{28,12},{1,17},{... | collective-permute-start | bytes 294920 | tf_op jit(solution)/shard_map/ppermute | solution.py:344
  81.5 17.9 %collective-permute-start.14 = (bf16[384,128]{1,0:T(8,128)(2,1)S(1)}, bf16[384,128]{1,0:T(8,128)(2,1)S(1)}, u32[]{:S(2)}, u32[]{:S(2)}) collective-permute-start(bf16[384,128]{1,0:T(8,128)(2,1)S(1)} %copy-done.14), channel_id=1, source_target_pairs={{0,4},{4,0},{8,12},{12,8},{16,20},{20,16},{24,28},{28,24},{1,5},{5... | collective-permute-start | bytes 294920 | tf_op jit(solution)/shard_map/ppermute | solution.py:344
  87.9 11.5 %collective-permute-start.15 = (bf16[384,128]{1,0:T(8,128)(2,1)S(1)}, bf16[384,128]{1,0:T(8,128)(2,1)S(1)}, u32[]{:S(2)}, u32[]{:S(2)}) collective-permute-start(bf16[384,128]{1,0:T(8,128)(2,1)S(1)} %copy-done.12), channel_id=1, source_target_pairs={{0,8},{4,12},{8,0},{12,4},{16,24},{20,28},{24,16},{28,20},{1,9},{5... | collective-permute-start | bytes 294920 | tf_op jit(solution)/shard_map/ppermute | solution.py:344
  87.9 11.5 %collective-permute-start.16 = (bf16[384,128]{1,0:T(8,128)(2,1)S(1)}, bf16[384,128]{1,0:T(8,128)(2,1)S(1)}, u32[]{:S(2)}, u32[]{:S(2)}) collective-permute-start(bf16[384,128]{1,0:T(8,128)(2,1)S(1)} %copy-done.10), channel_id=1, source_target_pairs={{0,12},{4,8},{8,4},{12,0},{16,28},{20,24},{24,20},{28,16},{1,13},{... | collective-permute-start | bytes 294920 | tf_op jit(solution)/shard_map/ppermute | solution.py:344
  90.6 8.9 %copy-start.5 = (bf16[384,128]{1,0:T(8,128)(2,1)S(1)}, bf16[384,128]{1,0:T(8,128)(2,1)}, u32[]{:S(2)}) copy-start(bf16[384,128]{1,0:T(8,128)(2,1)} %copy-done.4) | copy-start | bytes 294916
  (13 other events, 16.1 us)

commit v4 on v2

--- a/solution.py
+++ b/solution.py
@@ -67,117 +67,104 @@
     return dot(jnp.concatenate(pieces, 0), table)
 
 
-def virtual_rows(ref, nv):
-    rows = [ref[b, r * VSTEP : (r + 1) * VSTEP, :].astype(F32)[0:1] for b in range(ref.shape[0]) for r in range(nv)]
-    return jnp.concatenate(rows, 0).astype(BF)
-
-
-def block_rows(result, b, nv, wins, count):
-    parts = [
-        result[w * count + b * nv : w * count + (b + 1) * nv, p * BINS : (p + 1) * BINS]
-        for w in range(wins)
-        for p in range(2)
-    ]
-    return jnp.concatenate(parts, 0).astype(BF)
-
-
-def early_kernel(rec_ref, taps_ref, table_ref, virt_ref, rows_ref, toeplitz_ref, forward_ref, row):
+def early_kernel(pairs_ref, rec_ref, taps_ref, table_ref, picked_ref, toeplitz_ref, forward_ref, row, virt):
     nblk, chans, time = rec_ref.shape
     wins = time // WLEN - 1
     nv = chans // VSTEP
     count = nblk * nv
     build_toeplitz(taps_ref, row, toeplitz_ref)
     forward_ref[...] = table_ref[...].astype(BF)
-    rows = virtual_rows(rec_ref, nv)
-    rows_ref[...] = rows[:, :WLEN]
-    block = (rows[:, HALF:WLEN], rows[:, WLEN:])
-    result = transform([block], wins, count, toeplitz_ref[...], forward_ref[...])
+    rows = [
+        rec_ref[b, r * VSTEP : (r + 1) * VSTEP, HALF:].astype(F32)[0:1] for b in range(nblk) for r in range(nv)
+    ]
+    rows = jnp.concatenate(rows, 0).astype(BF)
+    result = transform([(rows[:, :HALF], rows[:, HALF:])], wins, count, toeplitz_ref[...], forward_ref[...])
     for b in range(nblk):
-        virt_ref[b] = block_rows(result, b, nv, wins, count)
-
-
-def early(records, taps):
+        parts = [
+            result[w * count + b * nv : w * count + (b + 1) * nv, p * BINS : (p + 1) * BINS]
+            for w in range(wins)
+            for p in range(2)
+        ]
+        virt[b] = jnp.concatenate(parts, 0).astype(BF)
+    for r in range(nblk):
+        for k in range(SLOTS):
+            picked_ref[r, k] = virt[pairs_ref[r, k]]
+
+
+def early(records, taps, pairs):
     nblk, chans, time = records.shape
-    nv = chans // VSTEP
-    vmem = pl.BlockSpec(memory_space=pltpu.VMEM)
+    rows = (time // WLEN - 1) * 2 * (chans // VSTEP)
+    smem, vmem = pl.BlockSpec(memory_space=pltpu.SMEM), pl.BlockSpec(memory_space=pltpu.VMEM)
     return pl.pallas_call(
         early_kernel,
-        in_specs=[vmem] * 3,
-        out_specs=[vmem] * 4,
+        in_specs=[smem, vmem, vmem, vmem],
+        out_specs=[vmem] * 3,
         out_shape=[
-            jax.ShapeDtypeStruct((nblk, (time // WLEN - 1) * 2 * nv, BINS), BF),
-            jax.ShapeDtypeStruct((nblk * nv, WLEN), BF),
+            jax.ShapeDtypeStruct((nblk, SLOTS, rows, BINS), BF),
             jax.ShapeDtypeStruct((WLEN, HALF), BF),
             jax.ShapeDtypeStruct((WLEN, 2 * BINS), BF),
         ],
-        scratch_shapes=[pltpu.VMEM((8, 512), F32)],
-        compiler_params=pltpu.CompilerParams(vmem_limit_bytes=40 * MIB),
+        scratch_shapes=[pltpu.VMEM((8, 512), F32), pltpu.VMEM((nblk, rows, BINS), BF)],
+        compiler_params=pltpu.CompilerParams(vmem_limit_bytes=16 * MIB),
         cost_estimate=pl.CostEstimate(flops=4 * 10**8, bytes_accessed=records.size * 2, transcendentals=0),
         name="early",
-    )(records, taps, jnp.asarray(dft_table()))
-
-
-def spectra_kernel(start, size, pairs_ref, me_ref, rec_ref, halo_ref, toeplitz_ref, forward_ref, *refs):
-    held, sems = refs[-2:]
+    )(pairs, records, taps, jnp.asarray(dft_table()))
+
+
+def spectra_kernel(sizes, pairs_ref, me_ref, rec_ref, halo_ref, toeplitz_ref, forward_ref, *refs):
     nblk, chans, time = rec_ref.shape
     wins = time // WLEN
     nv = chans // VSTEP
+    outs = [refs[nblk * q : nblk * (q + 1)] for q in range(len(sizes))]
+    spec, virt = refs[nblk * len(sizes) :]
     me = me_ref[0]
-    copies = []
-    for m in range(nblk):
-        source = rec_ref.at[me ^ m, pl.ds(start, size)]
-        copies.append(pltpu.make_async_copy(source, held.at[m], sems.at[m]))
-        copies[-1].start()
-    if len(refs) > nblk + 2:
-        rows_ref, virt_ref, outs, virt = refs[0], refs[1], refs[2 : nblk + 2], refs[nblk + 2]
-        block = (virtual_rows(halo_ref, nv), rows_ref[...])
-        result = transform([block], 1, nblk * nv, toeplitz_ref[...], forward_ref[...])
-        for b in range(nblk):
-            virt[b] = block_rows(result, b, nv, 1, nblk * nv)
-        for m in range(nblk):
-            for k in range(SLOTS):
-                block = pairs_ref[me ^ m, k]
-                lo = wins * 2 * size + k * wins * 2 * nv
-                outs[m][lo : lo + 2 * nv] = virt[block]
-                outs[m][lo + 2 * nv : lo + wins * 2 * nv] = virt_ref[block]
-    else:
-        outs = refs[:nblk]
     per = 2
     for m in range(0, nblk, per):
-        blocks = []
+        blocks = [(halo_ref[me ^ (m + u)], rec_ref[me ^ (m + u)]) for u in range(per)]
+        result = transform(blocks, wins, chans, toeplitz_ref[...], forward_ref[...])
         for u in range(per):
-            copies[m + u].wait()
-            blocks.append((halo_ref[me ^ (m + u), start : start + size], held[m + u]))
-        result = transform(blocks, wins, size, toeplitz_ref[...], forward_ref[...]).astype(BF)
+            at = u * wins * chans
+            for p in range(2):
+                spec[u, p] = result[at : at + chans, p * BINS : (p + 1) * BINS]
+            chosen = [spec[u, p, pl.ds(0, nv, stride=VSTEP), :] for p in range(2)]
+            virt[me ^ (m + u)] = jnp.concatenate(chosen, 0).astype(BF)
+        result = result.astype(BF)
         for u in range(per):
             for w in range(wins):
                 for p in range(2):
-                    lo = (u * wins + w) * size
-                    row = (w * 2 + p) * size
-                    outs[m + u][row : row + size] = result[lo : lo + size, p * BINS : (p + 1) * BINS]
-
-
-def spectra(records, halo, toeplitz, forward, pairs, me, start, size, virtual=()):
+                    lo = (u * wins + w) * chans
+                    for out, size in zip(outs, sizes):
+                        at = (w * 2 + p) * size
+                        out[m + u][at : at + size] = result[lo : lo + size, p * BINS : (p + 1) * BINS]
+                        lo += size
+    at = wins * 2 * sizes[0]
+    for m in range(nblk):
+        for k in range(SLOTS):
+            lo = at + k * 2 * nv
+            outs[0][m][lo : lo + 2 * nv] = virt[pairs_ref[me ^ m, k]]
+
+
+def spectra(records, halo, toeplitz, forward, pairs, me, sizes):
     nblk, chans, time = records.shape
     wins = time // WLEN
     nv = chans // VSTEP
-    shape = (wins * 2 * size + (SLOTS * wins * 2 * nv if virtual else 0), BINS)
+    shapes = []
+    for q, size in enumerate(sizes):
+        shapes += [(wins * 2 * size + (SLOTS * 2 * nv if q == 0 else 0), BINS)] * nblk
     smem, vmem = pl.BlockSpec(memory_space=pltpu.SMEM), pl.BlockSpec(memory_space=pltpu.VMEM)
-    operands = [pairs, me, records, halo, toeplitz, forward, *virtual]
-    scratch = [pltpu.VMEM((nblk, 2 * nv, BINS), BF)] if virtual else []
     outs = pl.pallas_call(
-        lambda *refs: spectra_kernel(start, size, *refs),
-        in_specs=[smem, smem, pl.BlockSpec(memory_space=pl.ANY)] + [vmem] * (len(operands) - 3),
-        out_specs=[vmem] * nblk,
-        out_shape=[jax.ShapeDtypeStruct(shape, BF)] * nblk,
-        scratch_shapes=scratch + [pltpu.VMEM((nblk, size, time), BF), pltpu.SemaphoreType.DMA((nblk,))],
-        compiler_params=pltpu.CompilerParams(vmem_limit_bytes=40 * MIB),
+        lambda *refs: spectra_kernel(sizes, *refs),
+        in_specs=[smem, smem, vmem, vmem, vmem, vmem],
+        out_specs=[vmem] * len(shapes),
+        out_shape=[jax.ShapeDtypeStruct(shape, BF) for shape in shapes],
+        scratch_shapes=[pltpu.VMEM((2, 2, chans, BINS), F32), pltpu.VMEM((nblk, 2 * nv, BINS), BF)],
+        compiler_params=pltpu.CompilerParams(vmem_limit_bytes=16 * MIB),
         cost_estimate=pl.CostEstimate(
-            flops=nblk * size * wins * 3 * 2 * 512 * 256, bytes_accessed=nblk * size * time * 3, transcendentals=0
+            flops=nblk * chans * wins * 3 * 2 * 512 * 256, bytes_accessed=nblk * chans * time * 3, transcendentals=0
         ),
         name="spectra",
-    )(*operands)
-    return list(outs)
+    )(pairs, me, records, halo, toeplitz, forward)
+    return [list(outs[i : i + nblk]) for i in range(0, len(outs), nblk)]
 
 
 def collect_kernel(rows, *refs):
@@ -195,26 +182,30 @@
         in_specs=[vmem] * len(chunks),
         out_specs=vmem,
         out_shape=jax.ShapeDtypeStruct((len(chunks), SLOTS, rows, BINS), BF),
-        compiler_params=pltpu.CompilerParams(vmem_limit_bytes=32 * MIB),
+        compiler_params=pltpu.CompilerParams(vmem_limit_bytes=8 * MIB),
         cost_estimate=pl.CostEstimate(flops=0, bytes_accessed=len(chunks) * rows * 2048, transcendentals=0),
         name="collect",
     )(*chunks)
 
 
 def sources_kernel(nsrc, nnar, wins, nv, me_ref, place_ref, *refs):
-    virts, out_ref, held, turned = refs[:nnar], refs[nnar], refs[nnar + 1], refs[nnar + 2]
+    lates, firsts = refs[:nnar], refs[nnar : 2 * nnar]
+    out_ref, late, first, turned = refs[2 * nnar :]
     nw = nsrc * wins
     pitch = BINS + 8
     for n in range(nnar):
-        held[place_ref[0] ^ n] = virts[n][...]
-
-    def turn(m, carry):
-        tiles = [[held[n, m, k].astype(F32) for n in range(nnar)] for k in range(SLOTS)]
+        late[place_ref[0] ^ n] = lates[n][...]
+        first[place_ref[0] ^ n] = firsts[n][...]
+
+    def turn(src, carry):
+        after = [[late[n, src, k].astype(F32) for n in range(nnar)] for k in range(SLOTS)]
+        start = [[first[n, me_ref[0] ^ src, k].astype(F32) for n in range(nnar)] for k in range(SLOTS)]
         for w in range(wins):
+            held = after if w else start
             for p in range(2):
-                at = (w * 2 + p) * nv
-                tile = jnp.concatenate([tiles[k][n][at : at + nv] for k in range(SLOTS) for n in range(nnar)], 0)
-                row = pl.multiple_of((p * nw + (me_ref[0] ^ m) * wins + w) * pitch, 8)
+                at = (max(w - 1, 0) * 2 + p) * nv
+                tile = jnp.concatenate([held[k][n][at : at + nv] for k in range(SLOTS) for n in range(nnar)], 0)
+                row = pl.multiple_of((p * nw + src * wins + w) * pitch, 8)
                 turned[pl.ds(row, BINS), :] = tile.T
         return carry
 
@@ -231,24 +222,25 @@
     lax.fori_loop(0, BINS, one, 0, unroll=8)
 
 
-def sources(virts, me, place, wins, nv):
-    nnar, nsrc = len(virts), virts[0].shape[0]
+def sources(lates, firsts, me, place, wins, nv):
+    nnar, nsrc = len(lates), lates[0].shape[0]
     nw = nsrc * wins
     width = SLOTS * nnar * nv
     smem, vmem = pl.BlockSpec(memory_space=pltpu.SMEM), pl.BlockSpec(memory_space=pltpu.VMEM)
     return pl.pallas_call(
         lambda *refs: sources_kernel(nsrc, nnar, wins, nv, *refs),
-        in_specs=[smem, smem] + [vmem] * nnar,
+        in_specs=[smem, smem] + [vmem] * (2 * nnar),
         out_specs=vmem,
         out_shape=jax.ShapeDtypeStruct((BINS, 2 * nw, 2 * width), BF),
         scratch_shapes=[
-            pltpu.VMEM((nnar,) + virts[0].shape, BF),
+            pltpu.VMEM((nnar,) + lates[0].shape, BF),
+            pltpu.VMEM((nnar,) + firsts[0].shape, BF),
             pltpu.VMEM((2 * nw * (BINS + 8), width), F32),
         ],
-        compiler_params=pltpu.CompilerParams(vmem_limit_bytes=40 * MIB),
-        cost_estimate=pl.CostEstimate(flops=10**8, bytes_accessed=8 * nnar * virts[0].size, transcendentals=0),
+        compiler_params=pltpu.CompilerParams(vmem_limit_bytes=(10 + 2 * nw * BINS * width * 6 // MIB) * MIB),
+        cost_estimate=pl.CostEstimate(flops=10**8, bytes_accessed=8 * nnar * lates[0].size, transcendentals=0),
         name="sources",
-    )(me, place, *virts)
+    )(me, place, *lates, *firsts)
 
 
 def stack_kernel(nw, wins, size, group, count_ref, me_ref, *refs):
@@ -304,21 +296,23 @@
 
         lax.fori_loop(0, BINS // pack, one, 0, unroll=8 // pack)
 
-    for q in range(0, group, 4):
+    rows = 8
+    for q in range(0, group, rows):
         lefts = []
-        for u in range(4):
+        for u in range(rows):
             at = step * group + q + u
             tiles = [cross[p, pl.ds(at, BINS, stride=pitch), :].astype(BF).T for p in range(2)]
             lefts.append(jnp.concatenate(tiles, 1))
         value = dot(jnp.concatenate(lefts, 0), lag[...]).astype(BF)
-        for u in range(4):
+        for u in range(rows):
             for k in range(SLOTS):
                 at = u * width + k * VIRTUAL_SOURCES
                 out_ref[0, k, q + u] = value[at : at + VIRTUAL_SOURCES]
 
 
 def stack(recvs, table, count, me, lag, before, start, size, wins, chans):
-    nw = wins * len(recvs)
+    nsrc = len(recvs)
+    nw = nsrc * wins
     group = 16
     pack = 2 if 4 * nw <= 128 else 1
     table = table.reshape(BINS // pack, pack * 2 * nw, table.shape[2])
@@ -352,7 +346,7 @@
         ),
         out_shape=jax.ShapeDtypeStruct(shape, BF),
         input_output_aliases=aliases,
-        compiler_params=pltpu.CompilerParams(vmem_limit_bytes=36 * MIB),
+        compiler_params=pltpu.CompilerParams(vmem_limit_bytes=(20 + table.size * 4 // MIB) * MIB),
         cost_estimate=pl.CostEstimate(
             flops=size * 128 * 256 * 256 * 4, bytes_accessed=2 * (table.size + size * 32768), transcendentals=0
         ),
@@ -373,37 +367,47 @@
     wins = time // WLEN
     nv = chans // VSTEP
     nwide, nnar = lax.axis_size("wide"), lax.axis_size("narrow")
-    half = chans // 2
+    sizes = (chans // 2,) * 2
     me = lax.axis_index("wide").astype(jnp.int32)[None]
     place = lax.axis_index("narrow").astype(jnp.int32)[None]
     halo = lax.ppermute(records[:, :, time - HALF :], "wide", [(i, i + 1) for i in range(nwide - 1)])
-    virt, rows, toeplitz, forward = early(records, taps[None])
-    near = spectra(records, halo, toeplitz, forward, pair_sources, me, 0, half, (rows, virt))
+    picked, toeplitz, forward = early(records, taps[None], pair_sources)
+    picked = lax.all_to_all(picked, "wide", split_axis=0, concat_axis=0, tiled=True)
+    chunks = spectra(records, halo, toeplitz, forward, pair_sources, me, sizes)
+    picked, (near, far) = lax.optimization_barrier((picked, chunks))
     order = list(range(nwide - 1, 0, -1))
-    for m in order[:-2]:
-        near[m] = swap(near[m], "wide", m)
-    held = after(halo, [near[n] for n in order[:2]])
-    far = spectra(records, held, toeplitz, forward, pair_sources, me, half, half)
-    for m in order[-2:]:
-        near[m] = swap(after(near[m], [far[0]]), "wide", m)
 
     top = nnar // 2
-    picked = collect(near, wins * 2 * nv)
-    slots = {0: picked, **{n: swap(picked, "narrow", n) for n in (top, 1) if n}}
+
+    def begin(value):
+        return {0: value, **{n: swap(value, "narrow", n) for n in (top, 1) if n}}
+
+    def finish(slots, waits):
+        bit = top
+        while bit:
+            for n in sorted(slots):
+                if n ^ bit not in slots:
+                    slots[n ^ bit] = swap(after(slots[n], waits), "narrow", bit)
+            bit //= 2
+        return [slots[n] for n in range(nnar)]
+
+    lates = begin(picked)
     for i, m in enumerate(order):
-        if i == 3:
-            waits = [far[n] for n in order[:2]]
-            bit = top
-            while bit:
-                for n in sorted(slots):
-                    if n ^ bit not in slots:
-                        slots[n ^ bit] = swap(after(slots[n], waits), "narrow", bit)
-                bit //= 2
+        waits = []
+        if i == len(order) - 2:
+            waits = [lates[n] for n in sorted(lates) if n]
+            lates = finish(lates, [near[order[1]]])
+        near[m] = swap(after(near[m], waits), "wide", m)
+    for i, m in enumerate(order):
         far[m] = swap(after(far[m], [near[order[min(i + 2, nwide - 2)]]]), "wide", m)
-    table = sources([slots[n] for n in range(nnar)], me, place, wins, nv)
+    firsts = finish(begin(collect(near, 2 * nv)), [far[n] for n in order[:2]])
+    table = sources(lates, firsts, me, place, wins, nv)
     lag = jnp.asarray(lag_table())
-    out = stack(near, table, pair_counts, me, lag, None, 0, half, wins, chans)
-    return stack(far, table, pair_counts, me, lag, out, half, half, wins, chans)
+    out, start = None, 0
+    for recvs, size in zip((near, far), sizes):
+        out = stack(recvs, table, pair_counts, me, lag, out, start, size, wins, chans)
+        start += size
+    return out
 
 
 def solution(mesh):

time: 105 us -> 94.6 us (0.901)
  starting transfers between devices: 47.2 us -> 41.7 us
  Pallas kernels: 31.7 us -> 27.7 us
  waiting for transfers between devices: 19.3 us -> 16.6 us
  local copies, waits for them, and re-layouts: 5.46 us -> 7.34 us
    ppermute x17 -> x20, starting transfers between devices: 42.3 us -> 31.8 us  [swap(): lax.ppermute(value, axis, [(i, i ^ mask) for i in range(lax.axis_size(axi...]
    ppermute x1, waiting for transfers between devices: 6.09 us -> 0.01 us  [on_device(): lax.ppermute(records[:, :, time - HALF:], 'wide', [(i, i + 1) for i in ra...]
    pallas_call x3 -> x2, Pallas kernels: 12.7 us -> 7.17 us  [the longest x1 5.25 us: spectra(): pl.pallas_call(lambda *refs: spectra_kernel(sizes, *refs), in_specs=[smem...]
    all_to_all x0 -> x1, starting transfers between devices: none -> 4.98 us  [on_device(): lax.all_to_all(picked, 'wide', split_axis=0, concat_axis=0, tiled=True)]
    ppermute x17 -> x20, waiting for transfers between devices: 13.2 us -> 15.2 us  [swap(): lax.ppermute(value, axis, [(i, i ^ mask) for i in range(lax.axis_size(axi...]
    unnamed x15, local copies, waits for them, and re-layouts: 4.38 us -> 6.26 us
    pallas_call x2, Pallas kernels: 17.7 us -> 19.2 us  [stack(): pl.pallas_call(lambda *refs: stack_kernel(nw, wins, size, group, *refs),...]
    all_to_all x0 -> x1, waiting for transfers between devices: none -> 1.46 us  [on_device(): lax.all_to_all(picked, 'wide', split_axis=0, concat_axis=0, tiled=True)]
  transfers between devices with their start and end apart: 18 -> 22, of which waited for: 6 -> 5; matrix products, arithmetic and copies ran while one was open for 1% -> 1% of each run, Pallas kernels for 16% -> 19%
where the time goes in v4:
time: 94.6 us; the launch traced here: 94.1 us
  starting transfers between devices  41.7 us (44%)
  Pallas kernels  27.7 us (29%)
  waiting for transfers between devices  16.6 us (18%)
  local copies, waits for them, and re-layouts  7.34 us (8%)
    ppermute x20, starting transfers between devices, swap(): lax.ppermute(value, axis, [(i, i ^ mask) for i in range(lax.axis_size(axi...  31.8 us
    pallas_call x2, Pallas kernels, stack(): pl.pallas_call(lambda *refs: stack_kernel(nw, wins, size, group, *refs),...  19.2 us
    ppermute x20, waiting for transfers between devices, swap(): lax.ppermute(value, axis, [(i, i ^ mask) for i in range(lax.axis_size(axi...  15.2 us
    unnamed x15, local copies, waits for them, and re-layouts  6.26 us
    pallas_call x1, Pallas kernels, spectra(): pl.pallas_call(lambda *refs: spectra_kernel(sizes, *refs), in_specs=[smem...  5.25 us
    all_to_all x1, starting transfers between devices, on_device(): lax.all_to_all(picked, 'wide', split_axis=0, concat_axis=0, tiled=True)  4.98 us
    ppermute x1, starting transfers between devices, on_device(): lax.ppermute(records[:, :, time - HALF:], 'wide', [(i, i + 1) for i in ra...  4.88 us
    pallas_call x1, Pallas kernels, early(): pl.pallas_call(early_kernel, in_specs=[smem, vmem, vmem, vmem], out_specs...  1.92 us
  transfers between devices with their start and end apart: 22, of which 5 were waited for; matrix products, arithmetic and copies ran while one was open for 1% of the time, Pallas kernels for 19%

profile of v4, /device:TPU:0, one launch (start us, length us, event | category | flops | bytes accessed | tf_op | source)
XLA Modules:
  0.0 94.1 jit_solution(10502295921834467755)
XLA Ops:
  0.0 1.1 %slice.3 = bf16[8,128,256]{2,1,0:T(8,128)(2,1)S(1)} slice(bf16[8,128,1536]{2,1,0:T(8,128)(2,1)} %refs_2_.1), slice={[0:8], [0:128], [1280:1536]} | slice | bytes 1048576 | tf_op jit(solution)/shard_map/slice | solution.py:373
  1.1 4.9 %collective-permute-start = (bf16[8,128,256]{2,1,0:T(8,128)(2,1)S(1)}, bf16[8,128,256]{2,1,0:T(8,128)(2,1)S(1)}, u32[]{:S(2)}, u32[]{:S(2)}) collective-permute-start(bf16[8,128,256]{2,1,0:T(8,128)(2,1)S(1)} %slice.3), channel_id=1, source_target_pairs={{0,4},{4,8},{8,12},{12,16},{16,20},{20,24},{24,28},{1,5},{5,9},{9,... | collective-permute-start | bytes 1572872 | tf_op jit(solution)/shard_map/ppermute | solution.py:373
  6.0 0.8 copy.8.pairs_ref.refs_0_
  6.7 1.9 %copy-done = bf16[8,128,1536]{2,1,0:T(8,128)(2,1)S(1)} copy-done((bf16[8,128,1536]{2,1,0:T(8,128)(2,1)S(1)}, bf16[8,128,1536]{2,1,0:T(8,128)(2,1)}, u32[]{:S(2)}) %copy-start) | copy-done | bytes 3145752
  8.6 1.0 %copy-done.3 = f32[512,256]{1,0:T(8,128)S(1)} copy-done((f32[512,256]{1,0:T(8,128)S(1)}, f32[512,256]{1,0:T(8,128)}, u32[]{:S(2)}) %copy-start.3) | copy-done | bytes 524312
  9.7 0.7 copy-done.4
  10.3 1.9 %early.1 = (bf16[8,4,32,128]{3,2,1,0:T(8,128)(2,1)}, bf16[512,256]{1,0:T(8,128)(2,1)S(1)}, bf16[512,256]{1,0:T(8,128)(2,1)S(1)}) custom-call(s32[8,4]{1,0:T(8,128)S(1)} %copy.8.pairs_ref.refs_0_, bf16[8,128,1536]{2,1,0:T(8,128)(2,1)S(1)} %copy-done, f32[1,201]{1,0:T(1,128)S(1)} %bitcast.6, f32[512,256]{1,0:T(8,128)S(1)} %copy-done.3), custom_call_target="tpu_custom_call" | custom-call | flops 400000000 | bytes 3145728 | tf_op jit(solution)/shard_map/early/pallas_call | solution.py:98
  12.3 5.0 %all-to-all-start = ((bf16[8,4,32,128]{3,2,1,0:T(8,128)(2,1)}), bf16[8,4,32,128]{3,2,1,0:T(8,128)(2,1)S(1)}, u32[]{:S(2)}, u32[]{:S(2)}) async-start(bf16[8,4,32,128]{3,2,1,0:T(8,128)(2,1)} %get-tuple-element.51), calls=%async_computation | async-start | bytes 524288 | tf_op jit(solution)/shard_map/all_to_all | solution.py:375
  17.3 1.9 %copy-done.1 = bf16[8,128,1536]{2,1,0:T(8,128)(2,1)S(1)} copy-done((bf16[8,128,1536]{2,1,0:T(8,128)(2,1)S(1)}, bf16[8,128,1536]{2,1,0:T(8,128)(2,1)}, u32[]{:S(2)}) %copy-start.1) | copy-done | bytes 3145752
  19.1 5.2 %spectra.1 = (bf16[448,128]{1,0:T(8,128)(2,1)S(1)}, bf16[448,128]{1,0:T(8,128)(2,1)S(1)}, bf16[448,128]{1,0:T(8,128)(2,1)S(1)}, bf16[448,128]{1,0:T(8,128)(2,1)S...) custom-call(s32[8,4]{1,0:T(8,128)S(1)} %copy.8.pairs_ref.refs_0_, ...), custom_call_target="tpu_custom_call" | custom-call | flops 2415919104 | bytes 4718592 | tf_op jit(solution)/shard_map/spectra/pallas_call | solution.py:155
  24.4 1.5 %all-to-all-done.refs_2_ = bf16[8,4,32,128]{3,2,1,0:T(8,128)(2,1)S(1)} async-done(((bf16[8,4,32,128]{3,2,1,0:T(8,128)(2,1)}), bf16[8,4,32,128]{3,2,1,0:T(8,128)(2,1)S(1)}, u32[]{:S(2)}, u32[]{:S(2)}) %all-to-all-start) | async-done | bytes 262176 | tf_op jit(solution)/shard_map/all_to_all | solution.py:375
  25.9 1.5 %collective-permute-start.6 = (bf16[8,4,32,128]{3,2,1,0:T(8,128)(2,1)S(1)}, bf16[8,4,32,128]{3,2,1,0:T(8,128)(2,1)S(1)}, u32[]{:S(2)}, u32[]{:S(2)}) collective-permute-start(bf16[8,4,32,128]{3,2,1,0:T(8,128)(2,1)S(1)} %all-to-all-done.refs_2_), channel_id=1, source_target_pairs={{0,2},{1,3},{2,0},{3,1},{4,6},{5,7},{6,4},{7,5},{8,10},{9,11},{10,... | collective-permute-start | bytes 786440 | tf_op jit(solution)/shard_map/ppermute | solution.py:358
  27.4 1.5 %collective-permute-start.1 = (bf16[448,128]{1,0:T(8,128)(2,1)S(1)}, bf16[448,128]{1,0:T(8,128)(2,1)S(1)}, u32[]{:S(2)}, u32[]{:S(2)}) collective-permute-start(bf16[448,128]{1,0:T(8,128)(2,1)S(1)} %get-tuple-element.72), channel_id=1, source_target_pairs={{0,4},{4,0},{8,12},{12,8},{16,20},{20,16},{24,28},{28,24},{1,5},{5... | collective-permute-start | bytes 344072 | tf_op jit(solution)/shard_map/ppermute | solution.py:358
  28.9 4.5 %collective-permute-start.15 = (bf16[448,128]{1,0:T(8,128)(2,1)S(1)}, bf16[448,128]{1,0:T(8,128)(2,1)S(1)}, u32[]{:S(2)}, u32[]{:S(2)}) collective-permute-start(bf16[448,128]{1,0:T(8,128)(2,1)S(1)} %get-tuple-element.92), channel_id=1, source_target_pairs={{0,24},{4,28},{8,16},{12,20},{16,8},{20,12},{24,0},{28,4},{1,25},{... | collective-permute-start | bytes 344072 | tf_op jit(solution)/shard_map/ppermute | solution.py:358
  33.4 3.2 %collective-permute-start.11 = (bf16[448,128]{1,0:T(8,128)(2,1)S(1)}, bf16[448,128]{1,0:T(8,128)(2,1)S(1)}, u32[]{:S(2)}, u32[]{:S(2)}) collective-permute-start(bf16[448,128]{1,0:T(8,128)(2,1)S(1)} %get-tuple-element.87), channel_id=1, source_target_pairs={{0,16},{4,20},{8,24},{12,28},{16,0},{20,4},{24,8},{28,12},{1,17},{... | collective-permute-start | bytes 344072 | tf_op jit(solution)/shard_map/ppermute | solution.py:358
  36.6 0.4 collective-permute-start.13
  36.9 4.5 %collective-permute-start.17 = (bf16[448,128]{1,0:T(8,128)(2,1)S(1)}, bf16[448,128]{1,0:T(8,128)(2,1)S(1)}, u32[]{:S(2)}, u32[]{:S(2)}) collective-permute-start(bf16[448,128]{1,0:T(8,128)(2,1)S(1)} %get-tuple-element.95), channel_id=1, source_target_pairs={{0,28},{4,24},{8,20},{12,16},{16,12},{20,8},{24,4},{28,0},{1,29},{... | collective-permute-start | bytes 344072 | tf_op jit(solution)/shard_map/ppermute | solution.py:358
  41.4 6.7 %collective-permute-done.11.refs_4_.refs_6_ = bf16[448,128]{1,0:T(8,128)(2,1)S(1)} collective-permute-done((bf16[448,128]{1,0:T(8,128)(2,1)S(1)}, bf16[448,128]{1,0:T(8,128)(2,1)S(1)}, u32[]{:S(2)}, u32[]{:S(2)}) %collective-permute-start.11) | collective-permute-done | bytes 114720 | tf_op jit(solution)/shard_map/ppermute | solution.py:358
  48.1 3.5 %collective-permute-done.13.refs_5_.refs_7_ = bf16[448,128]{1,0:T(8,128)(2,1)S(1)} collective-permute-done((bf16[448,128]{1,0:T(8,128)(2,1)S(1)}, bf16[448,128]{1,0:T(8,128)(2,1)S(1)}, u32[]{:S(2)}, u32[]{:S(2)}) %collective-permute-start.13) | collective-permute-done | bytes 114720 | tf_op jit(solution)/shard_map/ppermute | solution.py:358
  51.7 0.7 collective-permute-start.16
  52.3 2.9 %collective-permute-start.12 = (bf16[384,128]{1,0:T(8,128)(2,1)}, bf16[384,128]{1,0:T(8,128)(2,1)S(1)}, u32[]{:S(2)}, u32[]{:S(2)}) collective-permute-start(bf16[384,128]{1,0:T(8,128)(2,1)} %copy-done.6), channel_id=1, source_target_pairs={{0,24},{4,28},{8,16},{12,20},{16,8},{20,12},{24,0},{28,4},{1,25},{... | collective-permute-start | bytes 294920 | tf_op jit(solution)/shard_map/ppermute | solution.py:358
  55.2 1.4 %collective-permute-start.14 = (bf16[384,128]{1,0:T(8,128)(2,1)}, bf16[384,128]{1,0:T(8,128)(2,1)S(1)}, u32[]{:S(2)}, u32[]{:S(2)}) collective-permute-start(bf16[384,128]{1,0:T(8,128)(2,1)} %copy-done.5), channel_id=1, source_target_pairs={{0,28},{4,24},{8,20},{12,16},{16,12},{20,8},{24,4},{28,0},{1,29},{... | collective-permute-start | bytes 294920 | tf_op jit(solution)/shard_map/ppermute | solution.py:358
  56.6 1.2 %collective-permute-start.19 = (bf16[8,4,16,128]{3,2,1,0:T(8,128)(2,1)S(1)}, bf16[8,4,16,128]{3,2,1,0:T(8,128)(2,1)S(1)}, u32[]{:S(2)}, u32[]{:S(2)}) collective-permute-start(bf16[8,4,16,128]{3,2,1,0:T(8,128)(2,1)S(1)} %collect.1.refs_6_), channel_id=1, source_target_pairs={{0,2},{1,3},{2,0},{3,1},{4,6},{5,7},{6,4},{7,5},{8,10},{9,11},{10,... | collective-permute-start | bytes 393224 | tf_op jit(solution)/shard_map/ppermute | solution.py:358
  57.8 1.5 %collective-permute-done.12.refs_8_ = bf16[384,128]{1,0:T(8,128)(2,1)S(1)} collective-permute-done((bf16[384,128]{1,0:T(8,128)(2,1)}, bf16[384,128]{1,0:T(8,128)(2,1)S(1)}, u32[]{:S(2)}, u32[]{:S(2)}) %collective-permute-start.12) | collective-permute-done | bytes 98336 | tf_op jit(solution)/shard_map/ppermute | solution.py:358
  59.3 3.5 %collective-permute-done.14.refs_9_ = bf16[384,128]{1,0:T(8,128)(2,1)S(1)} collective-permute-done((bf16[384,128]{1,0:T(8,128)(2,1)}, bf16[384,128]{1,0:T(8,128)(2,1)S(1)}, u32[]{:S(2)}, u32[]{:S(2)}) %collective-permute-start.14) | collective-permute-done | bytes 98336 | tf_op jit(solution)/shard_map/ppermute | solution.py:358
  62.8 1.5 %collective-permute-start.20 = (bf16[8,4,16,128]{3,2,1,0:T(8,128)(2,1)S(1)}, bf16[8,4,16,128]{3,2,1,0:T(8,128)(2,1)S(1)}, u32[]{:S(2)}, u32[]{:S(2)}) collective-permute-start(bf16[8,4,16,128]{3,2,1,0:T(8,128)(2,1)S(1)} %collective-permute-done.18.refs_7_), channel_id=1, source_target_pairs={{0,2},{1,3},{2,0},{3,1},{4,6},{5,7},{6,4},{7,5},{8,10},{9,11},{10,... | collective-permute-start | bytes 393224 | tf_op jit(solution)/shard_map/ppermute | solution.py:358
  64.9 1.1 %collective-permute-start.2 = (bf16[384,128]{1,0:T(8,128)(2,1)S(1)}, bf16[384,128]{1,0:T(8,128)(2,1)S(1)}, u32[]{:S(2)}, u32[]{:S(2)}) collective-permute-start(bf16[384,128]{1,0:T(8,128)(2,1)S(1)} %get-tuple-element.73), channel_id=1, source_target_pairs={{0,4},{4,0},{8,12},{12,8},{16,20},{20,16},{24,28},{28,24},{1,5},{5... | collective-permute-start | bytes 294920 | tf_op jit(solution)/shard_map/ppermute | solution.py:358
  66.0 3.7 %collective-permute-start.3 = (bf16[384,128]{1,0:T(8,128)(2,1)S(1)}, bf16[384,128]{1,0:T(8,128)(2,1)S(1)}, u32[]{:S(2)}, u32[]{:S(2)}) collective-permute-start(bf16[384,128]{1,0:T(8,128)(2,1)S(1)} %get-tuple-element.75), channel_id=1, source_target_pairs={{0,8},{4,12},{8,0},{12,4},{16,24},{20,28},{24,16},{28,20},{1,9},{5... | collective-permute-start | bytes 294920 | tf_op jit(solution)/shard_map/ppermute | solution.py:358
  69.8 3.7 %collective-permute-start.10 = (bf16[384,128]{1,0:T(8,128)(2,1)S(1)}, bf16[384,128]{1,0:T(8,128)(2,1)S(1)}, u32[]{:S(2)}, u32[]{:S(2)}) collective-permute-start(bf16[384,128]{1,0:T(8,128)(2,1)S(1)} %get-tuple-element.85), channel_id=1, source_target_pairs={{0,20},{4,16},{8,28},{12,24},{16,4},{20,0},{24,12},{28,8},{1,21},{... | collective-permute-start | bytes 294920 | tf_op jit(solution)/shard_map/ppermute | solution.py:358
  73.6 1.3 %sources.1 = bf16[128,48,256]{2,1,0:T(8,128)(2,1)S(1)} custom-call(s32[1]{0:T(128)} %bitcast.refs_1_.refs_0_, s32[1]{0:T(128)} %bitcast.2.refs_1_, bf16[8,4,32,128]{3,2,1,0:T(8,128)(2,1)S(1)} %all-to-all-done.refs_2_, bf16[8,4,32,128]{3,2,1,0:T(8,128)(2,1)S(1)} %collective-permute-done.5.refs_3_, bf16[8,4,32,128]{3,2,1,0:T(8,128)(2,1)S(1)} %collective-permute-done.6.refs_4_, ...), custom_call_target="tpu_custom_call" | custom-call | flops 100000000 | bytes 4194304 | tf_op jit(solution)/shard_map/sources/pallas_call | solution.py:230
  74.9 9.6 %stack.2.refs_12_ = bf16[1,4,128,32,256]{4,3,2,1,0:T(8,128)(2,1)} custom-call(s32[1]{0:T(128)S(6)} %copy.11.refs_0_, s32[1]{0:T(128)} %bitcast.refs_1_.refs_0_, bf16[448,128]{1,0:T(8,128)(2,1)S(1)} %get-tuple-element.94.refs_0_.refs_2_, bf16[448,128]{1,0:T(8,128)(2,1)S(1)} %collective-permute-done.1.refs_1_.refs_3_, ...), custom_call_target="tpu_custom_call" | custom-call | flops 2147483648 | bytes 7340032 | tf_op jit(solution)/shard_map/stack/pallas_call | solution.py:331
  84.5 9.6 %stack.3 = bf16[1,4,128,32,256]{4,3,2,1,0:T(8,128)(2,1)} custom-call(s32[1]{0:T(128)S(6)} %copy.11.refs_0_, s32[1]{0:T(128)} %bitcast.refs_1_.refs_0_, bf16[384,128]{1,0:T(8,128)(2,1)S(1)} %get-tuple-element.70.refs_2_, bf16[384,128]{1,0:T(8,128)(2,1)S(1)} %collective-permute-done.2.refs_3_, ...), custom_call_target="tpu_custom_call", output_to_operand_aliasing={{}: (12, {})} | custom-call | flops 2147483648 | bytes 7340032 | tf_op jit(solution)/shard_map/stack/pallas_call | solution.py:331
  (34 shorter events, 0.3 us)
Async XLA Ops:
  1.1 16.2 %collective-permute-start = (bf16[8,128,256]{2,1,0:T(8,128)(2,1)S(1)}, bf16[8,128,256]{2,1,0:T(8,128)(2,1)S(1)}, u32[]{:S(2)}, u32[]{:S(2)}) collective-permute-start(bf16[8,128,256]{2,1,0:T(8,128)(2,1)S(1)} %slice.3), channel_id=1, source_target_pairs={{0,4},{4,8},{8,12},{12,16},{16,20},{20,24},{24,28},{1,5},{5,9},{9,... | collective-permute-start | bytes 1572872 | tf_op jit(solution)/shard_map/ppermute | solution.py:373
  6.7 1.9 %copy-start = (bf16[8,128,1536]{2,1,0:T(8,128)(2,1)S(1)}, bf16[8,128,1536]{2,1,0:T(8,128)(2,1)}, u32[]{:S(2)}) copy-start(bf16[8,128,1536]{2,1,0:T(8,128)(2,1)} %refs_2_.1) | copy-start | bytes 9437188
  8.6 1.0 %copy-start.3 = (f32[512,256]{1,0:T(8,128)S(1)}, f32[512,256]{1,0:T(8,128)}, u32[]{:S(2)}) copy-start(f32[512,256]{1,0:T(8,128)} %constant.13.clone.table_ref) | copy-start | bytes 1572868
  9.7 0.7 copy-start.4
  12.3 62.6 %copy-start.2 = (f32[256,256]{1,0:T(8,128)S(1)}, f32[256,256]{1,0:T(8,128)}, u32[]{:S(2)}) copy-start(f32[256,256]{1,0:T(8,128)} %constant.14.clone.refs_11_) | copy-start | bytes 786436
  12.3 13.6 %all-to-all-start = ((bf16[8,4,32,128]{3,2,1,0:T(8,128)(2,1)}), bf16[8,4,32,128]{3,2,1,0:T(8,128)(2,1)S(1)}, u32[]{:S(2)}, u32[]{:S(2)}) async-start(bf16[8,4,32,128]{3,2,1,0:T(8,128)(2,1)} %get-tuple-element.51), calls=%async_computation | async-start | bytes 524288 | tf_op jit(solution)/shard_map/all_to_all | solution.py:375
  17.2 1.9 %copy-start.1 = (bf16[8,128,1536]{2,1,0:T(8,128)(2,1)S(1)}, bf16[8,128,1536]{2,1,0:T(8,128)(2,1)}, u32[]{:S(2)}) copy-start(bf16[8,128,1536]{2,1,0:T(8,128)(2,1)} %refs_2_.1) | copy-start | bytes 9437188
  24.4 1.5 %copy-start.5 = (bf16[384,128]{1,0:T(8,128)(2,1)}, bf16[384,128]{1,0:T(8,128)(2,1)S(1)}, u32[]{:S(2)}) copy-start(bf16[384,128]{1,0:T(8,128)(2,1)S(1)} %get-tuple-element.91) | copy-start | bytes 294916
  24.4 1.5 %copy-start.6 = (bf16[384,128]{1,0:T(8,128)(2,1)}, bf16[384,128]{1,0:T(8,128)(2,1)S(1)}, u32[]{:S(2)}) copy-start(bf16[384,128]{1,0:T(8,128)(2,1)S(1)} %get-tuple-element.88) | copy-start | bytes 294916
  25.9 7.5 %collective-permute-start.6 = (bf16[8,4,32,128]{3,2,1,0:T(8,128)(2,1)S(1)}, bf16[8,4,32,128]{3,2,1,0:T(8,128)(2,1)S(1)}, u32[]{:S(2)}, u32[]{:S(2)}) collective-permute-start(bf16[8,4,32,128]{3,2,1,0:T(8,128)(2,1)S(1)} %all-to-all-done.refs_2_), channel_id=1, source_target_pairs={{0,2},{1,3},{2,0},{3,1},{4,6},{5,7},{6,4},{7,5},{8,10},{9,11},{10,... | collective-permute-start | bytes 786440 | tf_op jit(solution)/shard_map/ppermute | solution.py:358
  27.4 9.2 %collective-permute-start.5 = (bf16[8,4,32,128]{3,2,1,0:T(8,128)(2,1)S(1)}, bf16[8,4,32,128]{3,2,1,0:T(8,128)(2,1)S(1)}, u32[]{:S(2)}, u32[]{:S(2)}) collective-permute-start(bf16[8,4,32,128]{3,2,1,0:T(8,128)(2,1)S(1)} %all-to-all-done.refs_2_), channel_id=1, source_target_pairs={{0,1},{1,0},{2,3},{3,2},{4,5},{5,4},{6,7},{7,6},{8,9},{9,8},{10,11... | collective-permute-start | bytes 786440 | tf_op jit(solution)/shard_map/ppermute | solution.py:358
  27.4 9.5 %collective-permute-start.1 = (bf16[448,128]{1,0:T(8,128)(2,1)S(1)}, bf16[448,128]{1,0:T(8,128)(2,1)S(1)}, u32[]{:S(2)}, u32[]{:S(2)}) collective-permute-start(bf16[448,128]{1,0:T(8,128)(2,1)S(1)} %get-tuple-element.72), channel_id=1, source_target_pairs={{0,4},{4,0},{8,12},{12,8},{16,20},{20,16},{24,28},{28,24},{1,5},{5... | collective-permute-start | bytes 344072 | tf_op jit(solution)/shard_map/ppermute | solution.py:358
  28.9 12.5 %collective-permute-start.15 = (bf16[448,128]{1,0:T(8,128)(2,1)S(1)}, bf16[448,128]{1,0:T(8,128)(2,1)S(1)}, u32[]{:S(2)}, u32[]{:S(2)}) collective-permute-start(bf16[448,128]{1,0:T(8,128)(2,1)S(1)} %get-tuple-element.92), channel_id=1, source_target_pairs={{0,24},{4,28},{8,16},{12,20},{16,8},{20,12},{24,0},{28,4},{1,25},{... | collective-permute-start | bytes 344072 | tf_op jit(solution)/shard_map/ppermute | solution.py:358
  33.4 8.0 %collective-permute-start.9 = (bf16[448,128]{1,0:T(8,128)(2,1)S(1)}, bf16[448,128]{1,0:T(8,128)(2,1)S(1)}, u32[]{:S(2)}, u32[]{:S(2)}) collective-permute-start(bf16[448,128]{1,0:T(8,128)(2,1)S(1)} %get-tuple-element.84), channel_id=1, source_target_pairs={{0,12},{4,8},{8,4},{12,0},{16,28},{20,24},{24,20},{28,16},{1,13},{... | collective-permute-start | bytes 344072 | tf_op jit(solution)/shard_map/ppermute | solution.py:358
  33.4 14.7 %collective-permute-start.11 = (bf16[448,128]{1,0:T(8,128)(2,1)S(1)}, bf16[448,128]{1,0:T(8,128)(2,1)S(1)}, u32[]{:S(2)}, u32[]{:S(2)}) collective-permute-start(bf16[448,128]{1,0:T(8,128)(2,1)S(1)} %get-tuple-element.87), channel_id=1, source_target_pairs={{0,16},{4,20},{8,24},{12,28},{16,0},{20,4},{24,8},{28,12},{1,17},{... | collective-permute-start | bytes 344072 | tf_op jit(solution)/shard_map/ppermute | solution.py:358
  36.6 15.0 %collective-permute-start.13 = (bf16[448,128]{1,0:T(8,128)(2,1)S(1)}, bf16[448,128]{1,0:T(8,128)(2,1)S(1)}, u32[]{:S(2)}, u32[]{:S(2)}) collective-permute-start(bf16[448,128]{1,0:T(8,128)(2,1)S(1)} %get-tuple-element.90), channel_id=1, source_target_pairs={{0,20},{4,16},{8,28},{12,24},{16,4},{20,0},{24,12},{28,8},{1,21},{... | collective-permute-start | bytes 344072 | tf_op jit(solution)/shard_map/ppermute | solution.py:358
  36.9 14.6 %collective-permute-start.17 = (bf16[448,128]{1,0:T(8,128)(2,1)S(1)}, bf16[448,128]{1,0:T(8,128)(2,1)S(1)}, u32[]{:S(2)}, u32[]{:S(2)}) collective-permute-start(bf16[448,128]{1,0:T(8,128)(2,1)S(1)} %get-tuple-element.95), channel_id=1, source_target_pairs={{0,28},{4,24},{8,20},{12,16},{16,12},{20,8},{24,4},{28,0},{1,29},{... | collective-permute-start | bytes 344072 | tf_op jit(solution)/shard_map/ppermute | solution.py:358
  41.4 10.2 %collective-permute-start.7 = (bf16[448,128]{1,0:T(8,128)(2,1)S(1)}, bf16[448,128]{1,0:T(8,128)(2,1)S(1)}, u32[]{:S(2)}, u32[]{:S(2)}) collective-permute-start(bf16[448,128]{1,0:T(8,128)(2,1)S(1)} %get-tuple-element.81), channel_id=1, source_target_pairs={{0,8},{4,12},{8,0},{12,4},{16,24},{20,28},{24,16},{28,20},{1,9},{5... | collective-permute-start | bytes 344072 | tf_op jit(solution)/shard_map/ppermute | solution.py:358
  51.6 11.2 %collective-permute-start.18 = (bf16[8,4,16,128]{3,2,1,0:T(8,128)(2,1)S(1)}, bf16[8,4,16,128]{3,2,1,0:T(8,128)(2,1)S(1)}, u32[]{:S(2)}, u32[]{:S(2)}) collective-permute-start(bf16[8,4,16,128]{3,2,1,0:T(8,128)(2,1)S(1)} %collect.1.refs_6_), channel_id=1, source_target_pairs={{0,1},{1,0},{2,3},{3,2},{4,5},{5,4},{6,7},{7,6},{8,9},{9,8},{10,11... | collective-permute-start | bytes 393224 | tf_op jit(solution)/shard_map/ppermute | solution.py:358
  51.7 18.2 %collective-permute-start.16 = (bf16[8,4,32,128]{3,2,1,0:T(8,128)(2,1)S(1)}, bf16[8,4,32,128]{3,2,1,0:T(8,128)(2,1)S(1)}, u32[]{:S(2)}, u32[]{:S(2)}) collective-permute-start(bf16[8,4,32,128]{3,2,1,0:T(8,128)(2,1)S(1)} %collective-permute-done.5.refs_3_), channel_id=1, source_target_pairs={{0,2},{1,3},{2,0},{3,1},{4,6},{5,7},{6,4},{7,5},{8,10},{9,11},{10,... | collective-permute-start | bytes 786440 | tf_op jit(solution)/shard_map/ppermute | solution.py:358
  52.3 7.0 %collective-permute-start.12 = (bf16[384,128]{1,0:T(8,128)(2,1)}, bf16[384,128]{1,0:T(8,128)(2,1)S(1)}, u32[]{:S(2)}, u32[]{:S(2)}) collective-permute-start(bf16[384,128]{1,0:T(8,128)(2,1)} %copy-done.6), channel_id=1, source_target_pairs={{0,24},{4,28},{8,16},{12,20},{16,8},{20,12},{24,0},{28,4},{1,25},{... | collective-permute-start | bytes 294920 | tf_op jit(solution)/shard_map/ppermute | solution.py:358
  55.2 7.6 %collective-permute-start.14 = (bf16[384,128]{1,0:T(8,128)(2,1)}, bf16[384,128]{1,0:T(8,128)(2,1)S(1)}, u32[]{:S(2)}, u32[]{:S(2)}) collective-permute-start(bf16[384,128]{1,0:T(8,128)(2,1)} %copy-done.5), channel_id=1, source_target_pairs={{0,28},{4,24},{8,20},{12,16},{16,12},{20,8},{24,4},{28,0},{1,29},{... | collective-permute-start | bytes 294920 | tf_op jit(solution)/shard_map/ppermute | solution.py:358
  56.6 13.1 %collective-permute-start.19 = (bf16[8,4,16,128]{3,2,1,0:T(8,128)(2,1)S(1)}, bf16[8,4,16,128]{3,2,1,0:T(8,128)(2,1)S(1)}, u32[]{:S(2)}, u32[]{:S(2)}) collective-permute-start(bf16[8,4,16,128]{3,2,1,0:T(8,128)(2,1)S(1)} %collect.1.refs_6_), channel_id=1, source_target_pairs={{0,2},{1,3},{2,0},{3,1},{4,6},{5,7},{6,4},{7,5},{8,10},{9,11},{10,... | collective-permute-start | bytes 393224 | tf_op jit(solution)/shard_map/ppermute | solution.py:358
  62.8 10.8 %collective-permute-start.20 = (bf16[8,4,16,128]{3,2,1,0:T(8,128)(2,1)S(1)}, bf16[8,4,16,128]{3,2,1,0:T(8,128)(2,1)S(1)}, u32[]{:S(2)}, u32[]{:S(2)}) collective-permute-start(bf16[8,4,16,128]{3,2,1,0:T(8,128)(2,1)S(1)} %collective-permute-done.18.refs_7_), channel_id=1, source_target_pairs={{0,2},{1,3},{2,0},{3,1},{4,6},{5,7},{6,4},{7,5},{8,10},{9,11},{10,... | collective-permute-start | bytes 393224 | tf_op jit(solution)/shard_map/ppermute | solution.py:358
  64.9 19.6 %collective-permute-start.2 = (bf16[384,128]{1,0:T(8,128)(2,1)S(1)}, bf16[384,128]{1,0:T(8,128)(2,1)S(1)}, u32[]{:S(2)}, u32[]{:S(2)}) collective-permute-start(bf16[384,128]{1,0:T(8,128)(2,1)S(1)} %get-tuple-element.73), channel_id=1, source_target_pairs={{0,4},{4,0},{8,12},{12,8},{16,20},{20,16},{24,28},{28,24},{1,5},{5... | collective-permute-start | bytes 294920 | tf_op jit(solution)/shard_map/ppermute | solution.py:358
  66.0 18.5 %collective-permute-start.3 = (bf16[384,128]{1,0:T(8,128)(2,1)S(1)}, bf16[384,128]{1,0:T(8,128)(2,1)S(1)}, u32[]{:S(2)}, u32[]{:S(2)}) collective-permute-start(bf16[384,128]{1,0:T(8,128)(2,1)S(1)} %get-tuple-element.75), channel_id=1, source_target_pairs={{0,8},{4,12},{8,0},{12,4},{16,24},{20,28},{24,16},{28,20},{1,9},{5... | collective-permute-start | bytes 294920 | tf_op jit(solution)/shard_map/ppermute | solution.py:358
  69.7 14.8 %collective-permute-start.4 = (bf16[384,128]{1,0:T(8,128)(2,1)S(1)}, bf16[384,128]{1,0:T(8,128)(2,1)S(1)}, u32[]{:S(2)}, u32[]{:S(2)}) collective-permute-start(bf16[384,128]{1,0:T(8,128)(2,1)S(1)} %get-tuple-element.77), channel_id=1, source_target_pairs={{0,12},{4,8},{8,4},{12,0},{16,28},{20,24},{24,20},{28,16},{1,13},{... | collective-permute-start | bytes 294920 | tf_op jit(solution)/shard_map/ppermute | solution.py:358
  69.8 14.6 %collective-permute-start.10 = (bf16[384,128]{1,0:T(8,128)(2,1)S(1)}, bf16[384,128]{1,0:T(8,128)(2,1)S(1)}, u32[]{:S(2)}, u32[]{:S(2)}) collective-permute-start(bf16[384,128]{1,0:T(8,128)(2,1)S(1)} %get-tuple-element.85), channel_id=1, source_target_pairs={{0,20},{4,16},{8,28},{12,24},{16,4},{20,0},{24,12},{28,8},{1,21},{... | collective-permute-start | bytes 294920 | tf_op jit(solution)/shard_map/ppermute | solution.py:358
  73.6 10.9 %collective-permute-start.8 = (bf16[384,128]{1,0:T(8,128)(2,1)S(1)}, bf16[384,128]{1,0:T(8,128)(2,1)S(1)}, u32[]{:S(2)}, u32[]{:S(2)}) collective-permute-start(bf16[384,128]{1,0:T(8,128)(2,1)S(1)} %get-tuple-element.82), channel_id=1, source_target_pairs={{0,16},{4,20},{8,24},{12,28},{16,0},{20,4},{24,8},{28,12},{1,17},{... | collective-permute-start | bytes 294920 | tf_op jit(solution)/shard_map/ppermute | solution.py:358

commit v5 on v4

--- a/solution.py
+++ b/solution.py
@@ -296,7 +296,7 @@
 
         lax.fori_loop(0, BINS // pack, one, 0, unroll=8 // pack)
 
-    rows = 8
+    rows = 2
     for q in range(0, group, rows):
         lefts = []
         for u in range(rows):
@@ -377,30 +377,15 @@
     picked, (near, far) = lax.optimization_barrier((picked, chunks))
     order = list(range(nwide - 1, 0, -1))
 
-    top = nnar // 2
-
-    def begin(value):
-        return {0: value, **{n: swap(value, "narrow", n) for n in (top, 1) if n}}
-
-    def finish(slots, waits):
-        bit = top
-        while bit:
-            for n in sorted(slots):
-                if n ^ bit not in slots:
-                    slots[n ^ bit] = swap(after(slots[n], waits), "narrow", bit)
-            bit //= 2
-        return [slots[n] for n in range(nnar)]
-
-    lates = begin(picked)
+    def gather(value):
+        return [value] + [swap(value, "narrow", n) for n in range(nnar - 1, 0, -1)][::-1]
+
+    lates = gather(picked)
     for i, m in enumerate(order):
-        waits = []
-        if i == len(order) - 2:
-            waits = [lates[n] for n in sorted(lates) if n]
-            lates = finish(lates, [near[order[1]]])
-        near[m] = swap(after(near[m], waits), "wide", m)
-    for i, m in enumerate(order):
-        far[m] = swap(after(far[m], [near[order[min(i + 2, nwide - 2)]]]), "wide", m)
-    firsts = finish(begin(collect(near, 2 * nv)), [far[n] for n in order[:2]])
+        near[m] = swap(after(near[m], lates[1:] if i >= len(order) - 2 else []), "wide", m)
+    firsts = gather(collect(near, 2 * nv))
+    for m in order:
+        far[m] = swap(after(far[m], firsts[1:]), "wide", m)
     table = sources(lates, firsts, me, place, wins, nv)
     lag = jnp.asarray(lag_table())
     out, start = None, 0

time: 94.6 us -> 96.3 us (1.018)
  starting transfers between devices: 41.7 us -> 46 us
  waiting for transfers between devices: 16.6 us -> 13.1 us
  local copies, waits for them, and re-layouts: 7.34 us -> 9.85 us
  Pallas kernels: 27.7 us -> 26.1 us
    ppermute x20, starting transfers between devices: 31.8 us -> 36.2 us  [swap(): lax.ppermute(value, axis, [(i, i ^ mask) for i in range(lax.axis_size(axi...]
    unnamed x15 -> x19, local copies, waits for them, and re-layouts: 6.26 us -> 8.78 us
    ppermute x20, waiting for transfers between devices: 15.2 us -> 13.1 us  [swap(): lax.ppermute(value, axis, [(i, i ^ mask) for i in range(lax.axis_size(axi...]
    pallas_call x2, Pallas kernels: 19.2 us -> 17.6 us  [stack(): pl.pallas_call(lambda *refs: stack_kernel(nw, wins, size, group, *refs),...]
    all_to_all x1, waiting for transfers between devices: 1.46 us -> 0.01 us  [on_device(): lax.all_to_all(picked, 'wide', split_axis=0, concat_axis=0, tiled=True)]
  transfers between devices with their start and end apart: 22 -> 22, of which waited for: 5 -> 5; matrix products, arithmetic and copies ran while one was open for 1% -> 1% of each run, Pallas kernels for 19% -> 18%
where the time goes in v5:
time: 96.3 us; the launch traced here: 95.9 us
  starting transfers between devices  46 us (48%)
  Pallas kernels  26.1 us (27%)
  waiting for transfers between devices  13.1 us (14%)
  local copies, waits for them, and re-layouts  9.85 us (10%)
    ppermute x20, starting transfers between devices, swap(): lax.ppermute(value, axis, [(i, i ^ mask) for i in range(lax.axis_size(axi...  36.2 us
    pallas_call x2, Pallas kernels, stack(): pl.pallas_call(lambda *refs: stack_kernel(nw, wins, size, group, *refs),...  17.6 us
    ppermute x20, waiting for transfers between devices, swap(): lax.ppermute(value, axis, [(i, i ^ mask) for i in range(lax.axis_size(axi...  13.1 us
    unnamed x19, local copies, waits for them, and re-layouts  8.78 us
    pallas_call x1, Pallas kernels, spectra(): pl.pallas_call(lambda *refs: spectra_kernel(sizes, *refs), in_specs=[smem...  5.25 us
    all_to_all x1, starting transfers between devices, on_device(): lax.all_to_all(picked, 'wide', split_axis=0, concat_axis=0, tiled=True)  4.98 us
    ppermute x1, starting transfers between devices, on_device(): lax.ppermute(records[:, :, time - HALF:], 'wide', [(i, i + 1) for i in ra...  4.88 us
  transfers between devices with their start and end apart: 22, of which 5 were waited for; matrix products, arithmetic and copies ran while one was open for 1% of the time, Pallas kernels for 18%

profile of v5, /device:TPU:0, one launch (start us, length us, event | category | flops | bytes accessed | tf_op | source)
XLA Modules:
  0.0 95.9 jit_solution(14776171171822479838)
XLA Ops:
  0.0 1.1 %slice.3 = bf16[8,128,256]{2,1,0:T(8,128)(2,1)S(1)} slice(bf16[8,128,1536]{2,1,0:T(8,128)(2,1)} %refs_2_.1), slice={[0:8], [0:128], [1280:1536]} | slice | bytes 1048576 | tf_op jit(solution)/shard_map/slice | solution.py:373
  1.1 4.9 %collective-permute-start = (bf16[8,128,256]{2,1,0:T(8,128)(2,1)S(1)}, bf16[8,128,256]{2,1,0:T(8,128)(2,1)S(1)}, u32[]{:S(2)}, u32[]{:S(2)}) collective-permute-start(bf16[8,128,256]{2,1,0:T(8,128)(2,1)S(1)} %slice.3), channel_id=1, source_target_pairs={{0,4},{4,8},{8,12},{12,16},{16,20},{20,24},{24,28},{1,5},{5,9},{9,... | collective-permute-start | bytes 1572872 | tf_op jit(solution)/shard_map/ppermute | solution.py:373
  6.0 0.8 copy.8.pairs_ref.refs_0_
  6.7 1.9 %copy-done = bf16[8,128,1536]{2,1,0:T(8,128)(2,1)S(1)} copy-done((bf16[8,128,1536]{2,1,0:T(8,128)(2,1)S(1)}, bf16[8,128,1536]{2,1,0:T(8,128)(2,1)}, u32[]{:S(2)}) %copy-start) | copy-done | bytes 3145752
  8.6 1.0 %copy-done.3 = f32[512,256]{1,0:T(8,128)S(1)} copy-done((f32[512,256]{1,0:T(8,128)S(1)}, f32[512,256]{1,0:T(8,128)}, u32[]{:S(2)}) %copy-start.3) | copy-done | bytes 524312
  9.7 0.7 copy-done.4
  10.3 1.9 %early.1 = (bf16[8,4,32,128]{3,2,1,0:T(8,128)(2,1)}, bf16[512,256]{1,0:T(8,128)(2,1)S(1)}, bf16[512,256]{1,0:T(8,128)(2,1)S(1)}) custom-call(s32[8,4]{1,0:T(8,128)S(1)} %copy.8.pairs_ref.refs_0_, bf16[8,128,1536]{2,1,0:T(8,128)(2,1)S(1)} %copy-done, f32[1,201]{1,0:T(1,128)S(1)} %bitcast.6, f32[512,256]{1,0:T(8,128)S(1)} %copy-done.3), custom_call_target="tpu_custom_call" | custom-call | flops 400000000 | bytes 3145728 | tf_op jit(solution)/shard_map/early/pallas_call | solution.py:98
  12.3 5.0 %all-to-all-start = ((bf16[8,4,32,128]{3,2,1,0:T(8,128)(2,1)}), bf16[8,4,32,128]{3,2,1,0:T(8,128)(2,1)S(1)}, u32[]{:S(2)}, u32[]{:S(2)}) async-start(bf16[8,4,32,128]{3,2,1,0:T(8,128)(2,1)} %get-tuple-element.50), calls=%async_computation | async-start | bytes 524288 | tf_op jit(solution)/shard_map/all_to_all | solution.py:375
  17.3 1.9 %copy-done.1 = bf16[8,128,1536]{2,1,0:T(8,128)(2,1)S(1)} copy-done((bf16[8,128,1536]{2,1,0:T(8,128)(2,1)S(1)}, bf16[8,128,1536]{2,1,0:T(8,128)(2,1)}, u32[]{:S(2)}) %copy-start.1) | copy-done | bytes 3145752
  19.1 5.2 %spectra.1 = (bf16[448,128]{1,0:T(8,128)(2,1)S(1)}, bf16[448,128]{1,0:T(8,128)(2,1)S(1)}, bf16[448,128]{1,0:T(8,128)(2,1)S(1)}, bf16[448,128]{1,0:T(8,128)(2,1)S...) custom-call(s32[8,4]{1,0:T(8,128)S(1)} %copy.8.pairs_ref.refs_0_, ...), custom_call_target="tpu_custom_call" | custom-call | flops 2415919104 | bytes 4718592 | tf_op jit(solution)/shard_map/spectra/pallas_call | solution.py:155
  25.0 0.6 copy-done.6
  27.3 1.2 %collective-permute-start.2 = (bf16[8,4,32,128]{3,2,1,0:T(8,128)(2,1)S(1)}, bf16[8,4,32,128]{3,2,1,0:T(8,128)(2,1)S(1)}, u32[]{:S(2)}, u32[]{:S(2)}) collective-permute-start(bf16[8,4,32,128]{3,2,1,0:T(8,128)(2,1)S(1)} %all-to-all-done.refs_2_), channel_id=1, source_target_pairs={{0,2},{1,3},{2,0},{3,1},{4,6},{5,7},{6,4},{7,5},{8,10},{9,11},{10,... | collective-permute-start | bytes 786440 | tf_op jit(solution)/shard_map/ppermute | solution.py:358
  28.8 3.3 %collective-permute-start.6 = (bf16[448,128]{1,0:T(8,128)(2,1)S(1)}, bf16[448,128]{1,0:T(8,128)(2,1)S(1)}, u32[]{:S(2)}, u32[]{:S(2)}) collective-permute-start(bf16[448,128]{1,0:T(8,128)(2,1)S(1)} %get-tuple-element.77), channel_id=1, source_target_pairs={{0,12},{4,8},{8,4},{12,0},{16,28},{20,24},{24,20},{28,16},{1,13},{... | collective-permute-start | bytes 344072 | tf_op jit(solution)/shard_map/ppermute | solution.py:358
  32.1 3.4 %collective-permute-start.7 = (bf16[448,128]{1,0:T(8,128)(2,1)S(1)}, bf16[448,128]{1,0:T(8,128)(2,1)S(1)}, u32[]{:S(2)}, u32[]{:S(2)}) collective-permute-start(bf16[448,128]{1,0:T(8,128)(2,1)S(1)} %get-tuple-element.78), channel_id=1, source_target_pairs={{0,16},{4,20},{8,24},{12,28},{16,0},{20,4},{24,8},{28,12},{1,17},{... | collective-permute-start | bytes 344072 | tf_op jit(solution)/shard_map/ppermute | solution.py:358
  35.6 4.2 %collective-permute-start.8 = (bf16[448,128]{1,0:T(8,128)(2,1)S(1)}, bf16[448,128]{1,0:T(8,128)(2,1)S(1)}, u32[]{:S(2)}, u32[]{:S(2)}) collective-permute-start(bf16[448,128]{1,0:T(8,128)(2,1)S(1)} %get-tuple-element.79), channel_id=1, source_target_pairs={{0,20},{4,16},{8,28},{12,24},{16,4},{20,0},{24,12},{28,8},{1,21},{... | collective-permute-start | bytes 344072 | tf_op jit(solution)/shard_map/ppermute | solution.py:358
  39.8 1.3 %collective-permute-done.2.refs_4_ = bf16[8,4,32,128]{3,2,1,0:T(8,128)(2,1)S(1)} collective-permute-done((bf16[8,4,32,128]{3,2,1,0:T(8,128)(2,1)S(1)}, bf16[8,4,32,128]{3,2,1,0:T(8,128)(2,1)S(1)}, u32[]{:S(2)}, u32[]{:S(2)}) %collective-permute-start.2) | collective-permute-done | bytes 262176 | tf_op jit(solution)/shard_map/ppermute | solution.py:358
  41.2 5.3 %collective-permute-start.9 = (bf16[448,128]{1,0:T(8,128)(2,1)S(1)}, bf16[448,128]{1,0:T(8,128)(2,1)S(1)}, u32[]{:S(2)}, u32[]{:S(2)}) collective-permute-start(bf16[448,128]{1,0:T(8,128)(2,1)S(1)} %get-tuple-element.80), channel_id=1, source_target_pairs={{0,24},{4,28},{8,16},{12,20},{16,8},{20,12},{24,0},{28,4},{1,25},{... | collective-permute-start | bytes 344072 | tf_op jit(solution)/shard_map/ppermute | solution.py:358
  46.5 0.9 collective-permute-start.10
  47.4 0.6 collective-permute-start.4
  48.0 2.0 %collective-permute-done.9.refs_6_.refs_8_ = bf16[448,128]{1,0:T(8,128)(2,1)S(1)} collective-permute-done((bf16[448,128]{1,0:T(8,128)(2,1)S(1)}, bf16[448,128]{1,0:T(8,128)(2,1)S(1)}, u32[]{:S(2)}, u32[]{:S(2)}) %collective-permute-start.9) | collective-permute-done | bytes 114720 | tf_op jit(solution)/shard_map/ppermute | solution.py:358
  50.1 5.2 %collective-permute-done.10.refs_7_.refs_9_ = bf16[448,128]{1,0:T(8,128)(2,1)S(1)} collective-permute-done((bf16[448,128]{1,0:T(8,128)(2,1)S(1)}, bf16[448,128]{1,0:T(8,128)(2,1)S(1)}, u32[]{:S(2)}, u32[]{:S(2)}) %collective-permute-start.10) | collective-permute-done | bytes 114720 | tf_op jit(solution)/shard_map/ppermute | solution.py:358
  55.6 1.6 %collective-permute-start.11 = (bf16[8,4,16,128]{3,2,1,0:T(8,128)(2,1)S(1)}, bf16[8,4,16,128]{3,2,1,0:T(8,128)(2,1)S(1)}, u32[]{:S(2)}, u32[]{:S(2)}) collective-permute-start(bf16[8,4,16,128]{3,2,1,0:T(8,128)(2,1)S(1)} %collect.1.refs_6_), channel_id=1, source_target_pairs={{0,1},{1,0},{2,3},{3,2},{4,5},{5,4},{6,7},{7,6},{8,9},{9,8},{10,11... | collective-permute-start | bytes 393224 | tf_op jit(solution)/shard_map/ppermute | solution.py:358
  57.2 3.5 %collective-permute-done.13.refs_9_ = bf16[8,4,16,128]{3,2,1,0:T(8,128)(2,1)S(1)} collective-permute-done((bf16[8,4,16,128]{3,2,1,0:T(8,128)(2,1)S(1)}, bf16[8,4,16,128]{3,2,1,0:T(8,128)(2,1)S(1)}, u32[]{:S(2)}, u32[]{:S(2)}) %collective-permute-start.13) | collective-permute-done | bytes 131104 | tf_op jit(solution)/shard_map/ppermute | solution.py:358
  60.7 1.0 %collective-permute-done.12.refs_8_ = bf16[8,4,16,128]{3,2,1,0:T(8,128)(2,1)S(1)} collective-permute-done((bf16[8,4,16,128]{3,2,1,0:T(8,128)(2,1)S(1)}, bf16[8,4,16,128]{3,2,1,0:T(8,128)(2,1)S(1)}, u32[]{:S(2)}, u32[]{:S(2)}) %collective-permute-start.12) | collective-permute-done | bytes 131104 | tf_op jit(solution)/shard_map/ppermute | solution.py:358
  61.7 1.5 %collective-permute-start.14 = (bf16[384,128]{1,0:T(8,128)(2,1)}, bf16[384,128]{1,0:T(8,128)(2,1)S(1)}, u32[]{:S(2)}, u32[]{:S(2)}) collective-permute-start(bf16[384,128]{1,0:T(8,128)(2,1)} %copy-done.8), channel_id=1, source_target_pairs={{0,4},{4,0},{8,12},{12,8},{16,20},{20,16},{24,28},{28,24},{1,5},{5... | collective-permute-start | bytes 294920 | tf_op jit(solution)/shard_map/ppermute | solution.py:358
  63.2 3.2 %collective-permute-start.15 = (bf16[384,128]{1,0:T(8,128)(2,1)}, bf16[384,128]{1,0:T(8,128)(2,1)S(1)}, u32[]{:S(2)}, u32[]{:S(2)}) collective-permute-start(bf16[384,128]{1,0:T(8,128)(2,1)} %copy-done.7), channel_id=1, source_target_pairs={{0,8},{4,12},{8,0},{12,4},{16,24},{20,28},{24,16},{28,20},{1,9},{5... | collective-permute-start | bytes 294920 | tf_op jit(solution)/shard_map/ppermute | solution.py:358
  67.2 4.9 %collective-permute-start.17 = (bf16[384,128]{1,0:T(8,128)(2,1)}, bf16[384,128]{1,0:T(8,128)(2,1)S(1)}, u32[]{:S(2)}, u32[]{:S(2)}) collective-permute-start(bf16[384,128]{1,0:T(8,128)(2,1)} %copy-done.5), channel_id=1, source_target_pairs={{0,16},{4,20},{8,24},{12,28},{16,0},{20,4},{24,8},{28,12},{1,17},{... | collective-permute-start | bytes 294920 | tf_op jit(solution)/shard_map/ppermute | solution.py:358
  72.1 1.3 %sources.1 = bf16[128,48,256]{2,1,0:T(8,128)(2,1)S(1)} custom-call(s32[1]{0:T(128)} %bitcast.refs_1_.refs_0_, s32[1]{0:T(128)} %bitcast.2.refs_1_, bf16[8,4,32,128]{3,2,1,0:T(8,128)(2,1)S(1)} %all-to-all-done.refs_2_, bf16[8,4,32,128]{3,2,1,0:T(8,128)(2,1)S(1)} %collective-permute-done.1.refs_3_, bf16[8,4,32,128]{3,2,1,0:T(8,128)(2,1)S(1)} %collective-permute-done.2.refs_4_, ...), custom_call_target="tpu_custom_call" | custom-call | flops 100000000 | bytes 4194304 | tf_op jit(solution)/shard_map/sources/pallas_call | solution.py:230
  73.4 3.1 %collective-permute-start.19 = (bf16[384,128]{1,0:T(8,128)(2,1)S(1)}, bf16[384,128]{1,0:T(8,128)(2,1)S(1)}, u32[]{:S(2)}, u32[]{:S(2)}) collective-permute-start(bf16[384,128]{1,0:T(8,128)(2,1)S(1)} %get-tuple-element.92), channel_id=1, source_target_pairs={{0,24},{4,28},{8,16},{12,20},{16,8},{20,12},{24,0},{28,4},{1,25},{... | collective-permute-start | bytes 294920 | tf_op jit(solution)/shard_map/ppermute | solution.py:358
  76.5 1.7 %collective-permute-start.20 = (bf16[384,128]{1,0:T(8,128)(2,1)S(1)}, bf16[384,128]{1,0:T(8,128)(2,1)S(1)}, u32[]{:S(2)}, u32[]{:S(2)}) collective-permute-start(bf16[384,128]{1,0:T(8,128)(2,1)S(1)} %get-tuple-element.94), channel_id=1, source_target_pairs={{0,28},{4,24},{8,20},{12,16},{16,12},{20,8},{24,4},{28,0},{1,29},{... | collective-permute-start | bytes 294920 | tf_op jit(solution)/shard_map/ppermute | solution.py:358
  78.2 8.8 %stack.2.refs_12_ = bf16[1,4,128,32,256]{4,3,2,1,0:T(8,128)(2,1)} custom-call(s32[1]{0:T(128)S(6)} %copy.11.refs_0_, s32[1]{0:T(128)} %bitcast.refs_1_.refs_0_, bf16[448,128]{1,0:T(8,128)(2,1)S(1)} %get-tuple-element.71.refs_0_.refs_2_, bf16[448,128]{1,0:T(8,128)(2,1)S(1)} %collective-permute-done.4.refs_1_.refs_3_, ...), custom_call_target="tpu_custom_call" | custom-call | flops 2147483648 | bytes 7340032 | tf_op jit(solution)/shard_map/stack/pallas_call | solution.py:331
  87.1 8.8 %stack.3 = bf16[1,4,128,32,256]{4,3,2,1,0:T(8,128)(2,1)} custom-call(s32[1]{0:T(128)S(6)} %copy.11.refs_0_, s32[1]{0:T(128)} %bitcast.refs_1_.refs_0_, bf16[384,128]{1,0:T(8,128)(2,1)S(1)} %get-tuple-element.69.refs_2_, bf16[384,128]{1,0:T(8,128)(2,1)S(1)} %collective-permute-done.14.refs_3_, ...), custom_call_target="tpu_custom_call", output_to_operand_aliasing={{}: (12, {})} | custom-call | flops 2147483648 | bytes 7340032 | tf_op jit(solution)/shard_map/stack/pallas_call | solution.py:331
  (38 shorter events, 3.1 us)
Async XLA Ops:
  1.1 16.2 %collective-permute-start = (bf16[8,128,256]{2,1,0:T(8,128)(2,1)S(1)}, bf16[8,128,256]{2,1,0:T(8,128)(2,1)S(1)}, u32[]{:S(2)}, u32[]{:S(2)}) collective-permute-start(bf16[8,128,256]{2,1,0:T(8,128)(2,1)S(1)} %slice.3), channel_id=1, source_target_pairs={{0,4},{4,8},{8,12},{12,16},{16,20},{20,24},{24,28},{1,5},{5,9},{9,... | collective-permute-start | bytes 1572872 | tf_op jit(solution)/shard_map/ppermute | solution.py:373
  6.7 1.9 %copy-start = (bf16[8,128,1536]{2,1,0:T(8,128)(2,1)S(1)}, bf16[8,128,1536]{2,1,0:T(8,128)(2,1)}, u32[]{:S(2)}) copy-start(bf16[8,128,1536]{2,1,0:T(8,128)(2,1)} %refs_2_.1) | copy-start | bytes 9437188
  8.6 1.0 %copy-start.3 = (f32[512,256]{1,0:T(8,128)S(1)}, f32[512,256]{1,0:T(8,128)}, u32[]{:S(2)}) copy-start(f32[512,256]{1,0:T(8,128)} %constant.13.clone.table_ref) | copy-start | bytes 1572868
  9.7 0.7 copy-start.4
  12.3 66.0 %copy-start.2 = (f32[256,256]{1,0:T(8,128)S(1)}, f32[256,256]{1,0:T(8,128)}, u32[]{:S(2)}) copy-start(f32[256,256]{1,0:T(8,128)} %constant.14.clone.refs_11_) | copy-start | bytes 786436
  12.3 14.7 %all-to-all-start = ((bf16[8,4,32,128]{3,2,1,0:T(8,128)(2,1)}), bf16[8,4,32,128]{3,2,1,0:T(8,128)(2,1)S(1)}, u32[]{:S(2)}, u32[]{:S(2)}) async-start(bf16[8,4,32,128]{3,2,1,0:T(8,128)(2,1)} %get-tuple-element.50), calls=%async_computation | async-start | bytes 524288 | tf_op jit(solution)/shard_map/all_to_all | solution.py:375
  17.2 1.9 %copy-start.1 = (bf16[8,128,1536]{2,1,0:T(8,128)(2,1)S(1)}, bf16[8,128,1536]{2,1,0:T(8,128)(2,1)}, u32[]{:S(2)}) copy-start(bf16[8,128,1536]{2,1,0:T(8,128)(2,1)} %refs_2_.1) | copy-start | bytes 9437188
  24.4 0.6 copy-start.5
  25.0 0.6 copy-start.6
  25.7 0.6 copy-start.7
  26.3 0.6 copy-start.8
  26.9 8.7 %collective-permute-start.3 = (bf16[8,4,32,128]{3,2,1,0:T(8,128)(2,1)S(1)}, bf16[8,4,32,128]{3,2,1,0:T(8,128)(2,1)S(1)}, u32[]{:S(2)}, u32[]{:S(2)}) collective-permute-start(bf16[8,4,32,128]{3,2,1,0:T(8,128)(2,1)S(1)} %all-to-all-done.refs_2_), channel_id=1, source_target_pairs={{0,3},{1,2},{2,1},{3,0},{4,7},{5,6},{6,5},{7,4},{8,11},{9,10},{10,... | collective-permute-start | bytes 786440 | tf_op jit(solution)/shard_map/ppermute | solution.py:358
  27.3 13.8 %collective-permute-start.2 = (bf16[8,4,32,128]{3,2,1,0:T(8,128)(2,1)S(1)}, bf16[8,4,32,128]{3,2,1,0:T(8,128)(2,1)S(1)}, u32[]{:S(2)}, u32[]{:S(2)}) collective-permute-start(bf16[8,4,32,128]{3,2,1,0:T(8,128)(2,1)S(1)} %all-to-all-done.refs_2_), channel_id=1, source_target_pairs={{0,2},{1,3},{2,0},{3,1},{4,6},{5,7},{6,4},{7,5},{8,10},{9,11},{10,... | collective-permute-start | bytes 786440 | tf_op jit(solution)/shard_map/ppermute | solution.py:358
  28.5 18.0 %collective-permute-start.1 = (bf16[8,4,32,128]{3,2,1,0:T(8,128)(2,1)S(1)}, bf16[8,4,32,128]{3,2,1,0:T(8,128)(2,1)S(1)}, u32[]{:S(2)}, u32[]{:S(2)}) collective-permute-start(bf16[8,4,32,128]{3,2,1,0:T(8,128)(2,1)S(1)} %all-to-all-done.refs_2_), channel_id=1, source_target_pairs={{0,1},{1,0},{2,3},{3,2},{4,5},{5,4},{6,7},{7,6},{8,9},{9,8},{10,11... | collective-permute-start | bytes 786440 | tf_op jit(solution)/shard_map/ppermute | solution.py:358
  28.8 18.6 %collective-permute-start.6 = (bf16[448,128]{1,0:T(8,128)(2,1)S(1)}, bf16[448,128]{1,0:T(8,128)(2,1)S(1)}, u32[]{:S(2)}, u32[]{:S(2)}) collective-permute-start(bf16[448,128]{1,0:T(8,128)(2,1)S(1)} %get-tuple-element.77), channel_id=1, source_target_pairs={{0,12},{4,8},{8,4},{12,0},{16,28},{20,24},{24,20},{28,16},{1,13},{... | collective-permute-start | bytes 344072 | tf_op jit(solution)/shard_map/ppermute | solution.py:358
  32.1 15.9 %collective-permute-start.7 = (bf16[448,128]{1,0:T(8,128)(2,1)S(1)}, bf16[448,128]{1,0:T(8,128)(2,1)S(1)}, u32[]{:S(2)}, u32[]{:S(2)}) collective-permute-start(bf16[448,128]{1,0:T(8,128)(2,1)S(1)} %get-tuple-element.78), channel_id=1, source_target_pairs={{0,16},{4,20},{8,24},{12,28},{16,0},{20,4},{24,8},{28,12},{1,17},{... | collective-permute-start | bytes 344072 | tf_op jit(solution)/shard_map/ppermute | solution.py:358
  35.6 12.4 %collective-permute-start.8 = (bf16[448,128]{1,0:T(8,128)(2,1)S(1)}, bf16[448,128]{1,0:T(8,128)(2,1)S(1)}, u32[]{:S(2)}, u32[]{:S(2)}) collective-permute-start(bf16[448,128]{1,0:T(8,128)(2,1)S(1)} %get-tuple-element.79), channel_id=1, source_target_pairs={{0,20},{4,16},{8,28},{12,24},{16,4},{20,0},{24,12},{28,8},{1,21},{... | collective-permute-start | bytes 344072 | tf_op jit(solution)/shard_map/ppermute | solution.py:358
  41.2 8.9 %collective-permute-start.9 = (bf16[448,128]{1,0:T(8,128)(2,1)S(1)}, bf16[448,128]{1,0:T(8,128)(2,1)S(1)}, u32[]{:S(2)}, u32[]{:S(2)}) collective-permute-start(bf16[448,128]{1,0:T(8,128)(2,1)S(1)} %get-tuple-element.80), channel_id=1, source_target_pairs={{0,24},{4,28},{8,16},{12,20},{16,8},{20,12},{24,0},{28,4},{1,25},{... | collective-permute-start | bytes 344072 | tf_op jit(solution)/shard_map/ppermute | solution.py:358
  46.5 8.7 %collective-permute-start.10 = (bf16[448,128]{1,0:T(8,128)(2,1)S(1)}, bf16[448,128]{1,0:T(8,128)(2,1)S(1)}, u32[]{:S(2)}, u32[]{:S(2)}) collective-permute-start(bf16[448,128]{1,0:T(8,128)(2,1)S(1)} %get-tuple-element.81), channel_id=1, source_target_pairs={{0,28},{4,24},{8,20},{12,16},{16,12},{20,8},{24,4},{28,0},{1,29},{... | collective-permute-start | bytes 344072 | tf_op jit(solution)/shard_map/ppermute | solution.py:358
  47.4 7.9 %collective-permute-start.4 = (bf16[448,128]{1,0:T(8,128)(2,1)S(1)}, bf16[448,128]{1,0:T(8,128)(2,1)S(1)}, u32[]{:S(2)}, u32[]{:S(2)}) collective-permute-start(bf16[448,128]{1,0:T(8,128)(2,1)S(1)} %get-tuple-element.74), channel_id=1, source_target_pairs={{0,4},{4,0},{8,12},{12,8},{16,20},{20,16},{24,28},{28,24},{1,5},{5... | collective-permute-start | bytes 344072 | tf_op jit(solution)/shard_map/ppermute | solution.py:358
  48.0 7.2 %collective-permute-start.5 = (bf16[448,128]{1,0:T(8,128)(2,1)S(1)}, bf16[448,128]{1,0:T(8,128)(2,1)S(1)}, u32[]{:S(2)}, u32[]{:S(2)}) collective-permute-start(bf16[448,128]{1,0:T(8,128)(2,1)S(1)} %get-tuple-element.76), channel_id=1, source_target_pairs={{0,8},{4,12},{8,0},{12,4},{16,24},{20,28},{24,16},{28,20},{1,9},{5... | collective-permute-start | bytes 344072 | tf_op jit(solution)/shard_map/ppermute | solution.py:358
  55.3 5.5 %collective-permute-start.13 = (bf16[8,4,16,128]{3,2,1,0:T(8,128)(2,1)S(1)}, bf16[8,4,16,128]{3,2,1,0:T(8,128)(2,1)S(1)}, u32[]{:S(2)}, u32[]{:S(2)}) collective-permute-start(bf16[8,4,16,128]{3,2,1,0:T(8,128)(2,1)S(1)} %collect.1.refs_6_), channel_id=1, source_target_pairs={{0,3},{1,2},{2,1},{3,0},{4,7},{5,6},{6,5},{7,4},{8,11},{9,10},{10,... | collective-permute-start | bytes 393224 | tf_op jit(solution)/shard_map/ppermute | solution.py:358
  55.4 6.4 %collective-permute-start.12 = (bf16[8,4,16,128]{3,2,1,0:T(8,128)(2,1)S(1)}, bf16[8,4,16,128]{3,2,1,0:T(8,128)(2,1)S(1)}, u32[]{:S(2)}, u32[]{:S(2)}) collective-permute-start(bf16[8,4,16,128]{3,2,1,0:T(8,128)(2,1)S(1)} %collect.1.refs_6_), channel_id=1, source_target_pairs={{0,2},{1,3},{2,0},{3,1},{4,6},{5,7},{6,4},{7,5},{8,10},{9,11},{10,... | collective-permute-start | bytes 393224 | tf_op jit(solution)/shard_map/ppermute | solution.py:358
  55.6 6.2 %collective-permute-start.11 = (bf16[8,4,16,128]{3,2,1,0:T(8,128)(2,1)S(1)}, bf16[8,4,16,128]{3,2,1,0:T(8,128)(2,1)S(1)}, u32[]{:S(2)}, u32[]{:S(2)}) collective-permute-start(bf16[8,4,16,128]{3,2,1,0:T(8,128)(2,1)S(1)} %collect.1.refs_6_), channel_id=1, source_target_pairs={{0,1},{1,0},{2,3},{3,2},{4,5},{5,4},{6,7},{7,6},{8,9},{9,8},{10,11... | collective-permute-start | bytes 393224 | tf_op jit(solution)/shard_map/ppermute | solution.py:358
  61.7 11.7 %collective-permute-start.14 = (bf16[384,128]{1,0:T(8,128)(2,1)}, bf16[384,128]{1,0:T(8,128)(2,1)S(1)}, u32[]{:S(2)}, u32[]{:S(2)}) collective-permute-start(bf16[384,128]{1,0:T(8,128)(2,1)} %copy-done.8), channel_id=1, source_target_pairs={{0,4},{4,0},{8,12},{12,8},{16,20},{20,16},{24,28},{28,24},{1,5},{5... | collective-permute-start | bytes 294920 | tf_op jit(solution)/shard_map/ppermute | solution.py:358
  63.2 13.3 %collective-permute-start.15 = (bf16[384,128]{1,0:T(8,128)(2,1)}, bf16[384,128]{1,0:T(8,128)(2,1)S(1)}, u32[]{:S(2)}, u32[]{:S(2)}) collective-permute-start(bf16[384,128]{1,0:T(8,128)(2,1)} %copy-done.7), channel_id=1, source_target_pairs={{0,8},{4,12},{8,0},{12,4},{16,24},{20,28},{24,16},{28,20},{1,9},{5... | collective-permute-start | bytes 294920 | tf_op jit(solution)/shard_map/ppermute | solution.py:358
  67.1 20.0 %collective-permute-start.16 = (bf16[384,128]{1,0:T(8,128)(2,1)}, bf16[384,128]{1,0:T(8,128)(2,1)S(1)}, u32[]{:S(2)}, u32[]{:S(2)}) collective-permute-start(bf16[384,128]{1,0:T(8,128)(2,1)} %copy-done.6), channel_id=1, source_target_pairs={{0,12},{4,8},{8,4},{12,0},{16,28},{20,24},{24,20},{28,16},{1,13},{... | collective-permute-start | bytes 294920 | tf_op jit(solution)/shard_map/ppermute | solution.py:358
  67.2 19.9 %collective-permute-start.17 = (bf16[384,128]{1,0:T(8,128)(2,1)}, bf16[384,128]{1,0:T(8,128)(2,1)S(1)}, u32[]{:S(2)}, u32[]{:S(2)}) collective-permute-start(bf16[384,128]{1,0:T(8,128)(2,1)} %copy-done.5), channel_id=1, source_target_pairs={{0,16},{4,20},{8,24},{12,28},{16,0},{20,4},{24,8},{28,12},{1,17},{... | collective-permute-start | bytes 294920 | tf_op jit(solution)/shard_map/ppermute | solution.py:358
  72.1 14.9 %collective-permute-start.18 = (bf16[384,128]{1,0:T(8,128)(2,1)S(1)}, bf16[384,128]{1,0:T(8,128)(2,1)S(1)}, u32[]{:S(2)}, u32[]{:S(2)}) collective-permute-start(bf16[384,128]{1,0:T(8,128)(2,1)S(1)} %get-tuple-element.90), channel_id=1, source_target_pairs={{0,20},{4,16},{8,28},{12,24},{16,4},{20,0},{24,12},{28,8},{1,21},{... | collective-permute-start | bytes 294920 | tf_op jit(solution)/shard_map/ppermute | solution.py:358
  73.4 13.6 %collective-permute-start.19 = (bf16[384,128]{1,0:T(8,128)(2,1)S(1)}, bf16[384,128]{1,0:T(8,128)(2,1)S(1)}, u32[]{:S(2)}, u32[]{:S(2)}) collective-permute-start(bf16[384,128]{1,0:T(8,128)(2,1)S(1)} %get-tuple-element.92), channel_id=1, source_target_pairs={{0,24},{4,28},{8,16},{12,20},{16,8},{20,12},{24,0},{28,4},{1,25},{... | collective-permute-start | bytes 294920 | tf_op jit(solution)/shard_map/ppermute | solution.py:358
  76.5 10.5 %collective-permute-start.20 = (bf16[384,128]{1,0:T(8,128)(2,1)S(1)}, bf16[384,128]{1,0:T(8,128)(2,1)S(1)}, u32[]{:S(2)}, u32[]{:S(2)}) collective-permute-start(bf16[384,128]{1,0:T(8,128)(2,1)S(1)} %get-tuple-element.94), channel_id=1, source_target_pairs={{0,28},{4,24},{8,20},{12,16},{16,12},{20,8},{24,4},{28,0},{1,29},{... | collective-permute-start | bytes 294920 | tf_op jit(solution)/shard_map/ppermute | solution.py:358

commit v6 on v5

--- a/solution.py
+++ b/solution.py
@@ -296,7 +296,7 @@
 
         lax.fori_loop(0, BINS // pack, one, 0, unroll=8 // pack)
 
-    rows = 2
+    rows = 4
     for q in range(0, group, rows):
         lefts = []
         for u in range(rows):
@@ -383,9 +383,9 @@
     lates = gather(picked)
     for i, m in enumerate(order):
         near[m] = swap(after(near[m], lates[1:] if i >= len(order) - 2 else []), "wide", m)
-    firsts = gather(collect(near, 2 * nv))
-    for m in order:
-        far[m] = swap(after(far[m], firsts[1:]), "wide", m)
+    for i, m in enumerate(order):
+        far[m] = swap(after(far[m], [near[order[min(i + 2, nwide - 2)]]]), "wide", m)
+    firsts = gather(after(collect(near, 2 * nv), [far[n] for n in order[:2]]))
     table = sources(lates, firsts, me, place, wins, nv)
     lag = jnp.asarray(lag_table())
     out, start = None, 0

time: 96.3 us -> 94.5 us (0.981)
  waiting for transfers between devices: 13.1 us -> 9.69 us
  starting transfers between devices: 46 us -> 47.6 us
    ppermute x20, waiting for transfers between devices: 13.1 us -> 9.68 us  [swap(): lax.ppermute(value, axis, [(i, i ^ mask) for i in range(lax.axis_size(axi...]
    ppermute x20, starting transfers between devices: 36.2 us -> 37.8 us  [swap(): lax.ppermute(value, axis, [(i, i ^ mask) for i in range(lax.axis_size(axi...]
  transfers between devices with their start and end apart: 22 -> 22, of which waited for: 5 -> 4; matrix products, arithmetic and copies ran while one was open for 1% -> 1% of each run, Pallas kernels for 18% -> 18%
where the time goes in v6:
time: 94.5 us; the launch traced here: 94.1 us
  starting transfers between devices  47.6 us (50%)
  Pallas kernels  26.2 us (28%)
  local copies, waits for them, and re-layouts  9.85 us (10%)
  waiting for transfers between devices  9.69 us (10%)
    ppermute x20, starting transfers between devices, swap(): lax.ppermute(value, axis, [(i, i ^ mask) for i in range(lax.axis_size(axi...  37.8 us
    pallas_call x2, Pallas kernels, stack(): pl.pallas_call(lambda *refs: stack_kernel(nw, wins, size, group, *refs),...  17.7 us
    ppermute x20, waiting for transfers between devices, swap(): lax.ppermute(value, axis, [(i, i ^ mask) for i in range(lax.axis_size(axi...  9.68 us
    unnamed x19, local copies, waits for them, and re-layouts  8.78 us
    pallas_call x1, Pallas kernels, spectra(): pl.pallas_call(lambda *refs: spectra_kernel(sizes, *refs), in_specs=[smem...  5.25 us
    all_to_all x1, starting transfers between devices, on_device(): lax.all_to_all(picked, 'wide', split_axis=0, concat_axis=0, tiled=True)  4.98 us
    ppermute x1, starting transfers between devices, on_device(): lax.ppermute(records[:, :, time - HALF:], 'wide', [(i, i + 1) for i in ra...  4.88 us
    pallas_call x1, Pallas kernels, early(): pl.pallas_call(early_kernel, in_specs=[smem, vmem, vmem, vmem], out_specs...  1.92 us
  transfers between devices with their start and end apart: 22, of which 4 were waited for; matrix products, arithmetic and copies ran while one was open for 1% of the time, Pallas kernels for 18%

profile of v6, /device:TPU:0, one launch (start us, length us, event | category | flops | bytes accessed | tf_op | source)
XLA Modules:
  0.0 94.1 jit_solution(5921810671136789185)
XLA Ops:
  0.0 1.1 %slice.3 = bf16[8,128,256]{2,1,0:T(8,128)(2,1)S(1)} slice(bf16[8,128,1536]{2,1,0:T(8,128)(2,1)} %refs_2_.1), slice={[0:8], [0:128], [1280:1536]} | slice | bytes 1048576 | tf_op jit(solution)/shard_map/slice | solution.py:373
  1.1 4.9 %collective-permute-start = (bf16[8,128,256]{2,1,0:T(8,128)(2,1)S(1)}, bf16[8,128,256]{2,1,0:T(8,128)(2,1)S(1)}, u32[]{:S(2)}, u32[]{:S(2)}) collective-permute-start(bf16[8,128,256]{2,1,0:T(8,128)(2,1)S(1)} %slice.3), channel_id=1, source_target_pairs={{0,4},{4,8},{8,12},{12,16},{16,20},{20,24},{24,28},{1,5},{5,9},{9,... | collective-permute-start | bytes 1572872 | tf_op jit(solution)/shard_map/ppermute | solution.py:373
  6.0 0.8 copy.8.pairs_ref.refs_0_
  6.7 1.9 %copy-done = bf16[8,128,1536]{2,1,0:T(8,128)(2,1)S(1)} copy-done((bf16[8,128,1536]{2,1,0:T(8,128)(2,1)S(1)}, bf16[8,128,1536]{2,1,0:T(8,128)(2,1)}, u32[]{:S(2)}) %copy-start) | copy-done | bytes 3145752
  8.6 1.0 %copy-done.3 = f32[512,256]{1,0:T(8,128)S(1)} copy-done((f32[512,256]{1,0:T(8,128)S(1)}, f32[512,256]{1,0:T(8,128)}, u32[]{:S(2)}) %copy-start.3) | copy-done | bytes 524312
  9.7 0.7 copy-done.4
  10.3 1.9 %early.1 = (bf16[8,4,32,128]{3,2,1,0:T(8,128)(2,1)}, bf16[512,256]{1,0:T(8,128)(2,1)S(1)}, bf16[512,256]{1,0:T(8,128)(2,1)S(1)}) custom-call(s32[8,4]{1,0:T(8,128)S(1)} %copy.8.pairs_ref.refs_0_, bf16[8,128,1536]{2,1,0:T(8,128)(2,1)S(1)} %copy-done, f32[1,201]{1,0:T(1,128)S(1)} %bitcast.6, f32[512,256]{1,0:T(8,128)S(1)} %copy-done.3), custom_call_target="tpu_custom_call" | custom-call | flops 400000000 | bytes 3145728 | tf_op jit(solution)/shard_map/early/pallas_call | solution.py:98
  12.3 5.0 %all-to-all-start = ((bf16[8,4,32,128]{3,2,1,0:T(8,128)(2,1)}), bf16[8,4,32,128]{3,2,1,0:T(8,128)(2,1)S(1)}, u32[]{:S(2)}, u32[]{:S(2)}) async-start(bf16[8,4,32,128]{3,2,1,0:T(8,128)(2,1)} %get-tuple-element.51), calls=%async_computation | async-start | bytes 524288 | tf_op jit(solution)/shard_map/all_to_all | solution.py:375
  17.3 1.9 %copy-done.1 = bf16[8,128,1536]{2,1,0:T(8,128)(2,1)S(1)} copy-done((bf16[8,128,1536]{2,1,0:T(8,128)(2,1)S(1)}, bf16[8,128,1536]{2,1,0:T(8,128)(2,1)}, u32[]{:S(2)}) %copy-start.1) | copy-done | bytes 3145752
  19.1 5.2 %spectra.1 = (bf16[448,128]{1,0:T(8,128)(2,1)S(1)}, bf16[448,128]{1,0:T(8,128)(2,1)S(1)}, bf16[448,128]{1,0:T(8,128)(2,1)S(1)}, bf16[448,128]{1,0:T(8,128)(2,1)S...) custom-call(s32[8,4]{1,0:T(8,128)S(1)} %copy.8.pairs_ref.refs_0_, ...), custom_call_target="tpu_custom_call" | custom-call | flops 2415919104 | bytes 4718592 | tf_op jit(solution)/shard_map/spectra/pallas_call | solution.py:155
  25.0 0.6 copy-done.6
  27.3 1.2 %collective-permute-start.2 = (bf16[8,4,32,128]{3,2,1,0:T(8,128)(2,1)S(1)}, bf16[8,4,32,128]{3,2,1,0:T(8,128)(2,1)S(1)}, u32[]{:S(2)}, u32[]{:S(2)}) collective-permute-start(bf16[8,4,32,128]{3,2,1,0:T(8,128)(2,1)S(1)} %all-to-all-done.refs_2_), channel_id=1, source_target_pairs={{0,2},{1,3},{2,0},{3,1},{4,6},{5,7},{6,4},{7,5},{8,10},{9,11},{10,... | collective-permute-start | bytes 786440 | tf_op jit(solution)/shard_map/ppermute | solution.py:358
  28.8 4.3 %collective-permute-start.12 = (bf16[448,128]{1,0:T(8,128)(2,1)S(1)}, bf16[448,128]{1,0:T(8,128)(2,1)S(1)}, u32[]{:S(2)}, u32[]{:S(2)}) collective-permute-start(bf16[448,128]{1,0:T(8,128)(2,1)S(1)} %get-tuple-element.88), channel_id=1, source_target_pairs={{0,16},{4,20},{8,24},{12,28},{16,0},{20,4},{24,8},{28,12},{1,17},{... | collective-permute-start | bytes 344072 | tf_op jit(solution)/shard_map/ppermute | solution.py:358
  33.5 2.0 %collective-permute-done.3.refs_5_ = bf16[8,4,32,128]{3,2,1,0:T(8,128)(2,1)S(1)} collective-permute-done((bf16[8,4,32,128]{3,2,1,0:T(8,128)(2,1)S(1)}, bf16[8,4,32,128]{3,2,1,0:T(8,128)(2,1)S(1)}, u32[]{:S(2)}, u32[]{:S(2)}) %collective-permute-start.3) | collective-permute-done | bytes 262176 | tf_op jit(solution)/shard_map/ppermute | solution.py:358
  35.5 3.4 %collective-permute-start.10 = (bf16[448,128]{1,0:T(8,128)(2,1)S(1)}, bf16[448,128]{1,0:T(8,128)(2,1)S(1)}, u32[]{:S(2)}, u32[]{:S(2)}) collective-permute-start(bf16[448,128]{1,0:T(8,128)(2,1)S(1)} %get-tuple-element.85), channel_id=1, source_target_pairs={{0,12},{4,8},{8,4},{12,0},{16,28},{20,24},{24,20},{28,16},{1,13},{... | collective-permute-start | bytes 344072 | tf_op jit(solution)/shard_map/ppermute | solution.py:358
  38.8 2.3 %collective-permute-done.2.refs_4_ = bf16[8,4,32,128]{3,2,1,0:T(8,128)(2,1)S(1)} collective-permute-done((bf16[8,4,32,128]{3,2,1,0:T(8,128)(2,1)S(1)}, bf16[8,4,32,128]{3,2,1,0:T(8,128)(2,1)S(1)}, u32[]{:S(2)}, u32[]{:S(2)}) %collective-permute-start.2) | collective-permute-done | bytes 262176 | tf_op jit(solution)/shard_map/ppermute | solution.py:358
  41.2 5.3 %collective-permute-start.16 = (bf16[448,128]{1,0:T(8,128)(2,1)S(1)}, bf16[448,128]{1,0:T(8,128)(2,1)S(1)}, u32[]{:S(2)}, u32[]{:S(2)}) collective-permute-start(bf16[448,128]{1,0:T(8,128)(2,1)S(1)} %get-tuple-element.94), channel_id=1, source_target_pairs={{0,24},{4,28},{8,16},{12,20},{16,8},{20,12},{24,0},{28,4},{1,25},{... | collective-permute-start | bytes 344072 | tf_op jit(solution)/shard_map/ppermute | solution.py:358
  46.5 0.9 collective-permute-start.17
  47.4 0.6 collective-permute-start.4
  48.0 3.8 %collective-permute-start.13 = (bf16[384,128]{1,0:T(8,128)(2,1)}, bf16[384,128]{1,0:T(8,128)(2,1)S(1)}, u32[]{:S(2)}, u32[]{:S(2)}) collective-permute-start(bf16[384,128]{1,0:T(8,128)(2,1)} %copy-done.8), channel_id=1, source_target_pairs={{0,24},{4,28},{8,16},{12,20},{16,8},{20,12},{24,0},{28,4},{1,25},{... | collective-permute-start | bytes 294920 | tf_op jit(solution)/shard_map/ppermute | solution.py:358
  51.9 3.5 %collective-permute-start.15 = (bf16[384,128]{1,0:T(8,128)(2,1)}, bf16[384,128]{1,0:T(8,128)(2,1)S(1)}, u32[]{:S(2)}, u32[]{:S(2)}) collective-permute-start(bf16[384,128]{1,0:T(8,128)(2,1)} %copy-done.7), channel_id=1, source_target_pairs={{0,28},{4,24},{8,20},{12,16},{16,12},{20,8},{24,4},{28,0},{1,29},{... | collective-permute-start | bytes 294920 | tf_op jit(solution)/shard_map/ppermute | solution.py:358
  55.4 4.3 %collective-permute-done.13.refs_8_ = bf16[384,128]{1,0:T(8,128)(2,1)S(1)} collective-permute-done((bf16[384,128]{1,0:T(8,128)(2,1)}, bf16[384,128]{1,0:T(8,128)(2,1)S(1)}, u32[]{:S(2)}, u32[]{:S(2)}) %collective-permute-start.13) | collective-permute-done | bytes 98336 | tf_op jit(solution)/shard_map/ppermute | solution.py:358
  59.7 1.1 %collective-permute-done.15.refs_9_ = bf16[384,128]{1,0:T(8,128)(2,1)S(1)} collective-permute-done((bf16[384,128]{1,0:T(8,128)(2,1)}, bf16[384,128]{1,0:T(8,128)(2,1)S(1)}, u32[]{:S(2)}, u32[]{:S(2)}) %collective-permute-start.15) | collective-permute-done | bytes 98336 | tf_op jit(solution)/shard_map/ppermute | solution.py:358
  60.9 0.7 collective-permute-start.19
  61.6 1.0 %collective-permute-start.18 = (bf16[8,4,16,128]{3,2,1,0:T(8,128)(2,1)S(1)}, bf16[8,4,16,128]{3,2,1,0:T(8,128)(2,1)S(1)}, u32[]{:S(2)}, u32[]{:S(2)}) collective-permute-start(bf16[8,4,16,128]{3,2,1,0:T(8,128)(2,1)S(1)} %collect.1.refs_6_), channel_id=1, source_target_pairs={{0,1},{1,0},{2,3},{3,2},{4,5},{5,4},{6,7},{7,6},{8,9},{9,8},{10,11... | collective-permute-start | bytes 393224 | tf_op jit(solution)/shard_map/ppermute | solution.py:358
  63.2 6.6 %collective-permute-start.11 = (bf16[384,128]{1,0:T(8,128)(2,1)}, bf16[384,128]{1,0:T(8,128)(2,1)S(1)}, u32[]{:S(2)}, u32[]{:S(2)}) collective-permute-start(bf16[384,128]{1,0:T(8,128)(2,1)} %copy-done.6), channel_id=1, source_target_pairs={{0,20},{4,16},{8,28},{12,24},{16,4},{20,0},{24,12},{28,8},{1,21},{... | collective-permute-start | bytes 294920 | tf_op jit(solution)/shard_map/ppermute | solution.py:358
  70.5 0.7 collective-permute-start.6
  71.2 2.5 %collective-permute-start.7 = (bf16[384,128]{1,0:T(8,128)(2,1)S(1)}, bf16[384,128]{1,0:T(8,128)(2,1)S(1)}, u32[]{:S(2)}, u32[]{:S(2)}) collective-permute-start(bf16[384,128]{1,0:T(8,128)(2,1)S(1)} %get-tuple-element.79), channel_id=1, source_target_pairs={{0,12},{4,8},{8,4},{12,0},{16,28},{20,24},{24,20},{28,16},{1,13},{... | collective-permute-start | bytes 294920 | tf_op jit(solution)/shard_map/ppermute | solution.py:358
  73.7 1.3 %collective-permute-start.9 = (bf16[384,128]{1,0:T(8,128)(2,1)S(1)}, bf16[384,128]{1,0:T(8,128)(2,1)S(1)}, u32[]{:S(2)}, u32[]{:S(2)}) collective-permute-start(bf16[384,128]{1,0:T(8,128)(2,1)S(1)} %get-tuple-element.83), channel_id=1, source_target_pairs={{0,16},{4,20},{8,24},{12,28},{16,0},{20,4},{24,8},{28,12},{1,17},{... | collective-permute-start | bytes 294920 | tf_op jit(solution)/shard_map/ppermute | solution.py:358
  75.0 1.3 %sources.1 = bf16[128,48,256]{2,1,0:T(8,128)(2,1)S(1)} custom-call(s32[1]{0:T(128)} %bitcast.refs_1_.refs_0_, s32[1]{0:T(128)} %bitcast.2.refs_1_, bf16[8,4,32,128]{3,2,1,0:T(8,128)(2,1)S(1)} %all-to-all-done.refs_2_, bf16[8,4,32,128]{3,2,1,0:T(8,128)(2,1)S(1)} %collective-permute-done.1.refs_3_, bf16[8,4,32,128]{3,2,1,0:T(8,128)(2,1)S(1)} %collective-permute-done.2.refs_4_, ...), custom_call_target="tpu_custom_call" | custom-call | flops 100000000 | bytes 4194304 | tf_op jit(solution)/shard_map/sources/pallas_call | solution.py:230
  76.4 8.8 %stack.2.refs_12_ = bf16[1,4,128,32,256]{4,3,2,1,0:T(8,128)(2,1)} custom-call(s32[1]{0:T(128)S(6)} %copy.11.refs_0_, s32[1]{0:T(128)} %bitcast.refs_1_.refs_0_, bf16[448,128]{1,0:T(8,128)(2,1)S(1)} %get-tuple-element.93.refs_0_.refs_2_, bf16[448,128]{1,0:T(8,128)(2,1)S(1)} %collective-permute-done.4.refs_1_.refs_3_, ...), custom_call_target="tpu_custom_call" | custom-call | flops 2147483648 | bytes 7340032 | tf_op jit(solution)/shard_map/stack/pallas_call | solution.py:331
  85.2 8.8 %stack.3 = bf16[1,4,128,32,256]{4,3,2,1,0:T(8,128)(2,1)} custom-call(s32[1]{0:T(128)S(6)} %copy.11.refs_0_, s32[1]{0:T(128)} %bitcast.refs_1_.refs_0_, bf16[384,128]{1,0:T(8,128)(2,1)S(1)} %get-tuple-element.70.refs_2_, bf16[384,128]{1,0:T(8,128)(2,1)S(1)} %collective-permute-done.5.refs_3_, ...), custom_call_target="tpu_custom_call", output_to_operand_aliasing={{}: (12, {})} | custom-call | flops 2147483648 | bytes 7340032 | tf_op jit(solution)/shard_map/stack/pallas_call | solution.py:331
  (38 shorter events, 3.8 us)
Async XLA Ops:
  1.1 16.2 %collective-permute-start = (bf16[8,128,256]{2,1,0:T(8,128)(2,1)S(1)}, bf16[8,128,256]{2,1,0:T(8,128)(2,1)S(1)}, u32[]{:S(2)}, u32[]{:S(2)}) collective-permute-start(bf16[8,128,256]{2,1,0:T(8,128)(2,1)S(1)} %slice.3), channel_id=1, source_target_pairs={{0,4},{4,8},{8,12},{12,16},{16,20},{20,24},{24,28},{1,5},{5,9},{9,... | collective-permute-start | bytes 1572872 | tf_op jit(solution)/shard_map/ppermute | solution.py:373
  6.7 1.9 %copy-start = (bf16[8,128,1536]{2,1,0:T(8,128)(2,1)S(1)}, bf16[8,128,1536]{2,1,0:T(8,128)(2,1)}, u32[]{:S(2)}) copy-start(bf16[8,128,1536]{2,1,0:T(8,128)(2,1)} %refs_2_.1) | copy-start | bytes 9437188
  8.6 1.0 %copy-start.3 = (f32[512,256]{1,0:T(8,128)S(1)}, f32[512,256]{1,0:T(8,128)}, u32[]{:S(2)}) copy-start(f32[512,256]{1,0:T(8,128)} %constant.13.clone.table_ref) | copy-start | bytes 1572868
  9.7 0.7 copy-start.4
  12.3 64.1 %copy-start.2 = (f32[256,256]{1,0:T(8,128)S(1)}, f32[256,256]{1,0:T(8,128)}, u32[]{:S(2)}) copy-start(f32[256,256]{1,0:T(8,128)} %constant.14.clone.refs_11_) | copy-start | bytes 786436
  12.3 14.7 %all-to-all-start = ((bf16[8,4,32,128]{3,2,1,0:T(8,128)(2,1)}), bf16[8,4,32,128]{3,2,1,0:T(8,128)(2,1)S(1)}, u32[]{:S(2)}, u32[]{:S(2)}) async-start(bf16[8,4,32,128]{3,2,1,0:T(8,128)(2,1)} %get-tuple-element.51), calls=%async_computation | async-start | bytes 524288 | tf_op jit(solution)/shard_map/all_to_all | solution.py:375
  17.2 1.9 %copy-start.1 = (bf16[8,128,1536]{2,1,0:T(8,128)(2,1)S(1)}, bf16[8,128,1536]{2,1,0:T(8,128)(2,1)}, u32[]{:S(2)}) copy-start(bf16[8,128,1536]{2,1,0:T(8,128)(2,1)} %refs_2_.1) | copy-start | bytes 9437188
  24.4 0.6 copy-start.5
  25.0 0.6 copy-start.6
  25.7 0.6 copy-start.7
  26.3 0.6 copy-start.8
  26.9 8.5 %collective-permute-start.3 = (bf16[8,4,32,128]{3,2,1,0:T(8,128)(2,1)S(1)}, bf16[8,4,32,128]{3,2,1,0:T(8,128)(2,1)S(1)}, u32[]{:S(2)}, u32[]{:S(2)}) collective-permute-start(bf16[8,4,32,128]{3,2,1,0:T(8,128)(2,1)S(1)} %all-to-all-done.refs_2_), channel_id=1, source_target_pairs={{0,3},{1,2},{2,1},{3,0},{4,7},{5,6},{6,5},{7,4},{8,11},{9,10},{10,... | collective-permute-start | bytes 786440 | tf_op jit(solution)/shard_map/ppermute | solution.py:358
  27.3 13.8 %collective-permute-start.2 = (bf16[8,4,32,128]{3,2,1,0:T(8,128)(2,1)S(1)}, bf16[8,4,32,128]{3,2,1,0:T(8,128)(2,1)S(1)}, u32[]{:S(2)}, u32[]{:S(2)}) collective-permute-start(bf16[8,4,32,128]{3,2,1,0:T(8,128)(2,1)S(1)} %all-to-all-done.refs_2_), channel_id=1, source_target_pairs={{0,2},{1,3},{2,0},{3,1},{4,6},{5,7},{6,4},{7,5},{8,10},{9,11},{10,... | collective-permute-start | bytes 786440 | tf_op jit(solution)/shard_map/ppermute | solution.py:358
  28.5 18.0 %collective-permute-start.1 = (bf16[8,4,32,128]{3,2,1,0:T(8,128)(2,1)S(1)}, bf16[8,4,32,128]{3,2,1,0:T(8,128)(2,1)S(1)}, u32[]{:S(2)}, u32[]{:S(2)}) collective-permute-start(bf16[8,4,32,128]{3,2,1,0:T(8,128)(2,1)S(1)} %all-to-all-done.refs_2_), channel_id=1, source_target_pairs={{0,1},{1,0},{2,3},{3,2},{4,5},{5,4},{6,7},{7,6},{8,9},{9,8},{10,11... | collective-permute-start | bytes 786440 | tf_op jit(solution)/shard_map/ppermute | solution.py:358
  28.8 18.6 %collective-permute-start.12 = (bf16[448,128]{1,0:T(8,128)(2,1)S(1)}, bf16[448,128]{1,0:T(8,128)(2,1)S(1)}, u32[]{:S(2)}, u32[]{:S(2)}) collective-permute-start(bf16[448,128]{1,0:T(8,128)(2,1)S(1)} %get-tuple-element.88), channel_id=1, source_target_pairs={{0,16},{4,20},{8,24},{12,28},{16,0},{20,4},{24,8},{28,12},{1,17},{... | collective-permute-start | bytes 344072 | tf_op jit(solution)/shard_map/ppermute | solution.py:358
  33.1 14.9 %collective-permute-start.14 = (bf16[448,128]{1,0:T(8,128)(2,1)S(1)}, bf16[448,128]{1,0:T(8,128)(2,1)S(1)}, u32[]{:S(2)}, u32[]{:S(2)}) collective-permute-start(bf16[448,128]{1,0:T(8,128)(2,1)S(1)} %get-tuple-element.91), channel_id=1, source_target_pairs={{0,20},{4,16},{8,28},{12,24},{16,4},{20,0},{24,12},{28,8},{1,21},{... | collective-permute-start | bytes 344072 | tf_op jit(solution)/shard_map/ppermute | solution.py:358
  35.5 12.6 %collective-permute-start.10 = (bf16[448,128]{1,0:T(8,128)(2,1)S(1)}, bf16[448,128]{1,0:T(8,128)(2,1)S(1)}, u32[]{:S(2)}, u32[]{:S(2)}) collective-permute-start(bf16[448,128]{1,0:T(8,128)(2,1)S(1)} %get-tuple-element.85), channel_id=1, source_target_pairs={{0,12},{4,8},{8,4},{12,0},{16,28},{20,24},{24,20},{28,16},{1,13},{... | collective-permute-start | bytes 344072 | tf_op jit(solution)/shard_map/ppermute | solution.py:358
  41.2 10.7 %collective-permute-start.16 = (bf16[448,128]{1,0:T(8,128)(2,1)S(1)}, bf16[448,128]{1,0:T(8,128)(2,1)S(1)}, u32[]{:S(2)}, u32[]{:S(2)}) collective-permute-start(bf16[448,128]{1,0:T(8,128)(2,1)S(1)} %get-tuple-element.94), channel_id=1, source_target_pairs={{0,24},{4,28},{8,16},{12,20},{16,8},{20,12},{24,0},{28,4},{1,25},{... | collective-permute-start | bytes 344072 | tf_op jit(solution)/shard_map/ppermute | solution.py:358
  46.5 8.9 %collective-permute-start.17 = (bf16[448,128]{1,0:T(8,128)(2,1)S(1)}, bf16[448,128]{1,0:T(8,128)(2,1)S(1)}, u32[]{:S(2)}, u32[]{:S(2)}) collective-permute-start(bf16[448,128]{1,0:T(8,128)(2,1)S(1)} %get-tuple-element.95), channel_id=1, source_target_pairs={{0,28},{4,24},{8,20},{12,16},{16,12},{20,8},{24,4},{28,0},{1,29},{... | collective-permute-start | bytes 344072 | tf_op jit(solution)/shard_map/ppermute | solution.py:358
  47.4 8.0 %collective-permute-start.4 = (bf16[448,128]{1,0:T(8,128)(2,1)S(1)}, bf16[448,128]{1,0:T(8,128)(2,1)S(1)}, u32[]{:S(2)}, u32[]{:S(2)}) collective-permute-start(bf16[448,128]{1,0:T(8,128)(2,1)S(1)} %get-tuple-element.74), channel_id=1, source_target_pairs={{0,4},{4,0},{8,12},{12,8},{16,20},{20,16},{24,28},{28,24},{1,5},{5... | collective-permute-start | bytes 344072 | tf_op jit(solution)/shard_map/ppermute | solution.py:358
  48.0 7.4 %collective-permute-start.8 = (bf16[448,128]{1,0:T(8,128)(2,1)S(1)}, bf16[448,128]{1,0:T(8,128)(2,1)S(1)}, u32[]{:S(2)}, u32[]{:S(2)}) collective-permute-start(bf16[448,128]{1,0:T(8,128)(2,1)S(1)} %get-tuple-element.82), channel_id=1, source_target_pairs={{0,8},{4,12},{8,0},{12,4},{16,24},{20,28},{24,16},{28,20},{1,9},{5... | collective-permute-start | bytes 344072 | tf_op jit(solution)/shard_map/ppermute | solution.py:358
  48.0 11.6 %collective-permute-start.13 = (bf16[384,128]{1,0:T(8,128)(2,1)}, bf16[384,128]{1,0:T(8,128)(2,1)S(1)}, u32[]{:S(2)}, u32[]{:S(2)}) collective-permute-start(bf16[384,128]{1,0:T(8,128)(2,1)} %copy-done.8), channel_id=1, source_target_pairs={{0,24},{4,28},{8,16},{12,20},{16,8},{20,12},{24,0},{28,4},{1,25},{... | collective-permute-start | bytes 294920 | tf_op jit(solution)/shard_map/ppermute | solution.py:358
  51.9 8.9 %collective-permute-start.15 = (bf16[384,128]{1,0:T(8,128)(2,1)}, bf16[384,128]{1,0:T(8,128)(2,1)S(1)}, u32[]{:S(2)}, u32[]{:S(2)}) collective-permute-start(bf16[384,128]{1,0:T(8,128)(2,1)} %copy-done.7), channel_id=1, source_target_pairs={{0,28},{4,24},{8,20},{12,16},{16,12},{20,8},{24,4},{28,0},{1,29},{... | collective-permute-start | bytes 294920 | tf_op jit(solution)/shard_map/ppermute | solution.py:358
  60.7 9.7 %collective-permute-start.20 = (bf16[8,4,16,128]{3,2,1,0:T(8,128)(2,1)S(1)}, bf16[8,4,16,128]{3,2,1,0:T(8,128)(2,1)S(1)}, u32[]{:S(2)}, u32[]{:S(2)}) collective-permute-start(bf16[8,4,16,128]{3,2,1,0:T(8,128)(2,1)S(1)} %collect.1.refs_6_), channel_id=1, source_target_pairs={{0,3},{1,2},{2,1},{3,0},{4,7},{5,6},{6,5},{7,4},{8,11},{9,10},{10,... | collective-permute-start | bytes 393224 | tf_op jit(solution)/shard_map/ppermute | solution.py:358
  60.9 10.3 %collective-permute-start.19 = (bf16[8,4,16,128]{3,2,1,0:T(8,128)(2,1)S(1)}, bf16[8,4,16,128]{3,2,1,0:T(8,128)(2,1)S(1)}, u32[]{:S(2)}, u32[]{:S(2)}) collective-permute-start(bf16[8,4,16,128]{3,2,1,0:T(8,128)(2,1)S(1)} %collect.1.refs_6_), channel_id=1, source_target_pairs={{0,2},{1,3},{2,0},{3,1},{4,6},{5,7},{6,4},{7,5},{8,10},{9,11},{10,... | collective-permute-start | bytes 393224 | tf_op jit(solution)/shard_map/ppermute | solution.py:358
  61.6 12.1 %collective-permute-start.18 = (bf16[8,4,16,128]{3,2,1,0:T(8,128)(2,1)S(1)}, bf16[8,4,16,128]{3,2,1,0:T(8,128)(2,1)S(1)}, u32[]{:S(2)}, u32[]{:S(2)}) collective-permute-start(bf16[8,4,16,128]{3,2,1,0:T(8,128)(2,1)S(1)} %collect.1.refs_6_), channel_id=1, source_target_pairs={{0,1},{1,0},{2,3},{3,2},{4,5},{5,4},{6,7},{7,6},{8,9},{9,8},{10,11... | collective-permute-start | bytes 393224 | tf_op jit(solution)/shard_map/ppermute | solution.py:358
  63.2 22.0 %collective-permute-start.11 = (bf16[384,128]{1,0:T(8,128)(2,1)}, bf16[384,128]{1,0:T(8,128)(2,1)S(1)}, u32[]{:S(2)}, u32[]{:S(2)}) collective-permute-start(bf16[384,128]{1,0:T(8,128)(2,1)} %copy-done.6), channel_id=1, source_target_pairs={{0,20},{4,16},{8,28},{12,24},{16,4},{20,0},{24,12},{28,8},{1,21},{... | collective-permute-start | bytes 294920 | tf_op jit(solution)/shard_map/ppermute | solution.py:358
  69.8 15.4 %collective-permute-start.5 = (bf16[384,128]{1,0:T(8,128)(2,1)}, bf16[384,128]{1,0:T(8,128)(2,1)S(1)}, u32[]{:S(2)}, u32[]{:S(2)}) collective-permute-start(bf16[384,128]{1,0:T(8,128)(2,1)} %copy-done.5), channel_id=1, source_target_pairs={{0,4},{4,0},{8,12},{12,8},{16,20},{20,16},{24,28},{28,24},{1,5},{5... | collective-permute-start | bytes 294920 | tf_op jit(solution)/shard_map/ppermute | solution.py:358
  70.5 14.8 %collective-permute-start.6 = (bf16[384,128]{1,0:T(8,128)(2,1)S(1)}, bf16[384,128]{1,0:T(8,128)(2,1)S(1)}, u32[]{:S(2)}, u32[]{:S(2)}) collective-permute-start(bf16[384,128]{1,0:T(8,128)(2,1)S(1)} %get-tuple-element.77), channel_id=1, source_target_pairs={{0,8},{4,12},{8,0},{12,4},{16,24},{20,28},{24,16},{28,20},{1,9},{5... | collective-permute-start | bytes 294920 | tf_op jit(solution)/shard_map/ppermute | solution.py:358
  71.2 14.0 %collective-permute-start.7 = (bf16[384,128]{1,0:T(8,128)(2,1)S(1)}, bf16[384,128]{1,0:T(8,128)(2,1)S(1)}, u32[]{:S(2)}, u32[]{:S(2)}) collective-permute-start(bf16[384,128]{1,0:T(8,128)(2,1)S(1)} %get-tuple-element.79), channel_id=1, source_target_pairs={{0,12},{4,8},{8,4},{12,0},{16,28},{20,24},{24,20},{28,16},{1,13},{... | collective-permute-start | bytes 294920 | tf_op jit(solution)/shard_map/ppermute | solution.py:358
  73.7 11.5 %collective-permute-start.9 = (bf16[384,128]{1,0:T(8,128)(2,1)S(1)}, bf16[384,128]{1,0:T(8,128)(2,1)S(1)}, u32[]{:S(2)}, u32[]{:S(2)}) collective-permute-start(bf16[384,128]{1,0:T(8,128)(2,1)S(1)} %get-tuple-element.83), channel_id=1, source_target_pairs={{0,16},{4,20},{8,24},{12,28},{16,0},{20,4},{24,8},{28,12},{1,17},{... | collective-permute-start | bytes 294920 | tf_op jit(solution)/shard_map/ppermute | solution.py:358

commit v7 on v3

--- a/solution.py
+++ b/solution.py
@@ -81,7 +81,7 @@
     return jnp.concatenate(parts, 0).astype(BF)
 
 
-def rows_kernel(rec_ref, rows_ref, near_ref, same_ref):
+def rows_kernel(rec_ref, rows_ref, near_ref):
     time = rec_ref.shape[2]
     rows = virtual_rows(rec_ref, rec_ref.shape[1] // VSTEP)
     rows_ref[...] = rows
@@ -95,21 +95,16 @@
     return pl.pallas_call(
         rows_kernel,
         in_specs=[vmem],
-        out_specs=[vmem] * 3,
-        out_shape=[
-            jax.ShapeDtypeStruct((count, time), BF),
-            jax.ShapeDtypeStruct((count, HALF), BF),
-            jax.ShapeDtypeStruct(records.shape, BF),
-        ],
-        input_output_aliases={0: 2},
-        compiler_params=pltpu.CompilerParams(vmem_limit_bytes=40 * MIB),
+        out_specs=[vmem] * 2,
+        out_shape=[jax.ShapeDtypeStruct((count, time), BF), jax.ShapeDtypeStruct((count, HALF), BF)],
+        compiler_params=pltpu.CompilerParams(vmem_limit_bytes=8 * MIB),
         cost_estimate=pl.CostEstimate(flops=0, bytes_accessed=records.size, transcendentals=0),
         name="extract",
     )(records)
 
 
-def virtual_kernel(nblk, pairs_ref, me_ref, rows_ref, halo_ref, taps_ref, table_ref, *refs):
-    picks, (toeplitz_ref, forward_ref, row, virt) = refs[:nblk], refs[nblk:]
+def virtual_kernel(nblk, pairs_ref, rows_ref, halo_ref, taps_ref, table_ref, *refs):
+    picked_ref, toeplitz_ref, forward_ref, row, virt = refs
     count, time = rows_ref.shape
     nv, wins = count // nblk, time // WLEN
     build_toeplitz(taps_ref, row, toeplitz_ref)
@@ -118,27 +113,29 @@
     result = transform([block], wins, count, toeplitz_ref[...], forward_ref[...])
     for b in range(nblk):
         virt[b] = block_rows(result, b, nv, wins, count)
-    for m in range(nblk):
+    for r in range(nblk):
         for k in range(SLOTS):
-            picks[m][k] = virt[pairs_ref[me_ref[0] ^ m, k]]
-
-
-def virtual(rows, halo, taps, pairs, me, nblk):
+            picked_ref[r, k] = virt[pairs_ref[r, k]]
+
+
+def virtual(rows, halo, taps, pairs, nblk):
     count, time = rows.shape
     size = (time // WLEN) * 2 * (count // nblk)
     smem, vmem = pl.BlockSpec(memory_space=pltpu.SMEM), pl.BlockSpec(memory_space=pltpu.VMEM)
-    outs = pl.pallas_call(
+    return pl.pallas_call(
         lambda *refs: virtual_kernel(nblk, *refs),
-        in_specs=[smem, smem] + [vmem] * 4,
-        out_specs=[vmem] * (nblk + 2),
-        out_shape=[jax.ShapeDtypeStruct((SLOTS, size, BINS), BF)] * nblk
-        + [jax.ShapeDtypeStruct((WLEN, HALF), BF), jax.ShapeDtypeStruct((WLEN, 2 * BINS), BF)],
+        in_specs=[smem] + [vmem] * 4,
+        out_specs=[vmem] * 3,
+        out_shape=[
+            jax.ShapeDtypeStruct((nblk, SLOTS, size, BINS), BF),
+            jax.ShapeDtypeStruct((WLEN, HALF), BF),
+            jax.ShapeDtypeStruct((WLEN, 2 * BINS), BF),
+        ],
         scratch_shapes=[pltpu.VMEM((8, 512), F32), pltpu.VMEM((nblk, size, BINS), BF)],
-        compiler_params=pltpu.CompilerParams(vmem_limit_bytes=40 * MIB),
+        compiler_params=pltpu.CompilerParams(vmem_limit_bytes=16 * MIB),
         cost_estimate=pl.CostEstimate(flops=10**8, bytes_accessed=rows.size * 8, transcendentals=0),
         name="virtual",
-    )(pairs, me, rows, halo, taps, jnp.asarray(dft_table()))
-    return list(outs[:nblk]), outs[nblk], outs[nblk + 1]
+    )(pairs, rows, halo, taps, jnp.asarray(dft_table()))
 
 
 def spectra_kernel(sizes, me_ref, rec_ref, halo_ref, toeplitz_ref, forward_ref, *refs):
@@ -172,7 +169,7 @@
         in_specs=[smem] + [vmem] * 4,
         out_specs=[vmem] * len(shapes),
         out_shape=[jax.ShapeDtypeStruct(shape, BF) for shape in shapes],
-        compiler_params=pltpu.CompilerParams(vmem_limit_bytes=40 * MIB),
+        compiler_params=pltpu.CompilerParams(vmem_limit_bytes=16 * MIB),
         cost_estimate=pl.CostEstimate(
             flops=nblk * chans * wins * 3 * 2 * 512 * 256, bytes_accessed=nblk * chans * time * 3, transcendentals=0
         ),
@@ -181,20 +178,20 @@
     return [list(outs[i : i + nblk]) for i in range(0, len(outs), nblk)]
 
 
-def sources_kernel(nsrc, nnar, wins, nv, me_ref, place_ref, *refs):
+def sources_kernel(nsrc, nnar, wins, nv, place_ref, *refs):
     virts, out_ref, held, turned = refs[:nnar], refs[nnar], refs[nnar + 1], refs[nnar + 2]
     nw = nsrc * wins
     pitch = BINS + 8
     for n in range(nnar):
         held[place_ref[0] ^ n] = virts[n][...]
 
-    def turn(m, carry):
-        tiles = [[held[n, m, k].astype(F32) for n in range(nnar)] for k in range(SLOTS)]
+    def turn(src, carry):
+        tiles = [[held[n, src, k].astype(F32) for n in range(nnar)] for k in range(SLOTS)]
         for w in range(wins):
             for p in range(2):
                 at = (w * 2 + p) * nv
                 tile = jnp.concatenate([tiles[k][n][at : at + nv] for k in range(SLOTS) for n in range(nnar)], 0)
-                row = pl.multiple_of((p * nw + (me_ref[0] ^ m) * wins + w) * pitch, 8)
+                row = pl.multiple_of((p * nw + src * wins + w) * pitch, 8)
                 turned[pl.ds(row, BINS), :] = tile.T
         return carry
 
@@ -211,24 +208,24 @@
     lax.fori_loop(0, BINS, one, 0, unroll=8)
 
 
-def sources(virts, me, place, wins, nv):
+def sources(virts, place, wins, nv):
     nnar, nsrc = len(virts), virts[0].shape[0]
     nw = nsrc * wins
     width = SLOTS * nnar * nv
     smem, vmem = pl.BlockSpec(memory_space=pltpu.SMEM), pl.BlockSpec(memory_space=pltpu.VMEM)
     return pl.pallas_call(
         lambda *refs: sources_kernel(nsrc, nnar, wins, nv, *refs),
-        in_specs=[smem, smem] + [vmem] * nnar,
+        in_specs=[smem] + [vmem] * nnar,
         out_specs=vmem,
         out_shape=jax.ShapeDtypeStruct((BINS, 2 * nw, 2 * width), BF),
         scratch_shapes=[
             pltpu.VMEM((nnar,) + virts[0].shape, BF),
             pltpu.VMEM((2 * nw * (BINS + 8), width), F32),
         ],
-        compiler_params=pltpu.CompilerParams(vmem_limit_bytes=40 * MIB),
+        compiler_params=pltpu.CompilerParams(vmem_limit_bytes=(10 + 2 * nw * BINS * width * 6 // MIB) * MIB),
         cost_estimate=pl.CostEstimate(flops=10**8, bytes_accessed=8 * nnar * virts[0].size, transcendentals=0),
         name="sources",
-    )(me, place, *virts)
+    )(place, *virts)
 
 
 def stack_kernel(nw, wins, size, group, count_ref, me_ref, *refs):
@@ -332,7 +329,7 @@
         ),
         out_shape=jax.ShapeDtypeStruct(shape, BF),
         input_output_aliases=aliases,
-        compiler_params=pltpu.CompilerParams(vmem_limit_bytes=36 * MIB),
+        compiler_params=pltpu.CompilerParams(vmem_limit_bytes=(20 + table.size * 4 // MIB) * MIB),
         cost_estimate=pl.CostEstimate(
             flops=size * 128 * 256 * 256 * 4, bytes_accessed=2 * (table.size + size * 32768), transcendentals=0
         ),
@@ -358,30 +355,31 @@
     place = lax.axis_index("narrow").astype(jnp.int32)[None]
     ahead = [(i, i + 1) for i in range(nwide - 1)]
     order = list(range(nwide - 1, 0, -1))
-    rows, tip, records = extract(records)
+    rows, tip = extract(records)
     tip = lax.ppermute(tip, "wide", ahead)
     halo = lax.ppermute(after(records[:, :, time - HALF :], [tip]), "wide", ahead)
-    picked, toeplitz, forward = virtual(rows, tip, taps[None], pair_sources, me, nblk)
-    for m in order:
-        picked[m] = swap(picked[m], "wide", m)
+    picked, toeplitz, forward = virtual(rows, tip, taps[None], pair_sources, nblk)
+    picked = lax.all_to_all(picked, "wide", split_axis=0, concat_axis=0, tiled=True)
+    chunks = spectra(records, halo, toeplitz, forward, me, (half, half))
+    picked, (near, far) = lax.optimization_barrier((picked, chunks))
 
     top = nnar // 2
-    picked = jnp.stack(picked)
     slots = {0: picked, **{n: swap(picked, "narrow", n) for n in (top, 1) if n}}
-    near, far = spectra(records, halo, toeplitz, forward, me, (half, half))
     for i, m in enumerate(order):
-        if i == len(order) - 1:
-            bit = top
-            while bit:
-                for n in sorted(slots):
-                    if n ^ bit not in slots:
-                        slots[n ^ bit] = swap(after(slots[n], [near[order[1]]]), "narrow", bit)
-                bit //= 2
-        waits = [slots[n] for n in sorted(slots) if n] if i >= len(order) - 2 else []
+        waits = []
+        if i == len(order) - 2:
+            waits = [slots[n] for n in sorted(slots) if n]
         near[m] = swap(after(near[m], waits), "wide", m)
+    bit = top
+    while bit:
+        for n in sorted(slots):
+            if n ^ bit not in slots:
+                slots[n ^ bit] = swap(after(slots[n], [near[m] for m in order[:3]]), "narrow", bit)
+        bit //= 2
     for i, m in enumerate(order):
-        far[m] = swap(after(far[m], [near[order[min(i + 2, nwide - 2)]]]), "wide", m)
-    table = sources([slots[n] for n in range(nnar)], me, place, wins, nv)
+        waits = [near[order[min(i + 2, nwide - 2)]]] + ([slots[n] for n in sorted(slots) if n] if i >= 2 else [])
+        far[m] = swap(after(far[m], waits), "wide", m)
+    table = sources([slots[n] for n in range(nnar)], place, wins, nv)
     lag = jnp.asarray(lag_table())
     out = stack(near, table, pair_counts, me, lag, None, 0, half, wins, chans)
     return stack(far, table, pair_counts, me, lag, out, half, half, wins, chans)

time: 109 us -> 94 us (0.86)
  waiting for transfers between devices: 24.6 us -> 11.8 us
  local copies, waits for them, and re-layouts: 9.31 us -> 7.34 us
    ppermute x24 -> x17, waiting for transfers between devices: 23.2 us -> 8.25 us  [swap(): lax.ppermute(value, axis, [(i, i ^ mask) for i in range(lax.axis_size(axi...]
    ppermute x24 -> x17, starting transfers between devices: 38.6 us -> 32.2 us  [swap(): lax.ppermute(value, axis, [(i, i ^ mask) for i in range(lax.axis_size(axi...]
    all_to_all x0 -> x1, starting transfers between devices: none -> 5.72 us  [on_device(): lax.all_to_all(picked, 'wide', split_axis=0, concat_axis=0, tiled=True)]
    unnamed x47 -> x11, local copies, waits for them, and re-layouts: 9.26 us -> 6.26 us
    all_to_all x0 -> x1, waiting for transfers between devices: none -> 2.19 us  [on_device(): lax.all_to_all(picked, 'wide', split_axis=0, concat_axis=0, tiled=True)]
  transfers between devices with their start and end apart: 26 -> 20, of which waited for: 8 -> 5; matrix products, arithmetic and copies ran while one was open for 0% -> 2% of each run, Pallas kernels for 15% -> 19%
where the time goes in v7:
time: 94 us; the launch traced here: 93.5 us
  starting transfers between devices  47.2 us (50%)
  Pallas kernels  26.4 us (28%)
  waiting for transfers between devices  11.8 us (13%)
  local copies, waits for them, and re-layouts  7.34 us (8%)
    ppermute x17, starting transfers between devices, swap(): lax.ppermute(value, axis, [(i, i ^ mask) for i in range(lax.axis_size(axi...  32.2 us
    pallas_call x2, Pallas kernels, stack(): pl.pallas_call(lambda *refs: stack_kernel(nw, wins, size, group, *refs),...  17.6 us
    ppermute x17, waiting for transfers between devices, swap(): lax.ppermute(value, axis, [(i, i ^ mask) for i in range(lax.axis_size(axi...  8.25 us
    unnamed x11, local copies, waits for them, and re-layouts  6.26 us
    all_to_all x1, starting transfers between devices, on_device(): lax.all_to_all(picked, 'wide', split_axis=0, concat_axis=0, tiled=True)  5.72 us
    pallas_call x1, Pallas kernels, spectra(): pl.pallas_call(lambda *refs: spectra_kernel(sizes, *refs), in_specs=[smem...  5.25 us
    ppermute x1, starting transfers between devices, on_device(): tip = lax.ppermute(tip, 'wide', ahead)  4.98 us
    ppermute x1, starting transfers between devices, on_device(): lax.ppermute(after(records[:, :, time - HALF:], [tip]), 'wide', ahead)  4.24 us
  transfers between devices with their start and end apart: 20, of which 5 were waited for; matrix products, arithmetic and copies ran while one was open for 2% of the time, Pallas kernels for 19%

profile of v7, /device:TPU:0, one launch (start us, length us, event | category | flops | bytes accessed | tf_op | source)
XLA Modules:
  0.0 93.5 jit_solution(14018186813332537804)
XLA Ops:
  0.0 1.9 %copy-done = bf16[8,128,1536]{2,1,0:T(8,128)(2,1)S(1)} copy-done((bf16[8,128,1536]{2,1,0:T(8,128)(2,1)S(1)}, bf16[8,128,1536]{2,1,0:T(8,128)(2,1)}, u32[]{:S(2)}) %copy-start) | copy-done | bytes 3145752
  2.2 5.0 %collective-permute-start = (bf16[64,256]{1,0:T(8,128)(2,1)S(1)}, bf16[64,256]{1,0:T(8,128)(2,1)S(1)}, u32[]{:S(2)}, u32[]{:S(2)}) collective-permute-start(bf16[64,256]{1,0:T(8,128)(2,1)S(1)} %get-tuple-element.54), channel_id=1, source_target_pairs={{0,4},{4,8},{8,12},{12,16},{16,20},{20,24},{24,28},{1,5},{5,9},{9,... | collective-permute-start | bytes 98312 | tf_op jit(solution)/shard_map/ppermute | solution.py:359
  7.2 1.1 %slice.3 = bf16[8,128,256]{2,1,0:T(8,128)(2,1)S(1)} slice(bf16[8,128,1536]{2,1,0:T(8,128)(2,1)} %refs_1_.1), slice={[0:8], [0:128], [1280:1536]} | slice | bytes 1048576 | tf_op jit(solution)/shard_map/slice | solution.py:360
  8.8 4.2 %collective-permute-start.1 = (bf16[8,128,256]{2,1,0:T(8,128)(2,1)S(1)}, bf16[8,128,256]{2,1,0:T(8,128)(2,1)S(1)}, u32[]{:S(2)}, u32[]{:S(2)}) collective-permute-start(bf16[8,128,256]{2,1,0:T(8,128)(2,1)S(1)} %slice.3), channel_id=1, source_target_pairs={{0,4},{4,8},{8,12},{12,16},{16,20},{20,24},{24,28},{1,5},{5,9},{9,... | collective-permute-start | bytes 1572872 | tf_op jit(solution)/shard_map/ppermute | solution.py:360
  13.0 0.8 copy.8.refs_0_
  13.8 1.0 %copy-done.3 = f32[512,256]{1,0:T(8,128)S(1)} copy-done((f32[512,256]{1,0:T(8,128)S(1)}, f32[512,256]{1,0:T(8,128)}, u32[]{:S(2)}) %copy-start.3) | copy-done | bytes 524312
  14.8 0.7 copy-done.4
  15.5 1.9 %virtual.1 = (bf16[8,4,48,128]{3,2,1,0:T(8,128)(2,1)}, bf16[512,256]{1,0:T(8,128)(2,1)S(1)}, bf16[512,256]{1,0:T(8,128)(2,1)S(1)}) custom-call(s32[8,4]{1,0:T(8,128)S(1)} %copy.8.refs_0_, bf16[64,1536]{1,0:T(8,128)(2,1)S(1)} %get-tuple-element.53.refs_1_, bf16[64,256]{1,0:T(8,128)(2,1)S(1)} %collective-permute-done.refs_2_, f32[1,201]{1,0:T(1,128)S(1)} %bitcast.6, ...), custom_call_target="tpu_custom_call" | custom-call | flops 100000000 | bytes 786432 | tf_op jit(solution)/shard_map/virtual/pallas_call | solution.py:125
  17.4 5.7 %all-to-all-start = ((bf16[8,4,48,128]{3,2,1,0:T(8,128)(2,1)}), bf16[8,4,48,128]{3,2,1,0:T(8,128)(2,1)S(1)}, u32[]{:S(2)}, u32[]{:S(2)}) async-start(bf16[8,4,48,128]{3,2,1,0:T(8,128)(2,1)} %get-tuple-element.55), calls=%async_computation | async-start | bytes 786432 | tf_op jit(solution)/shard_map/all_to_all | solution.py:362
  23.2 0.9 collective-permute-done.1.refs_2_
  24.1 1.9 %copy-done.1 = bf16[8,128,1536]{2,1,0:T(8,128)(2,1)S(1)} copy-done((bf16[8,128,1536]{2,1,0:T(8,128)(2,1)S(1)}, bf16[8,128,1536]{2,1,0:T(8,128)(2,1)}, u32[]{:S(2)}) %copy-start.1) | copy-done | bytes 3145752
  26.0 5.3 %spectra.1 = (bf16[384,128]{1,0:T(8,128)(2,1)S(1)}, bf16[384,128]{1,0:T(8,128)(2,1)}, bf16[384,128]{1,0:T(8,128)(2,1)}, bf16[384,128]{1,0:T(8,128)(2,1)S(1)}, bf...) custom-call(s32[1]{0:T(128)} %bitcast.refs_0_.refs_1_, ...), custom_call_target="tpu_custom_call" | custom-call | flops 2415919104 | bytes 4718592 | tf_op jit(solution)/shard_map/spectra/pallas_call | solution.py:167
  31.2 2.2 %all-to-all-done.refs_1_ = bf16[8,4,48,128]{3,2,1,0:T(8,128)(2,1)S(1)} async-done(((bf16[8,4,48,128]{3,2,1,0:T(8,128)(2,1)}), bf16[8,4,48,128]{3,2,1,0:T(8,128)(2,1)S(1)}, u32[]{:S(2)}, u32[]{:S(2)}) %all-to-all-start) | async-done | bytes 393248 | tf_op jit(solution)/shard_map/all_to_all | solution.py:362
  33.4 5.2 %collective-permute-start.5 = (bf16[384,128]{1,0:T(8,128)(2,1)S(1)}, bf16[384,128]{1,0:T(8,128)(2,1)S(1)}, u32[]{:S(2)}, u32[]{:S(2)}) collective-permute-start(bf16[384,128]{1,0:T(8,128)(2,1)S(1)} %get-tuple-element.79), channel_id=1, source_target_pairs={{0,28},{4,24},{8,20},{12,16},{16,12},{20,8},{24,4},{28,0},{1,29},{... | collective-permute-start | bytes 294920 | tf_op jit(solution)/shard_map/ppermute | solution.py:341
  38.6 0.7 collective-permute-start.6
  39.3 4.7 %collective-permute-start.7 = (bf16[384,128]{1,0:T(8,128)(2,1)S(1)}, bf16[384,128]{1,0:T(8,128)(2,1)S(1)}, u32[]{:S(2)}, u32[]{:S(2)}) collective-permute-start(bf16[384,128]{1,0:T(8,128)(2,1)S(1)} %get-tuple-element.81), channel_id=1, source_target_pairs={{0,20},{4,16},{8,28},{12,24},{16,4},{20,0},{24,12},{28,8},{1,21},{... | collective-permute-start | bytes 294920 | tf_op jit(solution)/shard_map/ppermute | solution.py:341
  44.0 1.5 %collective-permute-start.4 = (bf16[8,4,48,128]{3,2,1,0:T(8,128)(2,1)S(1)}, bf16[8,4,48,128]{3,2,1,0:T(8,128)(2,1)S(1)}, u32[]{:S(2)}, u32[]{:S(2)}) collective-permute-start(bf16[8,4,48,128]{3,2,1,0:T(8,128)(2,1)S(1)} %all-to-all-done.refs_1_), channel_id=1, source_target_pairs={{0,2},{1,3},{2,0},{3,1},{4,6},{5,7},{6,4},{7,5},{8,10},{9,11},{10,... | collective-permute-start | bytes 1179656 | tf_op jit(solution)/shard_map/ppermute | solution.py:341
  45.5 7.7 %collective-permute-done.7.refs_7_ = bf16[384,128]{1,0:T(8,128)(2,1)S(1)} collective-permute-done((bf16[384,128]{1,0:T(8,128)(2,1)S(1)}, bf16[384,128]{1,0:T(8,128)(2,1)S(1)}, u32[]{:S(2)}, u32[]{:S(2)}) %collective-permute-start.7) | collective-permute-done | bytes 98336 | tf_op jit(solution)/shard_map/ppermute | solution.py:341
  53.2 1.5 %collective-permute-start.8 = (bf16[8,4,48,128]{3,2,1,0:T(8,128)(2,1)S(1)}, bf16[8,4,48,128]{3,2,1,0:T(8,128)(2,1)S(1)}, u32[]{:S(2)}, u32[]{:S(2)}) collective-permute-start(bf16[8,4,48,128]{3,2,1,0:T(8,128)(2,1)S(1)} %collective-permute-done.3.refs_2_), channel_id=1, source_target_pairs={{0,2},{1,3},{2,0},{3,1},{4,6},{5,7},{6,4},{7,5},{8,10},{9,11},{10,... | collective-permute-start | bytes 1179656 | tf_op jit(solution)/shard_map/ppermute | solution.py:341
  54.7 2.4 %collective-permute-start.14 = (bf16[384,128]{1,0:T(8,128)(2,1)S(1)}, bf16[384,128]{1,0:T(8,128)(2,1)S(1)}, u32[]{:S(2)}, u32[]{:S(2)}) collective-permute-start(bf16[384,128]{1,0:T(8,128)(2,1)S(1)} %get-tuple-element.93), channel_id=1, source_target_pairs={{0,12},{4,8},{8,4},{12,0},{16,28},{20,24},{24,20},{28,16},{1,13},{... | collective-permute-start | bytes 294920 | tf_op jit(solution)/shard_map/ppermute | solution.py:341
  57.1 2.7 %collective-permute-start.12 = (bf16[384,128]{1,0:T(8,128)(2,1)}, bf16[384,128]{1,0:T(8,128)(2,1)S(1)}, u32[]{:S(2)}, u32[]{:S(2)}) collective-permute-start(bf16[384,128]{1,0:T(8,128)(2,1)} %get-tuple-element.90), channel_id=1, source_target_pairs={{0,8},{4,12},{8,0},{12,4},{16,24},{20,28},{24,16},{28,20},{1,9},{5... | collective-permute-start | bytes 294920 | tf_op jit(solution)/shard_map/ppermute | solution.py:341
  59.8 1.5 %collective-permute-start.2 = (bf16[384,128]{1,0:T(8,128)(2,1)}, bf16[384,128]{1,0:T(8,128)(2,1)S(1)}, u32[]{:S(2)}, u32[]{:S(2)}) collective-permute-start(bf16[384,128]{1,0:T(8,128)(2,1)} %get-tuple-element.77), channel_id=1, source_target_pairs={{0,4},{4,0},{8,12},{12,8},{16,20},{20,16},{24,28},{28,24},{1,5},{5... | collective-permute-start | bytes 294920 | tf_op jit(solution)/shard_map/ppermute | solution.py:341
  61.2 0.5 collective-permute-done.16.refs_6_
  61.8 2.3 %collective-permute-start.18 = (bf16[384,128]{1,0:T(8,128)(2,1)}, bf16[384,128]{1,0:T(8,128)(2,1)S(1)}, u32[]{:S(2)}, u32[]{:S(2)}) collective-permute-start(bf16[384,128]{1,0:T(8,128)(2,1)} %get-tuple-element.99), channel_id=1, source_target_pairs={{0,28},{4,24},{8,20},{12,16},{16,12},{20,8},{24,4},{28,0},{1,29},{... | collective-permute-start | bytes 294920 | tf_op jit(solution)/shard_map/ppermute | solution.py:341
  64.1 3.0 %collective-permute-start.17 = (bf16[384,128]{1,0:T(8,128)(2,1)S(1)}, bf16[384,128]{1,0:T(8,128)(2,1)S(1)}, u32[]{:S(2)}, u32[]{:S(2)}) collective-permute-start(bf16[384,128]{1,0:T(8,128)(2,1)S(1)} %get-tuple-element.97), channel_id=1, source_target_pairs={{0,24},{4,28},{8,16},{12,20},{16,8},{20,12},{24,0},{28,4},{1,25},{... | collective-permute-start | bytes 294920 | tf_op jit(solution)/shard_map/ppermute | solution.py:341
  67.7 0.9 collective-permute-start.9
  68.6 2.7 %collective-permute-start.11 = (bf16[384,128]{1,0:T(8,128)(2,1)S(1)}, bf16[384,128]{1,0:T(8,128)(2,1)S(1)}, u32[]{:S(2)}, u32[]{:S(2)}) collective-permute-start(bf16[384,128]{1,0:T(8,128)(2,1)S(1)} %get-tuple-element.87), channel_id=1, source_target_pairs={{0,12},{4,8},{8,4},{12,0},{16,28},{20,24},{24,20},{28,16},{1,13},{... | collective-permute-start | bytes 294920 | tf_op jit(solution)/shard_map/ppermute | solution.py:341
  71.3 1.3 %sources.1 = bf16[128,48,256]{2,1,0:T(8,128)(2,1)S(1)} custom-call(s32[1]{0:T(128)} %bitcast.2.refs_0_, bf16[8,4,48,128]{3,2,1,0:T(8,128)(2,1)S(1)} %all-to-all-done.refs_1_, bf16[8,4,48,128]{3,2,1,0:T(8,128)(2,1)S(1)} %collective-permute-done.3.refs_2_, bf16[8,4,48,128]{3,2,1,0:T(8,128)(2,1)S(1)} %collective-permute-done.4.refs_3_, ...), custom_call_target="tpu_custom_call" | custom-call | flops 100000000 | bytes 6291456 | tf_op jit(solution)/shard_map/sources/pallas_call | solution.py:216
  72.6 0.7 collective-permute-start.13
  73.3 2.6 %collective-permute-start.15 = (bf16[384,128]{1,0:T(8,128)(2,1)S(1)}, bf16[384,128]{1,0:T(8,128)(2,1)S(1)}, u32[]{:S(2)}, u32[]{:S(2)}) collective-permute-start(bf16[384,128]{1,0:T(8,128)(2,1)S(1)} %get-tuple-element.94), channel_id=1, source_target_pairs={{0,20},{4,16},{8,28},{12,24},{16,4},{20,0},{24,12},{28,8},{1,21},{... | collective-permute-start | bytes 294920 | tf_op jit(solution)/shard_map/ppermute | solution.py:341
  75.9 8.8 %stack.2.refs_12_ = bf16[1,4,128,32,256]{4,3,2,1,0:T(8,128)(2,1)} custom-call(s32[1]{0:T(128)S(6)} %copy.10.refs_0_, s32[1]{0:T(128)} %bitcast.refs_0_.refs_1_, bf16[384,128]{1,0:T(8,128)(2,1)S(1)} %get-tuple-element.100.refs_2_, bf16[384,128]{1,0:T(8,128)(2,1)S(1)} %collective-permute-done.2.refs_3_, bf16[384,128]{1,0:T(8,128)(2,1)S(1)} %collective-permute-done.12.refs_4_, ...), custom_call_target="tpu_custom_call" | custom-call | flops 2147483648 | bytes 7340032 | tf_op jit(solution)/shard_map/stack/pallas_call | solution.py:314
  84.7 8.8 %stack.3 = bf16[1,4,128,32,256]{4,3,2,1,0:T(8,128)(2,1)} custom-call(s32[1]{0:T(128)S(6)} %copy.10.refs_0_, s32[1]{0:T(128)} %bitcast.refs_0_.refs_1_, bf16[384,128]{1,0:T(8,128)(2,1)S(1)} %get-tuple-element.75.refs_2_, bf16[384,128]{1,0:T(8,128)(2,1)S(1)} %collective-permute-done.9.refs_3_, ...), custom_call_target="tpu_custom_call", output_to_operand_aliasing={{}: (12, {})} | custom-call | flops 2147483648 | bytes 7340032 | tf_op jit(solution)/shard_map/stack/pallas_call | solution.py:314
  (26 shorter events, 0.8 us)
Async XLA Ops:
  0.0 1.9 %copy-start = (bf16[8,128,1536]{2,1,0:T(8,128)(2,1)S(1)}, bf16[8,128,1536]{2,1,0:T(8,128)(2,1)}, u32[]{:S(2)}) copy-start(bf16[8,128,1536]{2,1,0:T(8,128)(2,1)} %refs_1_.1) | copy-start | bytes 9437188
  2.2 73.7 %copy-start.2 = (f32[256,256]{1,0:T(8,128)S(1)}, f32[256,256]{1,0:T(8,128)}, u32[]{:S(2)}) copy-start(f32[256,256]{1,0:T(8,128)} %constant.14.clone.refs_11_) | copy-start | bytes 786436
  2.2 6.6 %collective-permute-start = (bf16[64,256]{1,0:T(8,128)(2,1)S(1)}, bf16[64,256]{1,0:T(8,128)(2,1)S(1)}, u32[]{:S(2)}, u32[]{:S(2)}) collective-permute-start(bf16[64,256]{1,0:T(8,128)(2,1)S(1)} %get-tuple-element.54), channel_id=1, source_target_pairs={{0,4},{4,8},{8,12},{12,16},{16,20},{20,24},{24,28},{1,5},{5,9},{9,... | collective-permute-start | bytes 98312 | tf_op jit(solution)/shard_map/ppermute | solution.py:359
  8.8 15.3 %collective-permute-start.1 = (bf16[8,128,256]{2,1,0:T(8,128)(2,1)S(1)}, bf16[8,128,256]{2,1,0:T(8,128)(2,1)S(1)}, u32[]{:S(2)}, u32[]{:S(2)}) collective-permute-start(bf16[8,128,256]{2,1,0:T(8,128)(2,1)S(1)} %slice.3), channel_id=1, source_target_pairs={{0,4},{4,8},{8,12},{12,16},{16,20},{20,24},{24,28},{1,5},{5,9},{9,... | collective-permute-start | bytes 1572872 | tf_op jit(solution)/shard_map/ppermute | solution.py:360
  13.8 1.0 %copy-start.3 = (f32[512,256]{1,0:T(8,128)S(1)}, f32[512,256]{1,0:T(8,128)}, u32[]{:S(2)}) copy-start(f32[512,256]{1,0:T(8,128)} %constant.13.clone.refs_4_) | copy-start | bytes 1572868
  14.8 0.7 copy-start.4
  17.4 16.0 %all-to-all-start = ((bf16[8,4,48,128]{3,2,1,0:T(8,128)(2,1)}), bf16[8,4,48,128]{3,2,1,0:T(8,128)(2,1)S(1)}, u32[]{:S(2)}, u32[]{:S(2)}) async-start(bf16[8,4,48,128]{3,2,1,0:T(8,128)(2,1)} %get-tuple-element.55), calls=%async_computation | async-start | bytes 786432 | tf_op jit(solution)/shard_map/all_to_all | solution.py:362
  24.1 1.9 %copy-start.1 = (bf16[8,128,1536]{2,1,0:T(8,128)(2,1)S(1)}, bf16[8,128,1536]{2,1,0:T(8,128)(2,1)}, u32[]{:S(2)}) copy-start(bf16[8,128,1536]{2,1,0:T(8,128)(2,1)} %refs_1_.1) | copy-start | bytes 9437188
  33.4 19.8 %collective-permute-start.3 = (bf16[8,4,48,128]{3,2,1,0:T(8,128)(2,1)S(1)}, bf16[8,4,48,128]{3,2,1,0:T(8,128)(2,1)S(1)}, u32[]{:S(2)}, u32[]{:S(2)}) collective-permute-start(bf16[8,4,48,128]{3,2,1,0:T(8,128)(2,1)S(1)} %all-to-all-done.refs_1_), channel_id=1, source_target_pairs={{0,1},{1,0},{2,3},{3,2},{4,5},{5,4},{6,7},{7,6},{8,9},{9,8},{10,11... | collective-permute-start | bytes 1179656 | tf_op jit(solution)/shard_map/ppermute | solution.py:341
  33.4 12.1 %collective-permute-start.5 = (bf16[384,128]{1,0:T(8,128)(2,1)S(1)}, bf16[384,128]{1,0:T(8,128)(2,1)S(1)}, u32[]{:S(2)}, u32[]{:S(2)}) collective-permute-start(bf16[384,128]{1,0:T(8,128)(2,1)S(1)} %get-tuple-element.79), channel_id=1, source_target_pairs={{0,28},{4,24},{8,20},{12,16},{16,12},{20,8},{24,4},{28,0},{1,29},{... | collective-permute-start | bytes 294920 | tf_op jit(solution)/shard_map/ppermute | solution.py:341
  38.6 6.9 %collective-permute-start.6 = (bf16[384,128]{1,0:T(8,128)(2,1)S(1)}, bf16[384,128]{1,0:T(8,128)(2,1)S(1)}, u32[]{:S(2)}, u32[]{:S(2)}) collective-permute-start(bf16[384,128]{1,0:T(8,128)(2,1)S(1)} %get-tuple-element.80), channel_id=1, source_target_pairs={{0,24},{4,28},{8,16},{12,20},{16,8},{20,12},{24,0},{28,4},{1,25},{... | collective-permute-start | bytes 294920 | tf_op jit(solution)/shard_map/ppermute | solution.py:341
  39.3 13.9 %collective-permute-start.7 = (bf16[384,128]{1,0:T(8,128)(2,1)S(1)}, bf16[384,128]{1,0:T(8,128)(2,1)S(1)}, u32[]{:S(2)}, u32[]{:S(2)}) collective-permute-start(bf16[384,128]{1,0:T(8,128)(2,1)S(1)} %get-tuple-element.81), channel_id=1, source_target_pairs={{0,20},{4,16},{8,28},{12,24},{16,4},{20,0},{24,12},{28,8},{1,21},{... | collective-permute-start | bytes 294920 | tf_op jit(solution)/shard_map/ppermute | solution.py:341
  44.0 13.1 %collective-permute-start.4 = (bf16[8,4,48,128]{3,2,1,0:T(8,128)(2,1)S(1)}, bf16[8,4,48,128]{3,2,1,0:T(8,128)(2,1)S(1)}, u32[]{:S(2)}, u32[]{:S(2)}) collective-permute-start(bf16[8,4,48,128]{3,2,1,0:T(8,128)(2,1)S(1)} %all-to-all-done.refs_1_), channel_id=1, source_target_pairs={{0,2},{1,3},{2,0},{3,1},{4,6},{5,7},{6,4},{7,5},{8,10},{9,11},{10,... | collective-permute-start | bytes 1179656 | tf_op jit(solution)/shard_map/ppermute | solution.py:341
  53.2 14.5 %collective-permute-start.8 = (bf16[8,4,48,128]{3,2,1,0:T(8,128)(2,1)S(1)}, bf16[8,4,48,128]{3,2,1,0:T(8,128)(2,1)S(1)}, u32[]{:S(2)}, u32[]{:S(2)}) collective-permute-start(bf16[8,4,48,128]{3,2,1,0:T(8,128)(2,1)S(1)} %collective-permute-done.3.refs_2_), channel_id=1, source_target_pairs={{0,2},{1,3},{2,0},{3,1},{4,6},{5,7},{6,4},{7,5},{8,10},{9,11},{10,... | collective-permute-start | bytes 1179656 | tf_op jit(solution)/shard_map/ppermute | solution.py:341
  54.7 7.1 %collective-permute-start.16 = (bf16[384,128]{1,0:T(8,128)(2,1)S(1)}, bf16[384,128]{1,0:T(8,128)(2,1)S(1)}, u32[]{:S(2)}, u32[]{:S(2)}) collective-permute-start(bf16[384,128]{1,0:T(8,128)(2,1)S(1)} %get-tuple-element.96), channel_id=1, source_target_pairs={{0,16},{4,20},{8,24},{12,28},{16,0},{20,4},{24,8},{28,12},{1,17},{... | collective-permute-start | bytes 294920 | tf_op jit(solution)/shard_map/ppermute | solution.py:341
  54.7 9.4 %collective-permute-start.14 = (bf16[384,128]{1,0:T(8,128)(2,1)S(1)}, bf16[384,128]{1,0:T(8,128)(2,1)S(1)}, u32[]{:S(2)}, u32[]{:S(2)}) collective-permute-start(bf16[384,128]{1,0:T(8,128)(2,1)S(1)} %get-tuple-element.93), channel_id=1, source_target_pairs={{0,12},{4,8},{8,4},{12,0},{16,28},{20,24},{24,20},{28,16},{1,13},{... | collective-permute-start | bytes 294920 | tf_op jit(solution)/shard_map/ppermute | solution.py:341
  57.1 10.7 %collective-permute-start.12 = (bf16[384,128]{1,0:T(8,128)(2,1)}, bf16[384,128]{1,0:T(8,128)(2,1)S(1)}, u32[]{:S(2)}, u32[]{:S(2)}) collective-permute-start(bf16[384,128]{1,0:T(8,128)(2,1)} %get-tuple-element.90), channel_id=1, source_target_pairs={{0,8},{4,12},{8,0},{12,4},{16,24},{20,28},{24,16},{28,20},{1,9},{5... | collective-permute-start | bytes 294920 | tf_op jit(solution)/shard_map/ppermute | solution.py:341
  59.8 8.0 %collective-permute-start.2 = (bf16[384,128]{1,0:T(8,128)(2,1)}, bf16[384,128]{1,0:T(8,128)(2,1)S(1)}, u32[]{:S(2)}, u32[]{:S(2)}) collective-permute-start(bf16[384,128]{1,0:T(8,128)(2,1)} %get-tuple-element.77), channel_id=1, source_target_pairs={{0,4},{4,0},{8,12},{12,8},{16,20},{20,16},{24,28},{28,24},{1,5},{5... | collective-permute-start | bytes 294920 | tf_op jit(solution)/shard_map/ppermute | solution.py:341
  61.8 10.8 %collective-permute-start.18 = (bf16[384,128]{1,0:T(8,128)(2,1)}, bf16[384,128]{1,0:T(8,128)(2,1)S(1)}, u32[]{:S(2)}, u32[]{:S(2)}) collective-permute-start(bf16[384,128]{1,0:T(8,128)(2,1)} %get-tuple-element.99), channel_id=1, source_target_pairs={{0,28},{4,24},{8,20},{12,16},{16,12},{20,8},{24,4},{28,0},{1,29},{... | collective-permute-start | bytes 294920 | tf_op jit(solution)/shard_map/ppermute | solution.py:341
  64.1 9.2 %collective-permute-start.17 = (bf16[384,128]{1,0:T(8,128)(2,1)S(1)}, bf16[384,128]{1,0:T(8,128)(2,1)S(1)}, u32[]{:S(2)}, u32[]{:S(2)}) collective-permute-start(bf16[384,128]{1,0:T(8,128)(2,1)S(1)} %get-tuple-element.97), channel_id=1, source_target_pairs={{0,24},{4,28},{8,16},{12,20},{16,8},{20,12},{24,0},{28,4},{1,25},{... | collective-permute-start | bytes 294920 | tf_op jit(solution)/shard_map/ppermute | solution.py:341
  67.7 16.9 %collective-permute-start.9 = (bf16[384,128]{1,0:T(8,128)(2,1)S(1)}, bf16[384,128]{1,0:T(8,128)(2,1)S(1)}, u32[]{:S(2)}, u32[]{:S(2)}) collective-permute-start(bf16[384,128]{1,0:T(8,128)(2,1)S(1)} %get-tuple-element.83), channel_id=1, source_target_pairs={{0,4},{4,0},{8,12},{12,8},{16,20},{20,16},{24,28},{28,24},{1,5},{5... | collective-permute-start | bytes 294920 | tf_op jit(solution)/shard_map/ppermute | solution.py:341
  68.6 16.0 %collective-permute-start.10 = (bf16[384,128]{1,0:T(8,128)(2,1)S(1)}, bf16[384,128]{1,0:T(8,128)(2,1)S(1)}, u32[]{:S(2)}, u32[]{:S(2)}) collective-permute-start(bf16[384,128]{1,0:T(8,128)(2,1)S(1)} %get-tuple-element.85), channel_id=1, source_target_pairs={{0,8},{4,12},{8,0},{12,4},{16,24},{20,28},{24,16},{28,20},{1,9},{5... | collective-permute-start | bytes 294920 | tf_op jit(solution)/shard_map/ppermute | solution.py:341
  68.6 16.0 %collective-permute-start.11 = (bf16[384,128]{1,0:T(8,128)(2,1)S(1)}, bf16[384,128]{1,0:T(8,128)(2,1)S(1)}, u32[]{:S(2)}, u32[]{:S(2)}) collective-permute-start(bf16[384,128]{1,0:T(8,128)(2,1)S(1)} %get-tuple-element.87), channel_id=1, source_target_pairs={{0,12},{4,8},{8,4},{12,0},{16,28},{20,24},{24,20},{28,16},{1,13},{... | collective-permute-start | bytes 294920 | tf_op jit(solution)/shard_map/ppermute | solution.py:341
  72.6 12.1 %collective-permute-start.13 = (bf16[384,128]{1,0:T(8,128)(2,1)S(1)}, bf16[384,128]{1,0:T(8,128)(2,1)S(1)}, u32[]{:S(2)}, u32[]{:S(2)}) collective-permute-start(bf16[384,128]{1,0:T(8,128)(2,1)S(1)} %get-tuple-element.91), channel_id=1, source_target_pairs={{0,16},{4,20},{8,24},{12,28},{16,0},{20,4},{24,8},{28,12},{1,17},{... | collective-permute-start | bytes 294920 | tf_op jit(solution)/shard_map/ppermute | solution.py:341
  73.3 11.4 %collective-permute-start.15 = (bf16[384,128]{1,0:T(8,128)(2,1)S(1)}, bf16[384,128]{1,0:T(8,128)(2,1)S(1)}, u32[]{:S(2)}, u32[]{:S(2)}) collective-permute-start(bf16[384,128]{1,0:T(8,128)(2,1)S(1)} %get-tuple-element.94), channel_id=1, source_target_pairs={{0,20},{4,16},{8,28},{12,24},{16,4},{20,0},{24,12},{28,8},{1,21},{... | collective-permute-start | bytes 294920 | tf_op jit(solution)/shard_map/ppermute | solution.py:341

commit v8 on v7

--- a/solution.py
+++ b/solution.py
@@ -115,7 +115,7 @@
         virt[b] = block_rows(result, b, nv, wins, count)
     for r in range(nblk):
         for k in range(SLOTS):
-            picked_ref[r, k] = virt[pairs_ref[r, k]]
+            picked_ref[r, k] = virt[pairs_ref[k, r]]
 
 
 def virtual(rows, halo, taps, pairs, nblk):
@@ -358,28 +358,18 @@
     rows, tip = extract(records)
     tip = lax.ppermute(tip, "wide", ahead)
     halo = lax.ppermute(after(records[:, :, time - HALF :], [tip]), "wide", ahead)
-    picked, toeplitz, forward = virtual(rows, tip, taps[None], pair_sources, nblk)
+    picked, toeplitz, forward = virtual(rows, tip, taps[None], pair_sources.T, nblk)
     picked = lax.all_to_all(picked, "wide", split_axis=0, concat_axis=0, tiled=True)
-    chunks = spectra(records, halo, toeplitz, forward, me, (half, half))
-    picked, (near, far) = lax.optimization_barrier((picked, chunks))
-
-    top = nnar // 2
-    slots = {0: picked, **{n: swap(picked, "narrow", n) for n in (top, 1) if n}}
+    near, far = spectra(records, halo, toeplitz, forward, me, (half, half))
+    picked = after(picked, [near[0]])
+
+    slots = [picked] + [swap(picked, "narrow", n) for n in range(nnar - 1, 0, -1)][::-1]
     for i, m in enumerate(order):
-        waits = []
-        if i == len(order) - 2:
-            waits = [slots[n] for n in sorted(slots) if n]
-        near[m] = swap(after(near[m], waits), "wide", m)
-    bit = top
-    while bit:
-        for n in sorted(slots):
-            if n ^ bit not in slots:
-                slots[n ^ bit] = swap(after(slots[n], [near[m] for m in order[:3]]), "narrow", bit)
-        bit //= 2
+        near[m] = swap(after(near[m], slots[1:3] if i == len(order) - 1 else []), "wide", m)
     for i, m in enumerate(order):
-        waits = [near[order[min(i + 2, nwide - 2)]]] + ([slots[n] for n in sorted(slots) if n] if i >= 2 else [])
+        waits = [near[order[min(i + 2, nwide - 2)]]] + (slots[1:] if i >= 2 else [])
         far[m] = swap(after(far[m], waits), "wide", m)
-    table = sources([slots[n] for n in range(nnar)], place, wins, nv)
+    table = sources(slots, place, wins, nv)
     lag = jnp.asarray(lag_table())
     out = stack(near, table, pair_counts, me, lag, None, 0, half, wins, chans)
     return stack(far, table, pair_counts, me, lag, out, half, half, wins, chans)

time: 94 us -> 96.8 us (1.030)
  starting transfers between devices: 47.2 us -> 57.2 us
  waiting for transfers between devices: 11.8 us -> 4.74 us
    ppermute x17, starting transfers between devices: 32.2 us -> 42.3 us  [swap(): lax.ppermute(value, axis, [(i, i ^ mask) for i in range(lax.axis_size(axi...]
    ppermute x17, waiting for transfers between devices: 8.25 us -> 1.12 us  [swap(): lax.ppermute(value, axis, [(i, i ^ mask) for i in range(lax.axis_size(axi...]
    unnamed x11 -> x12, local copies, waits for them, and re-layouts: 6.26 us -> 6.18 us
  transfers between devices with their start and end apart: 20 -> 20, of which waited for: 5 -> 4; matrix products, arithmetic and copies ran while one was open for 2% -> 1% of each run, Pallas kernels for 19% -> 18%
where the time goes in v8:
time: 96.8 us; the launch traced here: 96.4 us
  starting transfers between devices  57.2 us (59%)
  Pallas kernels  26.4 us (27%)
  local copies, waits for them, and re-layouts  7.26 us (8%)
  waiting for transfers between devices  4.74 us (5%)
    ppermute x17, starting transfers between devices, swap(): lax.ppermute(value, axis, [(i, i ^ mask) for i in range(lax.axis_size(axi...  42.3 us
    pallas_call x2, Pallas kernels, stack(): pl.pallas_call(lambda *refs: stack_kernel(nw, wins, size, group, *refs),...  17.6 us
    unnamed x12, local copies, waits for them, and re-layouts  6.18 us
    all_to_all x1, starting transfers between devices, on_device(): lax.all_to_all(picked, 'wide', split_axis=0, concat_axis=0, tiled=True)  5.72 us
    pallas_call x1, Pallas kernels, spectra(): pl.pallas_call(lambda *refs: spectra_kernel(sizes, *refs), in_specs=[smem...  5.23 us
    ppermute x1, starting transfers between devices, on_device(): tip = lax.ppermute(tip, 'wide', ahead)  4.98 us
    ppermute x1, starting transfers between devices, on_device(): lax.ppermute(after(records[:, :, time - HALF:], [tip]), 'wide', ahead)  4.24 us
    all_to_all x1, waiting for transfers between devices, on_device(): lax.all_to_all(picked, 'wide', split_axis=0, concat_axis=0, tiled=True)  2.11 us
  transfers between devices with their start and end apart: 20, of which 4 were waited for; matrix products, arithmetic and copies ran while one was open for 1% of the time, Pallas kernels for 18%

profile of v8, /device:TPU:0, one launch (start us, length us, event | category | flops | bytes accessed | tf_op | source)
XLA Modules:
  0.0 96.4 jit_solution(1609639071799166307)
XLA Ops:
  0.0 1.9 %copy-done = bf16[8,128,1536]{2,1,0:T(8,128)(2,1)S(1)} copy-done((bf16[8,128,1536]{2,1,0:T(8,128)(2,1)S(1)}, bf16[8,128,1536]{2,1,0:T(8,128)(2,1)}, u32[]{:S(2)}) %copy-start) | copy-done | bytes 3145752
  1.9 0.3 extract.1
  2.2 5.0 %collective-permute-start = (bf16[64,256]{1,0:T(8,128)(2,1)S(1)}, bf16[64,256]{1,0:T(8,128)(2,1)S(1)}, u32[]{:S(2)}, u32[]{:S(2)}) collective-permute-start(bf16[64,256]{1,0:T(8,128)(2,1)S(1)} %get-tuple-element.36), channel_id=1, source_target_pairs={{0,4},{4,8},{8,12},{12,16},{16,20},{20,24},{24,28},{1,5},{5,9},{9,... | collective-permute-start | bytes 98312 | tf_op jit(solution)/shard_map/ppermute | solution.py:359
  7.2 1.1 %slice.3 = bf16[8,128,256]{2,1,0:T(8,128)(2,1)S(1)} slice(bf16[8,128,1536]{2,1,0:T(8,128)(2,1)} %refs_1_.1), slice={[0:8], [0:128], [1280:1536]} | slice | bytes 1048576 | tf_op jit(solution)/shard_map/slice | solution.py:360
  8.3 0.5 collective-permute-done.refs_2_
  8.8 4.2 %collective-permute-start.1 = (bf16[8,128,256]{2,1,0:T(8,128)(2,1)S(1)}, bf16[8,128,256]{2,1,0:T(8,128)(2,1)S(1)}, u32[]{:S(2)}, u32[]{:S(2)}) collective-permute-start(bf16[8,128,256]{2,1,0:T(8,128)(2,1)S(1)} %slice.3), channel_id=1, source_target_pairs={{0,4},{4,8},{8,12},{12,16},{16,20},{20,24},{24,28},{1,5},{5,9},{9,... | collective-permute-start | bytes 1572872 | tf_op jit(solution)/shard_map/ppermute | solution.py:360
  13.0 1.0 %copy-done.3 = f32[512,256]{1,0:T(8,128)S(1)} copy-done((f32[512,256]{1,0:T(8,128)S(1)}, f32[512,256]{1,0:T(8,128)}, u32[]{:S(2)}) %copy-start.3) | copy-done | bytes 524312
  14.1 0.7 copy-done.4
  14.7 0.7 copy-done.5
  15.4 1.9 %virtual.1 = (bf16[8,4,48,128]{3,2,1,0:T(8,128)(2,1)}, bf16[512,256]{1,0:T(8,128)(2,1)S(1)}, bf16[512,256]{1,0:T(8,128)(2,1)S(1)}) custom-call(s32[4,8]{1,0:T(4,128)S(1)} %bitcast.7, bf16[64,1536]{1,0:T(8,128)(2,1)S(1)} %get-tuple-element.38.refs_1_, bf16[64,256]{1,0:T(8,128)(2,1)S(1)} %collective-permute-done.refs_2_, f32[1,201]{1,0:T(1,128)S(1)} %bitcast.8, ...), custom_call_target="tpu_custom_call" | custom-call | flops 100000000 | bytes 786432 | tf_op jit(solution)/shard_map/virtual/pallas_call | solution.py:125
  17.3 5.7 %all-to-all-start = ((bf16[8,4,48,128]{3,2,1,0:T(8,128)(2,1)}), bf16[8,4,48,128]{3,2,1,0:T(8,128)(2,1)S(1)}, u32[]{:S(2)}, u32[]{:S(2)}) async-start(bf16[8,4,48,128]{3,2,1,0:T(8,128)(2,1)} %get-tuple-element.44), calls=%async_computation | async-start | bytes 786432 | tf_op jit(solution)/shard_map/all_to_all | solution.py:362
  23.1 1.0 %collective-permute-done.1.refs_2_ = bf16[8,128,256]{2,1,0:T(8,128)(2,1)S(1)} collective-permute-done((bf16[8,128,256]{2,1,0:T(8,128)(2,1)S(1)}, bf16[8,128,256]{2,1,0:T(8,128)(2,1)S(1)}, u32[]{:S(2)}, u32[]{:S(2)}) %collective-permute-start.1) | collective-permute-done | bytes 524320 | tf_op jit(solution)/shard_map/ppermute | solution.py:360
  24.1 1.9 %copy-done.1 = bf16[8,128,1536]{2,1,0:T(8,128)(2,1)S(1)} copy-done((bf16[8,128,1536]{2,1,0:T(8,128)(2,1)S(1)}, bf16[8,128,1536]{2,1,0:T(8,128)(2,1)}, u32[]{:S(2)}) %copy-start.1) | copy-done | bytes 3145752
  26.0 5.2 %spectra.1 = (bf16[384,128]{1,0:T(8,128)(2,1)S(1)}, bf16[384,128]{1,0:T(8,128)(2,1)}, bf16[384,128]{1,0:T(8,128)(2,1)S(1)}, bf16[384,128]{1,0:T(8,128)(2,1)S(1)}...) custom-call(s32[1]{0:T(128)} %bitcast.refs_0_.refs_1_, ...), custom_call_target="tpu_custom_call" | custom-call | flops 2415919104 | bytes 4718592 | tf_op jit(solution)/shard_map/spectra/pallas_call | solution.py:167
  31.2 2.1 %all-to-all-done.refs_1_ = bf16[8,4,48,128]{3,2,1,0:T(8,128)(2,1)S(1)} async-done(((bf16[8,4,48,128]{3,2,1,0:T(8,128)(2,1)}), bf16[8,4,48,128]{3,2,1,0:T(8,128)(2,1)S(1)}, u32[]{:S(2)}, u32[]{:S(2)}) %all-to-all-start) | async-done | bytes 393248 | tf_op jit(solution)/shard_map/all_to_all | solution.py:362
  33.3 1.5 %collective-permute-start.3 = (bf16[8,4,48,128]{3,2,1,0:T(8,128)(2,1)S(1)}, bf16[8,4,48,128]{3,2,1,0:T(8,128)(2,1)S(1)}, u32[]{:S(2)}, u32[]{:S(2)}) collective-permute-start(bf16[8,4,48,128]{3,2,1,0:T(8,128)(2,1)S(1)} %all-to-all-done.refs_1_), channel_id=1, source_target_pairs={{0,2},{1,3},{2,0},{3,1},{4,6},{5,7},{6,4},{7,5},{8,10},{9,11},{10,... | collective-permute-start | bytes 1179656 | tf_op jit(solution)/shard_map/ppermute | solution.py:341
  34.8 0.6 collective-permute-start.5
  35.4 7.8 %collective-permute-start.13 = (bf16[384,128]{1,0:T(8,128)(2,1)S(1)}, bf16[384,128]{1,0:T(8,128)(2,1)S(1)}, u32[]{:S(2)}, u32[]{:S(2)}) collective-permute-start(bf16[384,128]{1,0:T(8,128)(2,1)S(1)} %get-tuple-element.60), channel_id=1, source_target_pairs={{0,16},{4,20},{8,24},{12,28},{16,0},{20,4},{24,8},{28,12},{1,17},{... | collective-permute-start | bytes 294920 | tf_op jit(solution)/shard_map/ppermute | solution.py:341
  43.3 1.1 %collective-permute-done.3.refs_3_ = bf16[8,4,48,128]{3,2,1,0:T(8,128)(2,1)S(1)} collective-permute-done((bf16[8,4,48,128]{3,2,1,0:T(8,128)(2,1)S(1)}, bf16[8,4,48,128]{3,2,1,0:T(8,128)(2,1)S(1)}, u32[]{:S(2)}, u32[]{:S(2)}) %collective-permute-start.3) | collective-permute-done | bytes 393248 | tf_op jit(solution)/shard_map/ppermute | solution.py:341
  44.4 3.2 %collective-permute-start.9 = (bf16[384,128]{1,0:T(8,128)(2,1)S(1)}, bf16[384,128]{1,0:T(8,128)(2,1)S(1)}, u32[]{:S(2)}, u32[]{:S(2)}) collective-permute-start(bf16[384,128]{1,0:T(8,128)(2,1)S(1)} %get-tuple-element.54), channel_id=1, source_target_pairs={{0,8},{4,12},{8,0},{12,4},{16,24},{20,28},{24,16},{28,20},{1,9},{5... | collective-permute-start | bytes 294920 | tf_op jit(solution)/shard_map/ppermute | solution.py:341
  47.5 2.6 %collective-permute-start.11 = (bf16[384,128]{1,0:T(8,128)(2,1)S(1)}, bf16[384,128]{1,0:T(8,128)(2,1)S(1)}, u32[]{:S(2)}, u32[]{:S(2)}) collective-permute-start(bf16[384,128]{1,0:T(8,128)(2,1)S(1)} %get-tuple-element.57), channel_id=1, source_target_pairs={{0,12},{4,8},{8,4},{12,0},{16,28},{20,24},{24,20},{28,16},{1,13},{... | collective-permute-start | bytes 294920 | tf_op jit(solution)/shard_map/ppermute | solution.py:341
  50.1 0.6 collective-permute-start.4
  50.8 4.3 %collective-permute-start.17 = (bf16[384,128]{1,0:T(8,128)(2,1)}, bf16[384,128]{1,0:T(8,128)(2,1)S(1)}, u32[]{:S(2)}, u32[]{:S(2)}) collective-permute-start(bf16[384,128]{1,0:T(8,128)(2,1)} %get-tuple-element.65), channel_id=1, source_target_pairs={{0,24},{4,28},{8,16},{12,20},{16,8},{20,12},{24,0},{28,4},{1,25},{... | collective-permute-start | bytes 294920 | tf_op jit(solution)/shard_map/ppermute | solution.py:341
  55.1 0.4 collective-permute-start.18
  55.5 7.5 %collective-permute-start.14 = (bf16[384,128]{1,0:T(8,128)(2,1)}, bf16[384,128]{1,0:T(8,128)(2,1)S(1)}, u32[]{:S(2)}, u32[]{:S(2)}) collective-permute-start(bf16[384,128]{1,0:T(8,128)(2,1)} %get-tuple-element.61), channel_id=1, source_target_pairs={{0,24},{4,28},{8,16},{12,20},{16,8},{20,12},{24,0},{28,4},{1,25},{... | collective-permute-start | bytes 294920 | tf_op jit(solution)/shard_map/ppermute | solution.py:341
  63.7 1.3 %sources.1 = bf16[128,48,256]{2,1,0:T(8,128)(2,1)S(1)} custom-call(s32[1]{0:T(128)} %bitcast.3.refs_0_, bf16[8,4,48,128]{3,2,1,0:T(8,128)(2,1)S(1)} %all-to-all-done.refs_1_, bf16[8,4,48,128]{3,2,1,0:T(8,128)(2,1)S(1)} %collective-permute-done.2.refs_2_, bf16[8,4,48,128]{3,2,1,0:T(8,128)(2,1)S(1)} %collective-permute-done.3.refs_3_, ...), custom_call_target="tpu_custom_call" | custom-call | flops 100000000 | bytes 6291456 | tf_op jit(solution)/shard_map/sources/pallas_call | solution.py:216
  65.0 0.1 collective-permute-start.10
  65.1 5.0 %collective-permute-start.12 = (bf16[384,128]{1,0:T(8,128)(2,1)S(1)}, bf16[384,128]{1,0:T(8,128)(2,1)S(1)}, u32[]{:S(2)}, u32[]{:S(2)}) collective-permute-start(bf16[384,128]{1,0:T(8,128)(2,1)S(1)} %get-tuple-element.58), channel_id=1, source_target_pairs={{0,20},{4,16},{8,28},{12,24},{16,4},{20,0},{24,12},{28,8},{1,21},{... | collective-permute-start | bytes 294920 | tf_op jit(solution)/shard_map/ppermute | solution.py:341
  70.1 4.4 %collective-permute-start.7 = (bf16[384,128]{1,0:T(8,128)(2,1)S(1)}, bf16[384,128]{1,0:T(8,128)(2,1)S(1)}, u32[]{:S(2)}, u32[]{:S(2)}) collective-permute-start(bf16[384,128]{1,0:T(8,128)(2,1)S(1)} %get-tuple-element.50), channel_id=1, source_target_pairs={{0,8},{4,12},{8,0},{12,4},{16,24},{20,28},{24,16},{28,20},{1,9},{5... | collective-permute-start | bytes 294920 | tf_op jit(solution)/shard_map/ppermute | solution.py:341
  74.4 4.3 %collective-permute-start.8 = (bf16[384,128]{1,0:T(8,128)(2,1)S(1)}, bf16[384,128]{1,0:T(8,128)(2,1)S(1)}, u32[]{:S(2)}, u32[]{:S(2)}) collective-permute-start(bf16[384,128]{1,0:T(8,128)(2,1)S(1)} %get-tuple-element.52), channel_id=1, source_target_pairs={{0,12},{4,8},{8,4},{12,0},{16,28},{20,24},{24,20},{28,16},{1,13},{... | collective-permute-start | bytes 294920 | tf_op jit(solution)/shard_map/ppermute | solution.py:341
  78.7 8.8 %stack.2.refs_12_ = bf16[1,4,128,32,256]{4,3,2,1,0:T(8,128)(2,1)} custom-call(s32[1]{0:T(128)S(6)} %copy.9.refs_0_, s32[1]{0:T(128)} %bitcast.refs_0_.refs_1_, bf16[384,128]{1,0:T(8,128)(2,1)S(1)} %get-tuple-element.45.refs_2_, bf16[384,128]{1,0:T(8,128)(2,1)S(1)} %collective-permute-done.4.refs_3_, bf16[384,128]{1,0:T(8,128)(2,1)S(1)} %collective-permute-done.9.refs_4_, ...), custom_call_target="tpu_custom_call" | custom-call | flops 2147483648 | bytes 7340032 | tf_op jit(solution)/shard_map/stack/pallas_call | solution.py:314
  87.5 8.8 %stack.3 = bf16[1,4,128,32,256]{4,3,2,1,0:T(8,128)(2,1)} custom-call(s32[1]{0:T(128)S(6)} %copy.9.refs_0_, s32[1]{0:T(128)} %bitcast.refs_0_.refs_1_, bf16[384,128]{1,0:T(8,128)(2,1)S(1)} %get-tuple-element.41.refs_2_, bf16[384,128]{1,0:T(8,128)(2,1)S(1)} %collective-permute-done.6.refs_3_, ...), custom_call_target="tpu_custom_call", output_to_operand_aliasing={{}: (12, {})} | custom-call | flops 2147483648 | bytes 7340032 | tf_op jit(solution)/shard_map/stack/pallas_call | solution.py:314
  (27 shorter events, 0.1 us)
Async XLA Ops:
  0.0 1.9 %copy-start = (bf16[8,128,1536]{2,1,0:T(8,128)(2,1)S(1)}, bf16[8,128,1536]{2,1,0:T(8,128)(2,1)}, u32[]{:S(2)}) copy-start(bf16[8,128,1536]{2,1,0:T(8,128)(2,1)} %refs_1_.1) | copy-start | bytes 9437188
  2.2 76.5 %copy-start.2 = (f32[256,256]{1,0:T(8,128)S(1)}, f32[256,256]{1,0:T(8,128)}, u32[]{:S(2)}) copy-start(f32[256,256]{1,0:T(8,128)} %constant.14.clone.refs_11_) | copy-start | bytes 786436
  2.2 6.6 %collective-permute-start = (bf16[64,256]{1,0:T(8,128)(2,1)S(1)}, bf16[64,256]{1,0:T(8,128)(2,1)S(1)}, u32[]{:S(2)}, u32[]{:S(2)}) collective-permute-start(bf16[64,256]{1,0:T(8,128)(2,1)S(1)} %get-tuple-element.36), channel_id=1, source_target_pairs={{0,4},{4,8},{8,12},{12,16},{16,20},{20,24},{24,28},{1,5},{5,9},{9,... | collective-permute-start | bytes 98312 | tf_op jit(solution)/shard_map/ppermute | solution.py:359
  8.8 15.3 %collective-permute-start.1 = (bf16[8,128,256]{2,1,0:T(8,128)(2,1)S(1)}, bf16[8,128,256]{2,1,0:T(8,128)(2,1)S(1)}, u32[]{:S(2)}, u32[]{:S(2)}) collective-permute-start(bf16[8,128,256]{2,1,0:T(8,128)(2,1)S(1)} %slice.3), channel_id=1, source_target_pairs={{0,4},{4,8},{8,12},{12,16},{16,20},{20,24},{24,28},{1,5},{5,9},{9,... | collective-permute-start | bytes 1572872 | tf_op jit(solution)/shard_map/ppermute | solution.py:360
  13.0 1.0 %copy-start.3 = (f32[512,256]{1,0:T(8,128)S(1)}, f32[512,256]{1,0:T(8,128)}, u32[]{:S(2)}) copy-start(f32[512,256]{1,0:T(8,128)} %constant.13.clone.refs_4_) | copy-start | bytes 1572868
  14.1 0.7 copy-start.4
  14.7 0.7 copy-start.5
  17.3 16.0 %all-to-all-start = ((bf16[8,4,48,128]{3,2,1,0:T(8,128)(2,1)}), bf16[8,4,48,128]{3,2,1,0:T(8,128)(2,1)S(1)}, u32[]{:S(2)}, u32[]{:S(2)}) async-start(bf16[8,4,48,128]{3,2,1,0:T(8,128)(2,1)} %get-tuple-element.44), calls=%async_computation | async-start | bytes 786432 | tf_op jit(solution)/shard_map/all_to_all | solution.py:362
  24.1 1.9 %copy-start.1 = (bf16[8,128,1536]{2,1,0:T(8,128)(2,1)S(1)}, bf16[8,128,1536]{2,1,0:T(8,128)(2,1)}, u32[]{:S(2)}) copy-start(bf16[8,128,1536]{2,1,0:T(8,128)(2,1)} %refs_1_.1) | copy-start | bytes 9437188
  33.3 11.1 %collective-permute-start.3 = (bf16[8,4,48,128]{3,2,1,0:T(8,128)(2,1)S(1)}, bf16[8,4,48,128]{3,2,1,0:T(8,128)(2,1)S(1)}, u32[]{:S(2)}, u32[]{:S(2)}) collective-permute-start(bf16[8,4,48,128]{3,2,1,0:T(8,128)(2,1)S(1)} %all-to-all-done.refs_1_), channel_id=1, source_target_pairs={{0,2},{1,3},{2,0},{3,1},{4,6},{5,7},{6,4},{7,5},{8,10},{9,11},{10,... | collective-permute-start | bytes 1179656 | tf_op jit(solution)/shard_map/ppermute | solution.py:341
  34.8 12.7 %collective-permute-start.2 = (bf16[8,4,48,128]{3,2,1,0:T(8,128)(2,1)S(1)}, bf16[8,4,48,128]{3,2,1,0:T(8,128)(2,1)S(1)}, u32[]{:S(2)}, u32[]{:S(2)}) collective-permute-start(bf16[8,4,48,128]{3,2,1,0:T(8,128)(2,1)S(1)} %all-to-all-done.refs_1_), channel_id=1, source_target_pairs={{0,1},{1,0},{2,3},{3,2},{4,5},{5,4},{6,7},{7,6},{8,9},{9,8},{10,11... | collective-permute-start | bytes 1179656 | tf_op jit(solution)/shard_map/ppermute | solution.py:341
  34.8 28.2 %collective-permute-start.5 = (bf16[8,4,48,128]{3,2,1,0:T(8,128)(2,1)S(1)}, bf16[8,4,48,128]{3,2,1,0:T(8,128)(2,1)S(1)}, u32[]{:S(2)}, u32[]{:S(2)}) collective-permute-start(bf16[8,4,48,128]{3,2,1,0:T(8,128)(2,1)S(1)} %all-to-all-done.refs_1_), channel_id=1, source_target_pairs={{0,3},{1,2},{2,1},{3,0},{4,7},{5,6},{6,5},{7,4},{8,11},{9,10},{10,... | collective-permute-start | bytes 1179656 | tf_op jit(solution)/shard_map/ppermute | solution.py:341
  35.4 14.7 %collective-permute-start.13 = (bf16[384,128]{1,0:T(8,128)(2,1)S(1)}, bf16[384,128]{1,0:T(8,128)(2,1)S(1)}, u32[]{:S(2)}, u32[]{:S(2)}) collective-permute-start(bf16[384,128]{1,0:T(8,128)(2,1)S(1)} %get-tuple-element.60), channel_id=1, source_target_pairs={{0,16},{4,20},{8,24},{12,28},{16,0},{20,4},{24,8},{28,12},{1,17},{... | collective-permute-start | bytes 294920 | tf_op jit(solution)/shard_map/ppermute | solution.py:341
  43.3 7.5 %collective-permute-start.15 = (bf16[384,128]{1,0:T(8,128)(2,1)S(1)}, bf16[384,128]{1,0:T(8,128)(2,1)S(1)}, u32[]{:S(2)}, u32[]{:S(2)}) collective-permute-start(bf16[384,128]{1,0:T(8,128)(2,1)S(1)} %get-tuple-element.63), channel_id=1, source_target_pairs={{0,20},{4,16},{8,28},{12,24},{16,4},{20,0},{24,12},{28,8},{1,21},{... | collective-permute-start | bytes 294920 | tf_op jit(solution)/shard_map/ppermute | solution.py:341
  44.4 10.8 %collective-permute-start.9 = (bf16[384,128]{1,0:T(8,128)(2,1)S(1)}, bf16[384,128]{1,0:T(8,128)(2,1)S(1)}, u32[]{:S(2)}, u32[]{:S(2)}) collective-permute-start(bf16[384,128]{1,0:T(8,128)(2,1)S(1)} %get-tuple-element.54), channel_id=1, source_target_pairs={{0,8},{4,12},{8,0},{12,4},{16,24},{20,28},{24,16},{28,20},{1,9},{5... | collective-permute-start | bytes 294920 | tf_op jit(solution)/shard_map/ppermute | solution.py:341
  47.5 8.0 %collective-permute-start.11 = (bf16[384,128]{1,0:T(8,128)(2,1)S(1)}, bf16[384,128]{1,0:T(8,128)(2,1)S(1)}, u32[]{:S(2)}, u32[]{:S(2)}) collective-permute-start(bf16[384,128]{1,0:T(8,128)(2,1)S(1)} %get-tuple-element.57), channel_id=1, source_target_pairs={{0,12},{4,8},{8,4},{12,0},{16,28},{20,24},{24,20},{28,16},{1,13},{... | collective-permute-start | bytes 294920 | tf_op jit(solution)/shard_map/ppermute | solution.py:341
  50.1 14.9 %collective-permute-start.4 = (bf16[384,128]{1,0:T(8,128)(2,1)}, bf16[384,128]{1,0:T(8,128)(2,1)S(1)}, u32[]{:S(2)}, u32[]{:S(2)}) collective-permute-start(bf16[384,128]{1,0:T(8,128)(2,1)} %get-tuple-element.47), channel_id=1, source_target_pairs={{0,4},{4,0},{8,12},{12,8},{16,20},{20,16},{24,28},{28,24},{1,5},{5... | collective-permute-start | bytes 294920 | tf_op jit(solution)/shard_map/ppermute | solution.py:341
  50.8 14.3 %collective-permute-start.17 = (bf16[384,128]{1,0:T(8,128)(2,1)}, bf16[384,128]{1,0:T(8,128)(2,1)S(1)}, u32[]{:S(2)}, u32[]{:S(2)}) collective-permute-start(bf16[384,128]{1,0:T(8,128)(2,1)} %get-tuple-element.65), channel_id=1, source_target_pairs={{0,24},{4,28},{8,16},{12,20},{16,8},{20,12},{24,0},{28,4},{1,25},{... | collective-permute-start | bytes 294920 | tf_op jit(solution)/shard_map/ppermute | solution.py:341
  55.1 14.9 %collective-permute-start.18 = (bf16[384,128]{1,0:T(8,128)(2,1)}, bf16[384,128]{1,0:T(8,128)(2,1)S(1)}, u32[]{:S(2)}, u32[]{:S(2)}) collective-permute-start(bf16[384,128]{1,0:T(8,128)(2,1)} %get-tuple-element.66), channel_id=1, source_target_pairs={{0,28},{4,24},{8,20},{12,16},{16,12},{20,8},{24,4},{28,0},{1,29},{... | collective-permute-start | bytes 294920 | tf_op jit(solution)/shard_map/ppermute | solution.py:341
  55.5 14.6 %collective-permute-start.14 = (bf16[384,128]{1,0:T(8,128)(2,1)}, bf16[384,128]{1,0:T(8,128)(2,1)S(1)}, u32[]{:S(2)}, u32[]{:S(2)}) collective-permute-start(bf16[384,128]{1,0:T(8,128)(2,1)} %get-tuple-element.61), channel_id=1, source_target_pairs={{0,24},{4,28},{8,16},{12,20},{16,8},{20,12},{24,0},{28,4},{1,25},{... | collective-permute-start | bytes 294920 | tf_op jit(solution)/shard_map/ppermute | solution.py:341
  63.0 11.4 %collective-permute-start.16 = (bf16[384,128]{1,0:T(8,128)(2,1)S(1)}, bf16[384,128]{1,0:T(8,128)(2,1)S(1)}, u32[]{:S(2)}, u32[]{:S(2)}) collective-permute-start(bf16[384,128]{1,0:T(8,128)(2,1)S(1)} %get-tuple-element.64), channel_id=1, source_target_pairs={{0,28},{4,24},{8,20},{12,16},{16,12},{20,8},{24,4},{28,0},{1,29},{... | collective-permute-start | bytes 294920 | tf_op jit(solution)/shard_map/ppermute | solution.py:341
  65.0 22.5 %collective-permute-start.10 = (bf16[384,128]{1,0:T(8,128)(2,1)S(1)}, bf16[384,128]{1,0:T(8,128)(2,1)S(1)}, u32[]{:S(2)}, u32[]{:S(2)}) collective-permute-start(bf16[384,128]{1,0:T(8,128)(2,1)S(1)} %get-tuple-element.55), channel_id=1, source_target_pairs={{0,16},{4,20},{8,24},{12,28},{16,0},{20,4},{24,8},{28,12},{1,17},{... | collective-permute-start | bytes 294920 | tf_op jit(solution)/shard_map/ppermute | solution.py:341
  65.1 22.4 %collective-permute-start.12 = (bf16[384,128]{1,0:T(8,128)(2,1)S(1)}, bf16[384,128]{1,0:T(8,128)(2,1)S(1)}, u32[]{:S(2)}, u32[]{:S(2)}) collective-permute-start(bf16[384,128]{1,0:T(8,128)(2,1)S(1)} %get-tuple-element.58), channel_id=1, source_target_pairs={{0,20},{4,16},{8,28},{12,24},{16,4},{20,0},{24,12},{28,8},{1,21},{... | collective-permute-start | bytes 294920 | tf_op jit(solution)/shard_map/ppermute | solution.py:341
  70.1 17.5 %collective-permute-start.6 = (bf16[384,128]{1,0:T(8,128)(2,1)S(1)}, bf16[384,128]{1,0:T(8,128)(2,1)S(1)}, u32[]{:S(2)}, u32[]{:S(2)}) collective-permute-start(bf16[384,128]{1,0:T(8,128)(2,1)S(1)} %get-tuple-element.48), channel_id=1, source_target_pairs={{0,4},{4,0},{8,12},{12,8},{16,20},{20,16},{24,28},{28,24},{1,5},{5... | collective-permute-start | bytes 294920 | tf_op jit(solution)/shard_map/ppermute | solution.py:341
  70.1 17.5 %collective-permute-start.7 = (bf16[384,128]{1,0:T(8,128)(2,1)S(1)}, bf16[384,128]{1,0:T(8,128)(2,1)S(1)}, u32[]{:S(2)}, u32[]{:S(2)}) collective-permute-start(bf16[384,128]{1,0:T(8,128)(2,1)S(1)} %get-tuple-element.50), channel_id=1, source_target_pairs={{0,8},{4,12},{8,0},{12,4},{16,24},{20,28},{24,16},{28,20},{1,9},{5... | collective-permute-start | bytes 294920 | tf_op jit(solution)/shard_map/ppermute | solution.py:341
  74.4 13.1 %collective-permute-start.8 = (bf16[384,128]{1,0:T(8,128)(2,1)S(1)}, bf16[384,128]{1,0:T(8,128)(2,1)S(1)}, u32[]{:S(2)}, u32[]{:S(2)}) collective-permute-start(bf16[384,128]{1,0:T(8,128)(2,1)S(1)} %get-tuple-element.52), channel_id=1, source_target_pairs={{0,12},{4,8},{8,4},{12,0},{16,28},{20,24},{24,20},{28,16},{1,13},{... | collective-permute-start | bytes 294920 | tf_op jit(solution)/shard_map/ppermute | solution.py:341

commit v9 on v7

--- a/solution.py
+++ b/solution.py
@@ -228,108 +228,107 @@
     )(place, *virts)
 
 
-def stack_kernel(nw, wins, size, group, count_ref, me_ref, *refs):
+def stack_kernel(nw, wins, start, size, group, count_ref, me_ref, *refs):
     nsrc = nw // wins
     recvs, src_ref, lag_ref = refs[:nsrc], refs[nsrc], refs[nsrc + 1]
-    out_ref, lag, wide, turned, cross = refs[-5:]
-    step = pl.program_id(0)
+    out_ref, wide, turned, cross, held, sems = refs[-6:]
     width = SLOTS * VIRTUAL_SOURCES
     depth = 2 * nw
     pack = src_ref.shape[1] // depth
     full = pack * depth
     pitch, bpitch = size + 8, BINS + 8
 
-    @pl.when(step == 0)
-    def _():
-        lag[...] = lag_ref[...].astype(BF)
-        for m in range(nsrc):
-            src = me_ref[0] ^ m
-            for w in range(wins):
-                for p in range(2):
-                    row = pl.multiple_of((p * nw + src * wins + w) * pitch, 8)
-                    at = (w * 2 + p) * size
-                    wide[pl.ds(row, size), :] = recvs[m][at : at + size].astype(F32)
-
-        def turn(i, carry):
-            flat = wide[pl.ds(i, depth, stride=pitch), :]
-            flat = jnp.concatenate([flat] * pack, 0).T
-            if pack > 1:
-                flat = jnp.where(own, flat, 0.0)
-            for c in range(0, full, 128):
-                part = flat[:, c : min(c + 128, full)]
-                turned[c // 128, pl.ds(pl.multiple_of(i * bpitch, 8), BINS), 0 : part.shape[1]] = part
-            return carry
-
-        shape = (BINS, full)
-        own = lax.broadcasted_iota(jnp.int32, shape, 0) % pack == lax.broadcasted_iota(jnp.int32, shape, 1) // depth
-        lax.fori_loop(0, size, turn, 0, unroll=8)
-        slot = lax.broadcasted_iota(jnp.int32, (1, 2 * width), 1) % width // VIRTUAL_SOURCES
-        scale = jnp.where(slot < count_ref[0], 1.0 / math.sqrt(nw), 0.0).astype(F32)
-
-        def one(j, carry):
-            rows = []
-            for u in range(pack):
-                at = pl.ds(j * pack + u, size, stride=bpitch)
-                rows.append(jnp.concatenate([turned[c, at, :] for c in range(turned.shape[0])], 1))
-            left = jnp.concatenate(rows, 0)[:, :full].astype(BF)
-            value = dot(left, src_ref[j]) * scale
-            for u in range(pack):
-                at = pl.ds(pl.multiple_of((j * pack + u) * pitch, 8), size)
-                for p in range(2):
-                    cross[p, at, :] = value[u * size : (u + 1) * size, p * width : (p + 1) * width]
-            return carry
-
-        lax.fori_loop(0, BINS // pack, one, 0, unroll=8 // pack)
-
-    for q in range(0, group, 4):
-        lefts = []
-        for u in range(4):
-            at = step * group + q + u
-            tiles = [cross[p, pl.ds(at, BINS, stride=pitch), :].astype(BF).T for p in range(2)]
-            lefts.append(jnp.concatenate(tiles, 1))
-        value = dot(jnp.concatenate(lefts, 0), lag[...]).astype(BF)
-        for u in range(4):
-            for k in range(SLOTS):
-                at = u * width + k * VIRTUAL_SOURCES
-                out_ref[0, k, q + u] = value[at : at + VIRTUAL_SOURCES]
+    lag = lag_ref[...].astype(BF)
+    for m in range(nsrc):
+        src = me_ref[0] ^ m
+        for w in range(wins):
+            for p in range(2):
+                row = pl.multiple_of((p * nw + src * wins + w) * pitch, 8)
+                at = (w * 2 + p) * size
+                wide[pl.ds(row, size), :] = recvs[m][at : at + size].astype(F32)
+
+    shape = (BINS, full)
+    own = lax.broadcasted_iota(jnp.int32, shape, 0) % pack == lax.broadcasted_iota(jnp.int32, shape, 1) // depth
+
+    def turn(i, carry):
+        flat = wide[pl.ds(i, depth, stride=pitch), :]
+        flat = jnp.concatenate([flat] * pack, 0).T
+        if pack > 1:
+            flat = jnp.where(own, flat, 0.0)
+        for c in range(0, full, 128):
+            part = flat[:, c : min(c + 128, full)]
+            turned[c // 128, pl.ds(pl.multiple_of(i * bpitch, 8), BINS), 0 : part.shape[1]] = part
+        return carry
+
+    lax.fori_loop(0, size, turn, 0, unroll=8)
+    slot = lax.broadcasted_iota(jnp.int32, (1, 2 * width), 1) % width // VIRTUAL_SOURCES
+    scale = jnp.where(slot < count_ref[0], 1.0 / math.sqrt(nw), 0.0).astype(F32)
+
+    def one(j, carry):
+        rows = []
+        for u in range(pack):
+            at = pl.ds(j * pack + u, size, stride=bpitch)
+            rows.append(jnp.concatenate([turned[c, at, :] for c in range(turned.shape[0])], 1))
+        left = jnp.concatenate(rows, 0)[:, :full].astype(BF)
+        value = dot(left, src_ref[j]) * scale
+        for u in range(pack):
+            at = pl.ds(pl.multiple_of((j * pack + u) * pitch, 8), size)
+            for p in range(2):
+                cross[p, at, :] = value[u * size : (u + 1) * size, p * width : (p + 1) * width]
+        return carry
+
+    lax.fori_loop(0, BINS // pack, one, 0, unroll=8 // pack)
+
+    rows = 4
+    copies = []
+    for step in range(size // group):
+        for q in range(0, group, rows):
+            lefts = []
+            for u in range(rows):
+                at = step * group + q + u
+                tiles = [cross[p, pl.ds(at, BINS, stride=pitch), :].astype(BF).T for p in range(2)]
+                lefts.append(jnp.concatenate(tiles, 1))
+            value = dot(jnp.concatenate(lefts, 0), lag).astype(BF)
+            for u in range(rows):
+                for k in range(SLOTS):
+                    at = u * width + k * VIRTUAL_SOURCES
+                    held[step, k, q + u] = value[at : at + VIRTUAL_SOURCES]
+        target = out_ref.at[0, :, pl.ds(start + step * group, group)]
+        copies.append(pltpu.make_async_copy(held.at[step], target, sems.at[step]))
+        copies[-1].start()
+    for copy in copies:
+        copy.wait()
 
 
 def stack(recvs, table, count, me, lag, before, start, size, wins, chans):
     nw = wins * len(recvs)
-    group = 16
+    group = 8
     pack = 2 if 4 * nw <= 128 else 1
     table = table.reshape(BINS // pack, pack * 2 * nw, table.shape[2])
     shape = (1, SLOTS, chans, VIRTUAL_SOURCES, LAG_COUNT)
-    first = start // group
+    smem, vmem = pl.BlockSpec(memory_space=pltpu.SMEM), pl.BlockSpec(memory_space=pltpu.VMEM)
     operands = [count, me, *recvs, table, lag]
-    in_specs = [pl.BlockSpec(recv.shape, lambda t, c, e: (0, 0)) for recv in recvs] + [
-        pl.BlockSpec(table.shape, lambda t, c, e: (0,) * 3),
-        pl.BlockSpec(lag.shape, lambda t, c, e: (0, 0)),
-    ]
+    in_specs = [smem, smem] + [vmem] * (len(operands) - 2)
     aliases = {}
     if before is not None:
         operands.append(before)
         in_specs.append(pl.BlockSpec(memory_space=pl.ANY))
         aliases = {len(operands) - 1: 0}
+    steps = size // group
     return pl.pallas_call(
-        lambda *refs: stack_kernel(nw, wins, size, group, *refs),
-        grid_spec=pltpu.PrefetchScalarGridSpec(
-            num_scalar_prefetch=2,
-            grid=(size // group,),
-            in_specs=in_specs,
-            out_specs=pl.BlockSpec(
-                (1, SLOTS, group, VIRTUAL_SOURCES, LAG_COUNT), lambda t, c, e: (0, 0, first + t, 0, 0)
-            ),
-            scratch_shapes=[
-                pltpu.VMEM(lag.shape, BF),
-                pltpu.VMEM((2 * nw * (size + 8), BINS), F32),
-                pltpu.VMEM((-(-2 * nw * pack // 128), size * (BINS + 8), 128), F32),
-                pltpu.VMEM((2, BINS * (size + 8), SLOTS * VIRTUAL_SOURCES), F32),
-            ],
-        ),
+        lambda *refs: stack_kernel(nw, wins, start, size, group, *refs),
+        in_specs=in_specs,
+        out_specs=pl.BlockSpec(memory_space=pl.ANY),
+        scratch_shapes=[
+            pltpu.VMEM((2 * nw * (size + 8), BINS), F32),
+            pltpu.VMEM((-(-2 * nw * pack // 128), size * (BINS + 8), 128), F32),
+            pltpu.VMEM((2, BINS * (size + 8), SLOTS * VIRTUAL_SOURCES), F32),
+            pltpu.VMEM((steps, SLOTS, group, VIRTUAL_SOURCES, LAG_COUNT), BF),
+            pltpu.SemaphoreType.DMA((steps,)),
+        ],
         out_shape=jax.ShapeDtypeStruct(shape, BF),
         input_output_aliases=aliases,
-        compiler_params=pltpu.CompilerParams(vmem_limit_bytes=(20 + table.size * 4 // MIB) * MIB),
+        compiler_params=pltpu.CompilerParams(vmem_limit_bytes=32 * MIB),
         cost_estimate=pl.CostEstimate(
             flops=size * 128 * 256 * 256 * 4, bytes_accessed=2 * (table.size + size * 32768), transcendentals=0
         ),

time: 94 us -> 92.2 us (0.981)
  Pallas kernels: 26.4 us -> 24.6 us
    pallas_call x2, Pallas kernels: 17.6 us -> 15.8 us  [stack(): pl.pallas_call(lambda *refs: stack_kernel(nw, wins, start, size, group, *...]
  transfers between devices with their start and end apart: 20 -> 20, of which waited for: 5 -> 5; matrix products, arithmetic and copies ran while one was open for 2% -> 2% of each run, Pallas kernels for 19% -> 18%
where the time goes in v9:
time: 92.2 us; the launch traced here: 91.7 us
  starting transfers between devices  47.2 us (51%)
  Pallas kernels  24.6 us (27%)
  waiting for transfers between devices  11.9 us (13%)
  local copies, waits for them, and re-layouts  7.34 us (8%)
    ppermute x17, starting transfers between devices, swap(): lax.ppermute(value, axis, [(i, i ^ mask) for i in range(lax.axis_size(axi...  32.2 us
    pallas_call x2, Pallas kernels, stack(): pl.pallas_call(lambda *refs: stack_kernel(nw, wins, start, size, group, *...  15.8 us
    ppermute x17, waiting for transfers between devices, swap(): lax.ppermute(value, axis, [(i, i ^ mask) for i in range(lax.axis_size(axi...  8.25 us
    unnamed x11, local copies, waits for them, and re-layouts  6.26 us
    all_to_all x1, starting transfers between devices, on_device(): lax.all_to_all(picked, 'wide', split_axis=0, concat_axis=0, tiled=True)  5.72 us
    pallas_call x1, Pallas kernels, spectra(): pl.pallas_call(lambda *refs: spectra_kernel(sizes, *refs), in_specs=[smem...  5.25 us
    ppermute x1, starting transfers between devices, on_device(): tip = lax.ppermute(tip, 'wide', ahead)  4.98 us
    ppermute x1, starting transfers between devices, on_device(): lax.ppermute(after(records[:, :, time - HALF:], [tip]), 'wide', ahead)  4.24 us
  transfers between devices with their start and end apart: 20, of which 5 were waited for; matrix products, arithmetic and copies ran while one was open for 2% of the time, Pallas kernels for 18%

profile of v9, /device:TPU:0, one launch (start us, length us, event | category | flops | bytes accessed | tf_op | source)
XLA Modules:
  0.0 91.7 jit_solution(16755325614648634201)
XLA Ops:
  0.0 1.9 %copy-done = bf16[8,128,1536]{2,1,0:T(8,128)(2,1)S(1)} copy-done((bf16[8,128,1536]{2,1,0:T(8,128)(2,1)S(1)}, bf16[8,128,1536]{2,1,0:T(8,128)(2,1)}, u32[]{:S(2)}) %copy-start) | copy-done | bytes 3145752
  2.2 5.0 %collective-permute-start = (bf16[64,256]{1,0:T(8,128)(2,1)S(1)}, bf16[64,256]{1,0:T(8,128)(2,1)S(1)}, u32[]{:S(2)}, u32[]{:S(2)}) collective-permute-start(bf16[64,256]{1,0:T(8,128)(2,1)S(1)} %get-tuple-element.54), channel_id=1, source_target_pairs={{0,4},{4,8},{8,12},{12,16},{16,20},{20,24},{24,28},{1,5},{5,9},{9,... | collective-permute-start | bytes 98312 | tf_op jit(solution)/shard_map/ppermute | solution.py:358
  7.2 1.1 %slice.3 = bf16[8,128,256]{2,1,0:T(8,128)(2,1)S(1)} slice(bf16[8,128,1536]{2,1,0:T(8,128)(2,1)} %refs_1_.1), slice={[0:8], [0:128], [1280:1536]} | slice | bytes 1048576 | tf_op jit(solution)/shard_map/slice | solution.py:359
  8.8 4.2 %collective-permute-start.1 = (bf16[8,128,256]{2,1,0:T(8,128)(2,1)S(1)}, bf16[8,128,256]{2,1,0:T(8,128)(2,1)S(1)}, u32[]{:S(2)}, u32[]{:S(2)}) collective-permute-start(bf16[8,128,256]{2,1,0:T(8,128)(2,1)S(1)} %slice.3), channel_id=1, source_target_pairs={{0,4},{4,8},{8,12},{12,16},{16,20},{20,24},{24,28},{1,5},{5,9},{9,... | collective-permute-start | bytes 1572872 | tf_op jit(solution)/shard_map/ppermute | solution.py:359
  13.0 0.8 copy.8.refs_0_
  13.8 1.0 %copy-done.3 = f32[512,256]{1,0:T(8,128)S(1)} copy-done((f32[512,256]{1,0:T(8,128)S(1)}, f32[512,256]{1,0:T(8,128)}, u32[]{:S(2)}) %copy-start.3) | copy-done | bytes 524312
  14.8 0.7 copy-done.4
  15.5 2.0 %virtual.1 = (bf16[8,4,48,128]{3,2,1,0:T(8,128)(2,1)}, bf16[512,256]{1,0:T(8,128)(2,1)S(1)}, bf16[512,256]{1,0:T(8,128)(2,1)S(1)}) custom-call(s32[8,4]{1,0:T(8,128)S(1)} %copy.8.refs_0_, bf16[64,1536]{1,0:T(8,128)(2,1)S(1)} %get-tuple-element.53.refs_1_, bf16[64,256]{1,0:T(8,128)(2,1)S(1)} %collective-permute-done.refs_2_, f32[1,201]{1,0:T(1,128)S(1)} %bitcast.6, ...), custom_call_target="tpu_custom_call" | custom-call | flops 100000000 | bytes 786432 | tf_op jit(solution)/shard_map/virtual/pallas_call | solution.py:125
  17.4 5.7 %all-to-all-start = ((bf16[8,4,48,128]{3,2,1,0:T(8,128)(2,1)}), bf16[8,4,48,128]{3,2,1,0:T(8,128)(2,1)S(1)}, u32[]{:S(2)}, u32[]{:S(2)}) async-start(bf16[8,4,48,128]{3,2,1,0:T(8,128)(2,1)} %get-tuple-element.55), calls=%async_computation | async-start | bytes 786432 | tf_op jit(solution)/shard_map/all_to_all | solution.py:361
  23.2 0.9 collective-permute-done.1.refs_2_
  24.1 1.9 %copy-done.1 = bf16[8,128,1536]{2,1,0:T(8,128)(2,1)S(1)} copy-done((bf16[8,128,1536]{2,1,0:T(8,128)(2,1)S(1)}, bf16[8,128,1536]{2,1,0:T(8,128)(2,1)}, u32[]{:S(2)}) %copy-start.1) | copy-done | bytes 3145752
  26.0 5.3 %spectra.1 = (bf16[384,128]{1,0:T(8,128)(2,1)S(1)}, bf16[384,128]{1,0:T(8,128)(2,1)}, bf16[384,128]{1,0:T(8,128)(2,1)}, bf16[384,128]{1,0:T(8,128)(2,1)S(1)}, bf...) custom-call(s32[1]{0:T(128)} %bitcast.refs_0_.refs_1_, ...), custom_call_target="tpu_custom_call" | custom-call | flops 2415919104 | bytes 4718592 | tf_op jit(solution)/shard_map/spectra/pallas_call | solution.py:167
  31.2 2.2 %all-to-all-done.refs_1_ = bf16[8,4,48,128]{3,2,1,0:T(8,128)(2,1)S(1)} async-done(((bf16[8,4,48,128]{3,2,1,0:T(8,128)(2,1)}), bf16[8,4,48,128]{3,2,1,0:T(8,128)(2,1)S(1)}, u32[]{:S(2)}, u32[]{:S(2)}) %all-to-all-start) | async-done | bytes 393248 | tf_op jit(solution)/shard_map/all_to_all | solution.py:361
  33.4 5.2 %collective-permute-start.5 = (bf16[384,128]{1,0:T(8,128)(2,1)S(1)}, bf16[384,128]{1,0:T(8,128)(2,1)S(1)}, u32[]{:S(2)}, u32[]{:S(2)}) collective-permute-start(bf16[384,128]{1,0:T(8,128)(2,1)S(1)} %get-tuple-element.79), channel_id=1, source_target_pairs={{0,28},{4,24},{8,20},{12,16},{16,12},{20,8},{24,4},{28,0},{1,29},{... | collective-permute-start | bytes 294920 | tf_op jit(solution)/shard_map/ppermute | solution.py:340
  38.6 0.7 collective-permute-start.6
  39.3 4.7 %collective-permute-start.7 = (bf16[384,128]{1,0:T(8,128)(2,1)S(1)}, bf16[384,128]{1,0:T(8,128)(2,1)S(1)}, u32[]{:S(2)}, u32[]{:S(2)}) collective-permute-start(bf16[384,128]{1,0:T(8,128)(2,1)S(1)} %get-tuple-element.81), channel_id=1, source_target_pairs={{0,20},{4,16},{8,28},{12,24},{16,4},{20,0},{24,12},{28,8},{1,21},{... | collective-permute-start | bytes 294920 | tf_op jit(solution)/shard_map/ppermute | solution.py:340
  44.0 1.5 %collective-permute-start.4 = (bf16[8,4,48,128]{3,2,1,0:T(8,128)(2,1)S(1)}, bf16[8,4,48,128]{3,2,1,0:T(8,128)(2,1)S(1)}, u32[]{:S(2)}, u32[]{:S(2)}) collective-permute-start(bf16[8,4,48,128]{3,2,1,0:T(8,128)(2,1)S(1)} %all-to-all-done.refs_1_), channel_id=1, source_target_pairs={{0,2},{1,3},{2,0},{3,1},{4,6},{5,7},{6,4},{7,5},{8,10},{9,11},{10,... | collective-permute-start | bytes 1179656 | tf_op jit(solution)/shard_map/ppermute | solution.py:340
  45.5 7.7 %collective-permute-done.7.refs_7_ = bf16[384,128]{1,0:T(8,128)(2,1)S(1)} collective-permute-done((bf16[384,128]{1,0:T(8,128)(2,1)S(1)}, bf16[384,128]{1,0:T(8,128)(2,1)S(1)}, u32[]{:S(2)}, u32[]{:S(2)}) %collective-permute-start.7) | collective-permute-done | bytes 98336 | tf_op jit(solution)/shard_map/ppermute | solution.py:340
  53.2 1.5 %collective-permute-start.8 = (bf16[8,4,48,128]{3,2,1,0:T(8,128)(2,1)S(1)}, bf16[8,4,48,128]{3,2,1,0:T(8,128)(2,1)S(1)}, u32[]{:S(2)}, u32[]{:S(2)}) collective-permute-start(bf16[8,4,48,128]{3,2,1,0:T(8,128)(2,1)S(1)} %collective-permute-done.3.refs_2_), channel_id=1, source_target_pairs={{0,2},{1,3},{2,0},{3,1},{4,6},{5,7},{6,4},{7,5},{8,10},{9,11},{10,... | collective-permute-start | bytes 1179656 | tf_op jit(solution)/shard_map/ppermute | solution.py:340
  54.7 2.4 %collective-permute-start.14 = (bf16[384,128]{1,0:T(8,128)(2,1)S(1)}, bf16[384,128]{1,0:T(8,128)(2,1)S(1)}, u32[]{:S(2)}, u32[]{:S(2)}) collective-permute-start(bf16[384,128]{1,0:T(8,128)(2,1)S(1)} %get-tuple-element.93), channel_id=1, source_target_pairs={{0,12},{4,8},{8,4},{12,0},{16,28},{20,24},{24,20},{28,16},{1,13},{... | collective-permute-start | bytes 294920 | tf_op jit(solution)/shard_map/ppermute | solution.py:340
  57.1 2.7 %collective-permute-start.12 = (bf16[384,128]{1,0:T(8,128)(2,1)}, bf16[384,128]{1,0:T(8,128)(2,1)S(1)}, u32[]{:S(2)}, u32[]{:S(2)}) collective-permute-start(bf16[384,128]{1,0:T(8,128)(2,1)} %get-tuple-element.90), channel_id=1, source_target_pairs={{0,8},{4,12},{8,0},{12,4},{16,24},{20,28},{24,16},{28,20},{1,9},{5... | collective-permute-start | bytes 294920 | tf_op jit(solution)/shard_map/ppermute | solution.py:340
  59.8 1.5 %collective-permute-start.2 = (bf16[384,128]{1,0:T(8,128)(2,1)}, bf16[384,128]{1,0:T(8,128)(2,1)S(1)}, u32[]{:S(2)}, u32[]{:S(2)}) collective-permute-start(bf16[384,128]{1,0:T(8,128)(2,1)} %get-tuple-element.77), channel_id=1, source_target_pairs={{0,4},{4,0},{8,12},{12,8},{16,20},{20,16},{24,28},{28,24},{1,5},{5... | collective-permute-start | bytes 294920 | tf_op jit(solution)/shard_map/ppermute | solution.py:340
  61.2 0.5 collective-permute-done.16.refs_6_
  61.8 2.3 %collective-permute-start.18 = (bf16[384,128]{1,0:T(8,128)(2,1)}, bf16[384,128]{1,0:T(8,128)(2,1)S(1)}, u32[]{:S(2)}, u32[]{:S(2)}) collective-permute-start(bf16[384,128]{1,0:T(8,128)(2,1)} %get-tuple-element.99), channel_id=1, source_target_pairs={{0,28},{4,24},{8,20},{12,16},{16,12},{20,8},{24,4},{28,0},{1,29},{... | collective-permute-start | bytes 294920 | tf_op jit(solution)/shard_map/ppermute | solution.py:340
  64.1 3.0 %collective-permute-start.17 = (bf16[384,128]{1,0:T(8,128)(2,1)S(1)}, bf16[384,128]{1,0:T(8,128)(2,1)S(1)}, u32[]{:S(2)}, u32[]{:S(2)}) collective-permute-start(bf16[384,128]{1,0:T(8,128)(2,1)S(1)} %get-tuple-element.97), channel_id=1, source_target_pairs={{0,24},{4,28},{8,16},{12,20},{16,8},{20,12},{24,0},{28,4},{1,25},{... | collective-permute-start | bytes 294920 | tf_op jit(solution)/shard_map/ppermute | solution.py:340
  67.7 0.9 collective-permute-start.9
  68.6 2.7 %collective-permute-start.11 = (bf16[384,128]{1,0:T(8,128)(2,1)S(1)}, bf16[384,128]{1,0:T(8,128)(2,1)S(1)}, u32[]{:S(2)}, u32[]{:S(2)}) collective-permute-start(bf16[384,128]{1,0:T(8,128)(2,1)S(1)} %get-tuple-element.87), channel_id=1, source_target_pairs={{0,12},{4,8},{8,4},{12,0},{16,28},{20,24},{24,20},{28,16},{1,13},{... | collective-permute-start | bytes 294920 | tf_op jit(solution)/shard_map/ppermute | solution.py:340
  71.3 1.3 %sources.1 = bf16[128,48,256]{2,1,0:T(8,128)(2,1)S(1)} custom-call(s32[1]{0:T(128)} %bitcast.2.refs_0_, bf16[8,4,48,128]{3,2,1,0:T(8,128)(2,1)S(1)} %all-to-all-done.refs_1_, bf16[8,4,48,128]{3,2,1,0:T(8,128)(2,1)S(1)} %collective-permute-done.3.refs_2_, bf16[8,4,48,128]{3,2,1,0:T(8,128)(2,1)S(1)} %collective-permute-done.4.refs_3_, ...), custom_call_target="tpu_custom_call" | custom-call | flops 100000000 | bytes 6291456 | tf_op jit(solution)/shard_map/sources/pallas_call | solution.py:216
  72.6 0.7 collective-permute-start.13
  73.3 2.6 %collective-permute-start.15 = (bf16[384,128]{1,0:T(8,128)(2,1)S(1)}, bf16[384,128]{1,0:T(8,128)(2,1)S(1)}, u32[]{:S(2)}, u32[]{:S(2)}) collective-permute-start(bf16[384,128]{1,0:T(8,128)(2,1)S(1)} %get-tuple-element.94), channel_id=1, source_target_pairs={{0,20},{4,16},{8,28},{12,24},{16,4},{20,0},{24,12},{28,8},{1,21},{... | collective-permute-start | bytes 294920 | tf_op jit(solution)/shard_map/ppermute | solution.py:340
  75.9 7.9 %stack.2.refs_12_ = bf16[1,4,128,32,256]{4,3,2,1,0:T(8,128)(2,1)} custom-call(s32[1]{0:T(128)S(6)} %copy.10.refs_0_, s32[1]{0:T(128)} %bitcast.refs_0_.refs_1_, bf16[384,128]{1,0:T(8,128)(2,1)S(1)} %get-tuple-element.100.refs_2_, bf16[384,128]{1,0:T(8,128)(2,1)S(1)} %collective-permute-done.2.refs_3_, bf16[384,128]{1,0:T(8,128)(2,1)S(1)} %collective-permute-done.12.refs_4_, ...), custom_call_target="tpu_custom_call" | custom-call | flops 2147483648 | bytes 7340032 | tf_op jit(solution)/shard_map/stack/pallas_call | solution.py:318
  83.8 7.9 %stack.3 = bf16[1,4,128,32,256]{4,3,2,1,0:T(8,128)(2,1)} custom-call(s32[1]{0:T(128)S(6)} %copy.10.refs_0_, s32[1]{0:T(128)} %bitcast.refs_0_.refs_1_, bf16[384,128]{1,0:T(8,128)(2,1)S(1)} %get-tuple-element.75.refs_2_, bf16[384,128]{1,0:T(8,128)(2,1)S(1)} %collective-permute-done.9.refs_3_, ...), custom_call_target="tpu_custom_call", output_to_operand_aliasing={{}: (12, {})} | custom-call | flops 2147483648 | bytes 7340032 | tf_op jit(solution)/shard_map/stack/pallas_call | solution.py:318
  (26 shorter events, 0.8 us)
Async XLA Ops:
  0.0 1.9 %copy-start = (bf16[8,128,1536]{2,1,0:T(8,128)(2,1)S(1)}, bf16[8,128,1536]{2,1,0:T(8,128)(2,1)}, u32[]{:S(2)}) copy-start(bf16[8,128,1536]{2,1,0:T(8,128)(2,1)} %refs_1_.1) | copy-start | bytes 9437188
  2.2 73.7 %copy-start.2 = (f32[256,256]{1,0:T(8,128)S(1)}, f32[256,256]{1,0:T(8,128)}, u32[]{:S(2)}) copy-start(f32[256,256]{1,0:T(8,128)} %constant.14.clone.refs_11_) | copy-start | bytes 786436
  2.2 6.6 %collective-permute-start = (bf16[64,256]{1,0:T(8,128)(2,1)S(1)}, bf16[64,256]{1,0:T(8,128)(2,1)S(1)}, u32[]{:S(2)}, u32[]{:S(2)}) collective-permute-start(bf16[64,256]{1,0:T(8,128)(2,1)S(1)} %get-tuple-element.54), channel_id=1, source_target_pairs={{0,4},{4,8},{8,12},{12,16},{16,20},{20,24},{24,28},{1,5},{5,9},{9,... | collective-permute-start | bytes 98312 | tf_op jit(solution)/shard_map/ppermute | solution.py:358
  8.8 15.3 %collective-permute-start.1 = (bf16[8,128,256]{2,1,0:T(8,128)(2,1)S(1)}, bf16[8,128,256]{2,1,0:T(8,128)(2,1)S(1)}, u32[]{:S(2)}, u32[]{:S(2)}) collective-permute-start(bf16[8,128,256]{2,1,0:T(8,128)(2,1)S(1)} %slice.3), channel_id=1, source_target_pairs={{0,4},{4,8},{8,12},{12,16},{16,20},{20,24},{24,28},{1,5},{5,9},{9,... | collective-permute-start | bytes 1572872 | tf_op jit(solution)/shard_map/ppermute | solution.py:359
  13.8 1.0 %copy-start.3 = (f32[512,256]{1,0:T(8,128)S(1)}, f32[512,256]{1,0:T(8,128)}, u32[]{:S(2)}) copy-start(f32[512,256]{1,0:T(8,128)} %constant.13.clone.refs_4_) | copy-start | bytes 1572868
  14.8 0.7 copy-start.4
  17.4 16.0 %all-to-all-start = ((bf16[8,4,48,128]{3,2,1,0:T(8,128)(2,1)}), bf16[8,4,48,128]{3,2,1,0:T(8,128)(2,1)S(1)}, u32[]{:S(2)}, u32[]{:S(2)}) async-start(bf16[8,4,48,128]{3,2,1,0:T(8,128)(2,1)} %get-tuple-element.55), calls=%async_computation | async-start | bytes 786432 | tf_op jit(solution)/shard_map/all_to_all | solution.py:361
  24.1 1.9 %copy-start.1 = (bf16[8,128,1536]{2,1,0:T(8,128)(2,1)S(1)}, bf16[8,128,1536]{2,1,0:T(8,128)(2,1)}, u32[]{:S(2)}) copy-start(bf16[8,128,1536]{2,1,0:T(8,128)(2,1)} %refs_1_.1) | copy-start | bytes 9437188
  33.4 19.8 %collective-permute-start.3 = (bf16[8,4,48,128]{3,2,1,0:T(8,128)(2,1)S(1)}, bf16[8,4,48,128]{3,2,1,0:T(8,128)(2,1)S(1)}, u32[]{:S(2)}, u32[]{:S(2)}) collective-permute-start(bf16[8,4,48,128]{3,2,1,0:T(8,128)(2,1)S(1)} %all-to-all-done.refs_1_), channel_id=1, source_target_pairs={{0,1},{1,0},{2,3},{3,2},{4,5},{5,4},{6,7},{7,6},{8,9},{9,8},{10,11... | collective-permute-start | bytes 1179656 | tf_op jit(solution)/shard_map/ppermute | solution.py:340
  33.4 12.1 %collective-permute-start.5 = (bf16[384,128]{1,0:T(8,128)(2,1)S(1)}, bf16[384,128]{1,0:T(8,128)(2,1)S(1)}, u32[]{:S(2)}, u32[]{:S(2)}) collective-permute-start(bf16[384,128]{1,0:T(8,128)(2,1)S(1)} %get-tuple-element.79), channel_id=1, source_target_pairs={{0,28},{4,24},{8,20},{12,16},{16,12},{20,8},{24,4},{28,0},{1,29},{... | collective-permute-start | bytes 294920 | tf_op jit(solution)/shard_map/ppermute | solution.py:340
  38.6 6.9 %collective-permute-start.6 = (bf16[384,128]{1,0:T(8,128)(2,1)S(1)}, bf16[384,128]{1,0:T(8,128)(2,1)S(1)}, u32[]{:S(2)}, u32[]{:S(2)}) collective-permute-start(bf16[384,128]{1,0:T(8,128)(2,1)S(1)} %get-tuple-element.80), channel_id=1, source_target_pairs={{0,24},{4,28},{8,16},{12,20},{16,8},{20,12},{24,0},{28,4},{1,25},{... | collective-permute-start | bytes 294920 | tf_op jit(solution)/shard_map/ppermute | solution.py:340
  39.3 13.9 %collective-permute-start.7 = (bf16[384,128]{1,0:T(8,128)(2,1)S(1)}, bf16[384,128]{1,0:T(8,128)(2,1)S(1)}, u32[]{:S(2)}, u32[]{:S(2)}) collective-permute-start(bf16[384,128]{1,0:T(8,128)(2,1)S(1)} %get-tuple-element.81), channel_id=1, source_target_pairs={{0,20},{4,16},{8,28},{12,24},{16,4},{20,0},{24,12},{28,8},{1,21},{... | collective-permute-start | bytes 294920 | tf_op jit(solution)/shard_map/ppermute | solution.py:340
  44.0 13.1 %collective-permute-start.4 = (bf16[8,4,48,128]{3,2,1,0:T(8,128)(2,1)S(1)}, bf16[8,4,48,128]{3,2,1,0:T(8,128)(2,1)S(1)}, u32[]{:S(2)}, u32[]{:S(2)}) collective-permute-start(bf16[8,4,48,128]{3,2,1,0:T(8,128)(2,1)S(1)} %all-to-all-done.refs_1_), channel_id=1, source_target_pairs={{0,2},{1,3},{2,0},{3,1},{4,6},{5,7},{6,4},{7,5},{8,10},{9,11},{10,... | collective-permute-start | bytes 1179656 | tf_op jit(solution)/shard_map/ppermute | solution.py:340
  53.2 14.5 %collective-permute-start.8 = (bf16[8,4,48,128]{3,2,1,0:T(8,128)(2,1)S(1)}, bf16[8,4,48,128]{3,2,1,0:T(8,128)(2,1)S(1)}, u32[]{:S(2)}, u32[]{:S(2)}) collective-permute-start(bf16[8,4,48,128]{3,2,1,0:T(8,128)(2,1)S(1)} %collective-permute-done.3.refs_2_), channel_id=1, source_target_pairs={{0,2},{1,3},{2,0},{3,1},{4,6},{5,7},{6,4},{7,5},{8,10},{9,11},{10,... | collective-permute-start | bytes 1179656 | tf_op jit(solution)/shard_map/ppermute | solution.py:340
  54.7 7.1 %collective-permute-start.16 = (bf16[384,128]{1,0:T(8,128)(2,1)S(1)}, bf16[384,128]{1,0:T(8,128)(2,1)S(1)}, u32[]{:S(2)}, u32[]{:S(2)}) collective-permute-start(bf16[384,128]{1,0:T(8,128)(2,1)S(1)} %get-tuple-element.96), channel_id=1, source_target_pairs={{0,16},{4,20},{8,24},{12,28},{16,0},{20,4},{24,8},{28,12},{1,17},{... | collective-permute-start | bytes 294920 | tf_op jit(solution)/shard_map/ppermute | solution.py:340
  54.7 9.4 %collective-permute-start.14 = (bf16[384,128]{1,0:T(8,128)(2,1)S(1)}, bf16[384,128]{1,0:T(8,128)(2,1)S(1)}, u32[]{:S(2)}, u32[]{:S(2)}) collective-permute-start(bf16[384,128]{1,0:T(8,128)(2,1)S(1)} %get-tuple-element.93), channel_id=1, source_target_pairs={{0,12},{4,8},{8,4},{12,0},{16,28},{20,24},{24,20},{28,16},{1,13},{... | collective-permute-start | bytes 294920 | tf_op jit(solution)/shard_map/ppermute | solution.py:340
  57.1 10.7 %collective-permute-start.12 = (bf16[384,128]{1,0:T(8,128)(2,1)}, bf16[384,128]{1,0:T(8,128)(2,1)S(1)}, u32[]{:S(2)}, u32[]{:S(2)}) collective-permute-start(bf16[384,128]{1,0:T(8,128)(2,1)} %get-tuple-element.90), channel_id=1, source_target_pairs={{0,8},{4,12},{8,0},{12,4},{16,24},{20,28},{24,16},{28,20},{1,9},{5... | collective-permute-start | bytes 294920 | tf_op jit(solution)/shard_map/ppermute | solution.py:340
  59.8 8.0 %collective-permute-start.2 = (bf16[384,128]{1,0:T(8,128)(2,1)}, bf16[384,128]{1,0:T(8,128)(2,1)S(1)}, u32[]{:S(2)}, u32[]{:S(2)}) collective-permute-start(bf16[384,128]{1,0:T(8,128)(2,1)} %get-tuple-element.77), channel_id=1, source_target_pairs={{0,4},{4,0},{8,12},{12,8},{16,20},{20,16},{24,28},{28,24},{1,5},{5... | collective-permute-start | bytes 294920 | tf_op jit(solution)/shard_map/ppermute | solution.py:340
  61.8 10.8 %collective-permute-start.18 = (bf16[384,128]{1,0:T(8,128)(2,1)}, bf16[384,128]{1,0:T(8,128)(2,1)S(1)}, u32[]{:S(2)}, u32[]{:S(2)}) collective-permute-start(bf16[384,128]{1,0:T(8,128)(2,1)} %get-tuple-element.99), channel_id=1, source_target_pairs={{0,28},{4,24},{8,20},{12,16},{16,12},{20,8},{24,4},{28,0},{1,29},{... | collective-permute-start | bytes 294920 | tf_op jit(solution)/shard_map/ppermute | solution.py:340
  64.1 9.2 %collective-permute-start.17 = (bf16[384,128]{1,0:T(8,128)(2,1)S(1)}, bf16[384,128]{1,0:T(8,128)(2,1)S(1)}, u32[]{:S(2)}, u32[]{:S(2)}) collective-permute-start(bf16[384,128]{1,0:T(8,128)(2,1)S(1)} %get-tuple-element.97), channel_id=1, source_target_pairs={{0,24},{4,28},{8,16},{12,20},{16,8},{20,12},{24,0},{28,4},{1,25},{... | collective-permute-start | bytes 294920 | tf_op jit(solution)/shard_map/ppermute | solution.py:340
  67.7 16.1 %collective-permute-start.9 = (bf16[384,128]{1,0:T(8,128)(2,1)S(1)}, bf16[384,128]{1,0:T(8,128)(2,1)S(1)}, u32[]{:S(2)}, u32[]{:S(2)}) collective-permute-start(bf16[384,128]{1,0:T(8,128)(2,1)S(1)} %get-tuple-element.83), channel_id=1, source_target_pairs={{0,4},{4,0},{8,12},{12,8},{16,20},{20,16},{24,28},{28,24},{1,5},{5... | collective-permute-start | bytes 294920 | tf_op jit(solution)/shard_map/ppermute | solution.py:340
  68.6 15.2 %collective-permute-start.10 = (bf16[384,128]{1,0:T(8,128)(2,1)S(1)}, bf16[384,128]{1,0:T(8,128)(2,1)S(1)}, u32[]{:S(2)}, u32[]{:S(2)}) collective-permute-start(bf16[384,128]{1,0:T(8,128)(2,1)S(1)} %get-tuple-element.85), channel_id=1, source_target_pairs={{0,8},{4,12},{8,0},{12,4},{16,24},{20,28},{24,16},{28,20},{1,9},{5... | collective-permute-start | bytes 294920 | tf_op jit(solution)/shard_map/ppermute | solution.py:340
  68.6 15.2 %collective-permute-start.11 = (bf16[384,128]{1,0:T(8,128)(2,1)S(1)}, bf16[384,128]{1,0:T(8,128)(2,1)S(1)}, u32[]{:S(2)}, u32[]{:S(2)}) collective-permute-start(bf16[384,128]{1,0:T(8,128)(2,1)S(1)} %get-tuple-element.87), channel_id=1, source_target_pairs={{0,12},{4,8},{8,4},{12,0},{16,28},{20,24},{24,20},{28,16},{1,13},{... | collective-permute-start | bytes 294920 | tf_op jit(solution)/shard_map/ppermute | solution.py:340
  72.6 11.2 %collective-permute-start.13 = (bf16[384,128]{1,0:T(8,128)(2,1)S(1)}, bf16[384,128]{1,0:T(8,128)(2,1)S(1)}, u32[]{:S(2)}, u32[]{:S(2)}) collective-permute-start(bf16[384,128]{1,0:T(8,128)(2,1)S(1)} %get-tuple-element.91), channel_id=1, source_target_pairs={{0,16},{4,20},{8,24},{12,28},{16,0},{20,4},{24,8},{28,12},{1,17},{... | collective-permute-start | bytes 294920 | tf_op jit(solution)/shard_map/ppermute | solution.py:340
  73.3 10.5 %collective-permute-start.15 = (bf16[384,128]{1,0:T(8,128)(2,1)S(1)}, bf16[384,128]{1,0:T(8,128)(2,1)S(1)}, u32[]{:S(2)}, u32[]{:S(2)}) collective-permute-start(bf16[384,128]{1,0:T(8,128)(2,1)S(1)} %get-tuple-element.94), channel_id=1, source_target_pairs={{0,20},{4,16},{8,28},{12,24},{16,4},{20,0},{24,12},{28,8},{1,21},{... | collective-permute-start | bytes 294920 | tf_op jit(solution)/shard_map/ppermute | solution.py:340

commit v10 on v9

--- a/solution.py
+++ b/solution.py
@@ -143,7 +143,7 @@
     wins = time // WLEN
     outs = [refs[nblk * q : nblk * (q + 1)] for q in range(len(sizes))]
     me = me_ref[0]
-    per = 2
+    per = 4
     for m in range(0, nblk, per):
         blocks = [(halo_ref[me ^ (m + u)], rec_ref[me ^ (m + u)]) for u in range(per)]
         result = transform(blocks, wins, chans, toeplitz_ref[...], forward_ref[...]).astype(BF)
@@ -169,7 +169,7 @@
         in_specs=[smem] + [vmem] * 4,
         out_specs=[vmem] * len(shapes),
         out_shape=[jax.ShapeDtypeStruct(shape, BF) for shape in shapes],
-        compiler_params=pltpu.CompilerParams(vmem_limit_bytes=16 * MIB),
+        compiler_params=pltpu.CompilerParams(vmem_limit_bytes=24 * MIB),
         cost_estimate=pl.CostEstimate(
             flops=nblk * chans * wins * 3 * 2 * 512 * 256, bytes_accessed=nblk * chans * time * 3, transcendentals=0
         ),
@@ -277,7 +277,7 @@
                 cross[p, at, :] = value[u * size : (u + 1) * size, p * width : (p + 1) * width]
         return carry
 
-    lax.fori_loop(0, BINS // pack, one, 0, unroll=8 // pack)
+    lax.fori_loop(0, BINS // pack, one, 0, unroll=16 // pack)
 
     rows = 4
     copies = []

time: 92.2 us -> 89.8 us (0.974)
  Pallas kernels: 24.6 us -> 22.1 us
    pallas_call x2, Pallas kernels: 15.8 us -> 13.4 us  [stack(): pl.pallas_call(lambda *refs: stack_kernel(nw, wins, start, size, group, *...]
  transfers between devices with their start and end apart: 20 -> 20, of which waited for: 5 -> 6; matrix products, arithmetic and copies ran while one was open for 2% -> 2% of each run, Pallas kernels for 18% -> 17%
where the time goes in v10:
time: 89.8 us; the launch traced here: 89.4 us
  starting transfers between devices  47 us (52%)
  Pallas kernels  22.1 us (25%)
  waiting for transfers between devices  12.2 us (14%)
  local copies, waits for them, and re-layouts  7.34 us (8%)
    ppermute x17, starting transfers between devices, swap(): lax.ppermute(value, axis, [(i, i ^ mask) for i in range(lax.axis_size(axi...  32.1 us
    pallas_call x2, Pallas kernels, stack(): pl.pallas_call(lambda *refs: stack_kernel(nw, wins, start, size, group, *...  13.4 us
    ppermute x17, waiting for transfers between devices, swap(): lax.ppermute(value, axis, [(i, i ^ mask) for i in range(lax.axis_size(axi...  8.42 us
    unnamed x11, local copies, waits for them, and re-layouts  6.26 us
    all_to_all x1, starting transfers between devices, on_device(): lax.all_to_all(picked, 'wide', split_axis=0, concat_axis=0, tiled=True)  5.72 us
    pallas_call x1, Pallas kernels, spectra(): pl.pallas_call(lambda *refs: spectra_kernel(sizes, *refs), in_specs=[smem...  5.1 us
    ppermute x1, starting transfers between devices, on_device(): tip = lax.ppermute(tip, 'wide', ahead)  4.98 us
    ppermute x1, starting transfers between devices, on_device(): lax.ppermute(after(records[:, :, time - HALF:], [tip]), 'wide', ahead)  4.24 us
  transfers between devices with their start and end apart: 20, of which 6 were waited for; matrix products, arithmetic and copies ran while one was open for 2% of the time, Pallas kernels for 17%

profile of v10, /device:TPU:0, one launch (start us, length us, event | category | flops | bytes accessed | tf_op | source)
XLA Modules:
  0.0 89.4 jit_solution(17935727544154494604)
XLA Ops:
  0.0 1.9 %copy-done = bf16[8,128,1536]{2,1,0:T(8,128)(2,1)S(1)} copy-done((bf16[8,128,1536]{2,1,0:T(8,128)(2,1)S(1)}, bf16[8,128,1536]{2,1,0:T(8,128)(2,1)}, u32[]{:S(2)}) %copy-start) | copy-done | bytes 3145752
  2.2 5.0 %collective-permute-start = (bf16[64,256]{1,0:T(8,128)(2,1)S(1)}, bf16[64,256]{1,0:T(8,128)(2,1)S(1)}, u32[]{:S(2)}, u32[]{:S(2)}) collective-permute-start(bf16[64,256]{1,0:T(8,128)(2,1)S(1)} %get-tuple-element.54), channel_id=1, source_target_pairs={{0,4},{4,8},{8,12},{12,16},{16,20},{20,24},{24,28},{1,5},{5,9},{9,... | collective-permute-start | bytes 98312 | tf_op jit(solution)/shard_map/ppermute | solution.py:358
  7.2 1.1 %slice.3 = bf16[8,128,256]{2,1,0:T(8,128)(2,1)S(1)} slice(bf16[8,128,1536]{2,1,0:T(8,128)(2,1)} %refs_1_.1), slice={[0:8], [0:128], [1280:1536]} | slice | bytes 1048576 | tf_op jit(solution)/shard_map/slice | solution.py:359
  8.8 4.2 %collective-permute-start.1 = (bf16[8,128,256]{2,1,0:T(8,128)(2,1)S(1)}, bf16[8,128,256]{2,1,0:T(8,128)(2,1)S(1)}, u32[]{:S(2)}, u32[]{:S(2)}) collective-permute-start(bf16[8,128,256]{2,1,0:T(8,128)(2,1)S(1)} %slice.3), channel_id=1, source_target_pairs={{0,4},{4,8},{8,12},{12,16},{16,20},{20,24},{24,28},{1,5},{5,9},{9,... | collective-permute-start | bytes 1572872 | tf_op jit(solution)/shard_map/ppermute | solution.py:359
  13.0 0.8 copy.8.refs_0_
  13.8 1.0 %copy-done.3 = f32[512,256]{1,0:T(8,128)S(1)} copy-done((f32[512,256]{1,0:T(8,128)S(1)}, f32[512,256]{1,0:T(8,128)}, u32[]{:S(2)}) %copy-start.3) | copy-done | bytes 524312
  14.8 0.7 copy-done.4
  15.5 1.9 %virtual.1 = (bf16[8,4,48,128]{3,2,1,0:T(8,128)(2,1)}, bf16[512,256]{1,0:T(8,128)(2,1)S(1)}, bf16[512,256]{1,0:T(8,128)(2,1)S(1)}) custom-call(s32[8,4]{1,0:T(8,128)S(1)} %copy.8.refs_0_, bf16[64,1536]{1,0:T(8,128)(2,1)S(1)} %get-tuple-element.53.refs_1_, bf16[64,256]{1,0:T(8,128)(2,1)S(1)} %collective-permute-done.refs_2_, f32[1,201]{1,0:T(1,128)S(1)} %bitcast.6, ...), custom_call_target="tpu_custom_call" | custom-call | flops 100000000 | bytes 786432 | tf_op jit(solution)/shard_map/virtual/pallas_call | solution.py:125
  17.4 5.7 %all-to-all-start = ((bf16[8,4,48,128]{3,2,1,0:T(8,128)(2,1)}), bf16[8,4,48,128]{3,2,1,0:T(8,128)(2,1)S(1)}, u32[]{:S(2)}, u32[]{:S(2)}) async-start(bf16[8,4,48,128]{3,2,1,0:T(8,128)(2,1)} %get-tuple-element.55), calls=%async_computation | async-start | bytes 786432 | tf_op jit(solution)/shard_map/all_to_all | solution.py:361
  23.2 0.9 %collective-permute-done.1.refs_2_ = bf16[8,128,256]{2,1,0:T(8,128)(2,1)S(1)} collective-permute-done((bf16[8,128,256]{2,1,0:T(8,128)(2,1)S(1)}, bf16[8,128,256]{2,1,0:T(8,128)(2,1)S(1)}, u32[]{:S(2)}, u32[]{:S(2)}) %collective-permute-start.1) | collective-permute-done | bytes 524320 | tf_op jit(solution)/shard_map/ppermute | solution.py:359
  24.1 1.9 %copy-done.1 = bf16[8,128,1536]{2,1,0:T(8,128)(2,1)S(1)} copy-done((bf16[8,128,1536]{2,1,0:T(8,128)(2,1)S(1)}, bf16[8,128,1536]{2,1,0:T(8,128)(2,1)}, u32[]{:S(2)}) %copy-start.1) | copy-done | bytes 3145752
  26.0 5.1 %spectra.1 = (bf16[384,128]{1,0:T(8,128)(2,1)S(1)}, bf16[384,128]{1,0:T(8,128)(2,1)}, bf16[384,128]{1,0:T(8,128)(2,1)}, bf16[384,128]{1,0:T(8,128)(2,1)S(1)}, bf...) custom-call(s32[1]{0:T(128)} %bitcast.refs_0_.refs_1_, ...), custom_call_target="tpu_custom_call" | custom-call | flops 2415919104 | bytes 4718592 | tf_op jit(solution)/shard_map/spectra/pallas_call | solution.py:167
  31.1 2.3 %all-to-all-done.refs_1_ = bf16[8,4,48,128]{3,2,1,0:T(8,128)(2,1)S(1)} async-done(((bf16[8,4,48,128]{3,2,1,0:T(8,128)(2,1)}), bf16[8,4,48,128]{3,2,1,0:T(8,128)(2,1)S(1)}, u32[]{:S(2)}, u32[]{:S(2)}) %all-to-all-start) | async-done | bytes 393248 | tf_op jit(solution)/shard_map/all_to_all | solution.py:361
  33.4 5.1 %collective-permute-start.5 = (bf16[384,128]{1,0:T(8,128)(2,1)S(1)}, bf16[384,128]{1,0:T(8,128)(2,1)S(1)}, u32[]{:S(2)}, u32[]{:S(2)}) collective-permute-start(bf16[384,128]{1,0:T(8,128)(2,1)S(1)} %get-tuple-element.79), channel_id=1, source_target_pairs={{0,28},{4,24},{8,20},{12,16},{16,12},{20,8},{24,4},{28,0},{1,29},{... | collective-permute-start | bytes 294920 | tf_op jit(solution)/shard_map/ppermute | solution.py:340
  38.5 0.7 collective-permute-start.6
  39.1 4.7 %collective-permute-start.7 = (bf16[384,128]{1,0:T(8,128)(2,1)S(1)}, bf16[384,128]{1,0:T(8,128)(2,1)S(1)}, u32[]{:S(2)}, u32[]{:S(2)}) collective-permute-start(bf16[384,128]{1,0:T(8,128)(2,1)S(1)} %get-tuple-element.81), channel_id=1, source_target_pairs={{0,20},{4,16},{8,28},{12,24},{16,4},{20,0},{24,12},{28,8},{1,21},{... | collective-permute-start | bytes 294920 | tf_op jit(solution)/shard_map/ppermute | solution.py:340
  43.8 1.5 %collective-permute-start.4 = (bf16[8,4,48,128]{3,2,1,0:T(8,128)(2,1)S(1)}, bf16[8,4,48,128]{3,2,1,0:T(8,128)(2,1)S(1)}, u32[]{:S(2)}, u32[]{:S(2)}) collective-permute-start(bf16[8,4,48,128]{3,2,1,0:T(8,128)(2,1)S(1)} %all-to-all-done.refs_1_), channel_id=1, source_target_pairs={{0,2},{1,3},{2,0},{3,1},{4,6},{5,7},{6,4},{7,5},{8,10},{9,11},{10,... | collective-permute-start | bytes 1179656 | tf_op jit(solution)/shard_map/ppermute | solution.py:340
  45.4 7.7 %collective-permute-done.7.refs_7_ = bf16[384,128]{1,0:T(8,128)(2,1)S(1)} collective-permute-done((bf16[384,128]{1,0:T(8,128)(2,1)S(1)}, bf16[384,128]{1,0:T(8,128)(2,1)S(1)}, u32[]{:S(2)}, u32[]{:S(2)}) %collective-permute-start.7) | collective-permute-done | bytes 98336 | tf_op jit(solution)/shard_map/ppermute | solution.py:340
  53.0 1.5 %collective-permute-start.8 = (bf16[8,4,48,128]{3,2,1,0:T(8,128)(2,1)S(1)}, bf16[8,4,48,128]{3,2,1,0:T(8,128)(2,1)S(1)}, u32[]{:S(2)}, u32[]{:S(2)}) collective-permute-start(bf16[8,4,48,128]{3,2,1,0:T(8,128)(2,1)S(1)} %collective-permute-done.3.refs_2_), channel_id=1, source_target_pairs={{0,2},{1,3},{2,0},{3,1},{4,6},{5,7},{6,4},{7,5},{8,10},{9,11},{10,... | collective-permute-start | bytes 1179656 | tf_op jit(solution)/shard_map/ppermute | solution.py:340
  54.5 2.4 %collective-permute-start.14 = (bf16[384,128]{1,0:T(8,128)(2,1)S(1)}, bf16[384,128]{1,0:T(8,128)(2,1)S(1)}, u32[]{:S(2)}, u32[]{:S(2)}) collective-permute-start(bf16[384,128]{1,0:T(8,128)(2,1)S(1)} %get-tuple-element.93), channel_id=1, source_target_pairs={{0,12},{4,8},{8,4},{12,0},{16,28},{20,24},{24,20},{28,16},{1,13},{... | collective-permute-start | bytes 294920 | tf_op jit(solution)/shard_map/ppermute | solution.py:340
  56.9 2.7 %collective-permute-start.12 = (bf16[384,128]{1,0:T(8,128)(2,1)}, bf16[384,128]{1,0:T(8,128)(2,1)S(1)}, u32[]{:S(2)}, u32[]{:S(2)}) collective-permute-start(bf16[384,128]{1,0:T(8,128)(2,1)} %get-tuple-element.90), channel_id=1, source_target_pairs={{0,8},{4,12},{8,0},{12,4},{16,24},{20,28},{24,16},{28,20},{1,9},{5... | collective-permute-start | bytes 294920 | tf_op jit(solution)/shard_map/ppermute | solution.py:340
  59.6 1.5 %collective-permute-start.2 = (bf16[384,128]{1,0:T(8,128)(2,1)}, bf16[384,128]{1,0:T(8,128)(2,1)S(1)}, u32[]{:S(2)}, u32[]{:S(2)}) collective-permute-start(bf16[384,128]{1,0:T(8,128)(2,1)} %get-tuple-element.77), channel_id=1, source_target_pairs={{0,4},{4,0},{8,12},{12,8},{16,20},{20,16},{24,28},{28,24},{1,5},{5... | collective-permute-start | bytes 294920 | tf_op jit(solution)/shard_map/ppermute | solution.py:340
  61.1 0.5 collective-permute-done.16.refs_6_
  61.6 2.3 %collective-permute-start.18 = (bf16[384,128]{1,0:T(8,128)(2,1)}, bf16[384,128]{1,0:T(8,128)(2,1)S(1)}, u32[]{:S(2)}, u32[]{:S(2)}) collective-permute-start(bf16[384,128]{1,0:T(8,128)(2,1)} %get-tuple-element.99), channel_id=1, source_target_pairs={{0,28},{4,24},{8,20},{12,16},{16,12},{20,8},{24,4},{28,0},{1,29},{... | collective-permute-start | bytes 294920 | tf_op jit(solution)/shard_map/ppermute | solution.py:340
  63.9 3.0 %collective-permute-start.17 = (bf16[384,128]{1,0:T(8,128)(2,1)S(1)}, bf16[384,128]{1,0:T(8,128)(2,1)S(1)}, u32[]{:S(2)}, u32[]{:S(2)}) collective-permute-start(bf16[384,128]{1,0:T(8,128)(2,1)S(1)} %get-tuple-element.97), channel_id=1, source_target_pairs={{0,24},{4,28},{8,16},{12,20},{16,8},{20,12},{24,0},{28,4},{1,25},{... | collective-permute-start | bytes 294920 | tf_op jit(solution)/shard_map/ppermute | solution.py:340
  67.6 0.9 %collective-permute-start.9 = (bf16[384,128]{1,0:T(8,128)(2,1)S(1)}, bf16[384,128]{1,0:T(8,128)(2,1)S(1)}, u32[]{:S(2)}, u32[]{:S(2)}) collective-permute-start(bf16[384,128]{1,0:T(8,128)(2,1)S(1)} %get-tuple-element.83), channel_id=1, source_target_pairs={{0,4},{4,0},{8,12},{12,8},{16,20},{20,16},{24,28},{28,24},{1,5},{5... | collective-permute-start | bytes 294920 | tf_op jit(solution)/shard_map/ppermute | solution.py:340
  68.5 2.7 %collective-permute-start.11 = (bf16[384,128]{1,0:T(8,128)(2,1)S(1)}, bf16[384,128]{1,0:T(8,128)(2,1)S(1)}, u32[]{:S(2)}, u32[]{:S(2)}) collective-permute-start(bf16[384,128]{1,0:T(8,128)(2,1)S(1)} %get-tuple-element.87), channel_id=1, source_target_pairs={{0,12},{4,8},{8,4},{12,0},{16,28},{20,24},{24,20},{28,16},{1,13},{... | collective-permute-start | bytes 294920 | tf_op jit(solution)/shard_map/ppermute | solution.py:340
  71.1 1.3 %sources.1 = bf16[128,48,256]{2,1,0:T(8,128)(2,1)S(1)} custom-call(s32[1]{0:T(128)} %bitcast.2.refs_0_, bf16[8,4,48,128]{3,2,1,0:T(8,128)(2,1)S(1)} %all-to-all-done.refs_1_, bf16[8,4,48,128]{3,2,1,0:T(8,128)(2,1)S(1)} %collective-permute-done.3.refs_2_, bf16[8,4,48,128]{3,2,1,0:T(8,128)(2,1)S(1)} %collective-permute-done.4.refs_3_, ...), custom_call_target="tpu_custom_call" | custom-call | flops 100000000 | bytes 6291456 | tf_op jit(solution)/shard_map/sources/pallas_call | solution.py:216
  72.5 0.7 collective-permute-start.13
  73.2 2.6 %collective-permute-start.15 = (bf16[384,128]{1,0:T(8,128)(2,1)S(1)}, bf16[384,128]{1,0:T(8,128)(2,1)S(1)}, u32[]{:S(2)}, u32[]{:S(2)}) collective-permute-start(bf16[384,128]{1,0:T(8,128)(2,1)S(1)} %get-tuple-element.94), channel_id=1, source_target_pairs={{0,20},{4,16},{8,28},{12,24},{16,4},{20,0},{24,12},{28,8},{1,21},{... | collective-permute-start | bytes 294920 | tf_op jit(solution)/shard_map/ppermute | solution.py:340
  75.7 6.7 %stack.2.refs_12_ = bf16[1,4,128,32,256]{4,3,2,1,0:T(8,128)(2,1)} custom-call(s32[1]{0:T(128)S(6)} %copy.10.refs_0_, s32[1]{0:T(128)} %bitcast.refs_0_.refs_1_, bf16[384,128]{1,0:T(8,128)(2,1)S(1)} %get-tuple-element.100.refs_2_, bf16[384,128]{1,0:T(8,128)(2,1)S(1)} %collective-permute-done.2.refs_3_, bf16[384,128]{1,0:T(8,128)(2,1)S(1)} %collective-permute-done.12.refs_4_, ...), custom_call_target="tpu_custom_call" | custom-call | flops 2147483648 | bytes 7340032 | tf_op jit(solution)/shard_map/stack/pallas_call | solution.py:318
  82.7 6.7 %stack.3 = bf16[1,4,128,32,256]{4,3,2,1,0:T(8,128)(2,1)} custom-call(s32[1]{0:T(128)S(6)} %copy.10.refs_0_, s32[1]{0:T(128)} %bitcast.refs_0_.refs_1_, bf16[384,128]{1,0:T(8,128)(2,1)S(1)} %get-tuple-element.75.refs_2_, bf16[384,128]{1,0:T(8,128)(2,1)S(1)} %collective-permute-done.9.refs_3_, ...), custom_call_target="tpu_custom_call", output_to_operand_aliasing={{}: (12, {})} | custom-call | flops 2147483648 | bytes 7340032 | tf_op jit(solution)/shard_map/stack/pallas_call | solution.py:318
  (26 shorter events, 1.0 us)
Async XLA Ops:
  0.0 1.9 %copy-start = (bf16[8,128,1536]{2,1,0:T(8,128)(2,1)S(1)}, bf16[8,128,1536]{2,1,0:T(8,128)(2,1)}, u32[]{:S(2)}) copy-start(bf16[8,128,1536]{2,1,0:T(8,128)(2,1)} %refs_1_.1) | copy-start | bytes 9437188
  2.2 73.5 %copy-start.2 = (f32[256,256]{1,0:T(8,128)S(1)}, f32[256,256]{1,0:T(8,128)}, u32[]{:S(2)}) copy-start(f32[256,256]{1,0:T(8,128)} %constant.14.clone.refs_11_) | copy-start | bytes 786436
  2.2 6.6 %collective-permute-start = (bf16[64,256]{1,0:T(8,128)(2,1)S(1)}, bf16[64,256]{1,0:T(8,128)(2,1)S(1)}, u32[]{:S(2)}, u32[]{:S(2)}) collective-permute-start(bf16[64,256]{1,0:T(8,128)(2,1)S(1)} %get-tuple-element.54), channel_id=1, source_target_pairs={{0,4},{4,8},{8,12},{12,16},{16,20},{20,24},{24,28},{1,5},{5,9},{9,... | collective-permute-start | bytes 98312 | tf_op jit(solution)/shard_map/ppermute | solution.py:358
  8.8 15.3 %collective-permute-start.1 = (bf16[8,128,256]{2,1,0:T(8,128)(2,1)S(1)}, bf16[8,128,256]{2,1,0:T(8,128)(2,1)S(1)}, u32[]{:S(2)}, u32[]{:S(2)}) collective-permute-start(bf16[8,128,256]{2,1,0:T(8,128)(2,1)S(1)} %slice.3), channel_id=1, source_target_pairs={{0,4},{4,8},{8,12},{12,16},{16,20},{20,24},{24,28},{1,5},{5,9},{9,... | collective-permute-start | bytes 1572872 | tf_op jit(solution)/shard_map/ppermute | solution.py:359
  13.8 1.0 %copy-start.3 = (f32[512,256]{1,0:T(8,128)S(1)}, f32[512,256]{1,0:T(8,128)}, u32[]{:S(2)}) copy-start(f32[512,256]{1,0:T(8,128)} %constant.13.clone.refs_4_) | copy-start | bytes 1572868
  14.8 0.7 copy-start.4
  17.4 16.0 %all-to-all-start = ((bf16[8,4,48,128]{3,2,1,0:T(8,128)(2,1)}), bf16[8,4,48,128]{3,2,1,0:T(8,128)(2,1)S(1)}, u32[]{:S(2)}, u32[]{:S(2)}) async-start(bf16[8,4,48,128]{3,2,1,0:T(8,128)(2,1)} %get-tuple-element.55), calls=%async_computation | async-start | bytes 786432 | tf_op jit(solution)/shard_map/all_to_all | solution.py:361
  24.1 1.9 %copy-start.1 = (bf16[8,128,1536]{2,1,0:T(8,128)(2,1)S(1)}, bf16[8,128,1536]{2,1,0:T(8,128)(2,1)}, u32[]{:S(2)}) copy-start(bf16[8,128,1536]{2,1,0:T(8,128)(2,1)} %refs_1_.1) | copy-start | bytes 9437188
  33.4 19.6 %collective-permute-start.3 = (bf16[8,4,48,128]{3,2,1,0:T(8,128)(2,1)S(1)}, bf16[8,4,48,128]{3,2,1,0:T(8,128)(2,1)S(1)}, u32[]{:S(2)}, u32[]{:S(2)}) collective-permute-start(bf16[8,4,48,128]{3,2,1,0:T(8,128)(2,1)S(1)} %all-to-all-done.refs_1_), channel_id=1, source_target_pairs={{0,1},{1,0},{2,3},{3,2},{4,5},{5,4},{6,7},{7,6},{8,9},{9,8},{10,11... | collective-permute-start | bytes 1179656 | tf_op jit(solution)/shard_map/ppermute | solution.py:340
  33.4 11.9 %collective-permute-start.5 = (bf16[384,128]{1,0:T(8,128)(2,1)S(1)}, bf16[384,128]{1,0:T(8,128)(2,1)S(1)}, u32[]{:S(2)}, u32[]{:S(2)}) collective-permute-start(bf16[384,128]{1,0:T(8,128)(2,1)S(1)} %get-tuple-element.79), channel_id=1, source_target_pairs={{0,28},{4,24},{8,20},{12,16},{16,12},{20,8},{24,4},{28,0},{1,29},{... | collective-permute-start | bytes 294920 | tf_op jit(solution)/shard_map/ppermute | solution.py:340
  38.5 6.9 %collective-permute-start.6 = (bf16[384,128]{1,0:T(8,128)(2,1)S(1)}, bf16[384,128]{1,0:T(8,128)(2,1)S(1)}, u32[]{:S(2)}, u32[]{:S(2)}) collective-permute-start(bf16[384,128]{1,0:T(8,128)(2,1)S(1)} %get-tuple-element.80), channel_id=1, source_target_pairs={{0,24},{4,28},{8,16},{12,20},{16,8},{20,12},{24,0},{28,4},{1,25},{... | collective-permute-start | bytes 294920 | tf_op jit(solution)/shard_map/ppermute | solution.py:340
  39.1 13.9 %collective-permute-start.7 = (bf16[384,128]{1,0:T(8,128)(2,1)S(1)}, bf16[384,128]{1,0:T(8,128)(2,1)S(1)}, u32[]{:S(2)}, u32[]{:S(2)}) collective-permute-start(bf16[384,128]{1,0:T(8,128)(2,1)S(1)} %get-tuple-element.81), channel_id=1, source_target_pairs={{0,20},{4,16},{8,28},{12,24},{16,4},{20,0},{24,12},{28,8},{1,21},{... | collective-permute-start | bytes 294920 | tf_op jit(solution)/shard_map/ppermute | solution.py:340
  43.8 13.1 %collective-permute-start.4 = (bf16[8,4,48,128]{3,2,1,0:T(8,128)(2,1)S(1)}, bf16[8,4,48,128]{3,2,1,0:T(8,128)(2,1)S(1)}, u32[]{:S(2)}, u32[]{:S(2)}) collective-permute-start(bf16[8,4,48,128]{3,2,1,0:T(8,128)(2,1)S(1)} %all-to-all-done.refs_1_), channel_id=1, source_target_pairs={{0,2},{1,3},{2,0},{3,1},{4,6},{5,7},{6,4},{7,5},{8,10},{9,11},{10,... | collective-permute-start | bytes 1179656 | tf_op jit(solution)/shard_map/ppermute | solution.py:340
  53.0 14.5 %collective-permute-start.8 = (bf16[8,4,48,128]{3,2,1,0:T(8,128)(2,1)S(1)}, bf16[8,4,48,128]{3,2,1,0:T(8,128)(2,1)S(1)}, u32[]{:S(2)}, u32[]{:S(2)}) collective-permute-start(bf16[8,4,48,128]{3,2,1,0:T(8,128)(2,1)S(1)} %collective-permute-done.3.refs_2_), channel_id=1, source_target_pairs={{0,2},{1,3},{2,0},{3,1},{4,6},{5,7},{6,4},{7,5},{8,10},{9,11},{10,... | collective-permute-start | bytes 1179656 | tf_op jit(solution)/shard_map/ppermute | solution.py:340
  54.5 7.1 %collective-permute-start.16 = (bf16[384,128]{1,0:T(8,128)(2,1)S(1)}, bf16[384,128]{1,0:T(8,128)(2,1)S(1)}, u32[]{:S(2)}, u32[]{:S(2)}) collective-permute-start(bf16[384,128]{1,0:T(8,128)(2,1)S(1)} %get-tuple-element.96), channel_id=1, source_target_pairs={{0,16},{4,20},{8,24},{12,28},{16,0},{20,4},{24,8},{28,12},{1,17},{... | collective-permute-start | bytes 294920 | tf_op jit(solution)/shard_map/ppermute | solution.py:340
  54.5 9.4 %collective-permute-start.14 = (bf16[384,128]{1,0:T(8,128)(2,1)S(1)}, bf16[384,128]{1,0:T(8,128)(2,1)S(1)}, u32[]{:S(2)}, u32[]{:S(2)}) collective-permute-start(bf16[384,128]{1,0:T(8,128)(2,1)S(1)} %get-tuple-element.93), channel_id=1, source_target_pairs={{0,12},{4,8},{8,4},{12,0},{16,28},{20,24},{24,20},{28,16},{1,13},{... | collective-permute-start | bytes 294920 | tf_op jit(solution)/shard_map/ppermute | solution.py:340
  56.9 10.7 %collective-permute-start.12 = (bf16[384,128]{1,0:T(8,128)(2,1)}, bf16[384,128]{1,0:T(8,128)(2,1)S(1)}, u32[]{:S(2)}, u32[]{:S(2)}) collective-permute-start(bf16[384,128]{1,0:T(8,128)(2,1)} %get-tuple-element.90), channel_id=1, source_target_pairs={{0,8},{4,12},{8,0},{12,4},{16,24},{20,28},{24,16},{28,20},{1,9},{5... | collective-permute-start | bytes 294920 | tf_op jit(solution)/shard_map/ppermute | solution.py:340
  59.6 8.0 %collective-permute-start.2 = (bf16[384,128]{1,0:T(8,128)(2,1)}, bf16[384,128]{1,0:T(8,128)(2,1)S(1)}, u32[]{:S(2)}, u32[]{:S(2)}) collective-permute-start(bf16[384,128]{1,0:T(8,128)(2,1)} %get-tuple-element.77), channel_id=1, source_target_pairs={{0,4},{4,0},{8,12},{12,8},{16,20},{20,16},{24,28},{28,24},{1,5},{5... | collective-permute-start | bytes 294920 | tf_op jit(solution)/shard_map/ppermute | solution.py:340
  61.6 10.8 %collective-permute-start.18 = (bf16[384,128]{1,0:T(8,128)(2,1)}, bf16[384,128]{1,0:T(8,128)(2,1)S(1)}, u32[]{:S(2)}, u32[]{:S(2)}) collective-permute-start(bf16[384,128]{1,0:T(8,128)(2,1)} %get-tuple-element.99), channel_id=1, source_target_pairs={{0,28},{4,24},{8,20},{12,16},{16,12},{20,8},{24,4},{28,0},{1,29},{... | collective-permute-start | bytes 294920 | tf_op jit(solution)/shard_map/ppermute | solution.py:340
  63.9 9.2 %collective-permute-start.17 = (bf16[384,128]{1,0:T(8,128)(2,1)S(1)}, bf16[384,128]{1,0:T(8,128)(2,1)S(1)}, u32[]{:S(2)}, u32[]{:S(2)}) collective-permute-start(bf16[384,128]{1,0:T(8,128)(2,1)S(1)} %get-tuple-element.97), channel_id=1, source_target_pairs={{0,24},{4,28},{8,16},{12,20},{16,8},{20,12},{24,0},{28,4},{1,25},{... | collective-permute-start | bytes 294920 | tf_op jit(solution)/shard_map/ppermute | solution.py:340
  67.6 14.9 %collective-permute-start.9 = (bf16[384,128]{1,0:T(8,128)(2,1)S(1)}, bf16[384,128]{1,0:T(8,128)(2,1)S(1)}, u32[]{:S(2)}, u32[]{:S(2)}) collective-permute-start(bf16[384,128]{1,0:T(8,128)(2,1)S(1)} %get-tuple-element.83), channel_id=1, source_target_pairs={{0,4},{4,0},{8,12},{12,8},{16,20},{20,16},{24,28},{28,24},{1,5},{5... | collective-permute-start | bytes 294920 | tf_op jit(solution)/shard_map/ppermute | solution.py:340
  68.5 14.0 %collective-permute-start.10 = (bf16[384,128]{1,0:T(8,128)(2,1)S(1)}, bf16[384,128]{1,0:T(8,128)(2,1)S(1)}, u32[]{:S(2)}, u32[]{:S(2)}) collective-permute-start(bf16[384,128]{1,0:T(8,128)(2,1)S(1)} %get-tuple-element.85), channel_id=1, source_target_pairs={{0,8},{4,12},{8,0},{12,4},{16,24},{20,28},{24,16},{28,20},{1,9},{5... | collective-permute-start | bytes 294920 | tf_op jit(solution)/shard_map/ppermute | solution.py:340
  68.5 14.0 %collective-permute-start.11 = (bf16[384,128]{1,0:T(8,128)(2,1)S(1)}, bf16[384,128]{1,0:T(8,128)(2,1)S(1)}, u32[]{:S(2)}, u32[]{:S(2)}) collective-permute-start(bf16[384,128]{1,0:T(8,128)(2,1)S(1)} %get-tuple-element.87), channel_id=1, source_target_pairs={{0,12},{4,8},{8,4},{12,0},{16,28},{20,24},{24,20},{28,16},{1,13},{... | collective-permute-start | bytes 294920 | tf_op jit(solution)/shard_map/ppermute | solution.py:340
  72.5 10.0 %collective-permute-start.13 = (bf16[384,128]{1,0:T(8,128)(2,1)S(1)}, bf16[384,128]{1,0:T(8,128)(2,1)S(1)}, u32[]{:S(2)}, u32[]{:S(2)}) collective-permute-start(bf16[384,128]{1,0:T(8,128)(2,1)S(1)} %get-tuple-element.91), channel_id=1, source_target_pairs={{0,16},{4,20},{8,24},{12,28},{16,0},{20,4},{24,8},{28,12},{1,17},{... | collective-permute-start | bytes 294920 | tf_op jit(solution)/shard_map/ppermute | solution.py:340
  73.2 9.5 %collective-permute-start.15 = (bf16[384,128]{1,0:T(8,128)(2,1)S(1)}, bf16[384,128]{1,0:T(8,128)(2,1)S(1)}, u32[]{:S(2)}, u32[]{:S(2)}) collective-permute-start(bf16[384,128]{1,0:T(8,128)(2,1)S(1)} %get-tuple-element.94), channel_id=1, source_target_pairs={{0,20},{4,16},{8,28},{12,24},{16,4},{20,0},{24,12},{28,8},{1,21},{... | collective-permute-start | bytes 294920 | tf_op jit(solution)/shard_map/ppermute | solution.py:340

commit v11 on v10

--- a/solution.py
+++ b/solution.py
@@ -260,7 +260,7 @@
             turned[c // 128, pl.ds(pl.multiple_of(i * bpitch, 8), BINS), 0 : part.shape[1]] = part
         return carry
 
-    lax.fori_loop(0, size, turn, 0, unroll=8)
+    lax.fori_loop(0, size, turn, 0, unroll=16)
     slot = lax.broadcasted_iota(jnp.int32, (1, 2 * width), 1) % width // VIRTUAL_SOURCES
     scale = jnp.where(slot < count_ref[0], 1.0 / math.sqrt(nw), 0.0).astype(F32)
 
@@ -277,7 +277,7 @@
                 cross[p, at, :] = value[u * size : (u + 1) * size, p * width : (p + 1) * width]
         return carry
 
-    lax.fori_loop(0, BINS // pack, one, 0, unroll=16 // pack)
+    lax.fori_loop(0, BINS // pack, one, 0, unroll=32 // pack)
 
     rows = 4
     copies = []

time: 89.8 us -> 88.9 us (0.990)
  Pallas kernels: 22.1 us -> 20.3 us
  waiting for transfers between devices: 12.2 us -> 13.1 us
    pallas_call x2, Pallas kernels: 13.4 us -> 11.6 us  [stack(): pl.pallas_call(lambda *refs: stack_kernel(nw, wins, start, size, group, *...]
    ppermute x17, waiting for transfers between devices: 8.42 us -> 9.33 us  [swap(): lax.ppermute(value, axis, [(i, i ^ mask) for i in range(lax.axis_size(axi...]
  transfers between devices with their start and end apart: 20 -> 20, of which waited for: 6 -> 7; matrix products, arithmetic and copies ran while one was open for 2% -> 2% of each run, Pallas kernels for 17% -> 16%
where the time goes in v11:
time: 88.9 us; the launch traced here: 88.5 us
  starting transfers between devices  47 us (53%)
  Pallas kernels  20.3 us (23%)
  waiting for transfers between devices  13.1 us (15%)
  local copies, waits for them, and re-layouts  7.34 us (8%)
    ppermute x17, starting transfers between devices, swap(): lax.ppermute(value, axis, [(i, i ^ mask) for i in range(lax.axis_size(axi...  32.1 us
    pallas_call x2, Pallas kernels, stack(): pl.pallas_call(lambda *refs: stack_kernel(nw, wins, start, size, group, *...  11.6 us
    ppermute x17, waiting for transfers between devices, swap(): lax.ppermute(value, axis, [(i, i ^ mask) for i in range(lax.axis_size(axi...  9.33 us
    unnamed x11, local copies, waits for them, and re-layouts  6.26 us
    all_to_all x1, starting transfers between devices, on_device(): lax.all_to_all(picked, 'wide', split_axis=0, concat_axis=0, tiled=True)  5.72 us
    pallas_call x1, Pallas kernels, spectra(): pl.pallas_call(lambda *refs: spectra_kernel(sizes, *refs), in_specs=[smem...  5.1 us
    ppermute x1, starting transfers between devices, on_device(): tip = lax.ppermute(tip, 'wide', ahead)  4.98 us
    ppermute x1, starting transfers between devices, on_device(): lax.ppermute(after(records[:, :, time - HALF:], [tip]), 'wide', ahead)  4.24 us
  transfers between devices with their start and end apart: 20, of which 7 were waited for; matrix products, arithmetic and copies ran while one was open for 2% of the time, Pallas kernels for 16%

profile of v11, /device:TPU:0, one launch (start us, length us, event | category | flops | bytes accessed | tf_op | source)
XLA Modules:
  0.0 88.5 jit_solution(8442346667997757627)
XLA Ops:
  0.0 1.9 %copy-done = bf16[8,128,1536]{2,1,0:T(8,128)(2,1)S(1)} copy-done((bf16[8,128,1536]{2,1,0:T(8,128)(2,1)S(1)}, bf16[8,128,1536]{2,1,0:T(8,128)(2,1)}, u32[]{:S(2)}) %copy-start) | copy-done | bytes 3145752
  2.2 5.0 %collective-permute-start = (bf16[64,256]{1,0:T(8,128)(2,1)S(1)}, bf16[64,256]{1,0:T(8,128)(2,1)S(1)}, u32[]{:S(2)}, u32[]{:S(2)}) collective-permute-start(bf16[64,256]{1,0:T(8,128)(2,1)S(1)} %get-tuple-element.54), channel_id=1, source_target_pairs={{0,4},{4,8},{8,12},{12,16},{16,20},{20,24},{24,28},{1,5},{5,9},{9,... | collective-permute-start | bytes 98312 | tf_op jit(solution)/shard_map/ppermute | solution.py:358
  7.2 1.1 %slice.3 = bf16[8,128,256]{2,1,0:T(8,128)(2,1)S(1)} slice(bf16[8,128,1536]{2,1,0:T(8,128)(2,1)} %refs_1_.1), slice={[0:8], [0:128], [1280:1536]} | slice | bytes 1048576 | tf_op jit(solution)/shard_map/slice | solution.py:359
  8.8 4.2 %collective-permute-start.1 = (bf16[8,128,256]{2,1,0:T(8,128)(2,1)S(1)}, bf16[8,128,256]{2,1,0:T(8,128)(2,1)S(1)}, u32[]{:S(2)}, u32[]{:S(2)}) collective-permute-start(bf16[8,128,256]{2,1,0:T(8,128)(2,1)S(1)} %slice.3), channel_id=1, source_target_pairs={{0,4},{4,8},{8,12},{12,16},{16,20},{20,24},{24,28},{1,5},{5,9},{9,... | collective-permute-start | bytes 1572872 | tf_op jit(solution)/shard_map/ppermute | solution.py:359
  13.0 0.8 copy.8.refs_0_
  13.8 1.0 %copy-done.3 = f32[512,256]{1,0:T(8,128)S(1)} copy-done((f32[512,256]{1,0:T(8,128)S(1)}, f32[512,256]{1,0:T(8,128)}, u32[]{:S(2)}) %copy-start.3) | copy-done | bytes 524312
  14.8 0.7 copy-done.4
  15.5 1.9 %virtual.1 = (bf16[8,4,48,128]{3,2,1,0:T(8,128)(2,1)}, bf16[512,256]{1,0:T(8,128)(2,1)S(1)}, bf16[512,256]{1,0:T(8,128)(2,1)S(1)}) custom-call(s32[8,4]{1,0:T(8,128)S(1)} %copy.8.refs_0_, bf16[64,1536]{1,0:T(8,128)(2,1)S(1)} %get-tuple-element.53.refs_1_, bf16[64,256]{1,0:T(8,128)(2,1)S(1)} %collective-permute-done.refs_2_, f32[1,201]{1,0:T(1,128)S(1)} %bitcast.6, ...), custom_call_target="tpu_custom_call" | custom-call | flops 100000000 | bytes 786432 | tf_op jit(solution)/shard_map/virtual/pallas_call | solution.py:125
  17.4 5.7 %all-to-all-start = ((bf16[8,4,48,128]{3,2,1,0:T(8,128)(2,1)}), bf16[8,4,48,128]{3,2,1,0:T(8,128)(2,1)S(1)}, u32[]{:S(2)}, u32[]{:S(2)}) async-start(bf16[8,4,48,128]{3,2,1,0:T(8,128)(2,1)} %get-tuple-element.55), calls=%async_computation | async-start | bytes 786432 | tf_op jit(solution)/shard_map/all_to_all | solution.py:361
  23.2 0.9 %collective-permute-done.1.refs_2_ = bf16[8,128,256]{2,1,0:T(8,128)(2,1)S(1)} collective-permute-done((bf16[8,128,256]{2,1,0:T(8,128)(2,1)S(1)}, bf16[8,128,256]{2,1,0:T(8,128)(2,1)S(1)}, u32[]{:S(2)}, u32[]{:S(2)}) %collective-permute-start.1) | collective-permute-done | bytes 524320 | tf_op jit(solution)/shard_map/ppermute | solution.py:359
  24.1 1.9 %copy-done.1 = bf16[8,128,1536]{2,1,0:T(8,128)(2,1)S(1)} copy-done((bf16[8,128,1536]{2,1,0:T(8,128)(2,1)S(1)}, bf16[8,128,1536]{2,1,0:T(8,128)(2,1)}, u32[]{:S(2)}) %copy-start.1) | copy-done | bytes 3145752
  26.0 5.1 %spectra.1 = (bf16[384,128]{1,0:T(8,128)(2,1)S(1)}, bf16[384,128]{1,0:T(8,128)(2,1)}, bf16[384,128]{1,0:T(8,128)(2,1)}, bf16[384,128]{1,0:T(8,128)(2,1)S(1)}, bf...) custom-call(s32[1]{0:T(128)} %bitcast.refs_0_.refs_1_, ...), custom_call_target="tpu_custom_call" | custom-call | flops 2415919104 | bytes 4718592 | tf_op jit(solution)/shard_map/spectra/pallas_call | solution.py:167
  31.1 2.3 %all-to-all-done.refs_1_ = bf16[8,4,48,128]{3,2,1,0:T(8,128)(2,1)S(1)} async-done(((bf16[8,4,48,128]{3,2,1,0:T(8,128)(2,1)}), bf16[8,4,48,128]{3,2,1,0:T(8,128)(2,1)S(1)}, u32[]{:S(2)}, u32[]{:S(2)}) %all-to-all-start) | async-done | bytes 393248 | tf_op jit(solution)/shard_map/all_to_all | solution.py:361
  33.4 5.1 %collective-permute-start.5 = (bf16[384,128]{1,0:T(8,128)(2,1)S(1)}, bf16[384,128]{1,0:T(8,128)(2,1)S(1)}, u32[]{:S(2)}, u32[]{:S(2)}) collective-permute-start(bf16[384,128]{1,0:T(8,128)(2,1)S(1)} %get-tuple-element.79), channel_id=1, source_target_pairs={{0,28},{4,24},{8,20},{12,16},{16,12},{20,8},{24,4},{28,0},{1,29},{... | collective-permute-start | bytes 294920 | tf_op jit(solution)/shard_map/ppermute | solution.py:340
  38.5 0.7 collective-permute-start.6
  39.1 4.7 %collective-permute-start.7 = (bf16[384,128]{1,0:T(8,128)(2,1)S(1)}, bf16[384,128]{1,0:T(8,128)(2,1)S(1)}, u32[]{:S(2)}, u32[]{:S(2)}) collective-permute-start(bf16[384,128]{1,0:T(8,128)(2,1)S(1)} %get-tuple-element.81), channel_id=1, source_target_pairs={{0,20},{4,16},{8,28},{12,24},{16,4},{20,0},{24,12},{28,8},{1,21},{... | collective-permute-start | bytes 294920 | tf_op jit(solution)/shard_map/ppermute | solution.py:340
  43.8 1.5 %collective-permute-start.4 = (bf16[8,4,48,128]{3,2,1,0:T(8,128)(2,1)S(1)}, bf16[8,4,48,128]{3,2,1,0:T(8,128)(2,1)S(1)}, u32[]{:S(2)}, u32[]{:S(2)}) collective-permute-start(bf16[8,4,48,128]{3,2,1,0:T(8,128)(2,1)S(1)} %all-to-all-done.refs_1_), channel_id=1, source_target_pairs={{0,2},{1,3},{2,0},{3,1},{4,6},{5,7},{6,4},{7,5},{8,10},{9,11},{10,... | collective-permute-start | bytes 1179656 | tf_op jit(solution)/shard_map/ppermute | solution.py:340
  45.4 7.7 %collective-permute-done.7.refs_7_ = bf16[384,128]{1,0:T(8,128)(2,1)S(1)} collective-permute-done((bf16[384,128]{1,0:T(8,128)(2,1)S(1)}, bf16[384,128]{1,0:T(8,128)(2,1)S(1)}, u32[]{:S(2)}, u32[]{:S(2)}) %collective-permute-start.7) | collective-permute-done | bytes 98336 | tf_op jit(solution)/shard_map/ppermute | solution.py:340
  53.0 1.5 %collective-permute-start.8 = (bf16[8,4,48,128]{3,2,1,0:T(8,128)(2,1)S(1)}, bf16[8,4,48,128]{3,2,1,0:T(8,128)(2,1)S(1)}, u32[]{:S(2)}, u32[]{:S(2)}) collective-permute-start(bf16[8,4,48,128]{3,2,1,0:T(8,128)(2,1)S(1)} %collective-permute-done.3.refs_2_), channel_id=1, source_target_pairs={{0,2},{1,3},{2,0},{3,1},{4,6},{5,7},{6,4},{7,5},{8,10},{9,11},{10,... | collective-permute-start | bytes 1179656 | tf_op jit(solution)/shard_map/ppermute | solution.py:340
  54.5 2.4 %collective-permute-start.14 = (bf16[384,128]{1,0:T(8,128)(2,1)S(1)}, bf16[384,128]{1,0:T(8,128)(2,1)S(1)}, u32[]{:S(2)}, u32[]{:S(2)}) collective-permute-start(bf16[384,128]{1,0:T(8,128)(2,1)S(1)} %get-tuple-element.93), channel_id=1, source_target_pairs={{0,12},{4,8},{8,4},{12,0},{16,28},{20,24},{24,20},{28,16},{1,13},{... | collective-permute-start | bytes 294920 | tf_op jit(solution)/shard_map/ppermute | solution.py:340
  56.9 2.7 %collective-permute-start.12 = (bf16[384,128]{1,0:T(8,128)(2,1)}, bf16[384,128]{1,0:T(8,128)(2,1)S(1)}, u32[]{:S(2)}, u32[]{:S(2)}) collective-permute-start(bf16[384,128]{1,0:T(8,128)(2,1)} %get-tuple-element.90), channel_id=1, source_target_pairs={{0,8},{4,12},{8,0},{12,4},{16,24},{20,28},{24,16},{28,20},{1,9},{5... | collective-permute-start | bytes 294920 | tf_op jit(solution)/shard_map/ppermute | solution.py:340
  59.6 1.5 %collective-permute-start.2 = (bf16[384,128]{1,0:T(8,128)(2,1)}, bf16[384,128]{1,0:T(8,128)(2,1)S(1)}, u32[]{:S(2)}, u32[]{:S(2)}) collective-permute-start(bf16[384,128]{1,0:T(8,128)(2,1)} %get-tuple-element.77), channel_id=1, source_target_pairs={{0,4},{4,0},{8,12},{12,8},{16,20},{20,16},{24,28},{28,24},{1,5},{5... | collective-permute-start | bytes 294920 | tf_op jit(solution)/shard_map/ppermute | solution.py:340
  61.6 2.3 %collective-permute-start.18 = (bf16[384,128]{1,0:T(8,128)(2,1)}, bf16[384,128]{1,0:T(8,128)(2,1)S(1)}, u32[]{:S(2)}, u32[]{:S(2)}) collective-permute-start(bf16[384,128]{1,0:T(8,128)(2,1)} %get-tuple-element.99), channel_id=1, source_target_pairs={{0,28},{4,24},{8,20},{12,16},{16,12},{20,8},{24,4},{28,0},{1,29},{... | collective-permute-start | bytes 294920 | tf_op jit(solution)/shard_map/ppermute | solution.py:340
  63.9 3.0 %collective-permute-start.17 = (bf16[384,128]{1,0:T(8,128)(2,1)S(1)}, bf16[384,128]{1,0:T(8,128)(2,1)S(1)}, u32[]{:S(2)}, u32[]{:S(2)}) collective-permute-start(bf16[384,128]{1,0:T(8,128)(2,1)S(1)} %get-tuple-element.97), channel_id=1, source_target_pairs={{0,24},{4,28},{8,16},{12,20},{16,8},{20,12},{24,0},{28,4},{1,25},{... | collective-permute-start | bytes 294920 | tf_op jit(solution)/shard_map/ppermute | solution.py:340
  67.6 0.9 %collective-permute-start.9 = (bf16[384,128]{1,0:T(8,128)(2,1)S(1)}, bf16[384,128]{1,0:T(8,128)(2,1)S(1)}, u32[]{:S(2)}, u32[]{:S(2)}) collective-permute-start(bf16[384,128]{1,0:T(8,128)(2,1)S(1)} %get-tuple-element.83), channel_id=1, source_target_pairs={{0,4},{4,0},{8,12},{12,8},{16,20},{20,16},{24,28},{28,24},{1,5},{5... | collective-permute-start | bytes 294920 | tf_op jit(solution)/shard_map/ppermute | solution.py:340
  68.5 2.7 %collective-permute-start.11 = (bf16[384,128]{1,0:T(8,128)(2,1)S(1)}, bf16[384,128]{1,0:T(8,128)(2,1)S(1)}, u32[]{:S(2)}, u32[]{:S(2)}) collective-permute-start(bf16[384,128]{1,0:T(8,128)(2,1)S(1)} %get-tuple-element.87), channel_id=1, source_target_pairs={{0,12},{4,8},{8,4},{12,0},{16,28},{20,24},{24,20},{28,16},{1,13},{... | collective-permute-start | bytes 294920 | tf_op jit(solution)/shard_map/ppermute | solution.py:340
  71.1 1.3 %sources.1 = bf16[128,48,256]{2,1,0:T(8,128)(2,1)S(1)} custom-call(s32[1]{0:T(128)} %bitcast.2.refs_0_, bf16[8,4,48,128]{3,2,1,0:T(8,128)(2,1)S(1)} %all-to-all-done.refs_1_, bf16[8,4,48,128]{3,2,1,0:T(8,128)(2,1)S(1)} %collective-permute-done.3.refs_2_, bf16[8,4,48,128]{3,2,1,0:T(8,128)(2,1)S(1)} %collective-permute-done.4.refs_3_, ...), custom_call_target="tpu_custom_call" | custom-call | flops 100000000 | bytes 6291456 | tf_op jit(solution)/shard_map/sources/pallas_call | solution.py:216
  72.5 0.7 collective-permute-start.13
  73.2 2.6 %collective-permute-start.15 = (bf16[384,128]{1,0:T(8,128)(2,1)S(1)}, bf16[384,128]{1,0:T(8,128)(2,1)S(1)}, u32[]{:S(2)}, u32[]{:S(2)}) collective-permute-start(bf16[384,128]{1,0:T(8,128)(2,1)S(1)} %get-tuple-element.94), channel_id=1, source_target_pairs={{0,20},{4,16},{8,28},{12,24},{16,4},{20,0},{24,12},{28,8},{1,21},{... | collective-permute-start | bytes 294920 | tf_op jit(solution)/shard_map/ppermute | solution.py:340
  75.7 5.8 %stack.2.refs_12_ = bf16[1,4,128,32,256]{4,3,2,1,0:T(8,128)(2,1)} custom-call(s32[1]{0:T(128)S(6)} %copy.10.refs_0_, s32[1]{0:T(128)} %bitcast.refs_0_.refs_1_, bf16[384,128]{1,0:T(8,128)(2,1)S(1)} %get-tuple-element.100.refs_2_, bf16[384,128]{1,0:T(8,128)(2,1)S(1)} %collective-permute-done.2.refs_3_, bf16[384,128]{1,0:T(8,128)(2,1)S(1)} %collective-permute-done.12.refs_4_, ...), custom_call_target="tpu_custom_call" | custom-call | flops 2147483648 | bytes 7340032 | tf_op jit(solution)/shard_map/stack/pallas_call | solution.py:318
  81.8 0.8 collective-permute-done.15.refs_7_
  82.7 5.8 %stack.3 = bf16[1,4,128,32,256]{4,3,2,1,0:T(8,128)(2,1)} custom-call(s32[1]{0:T(128)S(6)} %copy.10.refs_0_, s32[1]{0:T(128)} %bitcast.refs_0_.refs_1_, bf16[384,128]{1,0:T(8,128)(2,1)S(1)} %get-tuple-element.75.refs_2_, bf16[384,128]{1,0:T(8,128)(2,1)S(1)} %collective-permute-done.9.refs_3_, ...), custom_call_target="tpu_custom_call", output_to_operand_aliasing={{}: (12, {})} | custom-call | flops 2147483648 | bytes 7340032 | tf_op jit(solution)/shard_map/stack/pallas_call | solution.py:318
  (26 shorter events, 1.6 us)
Async XLA Ops:
  0.0 1.9 %copy-start = (bf16[8,128,1536]{2,1,0:T(8,128)(2,1)S(1)}, bf16[8,128,1536]{2,1,0:T(8,128)(2,1)}, u32[]{:S(2)}) copy-start(bf16[8,128,1536]{2,1,0:T(8,128)(2,1)} %refs_1_.1) | copy-start | bytes 9437188
  2.2 73.5 %copy-start.2 = (f32[256,256]{1,0:T(8,128)S(1)}, f32[256,256]{1,0:T(8,128)}, u32[]{:S(2)}) copy-start(f32[256,256]{1,0:T(8,128)} %constant.14.clone.refs_11_) | copy-start | bytes 786436
  2.2 6.6 %collective-permute-start = (bf16[64,256]{1,0:T(8,128)(2,1)S(1)}, bf16[64,256]{1,0:T(8,128)(2,1)S(1)}, u32[]{:S(2)}, u32[]{:S(2)}) collective-permute-start(bf16[64,256]{1,0:T(8,128)(2,1)S(1)} %get-tuple-element.54), channel_id=1, source_target_pairs={{0,4},{4,8},{8,12},{12,16},{16,20},{20,24},{24,28},{1,5},{5,9},{9,... | collective-permute-start | bytes 98312 | tf_op jit(solution)/shard_map/ppermute | solution.py:358
  8.8 15.3 %collective-permute-start.1 = (bf16[8,128,256]{2,1,0:T(8,128)(2,1)S(1)}, bf16[8,128,256]{2,1,0:T(8,128)(2,1)S(1)}, u32[]{:S(2)}, u32[]{:S(2)}) collective-permute-start(bf16[8,128,256]{2,1,0:T(8,128)(2,1)S(1)} %slice.3), channel_id=1, source_target_pairs={{0,4},{4,8},{8,12},{12,16},{16,20},{20,24},{24,28},{1,5},{5,9},{9,... | collective-permute-start | bytes 1572872 | tf_op jit(solution)/shard_map/ppermute | solution.py:359
  13.8 1.0 %copy-start.3 = (f32[512,256]{1,0:T(8,128)S(1)}, f32[512,256]{1,0:T(8,128)}, u32[]{:S(2)}) copy-start(f32[512,256]{1,0:T(8,128)} %constant.13.clone.refs_4_) | copy-start | bytes 1572868
  14.8 0.7 copy-start.4
  17.4 16.0 %all-to-all-start = ((bf16[8,4,48,128]{3,2,1,0:T(8,128)(2,1)}), bf16[8,4,48,128]{3,2,1,0:T(8,128)(2,1)S(1)}, u32[]{:S(2)}, u32[]{:S(2)}) async-start(bf16[8,4,48,128]{3,2,1,0:T(8,128)(2,1)} %get-tuple-element.55), calls=%async_computation | async-start | bytes 786432 | tf_op jit(solution)/shard_map/all_to_all | solution.py:361
  24.1 1.9 %copy-start.1 = (bf16[8,128,1536]{2,1,0:T(8,128)(2,1)S(1)}, bf16[8,128,1536]{2,1,0:T(8,128)(2,1)}, u32[]{:S(2)}) copy-start(bf16[8,128,1536]{2,1,0:T(8,128)(2,1)} %refs_1_.1) | copy-start | bytes 9437188
  33.4 19.6 %collective-permute-start.3 = (bf16[8,4,48,128]{3,2,1,0:T(8,128)(2,1)S(1)}, bf16[8,4,48,128]{3,2,1,0:T(8,128)(2,1)S(1)}, u32[]{:S(2)}, u32[]{:S(2)}) collective-permute-start(bf16[8,4,48,128]{3,2,1,0:T(8,128)(2,1)S(1)} %all-to-all-done.refs_1_), channel_id=1, source_target_pairs={{0,1},{1,0},{2,3},{3,2},{4,5},{5,4},{6,7},{7,6},{8,9},{9,8},{10,11... | collective-permute-start | bytes 1179656 | tf_op jit(solution)/shard_map/ppermute | solution.py:340
  33.4 11.9 %collective-permute-start.5 = (bf16[384,128]{1,0:T(8,128)(2,1)S(1)}, bf16[384,128]{1,0:T(8,128)(2,1)S(1)}, u32[]{:S(2)}, u32[]{:S(2)}) collective-permute-start(bf16[384,128]{1,0:T(8,128)(2,1)S(1)} %get-tuple-element.79), channel_id=1, source_target_pairs={{0,28},{4,24},{8,20},{12,16},{16,12},{20,8},{24,4},{28,0},{1,29},{... | collective-permute-start | bytes 294920 | tf_op jit(solution)/shard_map/ppermute | solution.py:340
  38.5 6.9 %collective-permute-start.6 = (bf16[384,128]{1,0:T(8,128)(2,1)S(1)}, bf16[384,128]{1,0:T(8,128)(2,1)S(1)}, u32[]{:S(2)}, u32[]{:S(2)}) collective-permute-start(bf16[384,128]{1,0:T(8,128)(2,1)S(1)} %get-tuple-element.80), channel_id=1, source_target_pairs={{0,24},{4,28},{8,16},{12,20},{16,8},{20,12},{24,0},{28,4},{1,25},{... | collective-permute-start | bytes 294920 | tf_op jit(solution)/shard_map/ppermute | solution.py:340
  39.1 13.9 %collective-permute-start.7 = (bf16[384,128]{1,0:T(8,128)(2,1)S(1)}, bf16[384,128]{1,0:T(8,128)(2,1)S(1)}, u32[]{:S(2)}, u32[]{:S(2)}) collective-permute-start(bf16[384,128]{1,0:T(8,128)(2,1)S(1)} %get-tuple-element.81), channel_id=1, source_target_pairs={{0,20},{4,16},{8,28},{12,24},{16,4},{20,0},{24,12},{28,8},{1,21},{... | collective-permute-start | bytes 294920 | tf_op jit(solution)/shard_map/ppermute | solution.py:340
  43.8 13.1 %collective-permute-start.4 = (bf16[8,4,48,128]{3,2,1,0:T(8,128)(2,1)S(1)}, bf16[8,4,48,128]{3,2,1,0:T(8,128)(2,1)S(1)}, u32[]{:S(2)}, u32[]{:S(2)}) collective-permute-start(bf16[8,4,48,128]{3,2,1,0:T(8,128)(2,1)S(1)} %all-to-all-done.refs_1_), channel_id=1, source_target_pairs={{0,2},{1,3},{2,0},{3,1},{4,6},{5,7},{6,4},{7,5},{8,10},{9,11},{10,... | collective-permute-start | bytes 1179656 | tf_op jit(solution)/shard_map/ppermute | solution.py:340
  53.0 14.5 %collective-permute-start.8 = (bf16[8,4,48,128]{3,2,1,0:T(8,128)(2,1)S(1)}, bf16[8,4,48,128]{3,2,1,0:T(8,128)(2,1)S(1)}, u32[]{:S(2)}, u32[]{:S(2)}) collective-permute-start(bf16[8,4,48,128]{3,2,1,0:T(8,128)(2,1)S(1)} %collective-permute-done.3.refs_2_), channel_id=1, source_target_pairs={{0,2},{1,3},{2,0},{3,1},{4,6},{5,7},{6,4},{7,5},{8,10},{9,11},{10,... | collective-permute-start | bytes 1179656 | tf_op jit(solution)/shard_map/ppermute | solution.py:340
  54.5 7.1 %collective-permute-start.16 = (bf16[384,128]{1,0:T(8,128)(2,1)S(1)}, bf16[384,128]{1,0:T(8,128)(2,1)S(1)}, u32[]{:S(2)}, u32[]{:S(2)}) collective-permute-start(bf16[384,128]{1,0:T(8,128)(2,1)S(1)} %get-tuple-element.96), channel_id=1, source_target_pairs={{0,16},{4,20},{8,24},{12,28},{16,0},{20,4},{24,8},{28,12},{1,17},{... | collective-permute-start | bytes 294920 | tf_op jit(solution)/shard_map/ppermute | solution.py:340
  54.5 9.4 %collective-permute-start.14 = (bf16[384,128]{1,0:T(8,128)(2,1)S(1)}, bf16[384,128]{1,0:T(8,128)(2,1)S(1)}, u32[]{:S(2)}, u32[]{:S(2)}) collective-permute-start(bf16[384,128]{1,0:T(8,128)(2,1)S(1)} %get-tuple-element.93), channel_id=1, source_target_pairs={{0,12},{4,8},{8,4},{12,0},{16,28},{20,24},{24,20},{28,16},{1,13},{... | collective-permute-start | bytes 294920 | tf_op jit(solution)/shard_map/ppermute | solution.py:340
  56.9 10.7 %collective-permute-start.12 = (bf16[384,128]{1,0:T(8,128)(2,1)}, bf16[384,128]{1,0:T(8,128)(2,1)S(1)}, u32[]{:S(2)}, u32[]{:S(2)}) collective-permute-start(bf16[384,128]{1,0:T(8,128)(2,1)} %get-tuple-element.90), channel_id=1, source_target_pairs={{0,8},{4,12},{8,0},{12,4},{16,24},{20,28},{24,16},{28,20},{1,9},{5... | collective-permute-start | bytes 294920 | tf_op jit(solution)/shard_map/ppermute | solution.py:340
  59.6 8.0 %collective-permute-start.2 = (bf16[384,128]{1,0:T(8,128)(2,1)}, bf16[384,128]{1,0:T(8,128)(2,1)S(1)}, u32[]{:S(2)}, u32[]{:S(2)}) collective-permute-start(bf16[384,128]{1,0:T(8,128)(2,1)} %get-tuple-element.77), channel_id=1, source_target_pairs={{0,4},{4,0},{8,12},{12,8},{16,20},{20,16},{24,28},{28,24},{1,5},{5... | collective-permute-start | bytes 294920 | tf_op jit(solution)/shard_map/ppermute | solution.py:340
  61.6 10.8 %collective-permute-start.18 = (bf16[384,128]{1,0:T(8,128)(2,1)}, bf16[384,128]{1,0:T(8,128)(2,1)S(1)}, u32[]{:S(2)}, u32[]{:S(2)}) collective-permute-start(bf16[384,128]{1,0:T(8,128)(2,1)} %get-tuple-element.99), channel_id=1, source_target_pairs={{0,28},{4,24},{8,20},{12,16},{16,12},{20,8},{24,4},{28,0},{1,29},{... | collective-permute-start | bytes 294920 | tf_op jit(solution)/shard_map/ppermute | solution.py:340
  63.9 9.2 %collective-permute-start.17 = (bf16[384,128]{1,0:T(8,128)(2,1)S(1)}, bf16[384,128]{1,0:T(8,128)(2,1)S(1)}, u32[]{:S(2)}, u32[]{:S(2)}) collective-permute-start(bf16[384,128]{1,0:T(8,128)(2,1)S(1)} %get-tuple-element.97), channel_id=1, source_target_pairs={{0,24},{4,28},{8,16},{12,20},{16,8},{20,12},{24,0},{28,4},{1,25},{... | collective-permute-start | bytes 294920 | tf_op jit(solution)/shard_map/ppermute | solution.py:340
  67.6 14.0 %collective-permute-start.9 = (bf16[384,128]{1,0:T(8,128)(2,1)S(1)}, bf16[384,128]{1,0:T(8,128)(2,1)S(1)}, u32[]{:S(2)}, u32[]{:S(2)}) collective-permute-start(bf16[384,128]{1,0:T(8,128)(2,1)S(1)} %get-tuple-element.83), channel_id=1, source_target_pairs={{0,4},{4,0},{8,12},{12,8},{16,20},{20,16},{24,28},{28,24},{1,5},{5... | collective-permute-start | bytes 294920 | tf_op jit(solution)/shard_map/ppermute | solution.py:340
  68.5 13.1 %collective-permute-start.10 = (bf16[384,128]{1,0:T(8,128)(2,1)S(1)}, bf16[384,128]{1,0:T(8,128)(2,1)S(1)}, u32[]{:S(2)}, u32[]{:S(2)}) collective-permute-start(bf16[384,128]{1,0:T(8,128)(2,1)S(1)} %get-tuple-element.85), channel_id=1, source_target_pairs={{0,8},{4,12},{8,0},{12,4},{16,24},{20,28},{24,16},{28,20},{1,9},{5... | collective-permute-start | bytes 294920 | tf_op jit(solution)/shard_map/ppermute | solution.py:340
  68.5 13.1 %collective-permute-start.11 = (bf16[384,128]{1,0:T(8,128)(2,1)S(1)}, bf16[384,128]{1,0:T(8,128)(2,1)S(1)}, u32[]{:S(2)}, u32[]{:S(2)}) collective-permute-start(bf16[384,128]{1,0:T(8,128)(2,1)S(1)} %get-tuple-element.87), channel_id=1, source_target_pairs={{0,12},{4,8},{8,4},{12,0},{16,28},{20,24},{24,20},{28,16},{1,13},{... | collective-permute-start | bytes 294920 | tf_op jit(solution)/shard_map/ppermute | solution.py:340
  72.5 9.4 %collective-permute-start.13 = (bf16[384,128]{1,0:T(8,128)(2,1)S(1)}, bf16[384,128]{1,0:T(8,128)(2,1)S(1)}, u32[]{:S(2)}, u32[]{:S(2)}) collective-permute-start(bf16[384,128]{1,0:T(8,128)(2,1)S(1)} %get-tuple-element.91), channel_id=1, source_target_pairs={{0,16},{4,20},{8,24},{12,28},{16,0},{20,4},{24,8},{28,12},{1,17},{... | collective-permute-start | bytes 294920 | tf_op jit(solution)/shard_map/ppermute | solution.py:340
  73.2 9.5 %collective-permute-start.15 = (bf16[384,128]{1,0:T(8,128)(2,1)S(1)}, bf16[384,128]{1,0:T(8,128)(2,1)S(1)}, u32[]{:S(2)}, u32[]{:S(2)}) collective-permute-start(bf16[384,128]{1,0:T(8,128)(2,1)S(1)} %get-tuple-element.94), channel_id=1, source_target_pairs={{0,20},{4,16},{8,28},{12,24},{16,4},{20,0},{24,12},{28,8},{1,21},{... | collective-permute-start | bytes 294920 | tf_op jit(solution)/shard_map/ppermute | solution.py:340

commit v12 on v11

--- a/solution.py
+++ b/solution.py
@@ -205,7 +205,7 @@
         out_ref[j] = jnp.concatenate([top, low], 0).astype(BF)
         return carry
 
-    lax.fori_loop(0, BINS, one, 0, unroll=8)
+    lax.fori_loop(0, BINS, one, 0, unroll=32)
 
 
 def sources(virts, place, wins, nv):
@@ -277,7 +277,7 @@
                 cross[p, at, :] = value[u * size : (u + 1) * size, p * width : (p + 1) * width]
         return carry
 
-    lax.fori_loop(0, BINS // pack, one, 0, unroll=32 // pack)
+    lax.fori_loop(0, BINS // pack, one, 0, unroll=64 // pack)
 
     rows = 4
     copies = []

time: 88.9 us -> 88.6 us (level)
  no operation moved by 1% of the time
where the time goes in v12:
time: 88.6 us; the launch traced here: 88.1 us
  starting transfers between devices  47 us (53%)
  Pallas kernels  19.6 us (22%)
  waiting for transfers between devices  13.4 us (15%)
  local copies, waits for them, and re-layouts  7.34 us (8%)
    ppermute x17, starting transfers between devices, swap(): lax.ppermute(value, axis, [(i, i ^ mask) for i in range(lax.axis_size(axi...  32.1 us
    pallas_call x2, Pallas kernels, stack(): pl.pallas_call(lambda *refs: stack_kernel(nw, wins, start, size, group, *...  11.1 us
    ppermute x17, waiting for transfers between devices, swap(): lax.ppermute(value, axis, [(i, i ^ mask) for i in range(lax.axis_size(axi...  9.61 us
    unnamed x11, local copies, waits for them, and re-layouts  6.26 us
    all_to_all x1, starting transfers between devices, on_device(): lax.all_to_all(picked, 'wide', split_axis=0, concat_axis=0, tiled=True)  5.72 us
    pallas_call x1, Pallas kernels, spectra(): pl.pallas_call(lambda *refs: spectra_kernel(sizes, *refs), in_specs=[smem...  5.1 us
    ppermute x1, starting transfers between devices, on_device(): tip = lax.ppermute(tip, 'wide', ahead)  4.98 us
    ppermute x1, starting transfers between devices, on_device(): lax.ppermute(after(records[:, :, time - HALF:], [tip]), 'wide', ahead)  4.24 us
  transfers between devices with their start and end apart: 20, of which 7 were waited for; matrix products, arithmetic and copies ran while one was open for 2% of the time, Pallas kernels for 16%

profile of v12, /device:TPU:0, one launch (start us, length us, event | category | flops | bytes accessed | tf_op | source)
XLA Modules:
  0.0 88.1 jit_solution(13048879896328281730)
XLA Ops:
  0.0 1.9 %copy-done = bf16[8,128,1536]{2,1,0:T(8,128)(2,1)S(1)} copy-done((bf16[8,128,1536]{2,1,0:T(8,128)(2,1)S(1)}, bf16[8,128,1536]{2,1,0:T(8,128)(2,1)}, u32[]{:S(2)}) %copy-start) | copy-done | bytes 3145752
  2.2 5.0 %collective-permute-start = (bf16[64,256]{1,0:T(8,128)(2,1)S(1)}, bf16[64,256]{1,0:T(8,128)(2,1)S(1)}, u32[]{:S(2)}, u32[]{:S(2)}) collective-permute-start(bf16[64,256]{1,0:T(8,128)(2,1)S(1)} %get-tuple-element.54), channel_id=1, source_target_pairs={{0,4},{4,8},{8,12},{12,16},{16,20},{20,24},{24,28},{1,5},{5,9},{9,... | collective-permute-start | bytes 98312 | tf_op jit(solution)/shard_map/ppermute | solution.py:358
  7.2 1.1 %slice.3 = bf16[8,128,256]{2,1,0:T(8,128)(2,1)S(1)} slice(bf16[8,128,1536]{2,1,0:T(8,128)(2,1)} %refs_1_.1), slice={[0:8], [0:128], [1280:1536]} | slice | bytes 1048576 | tf_op jit(solution)/shard_map/slice | solution.py:359
  8.8 4.2 %collective-permute-start.1 = (bf16[8,128,256]{2,1,0:T(8,128)(2,1)S(1)}, bf16[8,128,256]{2,1,0:T(8,128)(2,1)S(1)}, u32[]{:S(2)}, u32[]{:S(2)}) collective-permute-start(bf16[8,128,256]{2,1,0:T(8,128)(2,1)S(1)} %slice.3), channel_id=1, source_target_pairs={{0,4},{4,8},{8,12},{12,16},{16,20},{20,24},{24,28},{1,5},{5,9},{9,... | collective-permute-start | bytes 1572872 | tf_op jit(solution)/shard_map/ppermute | solution.py:359
  13.0 0.8 copy.8.refs_0_
  13.8 1.0 %copy-done.3 = f32[512,256]{1,0:T(8,128)S(1)} copy-done((f32[512,256]{1,0:T(8,128)S(1)}, f32[512,256]{1,0:T(8,128)}, u32[]{:S(2)}) %copy-start.3) | copy-done | bytes 524312
  14.8 0.7 copy-done.4
  15.5 2.0 %virtual.1 = (bf16[8,4,48,128]{3,2,1,0:T(8,128)(2,1)}, bf16[512,256]{1,0:T(8,128)(2,1)S(1)}, bf16[512,256]{1,0:T(8,128)(2,1)S(1)}) custom-call(s32[8,4]{1,0:T(8,128)S(1)} %copy.8.refs_0_, bf16[64,1536]{1,0:T(8,128)(2,1)S(1)} %get-tuple-element.53.refs_1_, bf16[64,256]{1,0:T(8,128)(2,1)S(1)} %collective-permute-done.refs_2_, f32[1,201]{1,0:T(1,128)S(1)} %bitcast.6, ...), custom_call_target="tpu_custom_call" | custom-call | flops 100000000 | bytes 786432 | tf_op jit(solution)/shard_map/virtual/pallas_call | solution.py:125
  17.4 5.7 %all-to-all-start = ((bf16[8,4,48,128]{3,2,1,0:T(8,128)(2,1)}), bf16[8,4,48,128]{3,2,1,0:T(8,128)(2,1)S(1)}, u32[]{:S(2)}, u32[]{:S(2)}) async-start(bf16[8,4,48,128]{3,2,1,0:T(8,128)(2,1)} %get-tuple-element.55), calls=%async_computation | async-start | bytes 786432 | tf_op jit(solution)/shard_map/all_to_all | solution.py:361
  23.2 0.9 %collective-permute-done.1.refs_2_ = bf16[8,128,256]{2,1,0:T(8,128)(2,1)S(1)} collective-permute-done((bf16[8,128,256]{2,1,0:T(8,128)(2,1)S(1)}, bf16[8,128,256]{2,1,0:T(8,128)(2,1)S(1)}, u32[]{:S(2)}, u32[]{:S(2)}) %collective-permute-start.1) | collective-permute-done | bytes 524320 | tf_op jit(solution)/shard_map/ppermute | solution.py:359
  24.1 1.9 %copy-done.1 = bf16[8,128,1536]{2,1,0:T(8,128)(2,1)S(1)} copy-done((bf16[8,128,1536]{2,1,0:T(8,128)(2,1)S(1)}, bf16[8,128,1536]{2,1,0:T(8,128)(2,1)}, u32[]{:S(2)}) %copy-start.1) | copy-done | bytes 3145752
  26.0 5.1 %spectra.1 = (bf16[384,128]{1,0:T(8,128)(2,1)S(1)}, bf16[384,128]{1,0:T(8,128)(2,1)}, bf16[384,128]{1,0:T(8,128)(2,1)}, bf16[384,128]{1,0:T(8,128)(2,1)S(1)}, bf...) custom-call(s32[1]{0:T(128)} %bitcast.refs_0_.refs_1_, ...), custom_call_target="tpu_custom_call" | custom-call | flops 2415919104 | bytes 4718592 | tf_op jit(solution)/shard_map/spectra/pallas_call | solution.py:167
  31.1 2.3 %all-to-all-done.refs_1_ = bf16[8,4,48,128]{3,2,1,0:T(8,128)(2,1)S(1)} async-done(((bf16[8,4,48,128]{3,2,1,0:T(8,128)(2,1)}), bf16[8,4,48,128]{3,2,1,0:T(8,128)(2,1)S(1)}, u32[]{:S(2)}, u32[]{:S(2)}) %all-to-all-start) | async-done | bytes 393248 | tf_op jit(solution)/shard_map/all_to_all | solution.py:361
  33.4 5.1 %collective-permute-start.5 = (bf16[384,128]{1,0:T(8,128)(2,1)S(1)}, bf16[384,128]{1,0:T(8,128)(2,1)S(1)}, u32[]{:S(2)}, u32[]{:S(2)}) collective-permute-start(bf16[384,128]{1,0:T(8,128)(2,1)S(1)} %get-tuple-element.79), channel_id=1, source_target_pairs={{0,28},{4,24},{8,20},{12,16},{16,12},{20,8},{24,4},{28,0},{1,29},{... | collective-permute-start | bytes 294920 | tf_op jit(solution)/shard_map/ppermute | solution.py:340
  38.5 0.7 collective-permute-start.6
  39.1 4.7 %collective-permute-start.7 = (bf16[384,128]{1,0:T(8,128)(2,1)S(1)}, bf16[384,128]{1,0:T(8,128)(2,1)S(1)}, u32[]{:S(2)}, u32[]{:S(2)}) collective-permute-start(bf16[384,128]{1,0:T(8,128)(2,1)S(1)} %get-tuple-element.81), channel_id=1, source_target_pairs={{0,20},{4,16},{8,28},{12,24},{16,4},{20,0},{24,12},{28,8},{1,21},{... | collective-permute-start | bytes 294920 | tf_op jit(solution)/shard_map/ppermute | solution.py:340
  43.8 1.5 %collective-permute-start.4 = (bf16[8,4,48,128]{3,2,1,0:T(8,128)(2,1)S(1)}, bf16[8,4,48,128]{3,2,1,0:T(8,128)(2,1)S(1)}, u32[]{:S(2)}, u32[]{:S(2)}) collective-permute-start(bf16[8,4,48,128]{3,2,1,0:T(8,128)(2,1)S(1)} %all-to-all-done.refs_1_), channel_id=1, source_target_pairs={{0,2},{1,3},{2,0},{3,1},{4,6},{5,7},{6,4},{7,5},{8,10},{9,11},{10,... | collective-permute-start | bytes 1179656 | tf_op jit(solution)/shard_map/ppermute | solution.py:340
  45.4 7.7 %collective-permute-done.7.refs_7_ = bf16[384,128]{1,0:T(8,128)(2,1)S(1)} collective-permute-done((bf16[384,128]{1,0:T(8,128)(2,1)S(1)}, bf16[384,128]{1,0:T(8,128)(2,1)S(1)}, u32[]{:S(2)}, u32[]{:S(2)}) %collective-permute-start.7) | collective-permute-done | bytes 98336 | tf_op jit(solution)/shard_map/ppermute | solution.py:340
  53.0 1.5 %collective-permute-start.8 = (bf16[8,4,48,128]{3,2,1,0:T(8,128)(2,1)S(1)}, bf16[8,4,48,128]{3,2,1,0:T(8,128)(2,1)S(1)}, u32[]{:S(2)}, u32[]{:S(2)}) collective-permute-start(bf16[8,4,48,128]{3,2,1,0:T(8,128)(2,1)S(1)} %collective-permute-done.3.refs_2_), channel_id=1, source_target_pairs={{0,2},{1,3},{2,0},{3,1},{4,6},{5,7},{6,4},{7,5},{8,10},{9,11},{10,... | collective-permute-start | bytes 1179656 | tf_op jit(solution)/shard_map/ppermute | solution.py:340
  54.5 2.4 %collective-permute-start.14 = (bf16[384,128]{1,0:T(8,128)(2,1)S(1)}, bf16[384,128]{1,0:T(8,128)(2,1)S(1)}, u32[]{:S(2)}, u32[]{:S(2)}) collective-permute-start(bf16[384,128]{1,0:T(8,128)(2,1)S(1)} %get-tuple-element.93), channel_id=1, source_target_pairs={{0,12},{4,8},{8,4},{12,0},{16,28},{20,24},{24,20},{28,16},{1,13},{... | collective-permute-start | bytes 294920 | tf_op jit(solution)/shard_map/ppermute | solution.py:340
  56.9 2.7 %collective-permute-start.12 = (bf16[384,128]{1,0:T(8,128)(2,1)}, bf16[384,128]{1,0:T(8,128)(2,1)S(1)}, u32[]{:S(2)}, u32[]{:S(2)}) collective-permute-start(bf16[384,128]{1,0:T(8,128)(2,1)} %get-tuple-element.90), channel_id=1, source_target_pairs={{0,8},{4,12},{8,0},{12,4},{16,24},{20,28},{24,16},{28,20},{1,9},{5... | collective-permute-start | bytes 294920 | tf_op jit(solution)/shard_map/ppermute | solution.py:340
  59.6 1.5 %collective-permute-start.2 = (bf16[384,128]{1,0:T(8,128)(2,1)}, bf16[384,128]{1,0:T(8,128)(2,1)S(1)}, u32[]{:S(2)}, u32[]{:S(2)}) collective-permute-start(bf16[384,128]{1,0:T(8,128)(2,1)} %get-tuple-element.77), channel_id=1, source_target_pairs={{0,4},{4,0},{8,12},{12,8},{16,20},{20,16},{24,28},{28,24},{1,5},{5... | collective-permute-start | bytes 294920 | tf_op jit(solution)/shard_map/ppermute | solution.py:340
  61.6 2.3 %collective-permute-start.18 = (bf16[384,128]{1,0:T(8,128)(2,1)}, bf16[384,128]{1,0:T(8,128)(2,1)S(1)}, u32[]{:S(2)}, u32[]{:S(2)}) collective-permute-start(bf16[384,128]{1,0:T(8,128)(2,1)} %get-tuple-element.99), channel_id=1, source_target_pairs={{0,28},{4,24},{8,20},{12,16},{16,12},{20,8},{24,4},{28,0},{1,29},{... | collective-permute-start | bytes 294920 | tf_op jit(solution)/shard_map/ppermute | solution.py:340
  63.9 3.0 %collective-permute-start.17 = (bf16[384,128]{1,0:T(8,128)(2,1)S(1)}, bf16[384,128]{1,0:T(8,128)(2,1)S(1)}, u32[]{:S(2)}, u32[]{:S(2)}) collective-permute-start(bf16[384,128]{1,0:T(8,128)(2,1)S(1)} %get-tuple-element.97), channel_id=1, source_target_pairs={{0,24},{4,28},{8,16},{12,20},{16,8},{20,12},{24,0},{28,4},{1,25},{... | collective-permute-start | bytes 294920 | tf_op jit(solution)/shard_map/ppermute | solution.py:340
  67.6 0.9 %collective-permute-start.9 = (bf16[384,128]{1,0:T(8,128)(2,1)S(1)}, bf16[384,128]{1,0:T(8,128)(2,1)S(1)}, u32[]{:S(2)}, u32[]{:S(2)}) collective-permute-start(bf16[384,128]{1,0:T(8,128)(2,1)S(1)} %get-tuple-element.83), channel_id=1, source_target_pairs={{0,4},{4,0},{8,12},{12,8},{16,20},{20,16},{24,28},{28,24},{1,5},{5... | collective-permute-start | bytes 294920 | tf_op jit(solution)/shard_map/ppermute | solution.py:340
  68.5 2.7 %collective-permute-start.11 = (bf16[384,128]{1,0:T(8,128)(2,1)S(1)}, bf16[384,128]{1,0:T(8,128)(2,1)S(1)}, u32[]{:S(2)}, u32[]{:S(2)}) collective-permute-start(bf16[384,128]{1,0:T(8,128)(2,1)S(1)} %get-tuple-element.87), channel_id=1, source_target_pairs={{0,12},{4,8},{8,4},{12,0},{16,28},{20,24},{24,20},{28,16},{1,13},{... | collective-permute-start | bytes 294920 | tf_op jit(solution)/shard_map/ppermute | solution.py:340
  71.1 1.2 %sources.1 = bf16[128,48,256]{2,1,0:T(8,128)(2,1)S(1)} custom-call(s32[1]{0:T(128)} %bitcast.2.refs_0_, bf16[8,4,48,128]{3,2,1,0:T(8,128)(2,1)S(1)} %all-to-all-done.refs_1_, bf16[8,4,48,128]{3,2,1,0:T(8,128)(2,1)S(1)} %collective-permute-done.3.refs_2_, bf16[8,4,48,128]{3,2,1,0:T(8,128)(2,1)S(1)} %collective-permute-done.4.refs_3_, ...), custom_call_target="tpu_custom_call" | custom-call | flops 100000000 | bytes 6291456 | tf_op jit(solution)/shard_map/sources/pallas_call | solution.py:216
  72.4 0.7 collective-permute-start.13
  73.1 2.6 %collective-permute-start.15 = (bf16[384,128]{1,0:T(8,128)(2,1)S(1)}, bf16[384,128]{1,0:T(8,128)(2,1)S(1)}, u32[]{:S(2)}, u32[]{:S(2)}) collective-permute-start(bf16[384,128]{1,0:T(8,128)(2,1)S(1)} %get-tuple-element.94), channel_id=1, source_target_pairs={{0,20},{4,16},{8,28},{12,24},{16,4},{20,0},{24,12},{28,8},{1,21},{... | collective-permute-start | bytes 294920 | tf_op jit(solution)/shard_map/ppermute | solution.py:340
  75.7 5.5 %stack.2.refs_12_ = bf16[1,4,128,32,256]{4,3,2,1,0:T(8,128)(2,1)} custom-call(s32[1]{0:T(128)S(6)} %copy.10.refs_0_, s32[1]{0:T(128)} %bitcast.refs_0_.refs_1_, bf16[384,128]{1,0:T(8,128)(2,1)S(1)} %get-tuple-element.100.refs_2_, bf16[384,128]{1,0:T(8,128)(2,1)S(1)} %collective-permute-done.2.refs_3_, bf16[384,128]{1,0:T(8,128)(2,1)S(1)} %collective-permute-done.12.refs_4_, ...), custom_call_target="tpu_custom_call" | custom-call | flops 2147483648 | bytes 7340032 | tf_op jit(solution)/shard_map/stack/pallas_call | solution.py:318
  81.8 0.8 collective-permute-done.15.refs_7_
  82.6 5.5 %stack.3 = bf16[1,4,128,32,256]{4,3,2,1,0:T(8,128)(2,1)} custom-call(s32[1]{0:T(128)S(6)} %copy.10.refs_0_, s32[1]{0:T(128)} %bitcast.refs_0_.refs_1_, bf16[384,128]{1,0:T(8,128)(2,1)S(1)} %get-tuple-element.75.refs_2_, bf16[384,128]{1,0:T(8,128)(2,1)S(1)} %collective-permute-done.9.refs_3_, ...), custom_call_target="tpu_custom_call", output_to_operand_aliasing={{}: (12, {})} | custom-call | flops 2147483648 | bytes 7340032 | tf_op jit(solution)/shard_map/stack/pallas_call | solution.py:318
  (26 shorter events, 1.9 us)
Async XLA Ops:
  0.0 1.9 %copy-start = (bf16[8,128,1536]{2,1,0:T(8,128)(2,1)S(1)}, bf16[8,128,1536]{2,1,0:T(8,128)(2,1)}, u32[]{:S(2)}) copy-start(bf16[8,128,1536]{2,1,0:T(8,128)(2,1)} %refs_1_.1) | copy-start | bytes 9437188
  2.2 73.5 %copy-start.2 = (f32[256,256]{1,0:T(8,128)S(1)}, f32[256,256]{1,0:T(8,128)}, u32[]{:S(2)}) copy-start(f32[256,256]{1,0:T(8,128)} %constant.14.clone.refs_11_) | copy-start | bytes 786436
  2.2 6.6 %collective-permute-start = (bf16[64,256]{1,0:T(8,128)(2,1)S(1)}, bf16[64,256]{1,0:T(8,128)(2,1)S(1)}, u32[]{:S(2)}, u32[]{:S(2)}) collective-permute-start(bf16[64,256]{1,0:T(8,128)(2,1)S(1)} %get-tuple-element.54), channel_id=1, source_target_pairs={{0,4},{4,8},{8,12},{12,16},{16,20},{20,24},{24,28},{1,5},{5,9},{9,... | collective-permute-start | bytes 98312 | tf_op jit(solution)/shard_map/ppermute | solution.py:358
  8.8 15.3 %collective-permute-start.1 = (bf16[8,128,256]{2,1,0:T(8,128)(2,1)S(1)}, bf16[8,128,256]{2,1,0:T(8,128)(2,1)S(1)}, u32[]{:S(2)}, u32[]{:S(2)}) collective-permute-start(bf16[8,128,256]{2,1,0:T(8,128)(2,1)S(1)} %slice.3), channel_id=1, source_target_pairs={{0,4},{4,8},{8,12},{12,16},{16,20},{20,24},{24,28},{1,5},{5,9},{9,... | collective-permute-start | bytes 1572872 | tf_op jit(solution)/shard_map/ppermute | solution.py:359
  13.8 1.0 %copy-start.3 = (f32[512,256]{1,0:T(8,128)S(1)}, f32[512,256]{1,0:T(8,128)}, u32[]{:S(2)}) copy-start(f32[512,256]{1,0:T(8,128)} %constant.13.clone.refs_4_) | copy-start | bytes 1572868
  14.8 0.7 copy-start.4
  17.4 16.0 %all-to-all-start = ((bf16[8,4,48,128]{3,2,1,0:T(8,128)(2,1)}), bf16[8,4,48,128]{3,2,1,0:T(8,128)(2,1)S(1)}, u32[]{:S(2)}, u32[]{:S(2)}) async-start(bf16[8,4,48,128]{3,2,1,0:T(8,128)(2,1)} %get-tuple-element.55), calls=%async_computation | async-start | bytes 786432 | tf_op jit(solution)/shard_map/all_to_all | solution.py:361
  24.1 1.9 %copy-start.1 = (bf16[8,128,1536]{2,1,0:T(8,128)(2,1)S(1)}, bf16[8,128,1536]{2,1,0:T(8,128)(2,1)}, u32[]{:S(2)}) copy-start(bf16[8,128,1536]{2,1,0:T(8,128)(2,1)} %refs_1_.1) | copy-start | bytes 9437188
  33.4 19.6 %collective-permute-start.3 = (bf16[8,4,48,128]{3,2,1,0:T(8,128)(2,1)S(1)}, bf16[8,4,48,128]{3,2,1,0:T(8,128)(2,1)S(1)}, u32[]{:S(2)}, u32[]{:S(2)}) collective-permute-start(bf16[8,4,48,128]{3,2,1,0:T(8,128)(2,1)S(1)} %all-to-all-done.refs_1_), channel_id=1, source_target_pairs={{0,1},{1,0},{2,3},{3,2},{4,5},{5,4},{6,7},{7,6},{8,9},{9,8},{10,11... | collective-permute-start | bytes 1179656 | tf_op jit(solution)/shard_map/ppermute | solution.py:340
  33.4 11.9 %collective-permute-start.5 = (bf16[384,128]{1,0:T(8,128)(2,1)S(1)}, bf16[384,128]{1,0:T(8,128)(2,1)S(1)}, u32[]{:S(2)}, u32[]{:S(2)}) collective-permute-start(bf16[384,128]{1,0:T(8,128)(2,1)S(1)} %get-tuple-element.79), channel_id=1, source_target_pairs={{0,28},{4,24},{8,20},{12,16},{16,12},{20,8},{24,4},{28,0},{1,29},{... | collective-permute-start | bytes 294920 | tf_op jit(solution)/shard_map/ppermute | solution.py:340
  38.5 6.9 %collective-permute-start.6 = (bf16[384,128]{1,0:T(8,128)(2,1)S(1)}, bf16[384,128]{1,0:T(8,128)(2,1)S(1)}, u32[]{:S(2)}, u32[]{:S(2)}) collective-permute-start(bf16[384,128]{1,0:T(8,128)(2,1)S(1)} %get-tuple-element.80), channel_id=1, source_target_pairs={{0,24},{4,28},{8,16},{12,20},{16,8},{20,12},{24,0},{28,4},{1,25},{... | collective-permute-start | bytes 294920 | tf_op jit(solution)/shard_map/ppermute | solution.py:340
  39.1 13.9 %collective-permute-start.7 = (bf16[384,128]{1,0:T(8,128)(2,1)S(1)}, bf16[384,128]{1,0:T(8,128)(2,1)S(1)}, u32[]{:S(2)}, u32[]{:S(2)}) collective-permute-start(bf16[384,128]{1,0:T(8,128)(2,1)S(1)} %get-tuple-element.81), channel_id=1, source_target_pairs={{0,20},{4,16},{8,28},{12,24},{16,4},{20,0},{24,12},{28,8},{1,21},{... | collective-permute-start | bytes 294920 | tf_op jit(solution)/shard_map/ppermute | solution.py:340
  43.8 13.1 %collective-permute-start.4 = (bf16[8,4,48,128]{3,2,1,0:T(8,128)(2,1)S(1)}, bf16[8,4,48,128]{3,2,1,0:T(8,128)(2,1)S(1)}, u32[]{:S(2)}, u32[]{:S(2)}) collective-permute-start(bf16[8,4,48,128]{3,2,1,0:T(8,128)(2,1)S(1)} %all-to-all-done.refs_1_), channel_id=1, source_target_pairs={{0,2},{1,3},{2,0},{3,1},{4,6},{5,7},{6,4},{7,5},{8,10},{9,11},{10,... | collective-permute-start | bytes 1179656 | tf_op jit(solution)/shard_map/ppermute | solution.py:340
  53.0 14.5 %collective-permute-start.8 = (bf16[8,4,48,128]{3,2,1,0:T(8,128)(2,1)S(1)}, bf16[8,4,48,128]{3,2,1,0:T(8,128)(2,1)S(1)}, u32[]{:S(2)}, u32[]{:S(2)}) collective-permute-start(bf16[8,4,48,128]{3,2,1,0:T(8,128)(2,1)S(1)} %collective-permute-done.3.refs_2_), channel_id=1, source_target_pairs={{0,2},{1,3},{2,0},{3,1},{4,6},{5,7},{6,4},{7,5},{8,10},{9,11},{10,... | collective-permute-start | bytes 1179656 | tf_op jit(solution)/shard_map/ppermute | solution.py:340
  54.5 7.1 %collective-permute-start.16 = (bf16[384,128]{1,0:T(8,128)(2,1)S(1)}, bf16[384,128]{1,0:T(8,128)(2,1)S(1)}, u32[]{:S(2)}, u32[]{:S(2)}) collective-permute-start(bf16[384,128]{1,0:T(8,128)(2,1)S(1)} %get-tuple-element.96), channel_id=1, source_target_pairs={{0,16},{4,20},{8,24},{12,28},{16,0},{20,4},{24,8},{28,12},{1,17},{... | collective-permute-start | bytes 294920 | tf_op jit(solution)/shard_map/ppermute | solution.py:340
  54.5 9.4 %collective-permute-start.14 = (bf16[384,128]{1,0:T(8,128)(2,1)S(1)}, bf16[384,128]{1,0:T(8,128)(2,1)S(1)}, u32[]{:S(2)}, u32[]{:S(2)}) collective-permute-start(bf16[384,128]{1,0:T(8,128)(2,1)S(1)} %get-tuple-element.93), channel_id=1, source_target_pairs={{0,12},{4,8},{8,4},{12,0},{16,28},{20,24},{24,20},{28,16},{1,13},{... | collective-permute-start | bytes 294920 | tf_op jit(solution)/shard_map/ppermute | solution.py:340
  56.9 10.7 %collective-permute-start.12 = (bf16[384,128]{1,0:T(8,128)(2,1)}, bf16[384,128]{1,0:T(8,128)(2,1)S(1)}, u32[]{:S(2)}, u32[]{:S(2)}) collective-permute-start(bf16[384,128]{1,0:T(8,128)(2,1)} %get-tuple-element.90), channel_id=1, source_target_pairs={{0,8},{4,12},{8,0},{12,4},{16,24},{20,28},{24,16},{28,20},{1,9},{5... | collective-permute-start | bytes 294920 | tf_op jit(solution)/shard_map/ppermute | solution.py:340
  59.6 8.0 %collective-permute-start.2 = (bf16[384,128]{1,0:T(8,128)(2,1)}, bf16[384,128]{1,0:T(8,128)(2,1)S(1)}, u32[]{:S(2)}, u32[]{:S(2)}) collective-permute-start(bf16[384,128]{1,0:T(8,128)(2,1)} %get-tuple-element.77), channel_id=1, source_target_pairs={{0,4},{4,0},{8,12},{12,8},{16,20},{20,16},{24,28},{28,24},{1,5},{5... | collective-permute-start | bytes 294920 | tf_op jit(solution)/shard_map/ppermute | solution.py:340
  61.6 10.8 %collective-permute-start.18 = (bf16[384,128]{1,0:T(8,128)(2,1)}, bf16[384,128]{1,0:T(8,128)(2,1)S(1)}, u32[]{:S(2)}, u32[]{:S(2)}) collective-permute-start(bf16[384,128]{1,0:T(8,128)(2,1)} %get-tuple-element.99), channel_id=1, source_target_pairs={{0,28},{4,24},{8,20},{12,16},{16,12},{20,8},{24,4},{28,0},{1,29},{... | collective-permute-start | bytes 294920 | tf_op jit(solution)/shard_map/ppermute | solution.py:340
  63.9 9.2 %collective-permute-start.17 = (bf16[384,128]{1,0:T(8,128)(2,1)S(1)}, bf16[384,128]{1,0:T(8,128)(2,1)S(1)}, u32[]{:S(2)}, u32[]{:S(2)}) collective-permute-start(bf16[384,128]{1,0:T(8,128)(2,1)S(1)} %get-tuple-element.97), channel_id=1, source_target_pairs={{0,24},{4,28},{8,16},{12,20},{16,8},{20,12},{24,0},{28,4},{1,25},{... | collective-permute-start | bytes 294920 | tf_op jit(solution)/shard_map/ppermute | solution.py:340
  67.6 13.6 %collective-permute-start.9 = (bf16[384,128]{1,0:T(8,128)(2,1)S(1)}, bf16[384,128]{1,0:T(8,128)(2,1)S(1)}, u32[]{:S(2)}, u32[]{:S(2)}) collective-permute-start(bf16[384,128]{1,0:T(8,128)(2,1)S(1)} %get-tuple-element.83), channel_id=1, source_target_pairs={{0,4},{4,0},{8,12},{12,8},{16,20},{20,16},{24,28},{28,24},{1,5},{5... | collective-permute-start | bytes 294920 | tf_op jit(solution)/shard_map/ppermute | solution.py:340
  68.5 12.7 %collective-permute-start.10 = (bf16[384,128]{1,0:T(8,128)(2,1)S(1)}, bf16[384,128]{1,0:T(8,128)(2,1)S(1)}, u32[]{:S(2)}, u32[]{:S(2)}) collective-permute-start(bf16[384,128]{1,0:T(8,128)(2,1)S(1)} %get-tuple-element.85), channel_id=1, source_target_pairs={{0,8},{4,12},{8,0},{12,4},{16,24},{20,28},{24,16},{28,20},{1,9},{5... | collective-permute-start | bytes 294920 | tf_op jit(solution)/shard_map/ppermute | solution.py:340
  68.5 12.7 %collective-permute-start.11 = (bf16[384,128]{1,0:T(8,128)(2,1)S(1)}, bf16[384,128]{1,0:T(8,128)(2,1)S(1)}, u32[]{:S(2)}, u32[]{:S(2)}) collective-permute-start(bf16[384,128]{1,0:T(8,128)(2,1)S(1)} %get-tuple-element.87), channel_id=1, source_target_pairs={{0,12},{4,8},{8,4},{12,0},{16,28},{20,24},{24,20},{28,16},{1,13},{... | collective-permute-start | bytes 294920 | tf_op jit(solution)/shard_map/ppermute | solution.py:340
  72.4 9.4 %collective-permute-start.13 = (bf16[384,128]{1,0:T(8,128)(2,1)S(1)}, bf16[384,128]{1,0:T(8,128)(2,1)S(1)}, u32[]{:S(2)}, u32[]{:S(2)}) collective-permute-start(bf16[384,128]{1,0:T(8,128)(2,1)S(1)} %get-tuple-element.91), channel_id=1, source_target_pairs={{0,16},{4,20},{8,24},{12,28},{16,0},{20,4},{24,8},{28,12},{1,17},{... | collective-permute-start | bytes 294920 | tf_op jit(solution)/shard_map/ppermute | solution.py:340
  73.1 9.5 %collective-permute-start.15 = (bf16[384,128]{1,0:T(8,128)(2,1)S(1)}, bf16[384,128]{1,0:T(8,128)(2,1)S(1)}, u32[]{:S(2)}, u32[]{:S(2)}) collective-permute-start(bf16[384,128]{1,0:T(8,128)(2,1)S(1)} %get-tuple-element.94), channel_id=1, source_target_pairs={{0,20},{4,16},{8,28},{12,24},{16,4},{20,0},{24,12},{28,8},{1,21},{... | collective-permute-start | bytes 294920 | tf_op jit(solution)/shard_map/ppermute | solution.py:340
